TPU v7x, 512 devices: a whole 4x8x8 slice. The times are simulated.
512 devices in a mesh: band: 16 (over z_hi, y), domain: 32 (over x, z_lo, core).
Axes of the slice: x: 4, y: 8, z: 8 (z_hi: 2, z_lo: 4; z = z_hi * 4 + z_lo), core: 2. Of those that a mesh axis runs over, the one named last changes fastest.
Arguments:
- orbitals: float32 [128, 128, 64, 128], P('band', 'domain'), may hold values from -160 to 160
- potential: float32 [128, 64, 128], P('domain'), may hold values from -2.5 to 0.5
Outputs:
- basis_out: float32 [128, 128, 64, 128], P('band', 'domain')
- residual: float32 [128, 128, 64, 128], P('band', 'domain')
All inputs are finite; a program needn't handle non-finite values.
Results may differ from a plain program's by a relative error of at most 0.00015.
Values sent between devices are 32-bit elements; how exact they have to be, the bound alone decides.
No kernel may reach another device: no remote copies, remote signals or barrier semaphores. Data moves between devices by JAX's collectives and lax.ppermute only.
A program may use at most 128 MiB of HBM per device.

v0:
```python
import jax
import jax.numpy as jnp
from jax import lax
from jax.sharding import PartitionSpec as P

STEPS = 2


stencil_weights = (-205.0 / 72.0, 8.0 / 5.0, -1.0 / 5.0, 8.0 / 315.0, -1.0 / 560.0)


def extended(cells, sides, width):
    for axis, dim in sides:
        count = lax.axis_size(axis)
        head = lax.slice_in_dim(cells, 0, width, axis=dim)
        tail = lax.slice_in_dim(cells, cells.shape[dim] - width, cells.shape[dim], axis=dim)
        cells = jnp.concatenate(
            [
                lax.ppermute(tail, axis, [(i, (i + 1) % count) for i in range(count)]),
                cells,
                lax.ppermute(head, axis, [((i + 1) % count, i) for i in range(count)]),
            ],
            axis=dim,
        )
    return cells


def spread(block, axis, holder):
    block = jnp.where(lax.axis_index(axis) == holder, block, jnp.zeros_like(block))
    return lax.psum(block, axis)


def cholesky_lower(matrix):
    size_now = matrix.shape[0]
    positions = jnp.arange(size_now, dtype=jnp.int32)

    def column_step(column_index, lower_now):
        unit = (positions == column_index).astype(matrix.dtype)
        row_part = jnp.dot(unit, lower_now, precision=lax.Precision.HIGHEST)
        column_part = jnp.dot(matrix, unit, precision=lax.Precision.HIGHEST)
        partial_column = column_part - jnp.dot(lower_now, row_part, precision=lax.Precision.HIGHEST)
        pivot = jnp.sqrt(jnp.dot(unit, partial_column, precision=lax.Precision.HIGHEST))
        fresh = jnp.where(
            positions >= column_index, partial_column / pivot, jnp.zeros_like(partial_column)
        )
        return lower_now + fresh[:, None] * unit[None, :]

    return lax.fori_loop(0, size_now, column_step, jnp.zeros_like(matrix))


def lower_inverse(lower_factor):
    size_now = lower_factor.shape[0]
    positions = jnp.arange(size_now, dtype=jnp.int32)

    def row_step(row_index, inverse_now):
        unit = (positions == row_index).astype(lower_factor.dtype)
        lower_row = jnp.dot(unit, lower_factor, precision=lax.Precision.HIGHEST)
        pivot = jnp.dot(lower_row, unit, precision=lax.Precision.HIGHEST)
        fresh = (unit - jnp.dot(lower_row, inverse_now, precision=lax.Precision.HIGHEST)) / pivot
        return inverse_now + unit[:, None] * fresh[None, :]

    return lax.fori_loop(0, size_now, row_step, jnp.zeros_like(lower_factor))


def cross_gram(left_rows, right_rows, cells_total):
    return (
        lax.dot_general(
            left_rows, right_rows, (((1,), (1,)), ((), ())), precision=lax.Precision.HIGHEST
        )
        / cells_total
    )


def combine_rows(weights, rows):
    return lax.dot_general(weights, rows, (((0,), (0,)), ((), ())), precision=lax.Precision.HIGHEST)


def lower_solve(inverse_factor, rows):
    return jnp.dot(inverse_factor, rows, precision=lax.Precision.HIGHEST)


def apply_hamiltonian(orbital_field, potential):
    padded = extended(orbital_field, (("domain", 1),), 4)
    slab_width = orbital_field.shape[1]
    laplacian = 3.0 * stencil_weights[0] * orbital_field
    for offset in range(1, 5):
        weight_now = stencil_weights[offset]
        beside = (
            padded[:, 4 + offset : 4 + offset + slab_width]
            + padded[:, 4 - offset : 4 - offset + slab_width]
        )
        beside = beside + jnp.roll(orbital_field, offset, 2) + jnp.roll(orbital_field, -offset, 2)
        beside = beside + jnp.roll(orbital_field, offset, 3) + jnp.roll(orbital_field, -offset, 3)
        laplacian = laplacian + weight_now * beside
    return -0.5 * laplacian + potential[None] * orbital_field


def send_owner(block_rows, step_index):
    return (spread(block_rows, "band", step_index), None)


def local(orbitals, potential):
    blocks, slab_width, rows_y, rows_z = orbitals.shape
    cells_total = float(slab_width * rows_y * rows_z * lax.axis_size("domain"))
    band_index = lax.axis_index("band")
    current = orbitals.reshape(blocks, -1)
    applied = None
    for step_index in range(STEPS):
        gram = lax.psum(cross_gram(current, current, cells_total), "domain")
        inverse_factor = lower_inverse(cholesky_lower(gram))
        local_basis = lower_solve(inverse_factor, current)
        basis, applied_basis = send_owner(local_basis, step_index)
        correlation = lax.psum(cross_gram(basis, current, cells_total), "domain")
        later = band_index > step_index
        owner = band_index == step_index
        projected = current - combine_rows(correlation, basis)
        current = jnp.where(later, projected, jnp.where(owner, basis, current))
    applied = apply_hamiltonian(current.reshape(orbitals.shape), potential).reshape(blocks, -1)
    block_gram, theta = lax.psum(
        (cross_gram(current, current, cells_total), cross_gram(current, applied, cells_total)),
        "domain",
    )
    inverse_block = lower_inverse(cholesky_lower(block_gram))
    halfway = lower_solve(inverse_block, theta)
    coeff = jnp.dot(inverse_block.T, halfway, precision=lax.Precision.HIGHEST)
    residual = applied - combine_rows(coeff, current)
    return (current.reshape(orbitals.shape), residual.reshape(orbitals.shape))


def solution(mesh):
    return jax.shard_map(
        local,
        mesh=mesh,
        in_specs=(P("band", "domain", None, None), P("domain", None, None)),
        out_specs=(P("band", "domain", None, None), P("band", "domain", None, None)),
        check_vma=False,
    )
```

profile of v0, /device:TPU:1, one launch (start us, length us, event | category | flops | bytes accessed | tf_op | source)
XLA Modules:
  0.0 903.1 jit_solution(14876765629694430939)
XLA Ops:
  7.2 4.6 fusion.95
  11.9 73.6 %psum.56 = f32[8,8]{1,0:T(8,128)S(1)} all-reduce(f32[8,8]{1,0:T(8,128)S(1)} %fusion.95), channel_id=1, replica_groups=mesh['band'=16,'domain'=32] {'domain'}, use_global_device_ids=true, to_apply=%region_0.0 | all-reduce | flops 64 | bytes 512 | tf_op jit(solution)/shard_map/psum | solution.py:109
  85.5 14.2 %while.90 = (s32[]{:T(128)}, f32[8,8]{1,0:T(8,128)S(1)}, f32[8,8]{1,0:T(8,128)S(1)}, s32[]{:T(128)}, s32[]{:T(128)}) while((s32[]{:T(128)}, f32[8,8]{1,0:T(8,128)S(1)}, f32[8,8]{1,0:T(8,128)S(1)}, s32[]{:T(128)}, s32[]{:T(128)}) %tuple.215), condition=%wide.region_2.3_spmd.clone.clone, body=%wide.region_1.2_spmd.clone.clone.sunk | while | flops 2714 | bytes 1705 | solution.py:48
  99.6 12.7 %while.87 = (s32[]{:T(128)}, f32[8,8]{1,0:T(8,128)S(1)}, f32[8,8]{1,0:T(8,128)S(1)}, s32[]{:T(128)}, s32[]{:T(128)}) while((s32[]{:T(128)}, f32[8,8]{1,0:T(8,128)S(1)}, f32[8,8]{1,0:T(8,128)S(1)}, s32[]{:T(128)}, s32[]{:T(128)}) %tuple.218), condition=%wide.region_4.5_spmd.clone, body=%wide.region_3.4_spmd.clone.sunk | while | flops 1874 | bytes 1308 | solution.py:62
  112.3 2.5 convolution_select_fusion.1
  114.9 190.7 %all-reduce.4.cloned.1.call-done = f32[8,32768]{1,0:T(8,128)} async-done(((f32[8,32768]{1,0:T(8,128)}), f32[8,32768]{1,0:T(8,128)}) %all-reduce.4.cloned.1.call-update) | async-done | bytes 1048592 | tf_op jit(solution)/shard_map/psum | solution.py:30
  305.6 3.8 convolution_multiply_fusion.4
  309.4 77.4 %psum.58 = f32[8,8]{1,0:T(8,128)S(1)} all-reduce(f32[8,8]{1,0:T(8,128)S(1)} %convolution_multiply_fusion.4), channel_id=1, replica_groups=mesh['band'=16,'domain'=32] {'domain'}, use_global_device_ids=true, to_apply=%region_6.7 | all-reduce | flops 64 | bytes 512 | tf_op jit(solution)/shard_map/psum | solution.py:113
  388.4 2.4 convolution_multiply_fusion.3
  390.8 67.5 %psum.59 = f32[8,8]{1,0:T(8,128)S(1)} all-reduce(f32[8,8]{1,0:T(8,128)S(1)} %convolution_multiply_fusion.3), channel_id=1, replica_groups=mesh['band'=16,'domain'=32] {'domain'}, use_global_device_ids=true, to_apply=%region_7.8 | all-reduce | flops 64 | bytes 512 | tf_op jit(solution)/shard_map/psum | solution.py:109
  458.4 14.3 %while.91 = (s32[]{:T(128)}, f32[8,8]{1,0:T(8,128)S(1)}, f32[8,8]{1,0:T(8,128)S(1)}, s32[]{:T(128)}, s32[]{:T(128)}) while((s32[]{:T(128)}, f32[8,8]{1,0:T(8,128)S(1)}, f32[8,8]{1,0:T(8,128)S(1)}, s32[]{:T(128)}, s32[]{:T(128)}) %tuple.221), condition=%wide.region_9.10_spmd.clone.clone, body=%wide.region_8.9_spmd.clone.clone.sunk | while | flops 2714 | bytes 1705 | solution.py:48
  472.7 12.7 %while.88 = (s32[]{:T(128)}, f32[8,8]{1,0:T(8,128)S(1)}, f32[8,8]{1,0:T(8,128)S(1)}, s32[]{:T(128)}, s32[]{:T(128)}) while((s32[]{:T(128)}, f32[8,8]{1,0:T(8,128)S(1)}, f32[8,8]{1,0:T(8,128)S(1)}, s32[]{:T(128)}, s32[]{:T(128)}) %tuple.224), condition=%wide.region_11.12_spmd.clone, body=%wide.region_10.11_spmd.clone.sunk | while | flops 1874 | bytes 1308 | solution.py:62
  487.4 183.8 %all-reduce.6.cloned.1.call-done = f32[8,32768]{1,0:T(8,128)} async-done(((f32[8,32768]{1,0:T(8,128)}), f32[8,32768]{1,0:T(8,128)}) %all-reduce.6.cloned.1.call-update) | async-done | bytes 1048592 | tf_op jit(solution)/shard_map/psum | solution.py:30
  671.2 3.8 convolution_multiply_fusion.2
  675.0 77.4 %psum.61 = f32[8,8]{1,0:T(8,128)S(1)} all-reduce(f32[8,8]{1,0:T(8,128)S(1)} %convolution_multiply_fusion.2), channel_id=1, replica_groups=mesh['band'=16,'domain'=32] {'domain'}, use_global_device_ids=true, to_apply=%region_13.14 | all-reduce | flops 64 | bytes 512 | tf_op jit(solution)/shard_map/psum | solution.py:113
  761.1 2.5 collective-permute-start
  763.6 3.2 collective-permute-start.1
  766.9 2.4 convolution_multiply_fusion.1
  775.5 10.7 %collective-permute-done = f32[8,4,64,128]{3,0,2,1:T(8,128)S(1)} collective-permute-done((f32[8,4,64,128]{3,0,2,1:T(8,128)S(1)}, f32[8,4,64,128]{3,0,2,1:T(8,128)S(1)}, u32[]{:S(2)}, u32[]{:S(2)}) %collective-permute-start) | collective-permute-done | bytes 1048608 | tf_op jit(solution)/shard_map/ppermute | solution.py:21
  787.8 8.6 fusion.107
  796.4 2.5 convolution_multiply_fusion
  798.9 67.8 %all-reduce = (f32[8,8]{1,0:T(8,128)S(1)}, f32[8,8]{1,0:T(8,128)S(1)}) all-reduce(f32[8,8]{1,0:T(8,128)S(1)} %convolution_multiply_fusion.1, f32[8,8]{1,0:T(8,128)S(1)} %convolution_multiply_fusion), channel_id=1, replica_groups=mesh['band'=16,'domain'=32] {'domain'}, use_global_device_ids=true, to_apply=%region_14.15 | all-reduce | flops 128 | bytes 1024 | tf_op jit(solution)/shard_map/psum | solution.py:119
  866.7 14.3 %while.92 = (s32[]{:T(128)}, f32[8,8]{1,0:T(8,128)S(1)}, f32[8,8]{1,0:T(8,128)S(1)}, s32[]{:T(128)}, s32[]{:T(128)}) while((s32[]{:T(128)}, f32[8,8]{1,0:T(8,128)S(1)}, f32[8,8]{1,0:T(8,128)S(1)}, s32[]{:T(128)}, s32[]{:T(128)}) %tuple.227), condition=%wide.region_16.17_spmd.clone.clone, body=%wide.region_15.16_spmd.clone.clone.sunk | while | flops 2714 | bytes 1705 | solution.py:48
  881.0 12.7 %while.89 = (s32[]{:T(128)}, f32[8,8]{1,0:T(8,128)S(1)}, f32[8,8]{1,0:T(8,128)S(1)}, s32[]{:T(128)}, s32[]{:T(128)}) while((s32[]{:T(128)}, f32[8,8]{1,0:T(8,128)S(1)}, f32[8,8]{1,0:T(8,128)S(1)}, s32[]{:T(128)}, s32[]{:T(128)}) %tuple.230), condition=%wide.region_18.19_spmd.clone, body=%wide.region_17.18_spmd.clone.sunk | while | flops 1874 | bytes 1308 | solution.py:62
  (287 shorter events, 86.6 us)
Async XLA Ops:
  7.2 105.2 %copy-start = (f32[8,4,64,128]{3,2,1,0:T(8,128)S(1)}, f32[8,4,64,128]{3,2,1,0:T(8,128)}, u32[]{:S(2)}) copy-start(f32[8,4,64,128]{3,2,1,0:T(8,128)} %param.14) | copy-start | bytes 3145732
  7.2 298.4 %all-reduce.4.cloned.1.call-start = ((), (), s32[]{:S(2)}) async-start(), calls=%async_computation | async-start | bytes 2097152 | tf_op jit(solution)/shard_map/psum | solution.py:30
  114.8 556.4 %all-reduce.6.cloned.1.call-start = ((), (), s32[]{:S(2)}) async-start(), calls=%async_computation.1 | async-start | bytes 2097152 | tf_op jit(solution)/shard_map/psum | solution.py:30
  305.6 81.3 %copy-start.1 = (f32[8,32768]{1,0:T(8,128)S(1)}, f32[8,32768]{1,0:T(8,128)}, u32[]{:S(2)}) copy-start(f32[8,32768]{1,0:T(8,128)} %all-reduce.4.cloned.1.call-done) | copy-start | bytes 3145732
  671.2 81.2 %copy-start.2 = (f32[8,32768]{1,0:T(8,128)S(1)}, f32[8,32768]{1,0:T(8,128)}, u32[]{:S(2)}) copy-start(f32[8,32768]{1,0:T(8,128)} %all-reduce.6.cloned.1.call-done) | copy-start | bytes 3145732
  761.1 25.1 %collective-permute-start = (f32[8,4,64,128]{3,0,2,1:T(8,128)S(1)}, f32[8,4,64,128]{3,0,2,1:T(8,128)S(1)}, u32[]{:S(2)}, u32[]{:S(2)}) collective-permute-start(f32[8,4,64,128]{3,0,2,1:T(8,128)S(1)} %bitcast.225), channel_id=1, source_target_pairs={{1,0},{2,1},{3,2},{4,3},{5,4},{6,5},{7,6},{8,7},{9,8},{10,9},{11,1... | collective-permute-start | bytes 3145736 | tf_op jit(solution)/shard_map/ppermute | solution.py:21
  763.6 23.2 %collective-permute-start.1 = (f32[8,4,64,128]{3,0,2,1:T(8,128)S(1)}, f32[8,4,64,128]{3,0,2,1:T(8,128)S(1)}, u32[]{:S(2)}, u32[]{:S(2)}) collective-permute-start(f32[8,4,64,128]{3,0,2,1:T(8,128)S(1)} %bitcast.226), channel_id=1, source_target_pairs={{0,1},{1,2},{2,3},{3,4},{4,5},{5,6},{6,7},{7,8},{8,9},{9,10},{10,1... | collective-permute-start | bytes 3145736 | tf_op jit(solution)/shard_map/ppermute | solution.py:19
  773.8 13.9 %copy-start.5 = (f32[4,64,128]{2,1,0:T(8,128)S(1)}, f32[4,64,128]{2,1,0:T(8,128)}, u32[]{:S(2)}) copy-start(f32[4,64,128]{2,1,0:T(8,128)} %param.15) | copy-start | bytes 393220
  786.2 1.0 copy-start.3
  786.8 1.0 copy-start.4
Sparse Core Ops, SparseCore 0:
  114.9 190.6 all-reduce.3
  487.5 183.6 all-reduce.5
where the time goes:
time: 906 us; the launch traced here: 903 us
  waiting for transfers between devices  386 us (43%)
  blocking collectives  364 us (40%)
  matrix products  88.1 us (10%)
  loops' own time  16.9 us (2%)
  local copies, waits for them, and re-layouts  15.9 us (2%)
  between operations  14.2 us (2%)
  other arithmetic  12.5 us (1%)
    psum x2, waiting for transfers between devices, spread(): return lax.psum(block, axis)  375 us
    psum x2, blocking collectives, local(): correlation = lax.psum(cross_gram(basis, current, cells_total), 'domain')  155 us
    psum x2, blocking collectives, local(): gram = lax.psum(cross_gram(current, current, cells_total), 'domain')  141 us
    psum x1, blocking collectives, local(): lax.psum((cross_gram(current, current, cells_total), cross_gram(current,...  67.8 us
    dot_general x6, matrix products, cross_gram(): lax.dot_general(left_rows, right_rows, (((1,), (1,)), ((), ())), precisio...  19.5 us
    dot_general x24, matrix products, row_step(): jnp.dot(lower_row, inverse_now, precision=lax.Precision.HIGHEST)  18.5 us
  transfers between devices with their start and end apart: 4, of which 4 were waited for; matrix products, arithmetic and copies ran while one was open for 1% of the time, Pallas kernels for 0%

commit v1 on v0

v1 whole, which is shorter than its diff:
```python
import jax
import jax.numpy as jnp
from jax import lax
from jax.experimental import pallas as pl
from jax.experimental.pallas import tpu as pltpu
from jax.sharding import PartitionSpec as P

stencil_weights = (-205.0 / 72.0, 8.0 / 5.0, -1.0 / 5.0, 8.0 / 315.0, -1.0 / 560.0)
BLK = 8
RING = 8
F32 = jnp.float32
VMEM = pl.BlockSpec(memory_space=pltpu.VMEM)
SMEM = pl.BlockSpec(memory_space=pltpu.SMEM)


def call(kernel, outs, scratch=(), specs=None, flops=0, bytes_moved=0):
    return pl.pallas_call(
        kernel,
        out_shape=outs,
        in_specs=specs,
        out_specs=jax.tree.map(lambda _: VMEM, outs),
        scratch_shapes=scratch,
        compiler_params=pltpu.CompilerParams(vmem_limit_bytes=32 * 1024 * 1024),
        cost_estimate=pl.CostEstimate(flops=flops, bytes_accessed=bytes_moved, transcendentals=0),
    )


def lanes():
    return lax.broadcasted_iota(jnp.int32, (8, 128), 1)


def subs():
    return lax.broadcasted_iota(jnp.int32, (8, 128), 0)


def pair_sums(first, second, chunks, symmetric):
    lane = lanes()
    result = jnp.zeros((8, 128), F32)
    for low in (0, 4):
        partners = second[low:] if symmetric else second

        def body(c, sums, low=low, partners=partners):
            left = [load(c) for load in first[low : low + 4]]
            right = [load(c) for load in partners]
            return tuple(
                s + left[n // len(partners)] * right[n % len(partners)]
                for n, s in enumerate(sums)
            )

        zero = jnp.zeros((8, 128), F32)
        sums = lax.fori_loop(0, chunks, body, (zero,) * (4 * len(partners)))
        for i in range(4):
            rows = [
                jnp.sum(s, axis=0, keepdims=True)
                for s in sums[i * len(partners) : (i + 1) * len(partners)]
            ]
            rows = [jnp.zeros((1, 128), F32)] * (8 - len(rows)) + rows
            column = jnp.sum(jnp.concatenate(rows, axis=0), axis=1, keepdims=True)
            result = jnp.where(lane == low + i, column, result)
    return result


def loader(ref, index):
    return lambda c: ref[index, pl.ds(pl.multiple_of(c * 8, 8), 8), :]


def move(tile, source, target):
    lane = lanes()
    if source != target:
        tile = pltpu.roll(tile, (target - source) % 128, 1)
    return jnp.where((lane >= target) & (lane < target + 8), tile, 0.0)


def flipped(sums):
    return jnp.transpose(jnp.concatenate([sums, jnp.zeros((120, 128), F32)], axis=0))


def completed(sums, turned, slot):
    lane, sub = lanes(), subs()
    other = turned[8 * slot : 8 * slot + 8, :]
    if slot:
        other = pltpu.roll(other, 8 * slot, 1)
    missing = (lane >= 8 * slot + 4) & (lane < 8 * slot + 8) & (sub < 4)
    return jnp.where(missing, other, sums)


def spread_lane(tile, k):
    return jnp.broadcast_to(tile[:, k : k + 1], (8, 128))


def rows_of(refs):
    return [(r, i) for r in refs for i in range(r.shape[0])]


def gram_kernel(*refs):
    *pieces, own, out = refs
    chunks = own.shape[1] // 8
    gathered = [loader(r, i) for r, i in rows_of(pieces)]
    low, high = gathered[:8], gathered[8:]
    block = [loader(own, i) for i in range(BLK)]
    total = jnp.zeros((8, 128), F32)
    tiles = (
        (low, low, True),
        (low, high, False),
        (low, block, False),
        (high, high, True),
        (high, block, False),
        (block, block, True),
    )
    for slot, (first, second, symmetric) in enumerate(tiles):
        total = total + move(pair_sums(first, second, chunks, symmetric), 0, 8 * slot)
    for n in range(out.shape[0]):
        out[n] = total


def combine_kernel(cells_total, band_ref, sums_ref, *refs):
    *pieces, own, out, splat = refs
    band = band_ref[0]
    lane, sub = lanes(), subs()
    sums = jnp.sum(sums_ref[...], axis=0) / cells_total
    turned = flipped(sums)
    w0 = (
        move(completed(sums, turned, 0), 0, 0)
        + move(turned[8:16, :], 0, 8)
        + move(turned[16:24, :], 0, 16)
    )
    w1 = (
        move(sums, 8, 0)
        + move(completed(sums, turned, 3), 24, 8)
        + move(turned[32:40, :], 0, 16)
    )
    w2 = (
        move(sums, 16, 0)
        + move(sums, 32, 8)
        + move(completed(sums, turned, 5), 40, 16)
        + jnp.where(lane == 40 + sub, 1.0, 0.0)
    )
    later = band >= 2
    second = band == 1

    def taken(position):
        place = position & 7
        return later | (second & (place >= 2) & (place <= 5))

    row_in = taken(sub)
    lane_in = (lane >= 16) | taken(lane)
    kept = row_in & lane_in
    w0 = jnp.where(lane < 24, jnp.where(kept, w0, jnp.where(lane == sub, 1.0, 0.0)), 0.0)
    w1 = jnp.where(lane < 24, jnp.where(kept, w1, jnp.where(lane == 8 + sub, 1.0, 0.0)), 0.0)
    w0 = w0 + jnp.where(lane == 24 + sub, 1.0, 0.0)
    w1 = w1 + jnp.where(lane == 32 + sub, 1.0, 0.0)
    w2 = jnp.where(lane_in, w2, 0.0)
    tiles = [w0, w1, w2]
    for k in range(16):
        v, s = divmod(k, 8)
        row = tiles[v][s : s + 1, :]
        row = row / jnp.broadcast_to(row[:, k : k + 1], (1, 128))
        row = jnp.broadcast_to(row, (8, 128))
        for u in range(v, 3):
            column = spread_lane(tiles[u], k)
            if u == v:
                column = jnp.where(sub > s, column, 0.0)
            tiles[u] = tiles[u] - column * row
    plain = tiles[2]
    scaled = plain
    for k in range(8):
        row = scaled[k : k + 1, :]
        row = row / jnp.broadcast_to(row[:, 16 + k : 17 + k], (1, 128))
        column = jnp.where(sub > k, spread_lane(scaled, 16 + k), 0.0)
        scaled = scaled - column * jnp.broadcast_to(row, (8, 128))
    pivots = jnp.sum(jnp.where(lane == 16 + sub, scaled, 0.0), axis=1, keepdims=True)
    scaled = scaled / jnp.sqrt(jnp.broadcast_to(pivots, (8, 128)))
    weights = jnp.where(later, plain, scaled)
    for c in range(24):
        splat[c] = spread_lane(weights, 24 + c)
    rows = rows_of(pieces) + [(own, i) for i in range(BLK)]

    def body(c, carry):
        part = pl.ds(pl.multiple_of(c * 16, 16), 16)
        inputs = [r[i, part, :] for r, i in rows]
        for i in range(BLK):
            total = splat[0, pl.ds(i, 1), :] * inputs[0]
            for n in range(1, 24):
                total = total + splat[n, pl.ds(i, 1), :] * inputs[n]
            out[i, part, :] = total
        return carry

    lax.fori_loop(0, own.shape[1] // 16, body, 0)


def inner_kernel(f_ref, v_ref, out, gram):
    def body(i, carry):
        layers = [f_ref[i, x] for x in range(4)]
        for x in range(4):
            here = layers[x]
            total = 3.0 * stencil_weights[0] * here
            for offset in range(1, 5):
                beside = pltpu.roll(here, offset, 0) + pltpu.roll(here, 64 - offset, 0)
                beside = beside + pltpu.roll(here, offset, 1) + pltpu.roll(here, 128 - offset, 1)
                if x + offset < 4:
                    beside = beside + layers[x + offset]
                if x - offset >= 0:
                    beside = beside + layers[x - offset]
                total = total + stencil_weights[offset] * beside
            out[i, x] = -0.5 * total + v_ref[x] * here
        return carry

    lax.fori_loop(0, BLK, body, 0)

    def row(i):
        return lambda c: f_ref[i, c // 8, pl.ds(pl.multiple_of((c % 8) * 8, 8), 8), :]

    rows = [row(i) for i in range(BLK)]
    gram[...] = pair_sums(rows, rows, 32, True)


def edge_kernel(f_ref, inner_ref, left_ref, right_ref, gram_ref, out, sums):
    def body(i, carry):
        for x in range(4):
            total = None
            for offset in range(1, 5):
                if x + offset >= 4:
                    term = stencil_weights[offset] * right_ref[i, x + offset - 4]
                    total = term if total is None else total + term
                if x - offset < 0:
                    term = stencil_weights[offset] * left_ref[i, x - offset + 4]
                    total = term if total is None else total + term
            out[i, x] = inner_ref[i, x] - 0.5 * total
        return carry

    lax.fori_loop(0, BLK, body, 0)

    def row(ref, i):
        return lambda c: ref[i, c // 8, pl.ds(pl.multiple_of((c % 8) * 8, 8), 8), :]

    theta = pair_sums(
        [row(out, i) for i in range(BLK)], [row(f_ref, i) for i in range(BLK)], 32, False
    )
    total = gram_ref[...] + move(theta, 0, 8)
    for n in range(sums.shape[0]):
        sums[n] = total


def residual_kernel(cells_total, sums_ref, f_ref, h_ref, out, splat):
    lane, sub = lanes(), subs()
    sums = jnp.sum(sums_ref[...], axis=0) / cells_total
    work = completed(sums, flipped(sums), 0)
    for k in range(8):
        row = work[k : k + 1, :]
        row = jnp.broadcast_to(row / jnp.broadcast_to(row[:, k : k + 1], (1, 128)), (8, 128))
        work = jnp.where(sub == k, row, work - spread_lane(work, k) * row)
    for j in range(8):
        splat[j] = spread_lane(work, 8 + j)

    def body(c, carry):
        part = pl.ds(pl.multiple_of(c * 16, 16), 16)
        inputs = [f_ref[i, part, :] for i in range(BLK)]
        for j in range(BLK):
            total = h_ref[j, part, :]
            for i in range(BLK):
                total = total - splat[j, pl.ds(i, 1), :] * inputs[i]
            out[j, part, :] = total
        return carry

    lax.fori_loop(0, f_ref.shape[1] // 16, body, 0)


def domain_parts(copies):
    return lax.all_to_all(copies, "domain", 0, 0)


def ring_shift(block, step):
    pairs = [(z * RING + y, z * RING + (y + step) % RING) for z in range(2) for y in range(RING)]
    return lax.ppermute(block, "band", pairs)


def local(orbitals, potential):
    blocks, slab_width, rows_y, rows_z = orbitals.shape
    domain = lax.axis_size("domain")
    cells_total = float(slab_width * rows_y * rows_z * domain)
    band = lax.axis_index("band")
    flat = (blocks, slab_width * rows_y, rows_z)
    own = orbitals.reshape(flat)
    quarters = [own[2 * k : 2 * k + 2] for k in range(4)]
    piece = jnp.where(band < 2, quarters[0], 0.0)
    for k in (1, 3, 2):
        piece = piece + lax.ppermute(quarters[k], "band", [(0, 2 * k), (1, 2 * k + 1)])
    crossed = lax.ppermute(piece, "band", [(y, y + RING) for y in range(RING)])
    piece = jnp.where(band < RING, piece, crossed)
    pieces = [piece]
    up = down = piece
    for _ in range(3):
        up, down = ring_shift(up, 1), ring_shift(down, -1)
        pieces += [up, down]
    pieces += [ring_shift(up[:1], 1), ring_shift(down[1:], -1)]

    big = flat[0] * flat[1] * flat[2]
    sums = call(
        gram_kernel,
        jax.ShapeDtypeStruct((domain, 8, 128), F32),
        specs=[VMEM] * 10,
        flops=40 * big,
        bytes_moved=12 * big,
    )(*pieces, own)
    sums = domain_parts(sums)
    basis = call(
        lambda *refs: combine_kernel(cells_total, *refs),
        jax.ShapeDtypeStruct(flat, F32),
        scratch=[pltpu.VMEM((24, 8, 128), F32)],
        specs=[SMEM] + [VMEM] * 11,
        flops=48 * big,
        bytes_moved=16 * big,
    )(band.reshape(1).astype(jnp.int32), sums, *pieces, own)
    field = basis.reshape(orbitals.shape)
    count = domain
    left = lax.ppermute(field, "domain", [(i, (i + 1) % count) for i in range(count)])
    right = lax.ppermute(field, "domain", [((i + 1) % count, i) for i in range(count)])
    inner, gram = call(
        inner_kernel,
        (
            jax.ShapeDtypeStruct(orbitals.shape, F32),
            jax.ShapeDtypeStruct((8, 128), F32),
        ),
        specs=[VMEM] * 2,
        flops=60 * big,
        bytes_moved=8 * big,
    )(field, potential)
    applied, sums = call(
        edge_kernel,
        (
            jax.ShapeDtypeStruct(orbitals.shape, F32),
            jax.ShapeDtypeStruct((domain, 8, 128), F32),
        ),
        specs=[VMEM] * 5,
        flops=40 * big,
        bytes_moved=20 * big,
    )(field, inner, left, right, gram)
    sums = domain_parts(sums)
    residual = call(
        lambda *refs: residual_kernel(cells_total, *refs),
        jax.ShapeDtypeStruct(flat, F32),
        scratch=[pltpu.VMEM((8, 8, 128), F32)],
        specs=[VMEM] * 3,
        flops=16 * big,
        bytes_moved=12 * big,
    )(sums, basis, applied.reshape(flat))
    return (field, residual.reshape(orbitals.shape))


def solution(mesh):
    return jax.shard_map(
        local,
        mesh=mesh,
        in_specs=(P("band", "domain", None, None), P("domain", None, None)),
        out_specs=(P("band", "domain", None, None), P("band", "domain", None, None)),
        check_vma=False,
    )
```

time: 906 us -> 160 us (0.18)
  waiting for transfers between devices: 386 us -> 47.6 us
  blocking collectives: 364 us -> 42.1 us
  matrix products: 88.1 us -> 0 us
  starting transfers between devices: 5.85 us -> 42.5 us
  Pallas kernels: 0 us -> 22.3 us
  loops' own time: 16.9 us -> 0 us
  local copies, waits for them, and re-layouts: 15.9 us -> 1.25 us
  between operations: 14.2 us -> 0.82 us
  other arithmetic: 12.5 us -> 1.37 us
    psum x2 -> x0, waiting for transfers between devices: 375 us -> none  [spread(): return lax.psum(block, axis)]
    psum x5 -> x0, blocking collectives: 364 us -> none  [the longest x2 155 us: local(): correlation = lax.psum(cross_gram(basis, current, cells_total), 'domain')]
    dot_general x133 -> x0, matrix products: 88.1 us -> none  [the longest x6 19.5 us: cross_gram(): lax.dot_general(left_rows, right_rows, (((1,), (1,)), ((), ())), precisio...]
    all_to_all x0 -> x2, blocking collectives: none -> 42.1 us  [domain_parts(): return lax.all_to_all(copies, 'domain', 0, 0)]
    ppermute x2 -> x14, starting transfers between devices: 5.77 us -> 42.5 us  [the longest x8 25.8 us: ring_shift(): return lax.ppermute(block, 'band', pairs)]
    ppermute x2 -> x14, waiting for transfers between devices: 11.3 us -> 47.6 us  [the longest x3 14.2 us: local(): lax.ppermute(quarters[k], 'band', [(0, 2 * k), (1, 2 * k + 1)])]
    pallas_call x0 -> x5, Pallas kernels: none -> 22.3 us  [the longest x1 7.93 us: local(): call(gram_kernel, jax.ShapeDtypeStruct((domain, 8, 128), F32), specs=[VME...]
    another operation x6 -> x0, loops' own time: 16.9 us -> none  [the longest x3 16.9 us: cholesky_lower(): return lax.fori_loop(0, size_now, column_step, jnp.zeros_like(matrix))]
  transfers between devices with their start and end apart: 4 -> 14, of which waited for: 4 -> 11; matrix products, arithmetic and copies ran while one was open for 1% -> 0% of each run, Pallas kernels for 0% -> 3%
where the time goes in v1:
time: 160 us; the launch traced here: 158 us
  waiting for transfers between devices  47.6 us (30%)
  starting transfers between devices  42.5 us (27%)
  blocking collectives  42.1 us (26%)
  Pallas kernels  22.3 us (14%)
    all_to_all x2, blocking collectives, domain_parts(): return lax.all_to_all(copies, 'domain', 0, 0)  42.1 us
    ppermute x8, starting transfers between devices, ring_shift(): return lax.ppermute(block, 'band', pairs)  25.8 us
    ppermute x3, waiting for transfers between devices, local(): lax.ppermute(quarters[k], 'band', [(0, 2 * k), (1, 2 * k + 1)])  14.2 us
    ppermute x8, waiting for transfers between devices, ring_shift(): return lax.ppermute(block, 'band', pairs)  11.7 us
    ppermute x1, waiting for transfers between devices, local(): lax.ppermute(field, 'domain', [((i + 1) % count, i) for i in range(count)])  11.5 us
    ppermute x3, starting transfers between devices, local(): lax.ppermute(quarters[k], 'band', [(0, 2 * k), (1, 2 * k + 1)])  9.65 us
    pallas_call x1, Pallas kernels, local(): call(gram_kernel, jax.ShapeDtypeStruct((domain, 8, 128), F32), specs=[VME...  7.93 us
    pallas_call x1, Pallas kernels, local(): call(lambda *refs: combine_kernel(cells_total, *refs), jax.ShapeDtypeStru...  5.42 us
  transfers between devices with their start and end apart: 14, of which 11 were waited for; matrix products, arithmetic and copies ran while one was open for 0% of the time, Pallas kernels for 3%

profile of v1, /device:TPU:1, one launch (start us, length us, event | category | flops | bytes accessed | tf_op | source)
XLA Modules:
  0.0 158.0 jit_solution(14360162750230590635)
XLA Ops:
  1.9 6.7 %collective-permute-start.1 = (f32[2,256,128]{2,1,0:T(8,128)S(1)}, f32[2,256,128]{2,1,0:T(8,128)S(1)}, u32[]{:S(2)}, u32[]{:S(2)}) collective-permute-start(f32[2,256,128]{2,1,0:T(8,128)S(1)} %bitcast.25), channel_id=1, source_target_pairs={{0,192},{32,224},{1,193},{33,225},{2,194},{34,226},{3,195},{35,227... | collective-permute-start | bytes 786440 | tf_op jit(solution)/shard_map/ppermute | solution.py:287
  11.6 14.2 %collective-permute-done.1 = f32[2,256,128]{2,1,0:T(8,128)S(1)} collective-permute-done((f32[2,256,128]{2,1,0:T(8,128)S(1)}, f32[2,256,128]{2,1,0:T(8,128)S(1)}, u32[]{:S(2)}, u32[]{:S(2)}) %collective-permute-start.1) | collective-permute-done | bytes 262176 | tf_op jit(solution)/shard_map/ppermute | solution.py:287
  27.3 5.3 %collective-permute-done.3 = f32[2,256,128]{2,1,0:T(8,128)S(1)} collective-permute-done((f32[2,256,128]{2,1,0:T(8,128)S(1)}, f32[2,256,128]{2,1,0:T(8,128)S(1)}, u32[]{:S(2)}, u32[]{:S(2)}) %collective-permute-start.3) | collective-permute-done | bytes 262176 | tf_op jit(solution)/shard_map/ppermute | solution.py:288
  32.7 1.9 %collective-permute-start.5 = (f32[2,256,128]{2,1,0:T(8,128)S(1)}, f32[2,256,128]{2,1,0:T(8,128)S(1)}, u32[]{:S(2)}, u32[]{:S(2)}) collective-permute-start(f32[2,256,128]{2,1,0:T(8,128)S(1)} %broadcast_select_fusion.refs_0_.refs_2_), channel_id=1, source_target_pairs={{0,224},{32,0},{64,32},{96,64},{128,96},{160,128},{192,160},{224,1... | collective-permute-start | bytes 786440 | tf_op jit(solution)/shard_map/ppermute | solution.py:274
  34.6 3.4 %collective-permute-start.4 = (f32[2,256,128]{2,1,0:T(8,128)S(1)}, f32[2,256,128]{2,1,0:T(8,128)S(1)}, u32[]{:S(2)}, u32[]{:S(2)}) collective-permute-start(f32[2,256,128]{2,1,0:T(8,128)S(1)} %broadcast_select_fusion.refs_0_.refs_2_), channel_id=1, source_target_pairs={{0,32},{32,64},{64,96},{96,128},{128,160},{160,192},{192,224},{224... | collective-permute-start | bytes 786440 | tf_op jit(solution)/shard_map/ppermute | solution.py:274
  38.0 3.2 %collective-permute-done.5.refs_2_.refs_4_ = f32[2,256,128]{2,1,0:T(8,128)S(1)} collective-permute-done((f32[2,256,128]{2,1,0:T(8,128)S(1)}, f32[2,256,128]{2,1,0:T(8,128)S(1)}, u32[]{:S(2)}, u32[]{:S(2)}) %collective-permute-start.5) | collective-permute-done | bytes 262176 | tf_op jit(solution)/shard_map/ppermute | solution.py:274
  41.2 4.3 %collective-permute-start.7 = (f32[2,256,128]{2,1,0:T(8,128)S(1)}, f32[2,256,128]{2,1,0:T(8,128)S(1)}, u32[]{:S(2)}, u32[]{:S(2)}) collective-permute-start(f32[2,256,128]{2,1,0:T(8,128)S(1)} %collective-permute-done.5.refs_2_.refs_4_), channel_id=1, source_target_pairs={{0,224},{32,0},{64,32},{96,64},{128,96},{160,128},{192,160},{224,1... | collective-permute-start | bytes 786440 | tf_op jit(solution)/shard_map/ppermute | solution.py:274
  46.3 1.9 %collective-permute-start.6 = (f32[2,256,128]{2,1,0:T(8,128)S(1)}, f32[2,256,128]{2,1,0:T(8,128)S(1)}, u32[]{:S(2)}, u32[]{:S(2)}) collective-permute-start(f32[2,256,128]{2,1,0:T(8,128)S(1)} %collective-permute-done.4.refs_1_.refs_3_), channel_id=1, source_target_pairs={{0,32},{32,64},{64,96},{96,128},{128,160},{160,192},{192,224},{224... | collective-permute-start | bytes 786440 | tf_op jit(solution)/shard_map/ppermute | solution.py:274
  48.8 5.5 %collective-permute-start.9 = (f32[2,256,128]{2,1,0:T(8,128)S(1)}, f32[2,256,128]{2,1,0:T(8,128)S(1)}, u32[]{:S(2)}, u32[]{:S(2)}) collective-permute-start(f32[2,256,128]{2,1,0:T(8,128)S(1)} %collective-permute-done.7.refs_4_.refs_6_), channel_id=1, source_target_pairs={{0,224},{32,0},{64,32},{96,64},{128,96},{160,128},{192,160},{224,1... | collective-permute-start | bytes 786440 | tf_op jit(solution)/shard_map/ppermute | solution.py:274
  55.1 1.9 %collective-permute-start.8 = (f32[2,256,128]{2,1,0:T(8,128)S(1)}, f32[2,256,128]{2,1,0:T(8,128)S(1)}, u32[]{:S(2)}, u32[]{:S(2)}) collective-permute-start(f32[2,256,128]{2,1,0:T(8,128)S(1)} %collective-permute-done.6.refs_3_.refs_5_), channel_id=1, source_target_pairs={{0,32},{32,64},{64,96},{96,128},{128,160},{160,192},{192,224},{224... | collective-permute-start | bytes 786440 | tf_op jit(solution)/shard_map/ppermute | solution.py:274
  57.6 5.0 %collective-permute-start.11 = (f32[1,256,128]{2,1,0:T(8,128)S(1)}, f32[1,256,128]{2,1,0:T(8,128)S(1)}, u32[]{:S(2)}, u32[]{:S(2)}) collective-permute-start(f32[1,256,128]{2,1,0:T(8,128)S(1)} %slice.38), channel_id=1, source_target_pairs={{0,224},{32,0},{64,32},{96,64},{128,96},{160,128},{192,160},{224,1... | collective-permute-start | bytes 393224 | tf_op jit(solution)/shard_map/ppermute | solution.py:274
  63.4 1.9 %collective-permute-start.10 = (f32[1,256,128]{2,1,0:T(8,128)S(1)}, f32[1,256,128]{2,1,0:T(8,128)S(1)}, u32[]{:S(2)}, u32[]{:S(2)}) collective-permute-start(f32[1,256,128]{2,1,0:T(8,128)S(1)} %slice.37), channel_id=1, source_target_pairs={{0,32},{32,64},{64,96},{96,128},{128,160},{160,192},{192,224},{224... | collective-permute-start | bytes 393224 | tf_op jit(solution)/shard_map/ppermute | solution.py:274
  65.4 5.0 %collective-permute-done.10.refs_7_.refs_9_ = f32[1,256,128]{2,1,0:T(8,128)S(1)} collective-permute-done((f32[1,256,128]{2,1,0:T(8,128)S(1)}, f32[1,256,128]{2,1,0:T(8,128)S(1)}, u32[]{:S(2)}, u32[]{:S(2)}) %collective-permute-start.10) | collective-permute-done | bytes 131104 | tf_op jit(solution)/shard_map/ppermute | solution.py:274
  70.3 7.9 %shard_map.41 = f32[32,8,128]{2,1,0:T(8,128)S(1)} custom-call(f32[2,256,128]{2,1,0:T(8,128)S(1)} %broadcast_select_fusion.refs_0_.refs_2_, f32[2,256,128]{2,1,0:T(8,128)S(1)} %collective-permute-done.4.refs_1_.refs_3_, f32[2,256,128]{2,1,0:T(8,128)S(1)} %collective-permute-done.5.refs_2_.refs_4_, f32[2,256,128]{2,1,0:T(8,128)S(1)} %collective-permute-done.6.refs_3_.refs_5_, ...), custom_call_target="tpu_custom_call" | custom-call | flops 10485760 | bytes 3145728 | tf_op jit(solution)/shard_map/pallas_call | solution.py:298
  78.3 27.2 %all_to_all.10.refs_1_ = f32[32,8,128]{2,1,0:T(8,128)S(1)} all-to-all(f32[32,8,128]{2,1,0:T(8,128)S(1)} %shard_map.41), channel_id=1, replica_groups=mesh['band'=16,'domain'=32] {'domain'}, dimensions={0} | all-to-all | bytes 262144 | tf_op jit(solution)/shard_map/all_to_all | solution.py:269
  105.5 5.4 %shard_map.42.refs_1_ = f32[8,256,128]{2,1,0:T(8,128)} custom-call(s32[1]{0:T(128)} %bitcast.refs_0_, f32[32,8,128]{2,1,0:T(8,128)S(1)} %all_to_all.10.refs_1_, f32[2,256,128]{2,1,0:T(8,128)S(1)} %broadcast_select_fusion.refs_0_.refs_2_, f32[2,256,128]{2,1,0:T(8,128)S(1)} %collective-permute-done.4.refs_1_.refs_3_, ...), custom_call_target="tpu_custom_call" | custom-call | flops 12582912 | bytes 4194304 | tf_op jit(solution)/shard_map/pallas_call | solution.py:306
  110.9 2.3 %collective-permute-start.13 = (f32[8,4,64,128]{3,2,1,0:T(8,128)}, f32[8,4,64,128]{3,2,1,0:T(8,128)S(1)}, u32[]{:S(2)}, u32[]{:S(2)}) collective-permute-start(f32[8,4,64,128]{3,2,1,0:T(8,128)} %bitcast.14), channel_id=1, source_target_pairs={{1,0},{2,1},{3,2},{4,3},{5,4},{6,5},{7,6},{8,7},{9,8},{10,9},{11,1... | collective-permute-start | bytes 3145736 | tf_op jit(solution)/shard_map/ppermute | solution.py:317
  113.2 3.3 %collective-permute-start.12 = (f32[8,4,64,128]{3,2,1,0:T(8,128)}, f32[8,4,64,128]{3,2,1,0:T(8,128)S(1)}, u32[]{:S(2)}, u32[]{:S(2)}) collective-permute-start(f32[8,4,64,128]{3,2,1,0:T(8,128)} %bitcast.15), channel_id=1, source_target_pairs={{0,1},{1,2},{2,3},{3,4},{4,5},{5,6},{6,7},{7,8},{8,9},{9,10},{10,1... | collective-permute-start | bytes 3145736 | tf_op jit(solution)/shard_map/ppermute | solution.py:316
  117.7 4.1 %shard_map.43 = (f32[8,4,64,128]{3,2,1,0:T(8,128)S(1)}, f32[8,128]{1,0:T(8,128)S(1)}) custom-call(f32[8,4,64,128]{3,2,1,0:T(8,128)S(1)} %bitcast.17, f32[4,64,128]{2,1,0:T(8,128)S(1)} %copy-done.2), custom_call_target="tpu_custom_call" | custom-call | flops 15728640 | bytes 2097152 | tf_op jit(solution)/shard_map/pallas_call | solution.py:318
  121.8 11.5 %collective-permute-done.13.right_ref = f32[8,4,64,128]{3,2,1,0:T(8,128)S(1)} collective-permute-done((f32[8,4,64,128]{3,2,1,0:T(8,128)}, f32[8,4,64,128]{3,2,1,0:T(8,128)S(1)}, u32[]{:S(2)}, u32[]{:S(2)}) %collective-permute-start.13) | collective-permute-done | bytes 1048608 | tf_op jit(solution)/shard_map/ppermute | solution.py:317
  133.3 4.9 %collective-permute-done.12.left_ref = f32[8,4,64,128]{3,2,1,0:T(8,128)S(1)} collective-permute-done((f32[8,4,64,128]{3,2,1,0:T(8,128)}, f32[8,4,64,128]{3,2,1,0:T(8,128)S(1)}, u32[]{:S(2)}, u32[]{:S(2)}) %collective-permute-start.12) | collective-permute-done | bytes 1048608 | tf_op jit(solution)/shard_map/ppermute | solution.py:316
  138.2 2.4 %shard_map.44 = (f32[8,4,64,128]{3,2,1,0:T(8,128)S(1)}, f32[32,8,128]{2,1,0:T(8,128)S(1)}) custom-call(f32[8,4,64,128]{3,2,1,0:T(8,128)S(1)} %bitcast.18, f32[8,4,64,128]{3,2,1,0:T(8,128)S(1)} %get-tuple-element.6.inner_ref, f32[8,4,64,128]{3,2,1,0:T(8,128)S(1)} %collective-permute-done.12.left_ref, f32[8,4,64,128]{3,2,1,0:T(8,128)S(1)} %collective-permute-done.13.right_ref, ...), custom_call_target="tpu_custom_call" | custom-call | flops 10485760 | bytes 5242880 | tf_op jit(solution)/shard_map/pallas_call | solution.py:328
  140.6 14.9 %all_to_all.11.refs_0_ = f32[32,8,128]{2,1,0:T(8,128)S(1)} all-to-all(f32[32,8,128]{2,1,0:T(8,128)S(1)} %get-tuple-element.8), channel_id=1, replica_groups=mesh['band'=16,'domain'=32] {'domain'}, dimensions={0} | all-to-all | bytes 262144 | tf_op jit(solution)/shard_map/all_to_all | solution.py:269
  155.5 2.5 %shard_map.45 = f32[8,256,128]{2,1,0:T(8,128)} custom-call(f32[32,8,128]{2,1,0:T(8,128)S(1)} %all_to_all.11.refs_0_, f32[8,256,128]{2,1,0:T(8,128)S(1)} %copy-done, f32[8,256,128]{2,1,0:T(8,128)S(1)} %bitcast.21), custom_call_target="tpu_custom_call" | custom-call | flops 4194304 | bytes 3145728 | tf_op jit(solution)/shard_map/pallas_call | solution.py:339
  (22 shorter events, 10.5 us)
Async XLA Ops:
  1.9 23.8 %collective-permute-start.1 = (f32[2,256,128]{2,1,0:T(8,128)S(1)}, f32[2,256,128]{2,1,0:T(8,128)S(1)}, u32[]{:S(2)}, u32[]{:S(2)}) collective-permute-start(f32[2,256,128]{2,1,0:T(8,128)S(1)} %bitcast.25), channel_id=1, source_target_pairs={{0,192},{32,224},{1,193},{33,225},{2,194},{34,226},{3,195},{35,227... | collective-permute-start | bytes 786440 | tf_op jit(solution)/shard_map/ppermute | solution.py:287
  8.7 17.1 %collective-permute-start = (f32[2,256,128]{2,1,0:T(8,128)S(1)}, f32[2,256,128]{2,1,0:T(8,128)S(1)}, u32[]{:S(2)}, u32[]{:S(2)}) collective-permute-start(f32[2,256,128]{2,1,0:T(8,128)S(1)} %bitcast.24), channel_id=1, source_target_pairs={{0,64},{32,96},{1,65},{33,97},{2,66},{34,98},{3,67},{35,99},{4,68}... | collective-permute-start | bytes 786440 | tf_op jit(solution)/shard_map/ppermute | solution.py:287
  10.0 15.8 %collective-permute-start.2 = (f32[2,256,128]{2,1,0:T(8,128)S(1)}, f32[2,256,128]{2,1,0:T(8,128)S(1)}, u32[]{:S(2)}, u32[]{:S(2)}) collective-permute-start(f32[2,256,128]{2,1,0:T(8,128)S(1)} %bitcast.23), channel_id=1, source_target_pairs={{0,128},{32,160},{1,129},{33,161},{2,130},{34,162},{3,131},{35,163... | collective-permute-start | bytes 786440 | tf_op jit(solution)/shard_map/ppermute | solution.py:287
  25.8 44.5 %copy-start.1 = (f32[8,4,64,128]{3,2,1,0:T(8,128)S(1)}, f32[8,4,64,128]{3,2,1,0:T(8,128)}, u32[]{:S(2)}) copy-start(f32[8,4,64,128]{3,2,1,0:T(8,128)} %param.2) | copy-start | bytes 3145732
  25.8 6.8 %collective-permute-start.3 = (f32[2,256,128]{2,1,0:T(8,128)S(1)}, f32[2,256,128]{2,1,0:T(8,128)S(1)}, u32[]{:S(2)}, u32[]{:S(2)}) collective-permute-start(f32[2,256,128]{2,1,0:T(8,128)S(1)} %fusion.1), channel_id=1, source_target_pairs={{0,256},{32,288},{64,320},{96,352},{128,384},{160,416},{192,448},{... | collective-permute-start | bytes 786440 | tf_op jit(solution)/shard_map/ppermute | solution.py:288
  32.7 8.5 %collective-permute-start.5 = (f32[2,256,128]{2,1,0:T(8,128)S(1)}, f32[2,256,128]{2,1,0:T(8,128)S(1)}, u32[]{:S(2)}, u32[]{:S(2)}) collective-permute-start(f32[2,256,128]{2,1,0:T(8,128)S(1)} %broadcast_select_fusion.refs_0_.refs_2_), channel_id=1, source_target_pairs={{0,224},{32,0},{64,32},{96,64},{128,96},{160,128},{192,160},{224,1... | collective-permute-start | bytes 786440 | tf_op jit(solution)/shard_map/ppermute | solution.py:274
  34.6 11.7 %collective-permute-start.4 = (f32[2,256,128]{2,1,0:T(8,128)S(1)}, f32[2,256,128]{2,1,0:T(8,128)S(1)}, u32[]{:S(2)}, u32[]{:S(2)}) collective-permute-start(f32[2,256,128]{2,1,0:T(8,128)S(1)} %broadcast_select_fusion.refs_0_.refs_2_), channel_id=1, source_target_pairs={{0,32},{32,64},{64,96},{96,128},{128,160},{160,192},{192,224},{224... | collective-permute-start | bytes 786440 | tf_op jit(solution)/shard_map/ppermute | solution.py:274
  41.2 7.6 %collective-permute-start.7 = (f32[2,256,128]{2,1,0:T(8,128)S(1)}, f32[2,256,128]{2,1,0:T(8,128)S(1)}, u32[]{:S(2)}, u32[]{:S(2)}) collective-permute-start(f32[2,256,128]{2,1,0:T(8,128)S(1)} %collective-permute-done.5.refs_2_.refs_4_), channel_id=1, source_target_pairs={{0,224},{32,0},{64,32},{96,64},{128,96},{160,128},{192,160},{224,1... | collective-permute-start | bytes 786440 | tf_op jit(solution)/shard_map/ppermute | solution.py:274
  46.3 8.8 %collective-permute-start.6 = (f32[2,256,128]{2,1,0:T(8,128)S(1)}, f32[2,256,128]{2,1,0:T(8,128)S(1)}, u32[]{:S(2)}, u32[]{:S(2)}) collective-permute-start(f32[2,256,128]{2,1,0:T(8,128)S(1)} %collective-permute-done.4.refs_1_.refs_3_), channel_id=1, source_target_pairs={{0,32},{32,64},{64,96},{96,128},{128,160},{160,192},{192,224},{224... | collective-permute-start | bytes 786440 | tf_op jit(solution)/shard_map/ppermute | solution.py:274
  48.8 8.8 %collective-permute-start.9 = (f32[2,256,128]{2,1,0:T(8,128)S(1)}, f32[2,256,128]{2,1,0:T(8,128)S(1)}, u32[]{:S(2)}, u32[]{:S(2)}) collective-permute-start(f32[2,256,128]{2,1,0:T(8,128)S(1)} %collective-permute-done.7.refs_4_.refs_6_), channel_id=1, source_target_pairs={{0,224},{32,0},{64,32},{96,64},{128,96},{160,128},{192,160},{224,1... | collective-permute-start | bytes 786440 | tf_op jit(solution)/shard_map/ppermute | solution.py:274
  55.1 8.3 %collective-permute-start.8 = (f32[2,256,128]{2,1,0:T(8,128)S(1)}, f32[2,256,128]{2,1,0:T(8,128)S(1)}, u32[]{:S(2)}, u32[]{:S(2)}) collective-permute-start(f32[2,256,128]{2,1,0:T(8,128)S(1)} %collective-permute-done.6.refs_3_.refs_5_), channel_id=1, source_target_pairs={{0,32},{32,64},{64,96},{96,128},{128,160},{160,192},{192,224},{224... | collective-permute-start | bytes 786440 | tf_op jit(solution)/shard_map/ppermute | solution.py:274
  57.6 7.7 %collective-permute-start.11 = (f32[1,256,128]{2,1,0:T(8,128)S(1)}, f32[1,256,128]{2,1,0:T(8,128)S(1)}, u32[]{:S(2)}, u32[]{:S(2)}) collective-permute-start(f32[1,256,128]{2,1,0:T(8,128)S(1)} %slice.38), channel_id=1, source_target_pairs={{0,224},{32,0},{64,32},{96,64},{128,96},{160,128},{192,160},{224,1... | collective-permute-start | bytes 393224 | tf_op jit(solution)/shard_map/ppermute | solution.py:274
  63.4 6.9 %collective-permute-start.10 = (f32[1,256,128]{2,1,0:T(8,128)S(1)}, f32[1,256,128]{2,1,0:T(8,128)S(1)}, u32[]{:S(2)}, u32[]{:S(2)}) collective-permute-start(f32[1,256,128]{2,1,0:T(8,128)S(1)} %slice.37), channel_id=1, source_target_pairs={{0,32},{32,64},{64,96},{96,128},{128,160},{160,192},{192,224},{224... | collective-permute-start | bytes 393224 | tf_op jit(solution)/shard_map/ppermute | solution.py:274
  105.5 11.0 %copy-start.2 = (f32[4,64,128]{2,1,0:T(8,128)S(1)}, f32[4,64,128]{2,1,0:T(8,128)}, u32[]{:S(2)}) copy-start(f32[4,64,128]{2,1,0:T(8,128)} %v_ref.1) | copy-start | bytes 393220
  110.9 22.4 %collective-permute-start.13 = (f32[8,4,64,128]{3,2,1,0:T(8,128)}, f32[8,4,64,128]{3,2,1,0:T(8,128)S(1)}, u32[]{:S(2)}, u32[]{:S(2)}) collective-permute-start(f32[8,4,64,128]{3,2,1,0:T(8,128)} %bitcast.14), channel_id=1, source_target_pairs={{1,0},{2,1},{3,2},{4,3},{5,4},{6,5},{7,6},{8,7},{9,8},{10,9},{11,1... | collective-permute-start | bytes 3145736 | tf_op jit(solution)/shard_map/ppermute | solution.py:317
  113.2 25.0 %collective-permute-start.12 = (f32[8,4,64,128]{3,2,1,0:T(8,128)}, f32[8,4,64,128]{3,2,1,0:T(8,128)S(1)}, u32[]{:S(2)}, u32[]{:S(2)}) collective-permute-start(f32[8,4,64,128]{3,2,1,0:T(8,128)} %bitcast.15), channel_id=1, source_target_pairs={{0,1},{1,2},{2,3},{3,4},{4,5},{5,6},{6,7},{7,8},{8,9},{9,10},{10,1... | collective-permute-start | bytes 3145736 | tf_op jit(solution)/shard_map/ppermute | solution.py:316
  116.5 1.2 copy-start

commit v2 on v1

v2 whole, which is shorter than its diff:
```python
import jax
import jax.numpy as jnp
from jax import lax
from jax.experimental import pallas as pl
from jax.experimental.pallas import tpu as pltpu
from jax.sharding import PartitionSpec as P

stencil_weights = (-205.0 / 72.0, 8.0 / 5.0, -1.0 / 5.0, 8.0 / 315.0, -1.0 / 560.0)
BLK = 8
RING = 8
F32 = jnp.float32
VMEM = pl.BlockSpec(memory_space=pltpu.VMEM)
SMEM = pl.BlockSpec(memory_space=pltpu.SMEM)


def call(kernel, outs, scratch=(), specs=None, flops=0, bytes_moved=0):
    return pl.pallas_call(
        kernel,
        out_shape=outs,
        in_specs=specs,
        out_specs=jax.tree.map(lambda _: VMEM, outs),
        scratch_shapes=scratch,
        compiler_params=pltpu.CompilerParams(vmem_limit_bytes=32 * 1024 * 1024),
        cost_estimate=pl.CostEstimate(flops=flops, bytes_accessed=bytes_moved, transcendentals=0),
    )


def lanes():
    return lax.broadcasted_iota(jnp.int32, (8, 128), 1)


def subs():
    return lax.broadcasted_iota(jnp.int32, (8, 128), 0)


def pair_sums(jobs, load, chunks):
    lane = lanes()
    result = jnp.zeros((8, 128), F32)
    zero_row = jnp.zeros((1, 128), F32)
    for pairs in jobs:
        used = sorted({n for pair in pairs for n in pair})

        def body(c, sums, pairs=pairs, used=used):
            for step in range(4):
                rows = {n: load[n](4 * c + step) for n in used}
                sums = tuple(s + rows[q] * rows[r] for s, (q, r) in zip(sums, pairs))
            return sums

        zero = jnp.zeros((8, 128), F32)
        sums = lax.fori_loop(0, chunks // 4, body, (zero,) * len(pairs))
        columns = {}
        for s, (q, r) in zip(sums, pairs):
            rows = columns.setdefault(32 * (r // 8) + q, [zero_row] * 8)
            rows[r % 8] = jnp.sum(s, axis=0, keepdims=True)
        for place, rows in columns.items():
            column = jnp.sum(jnp.concatenate(rows, axis=0), axis=1, keepdims=True)
            result = result + jnp.where(lane == place, column, 0.0)
    return result


def loader(ref, index):
    return lambda c: ref[index, pl.ds(pl.multiple_of(c * 8, 8), 8), :]


def move(tile, source, target):
    lane = lanes()
    if source != target:
        tile = pltpu.roll(tile, (target - source) % 128, 1)
    return jnp.where((lane >= target) & (lane < target + 8), tile, 0.0)


def spread_lane(tile, k):
    return jnp.broadcast_to(tile[:, k : k + 1], (8, 128))


def rows_of(refs):
    return [(r, i) for r in refs for i in range(r.shape[0])]


def unpacked(sums):
    lane = lanes()
    parts = [sums] + [pltpu.roll(sums, 128 - 32 * n, 1) for n in (1, 2)]
    return [jnp.where(lane < 32, part, 0.0) for part in parts]


def tall(tiles):
    return jnp.concatenate(tiles + [jnp.zeros((128 - 8 * len(tiles), 128), F32)], axis=0)


OWN = list(range(16, 24))
IMAGE = list(range(24, 32))


def split(pairs, size=36):
    if not pairs:
        return []
    count = -(-len(pairs) // size)
    size = -(-len(pairs) // count)
    return [pairs[n : n + size] for n in range(0, len(pairs), size)]


def stage_kernel(parts, fresh, imaged, last, *refs):
    out = refs[-1]
    pieces, refs = refs[:parts], refs[parts:-1]
    own, image, before = (refs[0], refs[1], refs[2:]) if imaged else (refs[0], None, refs[1:])
    chunks = own.shape[1] // 8
    load = {n: loader(r, i) for n, (r, i) in enumerate(rows_of(pieces))}
    load |= {n: loader(own, n - 16) for n in OWN}
    if imaged:
        load |= {n: loader(image, n - 24) for n in IMAGE}
    jobs = split([(q, r) for q in OWN for r in fresh])
    jobs += split([(q, r) for q in fresh for r in range(q + 1)])
    jobs += split([(q, r) for q in IMAGE for r in imaged])
    total = pair_sums(jobs, load, chunks)
    for part in before[: len(before) - last]:
        total = total + part[...]
    if last:
        for n in range(3):
            total = total + move(before[-1][...], 32 * n + 24, 96 + 8 * n)
        for n in range(out.shape[0]):
            out[n] = total
    else:
        out[...] = total


def combine_kernel(cells_total, band_ref, sums_ref, *refs):
    *pieces, own, out, weights_ref, gram_ref, shared, splat = refs
    band = band_ref[0]
    lane, sub = lanes(), subs()
    sums = jnp.sum(sums_ref[...], axis=0) / cells_total
    for n in range(shared.shape[0]):
        shared[n] = sums
    tiles = unpacked(sums)
    turned = jnp.transpose(tall(tiles))
    w0, w1, w2 = (
        jnp.where(lane < 24, tile + jnp.where(lane == sub + 8 * n, 0.0, turned[8 * n : 8 * n + 8]), 0.0)
        for n, tile in enumerate(tiles)
    )
    later = band >= 2
    second = band == 1

    def taken(position):
        place = position & 7
        return later | (second & (place >= 2) & (place <= 5))

    row_in = taken(sub)
    lane_in = (lane >= 16) | taken(lane)
    kept = row_in & lane_in
    w0 = jnp.where(kept, w0, jnp.where(lane == sub, 1.0, 0.0))
    w1 = jnp.where(kept, w1, jnp.where(lane == 8 + sub, 1.0, 0.0))
    w0 = w0 + jnp.where(lane == 24 + sub, 1.0, 0.0)
    w1 = w1 + jnp.where(lane == 32 + sub, 1.0, 0.0)
    w2 = jnp.where(lane_in, w2, 0.0) + jnp.where(lane == 40 + sub, 1.0, 0.0)
    tiles = [w0, w1, w2]
    for k in range(16):
        v, s = divmod(k, 8)
        row = tiles[v][s : s + 1, :]
        row = row / jnp.broadcast_to(row[:, k : k + 1], (1, 128))
        row = jnp.broadcast_to(row, (8, 128))
        for u in range(v, 3):
            column = spread_lane(tiles[u], k)
            if u == v:
                column = jnp.where(sub > s, column, 0.0)
            tiles[u] = tiles[u] - column * row
    plain = tiles[2]
    scaled = plain
    for k in range(8):
        row = scaled[k : k + 1, :]
        row = row / jnp.broadcast_to(row[:, 16 + k : 17 + k], (1, 128))
        column = jnp.where(sub > k, spread_lane(scaled, 16 + k), 0.0)
        scaled = scaled - column * jnp.broadcast_to(row, (8, 128))
    pivots = jnp.sum(jnp.where(lane == 16 + sub, scaled, 0.0), axis=1, keepdims=True)
    scaled = scaled / jnp.sqrt(jnp.broadcast_to(pivots, (8, 128)))
    weights = jnp.where(later, plain, scaled)
    weights_ref[...] = weights
    gram_ref[...] = jnp.where(later, move(plain, 16, 0), jnp.where(lane == sub, 1.0, 0.0))
    for c in range(24):
        splat[c] = spread_lane(weights, 24 + c)
    rows = rows_of(pieces) + [(own, i) for i in range(BLK)]

    def body(c, carry):
        part = pl.ds(pl.multiple_of(c * 16, 16), 16)
        inputs = [r[i, part, :] for r, i in rows]
        for i in range(BLK):
            total = splat[0, pl.ds(i, 1), :] * inputs[0]
            for n in range(1, 24):
                total = total + splat[n, pl.ds(i, 1), :] * inputs[n]
            out[i, part, :] = total
        return carry

    lax.fori_loop(0, own.shape[1] // 16, body, 0)


def inner_kernel(f_ref, v_ref, out, *sums):
    def body(i, carry):
        layers = [f_ref[i, x] for x in range(4)]
        for x in range(4):
            here = layers[x]
            total = 3.0 * stencil_weights[0] * here
            for offset in range(1, 5):
                beside = pltpu.roll(here, offset, 0) + pltpu.roll(here, 64 - offset, 0)
                beside = beside + pltpu.roll(here, offset, 1) + pltpu.roll(here, 128 - offset, 1)
                if x + offset < 4:
                    beside = beside + layers[x + offset]
                if x - offset >= 0:
                    beside = beside + layers[x - offset]
                total = total + stencil_weights[offset] * beside
            out[i, x] = -0.5 * total + v_ref[x] * here
        return carry

    lax.fori_loop(0, BLK, body, 0)
    if sums:

        def row(i):
            return lambda c: f_ref[i, c // 8, pl.ds(pl.multiple_of((c % 8) * 8, 8), 8), :]

        load = {n: row(n - 16) for n in OWN}
        sums[0][...] = pair_sums([[(q, r) for q in OWN for r in range(16, q + 1)]], load, 32)


def edged(inner, x, left, right):
    total = None
    for offset in range(1, 5):
        if x + offset >= 4:
            term = stencil_weights[offset] * right(x + offset - 4)
            total = term if total is None else total + term
        if x - offset < 0:
            term = stencil_weights[offset] * left(x - offset + 4)
            total = term if total is None else total + term
    return inner - 0.5 * total


def image_kernel(own, inner, left, right, out, sums):
    def body(i, carry):
        for x in range(4):
            part = pl.ds(64 * x, 64)
            out[i, part, :] = edged(
                inner[i, part, :],
                x,
                lambda n: left[i, pl.ds(64 * n, 64), :],
                lambda n: right[i, pl.ds(64 * n, 64), :],
            )
        return carry

    lax.fori_loop(0, BLK, body, 0)
    load = {n: loader(own, n - 16) for n in OWN}
    load |= {n: loader(out, n - 24) for n in IMAGE}
    jobs = split([(q, r) for q in IMAGE for r in OWN], 32)
    sums[...] = pair_sums(jobs, load, own.shape[1] // 8)


def dot(left, right, turn_left=False, turn_right=False):
    dims = (((0 if turn_left else 1,), (1 if turn_right else 0,)), ((), ()))
    return lax.dot_general(
        left, right, dims, precision=lax.Precision.HIGHEST, preferred_element_type=F32
    )


def places(y, home=None):
    row = lax.broadcasted_iota(jnp.int32, (128, 128), 0)
    lane = lax.broadcasted_iota(jnp.int32, (128, 128), 1)
    distance = (row + 2) >> 2
    distance = jnp.where(((row + 2) & 2) == 0, -distance, distance)
    piece = (y + distance) & 7
    target = (piece & 1) * 8 + (piece >> 1) * 2 + (row & 1)
    if home is None:
        target = jnp.where(row < 16, target, row)
    else:
        target = jnp.where((piece & 1) == home, -1, target)
        target = jnp.where(row < 16, target, row - 16 + 8 * home)
    return jnp.where((lane == target) & (row < 24), 1.0, 0.0)


def coeff_kernel(band_ref, weights_ref, gram_ref, own_ref, shared_ref, out):
    lane, sub = lanes(), subs()
    wide = lax.broadcasted_iota(jnp.int32, (128, 128), 1)
    row = lax.broadcasted_iota(jnp.int32, (128, 128), 0)
    place = places(band_ref[0] & 7)
    weights = jnp.where(lane < 24, pltpu.roll(weights_ref[...], 104, 1), 0.0)
    weights = dot(weights, place)

    def image_columns(matrix, place, source, target):
        columns = dot(place, matrix, turn_left=True)
        columns = pltpu.roll(columns, (target - source) % 128, 1)
        return jnp.where((wide >= target) & (wide < target + 8), columns, 0.0)

    def visiting(n):
        packed = shared_ref[n]
        home = tall([move(packed, 32 * k + 24, 0) for k in range(3)])
        away = tall([move(packed, 96 + 8 * k, 0) for k in range(3)])
        matrix = jnp.where(band_ref[0] < RING, home, away)
        return image_columns(matrix, places(n, n), 0, 8 * n)

    block0, block1 = visiting(0), visiting(1)
    block = image_columns(tall(unpacked(own_ref[...])), place, 24, 16)
    half = dot(weights, block0 + block1 + block)
    half = half + dot(weights, jnp.where(row < 16, block, 0.0), turn_right=True)
    theta = dot(half, tall([weights]), turn_right=True)
    work = gram_ref[...] + move(theta, 0, 8)
    for k in range(8):
        line = work[k : k + 1, :]
        line = jnp.broadcast_to(line / jnp.broadcast_to(line[:, k : k + 1], (1, 128)), (8, 128))
        work = jnp.where(sub == k, line, work - spread_lane(work, k) * line)
    for j in range(8):
        out[j] = spread_lane(work, 8 + j)


def residual_kernel(f_ref, inner_ref, left_ref, right_ref, splat, out):
    def body(c, carry):
        def part(x):
            return pl.ds(pl.multiple_of(64 * x + 8 * c, 8), 8)

        for x in range(4):
            inputs = [f_ref[i, part(x), :] for i in range(BLK)]
            for j in range(BLK):
                total = edged(
                    inner_ref[j, part(x), :],
                    x,
                    lambda n: left_ref[j, part(n), :],
                    lambda n: right_ref[j, part(n), :],
                )
                for i in range(BLK):
                    total = total - splat[j, pl.ds(i, 1), :] * inputs[i]
                out[j, part(x), :] = total
        return carry

    lax.fori_loop(0, 8, body, 0)


def domain_parts(copies):
    return lax.all_to_all(copies, "domain", 0, 0)


def ring_shift(block, step):
    pairs = [(z * RING + y, z * RING + (y + step) % RING) for z in range(2) for y in range(RING)]
    return lax.ppermute(block, "band", pairs)


def neighbours(block):
    count = lax.axis_size("domain")
    left = lax.ppermute(block, "domain", [(i, (i + 1) % count) for i in range(count)])
    right = lax.ppermute(block, "domain", [((i + 1) % count, i) for i in range(count)])
    return left, right


def local(orbitals, potential):
    blocks, slab_width, rows_y, rows_z = orbitals.shape
    domain, bands = lax.axis_size("domain"), lax.axis_size("band")
    cells_total = float(slab_width * rows_y * rows_z * domain)
    band = lax.axis_index("band")
    band_word = band.reshape(1).astype(jnp.int32)
    flat = (blocks, slab_width * rows_y, rows_z)
    big = flat[0] * flat[1] * flat[2]
    slab = jax.ShapeDtypeStruct(flat, F32)
    field = jax.ShapeDtypeStruct(orbitals.shape, F32)
    tile = jax.ShapeDtypeStruct((8, 128), F32)

    def inner_part(block, *sums):
        return call(
            inner_kernel,
            (field, *sums),
            specs=[VMEM] * 2,
            flops=60 * big,
            bytes_moved=8 * big,
        )(block, potential)

    own = orbitals.reshape(flat)
    quarters = [own[2 * k : 2 * k + 2] for k in range(4)]
    arrived = [
        lax.ppermute(quarters[k], "band", [(0, 2 * k), (1, 2 * k + 1)]) for k in (1, 3, 2)
    ]
    inner, sums = inner_part(orbitals, tile)
    arrived, inner, sums = lax.optimization_barrier((arrived, inner, sums))
    piece = jnp.where(band < 2, quarters[0], 0.0)
    for part in arrived:
        piece = piece + part
    left, right = neighbours(own)
    crossed = lax.ppermute(piece, "band", [(y, y + RING) for y in range(RING)])
    piece = jnp.where(band < RING, piece, crossed)

    def stage(fresh, imaged, pieces, *sums, guest=None):
        sources = (*pieces, own, *((image,) if imaged else ()), *sums)
        sources += () if guest is None else (guest,)
        return call(
            lambda *refs: stage_kernel(len(pieces), fresh, imaged, guest is not None, *refs),
            tile if guest is None else jax.ShapeDtypeStruct((domain, 8, 128), F32),
            specs=[VMEM] * len(sources),
            flops=20 * big,
            bytes_moved=10 * big,
        )(*sources)

    pieces = [piece]
    up, down = ring_shift(piece, 1), ring_shift(piece, -1)
    pieces += [up, down]
    up, down = ring_shift(up, 1), ring_shift(down, -1)
    sums = stage(range(6), (), pieces, sums)
    down, sums = lax.optimization_barrier((down, sums))
    pieces += [up, down]
    up, down = ring_shift(up, 1), ring_shift(down, -1)
    sums = stage(range(6, 10), (), pieces, sums)
    image, image_sums = call(
        image_kernel, (slab, tile), specs=[VMEM] * 4, flops=50 * big, bytes_moved=20 * big
    )(own, inner.reshape(flat), left, right)
    down, sums, image, image_sums = lax.optimization_barrier((down, sums, image, image_sums))
    pieces += [up, down]
    up, down = ring_shift(up[:1], 1), ring_shift(down[1:], -1)
    sums = stage(range(10, 14), range(14), pieces, sums, image_sums)
    guest = lax.ppermute(sums, "band", [(0, RING), (1, RING + 1)])
    pieces += [up, down]
    sums = stage(range(14, 16), range(14, 16), pieces, sums, guest=guest)
    sums = domain_parts(sums)
    basis, weights, gram, shared = call(
        lambda *refs: combine_kernel(cells_total, *refs),
        (slab, tile, tile, jax.ShapeDtypeStruct((RING, 8, 128), F32)),
        scratch=[pltpu.VMEM((24, 8, 128), F32)],
        specs=[SMEM] + [VMEM] * 11,
        flops=48 * big,
        bytes_moved=16 * big,
    )(band_word, sums, *pieces, own)
    left, right = neighbours(basis)
    own_sums = shared[0]
    rings = [list(range(RING)), list(range(RING, bands))]
    shared = lax.all_to_all(shared, "band", 0, 0, axis_index_groups=rings)
    inner = inner_part(basis.reshape(orbitals.shape))[0].reshape(flat)
    splat = call(
        coeff_kernel, jax.ShapeDtypeStruct((8, 8, 128), F32), specs=[SMEM] + [VMEM] * 4
    )(band_word, weights, gram, own_sums, shared)
    residual = call(
        residual_kernel, slab, specs=[VMEM] * 5, flops=30 * big, bytes_moved=20 * big
    )(basis, inner, left, right, splat)
    return (basis.reshape(orbitals.shape), residual.reshape(orbitals.shape))


def solution(mesh):
    return jax.shard_map(
        local,
        mesh=mesh,
        in_specs=(P("band", "domain", None, None), P("domain", None, None)),
        out_specs=(P("band", "domain", None, None), P("band", "domain", None, None)),
        check_vma=False,
    )
```

time: 160 us -> 148 us (0.925)
  blocking collectives: 42.1 us -> 28 us
  waiting for transfers between devices: 47.6 us -> 37.8 us
  starting transfers between devices: 42.5 us -> 51.8 us
  Pallas kernels: 22.3 us -> 25.2 us
    all_to_all x2 -> x1, blocking collectives: 42.1 us -> 28 us  [domain_parts(): return lax.all_to_all(copies, 'domain', 0, 0)]
    ppermute x2 -> x5, starting transfers between devices: 5.55 us -> 13.8 us  [the longest x2 6.58 us: neighbours(): lax.ppermute(block, 'domain', [(i, (i + 1) % count) for i in range(count)])]
    ppermute x8, waiting for transfers between devices: 11.7 us -> 4.54 us  [ring_shift(): return lax.ppermute(block, 'band', pairs)]
    ppermute x1, waiting for transfers between devices: 5.33 us -> 0.01 us  [local(): crossed = lax.ppermute(piece, 'band', [(y, y + RING) for y in range(RING)])]
    all_to_all x0 -> x1, starting transfers between devices: none -> 3.35 us  [local(): shared = lax.all_to_all(shared, 'band', 0, 0, axis_index_groups=rings)]
    ppermute x8, starting transfers between devices: 25.8 us -> 23 us  [ring_shift(): return lax.ppermute(block, 'band', pairs)]
    ppermute x2 -> x5, waiting for transfers between devices: 16.4 us -> 19.3 us  [the longest x2 17.5 us: neighbours(): lax.ppermute(block, 'domain', [((i + 1) % count, i) for i in range(count)])]
    pallas_call x5 -> x10, Pallas kernels: 22.3 us -> 25.2 us  [the longest x4 6.18 us: stage(): call(lambda *refs: stage_kernel(len(pieces), fresh, imaged, guest is not...]
  transfers between devices with their start and end apart: 14 -> 18, of which waited for: 11 -> 10; matrix products, arithmetic and copies ran while one was open for 0% -> 1% of each run, Pallas kernels for 3% -> 10%
where the time goes in v2:
time: 148 us; the launch traced here: 147 us
  starting transfers between devices  51.8 us (35%)
  waiting for transfers between devices  37.8 us (26%)
  blocking collectives  28 us (19%)
  Pallas kernels  25.2 us (17%)
  local copies, waits for them, and re-layouts  1.95 us (1%)
    all_to_all x1, blocking collectives, domain_parts(): return lax.all_to_all(copies, 'domain', 0, 0)  28 us
    ppermute x8, starting transfers between devices, ring_shift(): return lax.ppermute(block, 'band', pairs)  23 us
    ppermute x2, waiting for transfers between devices, neighbours(): lax.ppermute(block, 'domain', [((i + 1) % count, i) for i in range(count)])  17.5 us
    ppermute x3, waiting for transfers between devices, local(): lax.ppermute(quarters[k], 'band', [(0, 2 * k), (1, 2 * k + 1)])  11.5 us
    ppermute x3, starting transfers between devices, local(): lax.ppermute(quarters[k], 'band', [(0, 2 * k), (1, 2 * k + 1)])  9.65 us
    ppermute x2, starting transfers between devices, neighbours(): lax.ppermute(block, 'domain', [(i, (i + 1) % count) for i in range(count)])  6.58 us
    pallas_call x4, Pallas kernels, stage(): call(lambda *refs: stage_kernel(len(pieces), fresh, imaged, guest is not...  6.18 us
    pallas_call x2, Pallas kernels, inner_part(): call(inner_kernel, (field, *sums), specs=[VMEM] * 2, flops=60 * big, byte...  6.04 us
  transfers between devices with their start and end apart: 18, of which 10 were waited for; matrix products, arithmetic and copies ran while one was open for 1% of the time, Pallas kernels for 10%

profile of v2, /device:TPU:1, one launch (start us, length us, event | category | flops | bytes accessed | tf_op | source)
XLA Modules:
  0.0 147.0 jit_solution(7626907544623805388)
XLA Ops:
  2.0 5.1 %collective-permute-start = (f32[2,256,128]{2,1,0:T(8,128)S(1)}, f32[2,256,128]{2,1,0:T(8,128)S(1)}, u32[]{:S(2)}, u32[]{:S(2)}) collective-permute-start(f32[2,256,128]{2,1,0:T(8,128)S(1)} %bitcast.32), channel_id=1, source_target_pairs={{0,64},{32,96},{1,65},{33,97},{2,66},{34,98},{3,67},{35,99},{4,68}... | collective-permute-start | bytes 786440 | tf_op jit(solution)/shard_map/ppermute | solution.py:370
  7.1 2.3 %collective-permute-start.1 = (f32[2,256,128]{2,1,0:T(8,128)S(1)}, f32[2,256,128]{2,1,0:T(8,128)S(1)}, u32[]{:S(2)}, u32[]{:S(2)}) collective-permute-start(f32[2,256,128]{2,1,0:T(8,128)S(1)} %bitcast.31), channel_id=1, source_target_pairs={{0,192},{32,224},{1,193},{33,225},{2,194},{34,226},{3,195},{35,227... | collective-permute-start | bytes 786440 | tf_op jit(solution)/shard_map/ppermute | solution.py:370
  9.5 2.2 %collective-permute-start.2 = (f32[2,256,128]{2,1,0:T(8,128)S(1)}, f32[2,256,128]{2,1,0:T(8,128)S(1)}, u32[]{:S(2)}, u32[]{:S(2)}) collective-permute-start(f32[2,256,128]{2,1,0:T(8,128)S(1)} %bitcast.30), channel_id=1, source_target_pairs={{0,128},{32,160},{1,129},{33,161},{2,130},{34,162},{3,131},{35,163... | collective-permute-start | bytes 786440 | tf_op jit(solution)/shard_map/ppermute | solution.py:370
  11.7 3.3 %shard_map.41 = (f32[8,4,64,128]{3,2,1,0:T(8,128)S(1)}, f32[8,128]{1,0:T(8,128)S(1)}) custom-call(f32[8,4,64,128]{3,2,1,0:T(8,128)S(1)} %copy-done, f32[4,64,128]{2,1,0:T(8,128)S(1)} %copy-done.3), custom_call_target="tpu_custom_call" | custom-call | flops 15728640 | bytes 2097152 | tf_op jit(solution)/shard_map/pallas_call | solution.py:359
  15.0 11.5 %collective-permute-done.1 = f32[2,256,128]{2,1,0:T(8,128)S(1)} collective-permute-done((f32[2,256,128]{2,1,0:T(8,128)S(1)}, f32[2,256,128]{2,1,0:T(8,128)S(1)}, u32[]{:S(2)}, u32[]{:S(2)}) %collective-permute-start.1) | collective-permute-done | bytes 262176 | tf_op jit(solution)/shard_map/ppermute | solution.py:370
  28.6 4.5 %collective-permute-start.10 = (f32[8,256,128]{2,1,0:T(8,128)S(1)}, f32[8,256,128]{2,1,0:T(8,128)S(1)}, u32[]{:S(2)}, u32[]{:S(2)}) collective-permute-start(f32[8,256,128]{2,1,0:T(8,128)S(1)} %bitcast.17), channel_id=1, source_target_pairs={{0,1},{1,2},{2,3},{3,4},{4,5},{5,6},{6,7},{7,8},{8,9},{9,10},{10,1... | collective-permute-start | bytes 3145736 | tf_op jit(solution)/shard_map/ppermute | solution.py:341
  37.0 3.4 %collective-permute-start.4 = (f32[2,256,128]{2,1,0:T(8,128)S(1)}, f32[2,256,128]{2,1,0:T(8,128)S(1)}, u32[]{:S(2)}, u32[]{:S(2)}) collective-permute-start(f32[2,256,128]{2,1,0:T(8,128)S(1)} %broadcast_select_fusion.refs_0_.refs_2_), channel_id=1, source_target_pairs={{0,32},{32,64},{64,96},{96,128},{128,160},{160,192},{192,224},{224... | collective-permute-start | bytes 786440 | tf_op jit(solution)/shard_map/ppermute | solution.py:336
  40.4 2.1 %collective-permute-done.5.refs_2_.refs_4_ = f32[2,256,128]{2,1,0:T(8,128)S(1)} collective-permute-done((f32[2,256,128]{2,1,0:T(8,128)S(1)}, f32[2,256,128]{2,1,0:T(8,128)S(1)}, u32[]{:S(2)}, u32[]{:S(2)}) %collective-permute-start.5) | collective-permute-done | bytes 262176 | tf_op jit(solution)/shard_map/ppermute | solution.py:336
  42.5 4.3 %collective-permute-start.7 = (f32[2,256,128]{2,1,0:T(8,128)S(1)}, f32[2,256,128]{2,1,0:T(8,128)S(1)}, u32[]{:S(2)}, u32[]{:S(2)}) collective-permute-start(f32[2,256,128]{2,1,0:T(8,128)S(1)} %collective-permute-done.5.refs_2_.refs_4_), channel_id=1, source_target_pairs={{0,224},{32,0},{64,32},{96,64},{128,96},{160,128},{192,160},{224,1... | collective-permute-start | bytes 786440 | tf_op jit(solution)/shard_map/ppermute | solution.py:336
  51.5 4.3 %collective-permute-start.9 = (f32[2,256,128]{2,1,0:T(8,128)S(1)}, f32[2,256,128]{2,1,0:T(8,128)S(1)}, u32[]{:S(2)}, u32[]{:S(2)}) collective-permute-start(f32[2,256,128]{2,1,0:T(8,128)S(1)} %collective-permute-done.7.refs_4_.refs_6_), channel_id=1, source_target_pairs={{0,224},{32,0},{64,32},{96,64},{128,96},{160,128},{192,160},{224,1... | collective-permute-start | bytes 786440 | tf_op jit(solution)/shard_map/ppermute | solution.py:336
  59.5 5.5 %collective-permute-done.11.right = f32[8,256,128]{2,1,0:T(8,128)} collective-permute-done((f32[8,256,128]{2,1,0:T(8,128)S(1)}, f32[8,256,128]{2,1,0:T(8,128)}, u32[]{:S(2)}, u32[]{:S(2)}) %collective-permute-start.11) | collective-permute-done | bytes 1048608 | tf_op jit(solution)/shard_map/ppermute | solution.py:342
  64.9 2.6 %shard_map.44 = (f32[8,256,128]{2,1,0:T(8,128)S(1)}, f32[8,128]{1,0:T(8,128)S(1)}) custom-call(f32[8,256,128]{2,1,0:T(8,128)S(1)} %bitcast.21, f32[8,256,128]{2,1,0:T(8,128)S(1)} %bitcast.28, f32[8,256,128]{2,1,0:T(8,128)S(1)} %collective-permute-done.10.left, f32[8,256,128]{2,1,0:T(8,128)} %collective-permute-done.11.right), custom_call_target="tpu_custom_call" | custom-call | flops 13107200 | bytes 5242880 | tf_op jit(solution)/shard_map/pallas_call | solution.py:401
  69.5 3.4 %collective-permute-start.12 = (f32[1,256,128]{2,1,0:T(8,128)S(1)}, f32[1,256,128]{2,1,0:T(8,128)S(1)}, u32[]{:S(2)}, u32[]{:S(2)}) collective-permute-start(f32[1,256,128]{2,1,0:T(8,128)S(1)} %slice.41), channel_id=1, source_target_pairs={{0,32},{32,64},{64,96},{96,128},{128,160},{160,192},{192,224},{224... | collective-permute-start | bytes 393224 | tf_op jit(solution)/shard_map/ppermute | solution.py:336
  72.9 3.1 %shard_map.45.refs_11_ = f32[8,128]{1,0:T(8,128)S(1)} custom-call(f32[2,256,128]{2,1,0:T(8,128)S(1)} %broadcast_select_fusion.refs_0_.refs_2_, f32[2,256,128]{2,1,0:T(8,128)S(1)} %collective-permute-done.4.refs_1_.refs_3_, f32[2,256,128]{2,1,0:T(8,128)S(1)} %collective-permute-done.5.refs_2_.refs_4_, ...), custom_call_target="tpu_custom_call" | custom-call | flops 5242880 | bytes 2621440 | tf_op jit(solution)/shard_map/pallas_call | solution.py:384
  76.0 3.1 %collective-permute-start.14 = (f32[8,128]{1,0:T(8,128)S(1)}, f32[8,128]{1,0:T(8,128)S(1)}, u32[]{:S(2)}, u32[]{:S(2)}) collective-permute-start(f32[8,128]{1,0:T(8,128)S(1)} %shard_map.45.refs_11_), channel_id=1, source_target_pairs={{0,256},{32,288},{1,257},{33,289},{2,258},{34,290},{3,259},{35,291... | collective-permute-start | bytes 12296 | tf_op jit(solution)/shard_map/ppermute | solution.py:408
  80.9 28.0 %all_to_all.10.refs_1_ = f32[32,8,128]{2,1,0:T(8,128)S(1)} all-to-all(f32[32,8,128]{2,1,0:T(8,128)S(1)} %shard_map.46), channel_id=1, replica_groups=mesh['band'=16,'domain'=32] {'domain'}, dimensions={0} | all-to-all | bytes 262144 | tf_op jit(solution)/shard_map/all_to_all | solution.py:331
  108.8 5.4 %shard_map.47 = (f32[8,256,128]{2,1,0:T(8,128)}, f32[8,128]{1,0:T(8,128)S(1)}, f32[8,128]{1,0:T(8,128)S(1)}, f32[8,8,128]{2,1,0:T(8,128)}) custom-call(s32[1]{0:T(128)} %bitcast.refs_0_.band_ref, f32[32,8,128]{2,1,0:T(8,128)S(1)} %all_to_all.10.refs_1_, f32[2,256,128]{2,1,0:T(8,128)S(1)} %broadcast_select_fusion.refs_0_.refs_2_, ...), custom_call_target="tpu_custom_call" | custom-call | flops 12582912 | bytes 4194304 | tf_op jit(solution)/shard_map/pallas_call | solution.py:412
  114.2 2.1 %collective-permute-start.15 = (f32[8,256,128]{2,1,0:T(8,128)}, f32[8,256,128]{2,1,0:T(8,128)S(1)}, u32[]{:S(2)}, u32[]{:S(2)}) collective-permute-start(f32[8,256,128]{2,1,0:T(8,128)} %get-tuple-element.36.f_ref), channel_id=1, source_target_pairs={{0,1},{1,2},{2,3},{3,4},{4,5},{5,6},{6,7},{7,8},{8,9},{9,10},{10,1... | collective-permute-start | bytes 3145736 | tf_op jit(solution)/shard_map/ppermute | solution.py:341
  116.3 2.2 %collective-permute-start.16 = (f32[8,256,128]{2,1,0:T(8,128)}, f32[8,256,128]{2,1,0:T(8,128)}, u32[]{:S(2)}, u32[]{:S(2)}) collective-permute-start(f32[8,256,128]{2,1,0:T(8,128)} %get-tuple-element.36.f_ref), channel_id=1, source_target_pairs={{1,0},{2,1},{3,2},{4,3},{5,4},{6,5},{7,6},{8,7},{9,8},{10,9},{11,1... | collective-permute-start | bytes 3145736 | tf_op jit(solution)/shard_map/ppermute | solution.py:342
  118.5 3.4 %all-to-all-start.1 = ((f32[8,8,128]{2,1,0:T(8,128)}), f32[8,8,128]{2,1,0:T(8,128)S(1)}, u32[]{:S(2)}, u32[]{:S(2)}) async-start(f32[8,8,128]{2,1,0:T(8,128)} %get-tuple-element.39), calls=%async_computation.1 | async-start | bytes 65536 | tf_op jit(solution)/shard_map/all_to_all | solution.py:423
  123.8 2.7 %shard_map.48 = f32[8,4,64,128]{3,2,1,0:T(8,128)S(1)} custom-call(f32[8,4,64,128]{3,2,1,0:T(8,128)S(1)} %bitcast.26, f32[4,64,128]{2,1,0:T(8,128)S(1)} %copy-done.3), custom_call_target="tpu_custom_call" | custom-call | flops 15728640 | bytes 2097152 | tf_op jit(solution)/shard_map/pallas_call | solution.py:359
  126.6 2.4 %all-to-all-done.1.shared_ref = f32[8,8,128]{2,1,0:T(8,128)S(1)} async-done(((f32[8,8,128]{2,1,0:T(8,128)}), f32[8,8,128]{2,1,0:T(8,128)S(1)}, u32[]{:S(2)}, u32[]{:S(2)}) %all-to-all-start.1) | async-done | bytes 32800 | tf_op jit(solution)/shard_map/all_to_all | solution.py:423
  131.6 12.0 %collective-permute-done.16.right_ref = f32[8,256,128]{2,1,0:T(8,128)} collective-permute-done((f32[8,256,128]{2,1,0:T(8,128)}, f32[8,256,128]{2,1,0:T(8,128)}, u32[]{:S(2)}, u32[]{:S(2)}) %collective-permute-start.16) | collective-permute-done | bytes 1048608 | tf_op jit(solution)/shard_map/ppermute | solution.py:342
  143.6 3.4 %shard_map.50 = f32[8,256,128]{2,1,0:T(8,128)} custom-call(f32[8,256,128]{2,1,0:T(8,128)S(1)} %copy-done.2, f32[8,256,128]{2,1,0:T(8,128)S(1)} %bitcast.27, f32[8,256,128]{2,1,0:T(8,128)S(1)} %collective-permute-done.15.left_ref, f32[8,256,128]{2,1,0:T(8,128)} %collective-permute-done.16.right_ref, f32[8,8,128]{2,1,0:T(8,128)S(1)} %shard_map.49.splat), custom_call_target="tpu_custom_call" | custom-call | flops 7864320 | bytes 5242880 | tf_op jit(solution)/shard_map/pallas_call | solution.py:428
  (37 shorter events, 23.9 us)
Async XLA Ops:
  0.6 11.1 %copy-start = (f32[8,4,64,128]{3,2,1,0:T(8,128)S(1)}, f32[8,4,64,128]{3,2,1,0:T(8,128)}, u32[]{:S(2)}) copy-start(f32[8,4,64,128]{3,2,1,0:T(8,128)} %f_ref.1) | copy-start | bytes 3145732
  0.6 11.1 %copy-start.3 = (f32[4,64,128]{2,1,0:T(8,128)S(1)}, f32[4,64,128]{2,1,0:T(8,128)}, u32[]{:S(2)}) copy-start(f32[4,64,128]{2,1,0:T(8,128)} %v_ref.3) | copy-start | bytes 393220
  2.0 13.0 %collective-permute-start = (f32[2,256,128]{2,1,0:T(8,128)S(1)}, f32[2,256,128]{2,1,0:T(8,128)S(1)}, u32[]{:S(2)}, u32[]{:S(2)}) collective-permute-start(f32[2,256,128]{2,1,0:T(8,128)S(1)} %bitcast.32), channel_id=1, source_target_pairs={{0,64},{32,96},{1,65},{33,97},{2,66},{34,98},{3,67},{35,99},{4,68}... | collective-permute-start | bytes 786440 | tf_op jit(solution)/shard_map/ppermute | solution.py:370
  7.1 19.5 %collective-permute-start.1 = (f32[2,256,128]{2,1,0:T(8,128)S(1)}, f32[2,256,128]{2,1,0:T(8,128)S(1)}, u32[]{:S(2)}, u32[]{:S(2)}) collective-permute-start(f32[2,256,128]{2,1,0:T(8,128)S(1)} %bitcast.31), channel_id=1, source_target_pairs={{0,192},{32,224},{1,193},{33,225},{2,194},{34,226},{3,195},{35,227... | collective-permute-start | bytes 786440 | tf_op jit(solution)/shard_map/ppermute | solution.py:370
  9.5 17.1 %collective-permute-start.2 = (f32[2,256,128]{2,1,0:T(8,128)S(1)}, f32[2,256,128]{2,1,0:T(8,128)S(1)}, u32[]{:S(2)}, u32[]{:S(2)}) collective-permute-start(f32[2,256,128]{2,1,0:T(8,128)S(1)} %bitcast.30), channel_id=1, source_target_pairs={{0,128},{32,160},{1,129},{33,161},{2,130},{34,162},{3,131},{35,163... | collective-permute-start | bytes 786440 | tf_op jit(solution)/shard_map/ppermute | solution.py:370
  26.6 8.4 %collective-permute-start.3 = (f32[2,256,128]{2,1,0:T(8,128)S(1)}, f32[2,256,128]{2,1,0:T(8,128)}, u32[]{:S(2)}, u32[]{:S(2)}) collective-permute-start(f32[2,256,128]{2,1,0:T(8,128)S(1)} %fusion.1), channel_id=1, source_target_pairs={{0,256},{32,288},{64,320},{96,352},{128,384},{160,416},{192,448},{... | collective-permute-start | bytes 786440 | tf_op jit(solution)/shard_map/ppermute | solution.py:378
  28.6 30.8 %collective-permute-start.10 = (f32[8,256,128]{2,1,0:T(8,128)S(1)}, f32[8,256,128]{2,1,0:T(8,128)S(1)}, u32[]{:S(2)}, u32[]{:S(2)}) collective-permute-start(f32[8,256,128]{2,1,0:T(8,128)S(1)} %bitcast.17), channel_id=1, source_target_pairs={{0,1},{1,2},{2,3},{3,4},{4,5},{5,6},{6,7},{7,8},{8,9},{9,10},{10,1... | collective-permute-start | bytes 3145736 | tf_op jit(solution)/shard_map/ppermute | solution.py:341
  33.1 31.8 %collective-permute-start.11 = (f32[8,256,128]{2,1,0:T(8,128)S(1)}, f32[8,256,128]{2,1,0:T(8,128)}, u32[]{:S(2)}, u32[]{:S(2)}) collective-permute-start(f32[8,256,128]{2,1,0:T(8,128)S(1)} %bitcast.18), channel_id=1, source_target_pairs={{1,0},{2,1},{3,2},{4,3},{5,4},{6,5},{7,6},{8,7},{9,8},{10,9},{11,1... | collective-permute-start | bytes 3145736 | tf_op jit(solution)/shard_map/ppermute | solution.py:342
  35.1 7.4 %collective-permute-start.5 = (f32[2,256,128]{2,1,0:T(8,128)S(1)}, f32[2,256,128]{2,1,0:T(8,128)S(1)}, u32[]{:S(2)}, u32[]{:S(2)}) collective-permute-start(f32[2,256,128]{2,1,0:T(8,128)S(1)} %broadcast_select_fusion.refs_0_.refs_2_), channel_id=1, source_target_pairs={{0,224},{32,0},{64,32},{96,64},{128,96},{160,128},{192,160},{224,1... | collective-permute-start | bytes 786440 | tf_op jit(solution)/shard_map/ppermute | solution.py:336
  37.0 10.5 %collective-permute-start.4 = (f32[2,256,128]{2,1,0:T(8,128)S(1)}, f32[2,256,128]{2,1,0:T(8,128)S(1)}, u32[]{:S(2)}, u32[]{:S(2)}) collective-permute-start(f32[2,256,128]{2,1,0:T(8,128)S(1)} %broadcast_select_fusion.refs_0_.refs_2_), channel_id=1, source_target_pairs={{0,32},{32,64},{64,96},{96,128},{128,160},{160,192},{192,224},{224... | collective-permute-start | bytes 786440 | tf_op jit(solution)/shard_map/ppermute | solution.py:336
  42.5 9.0 %collective-permute-start.7 = (f32[2,256,128]{2,1,0:T(8,128)S(1)}, f32[2,256,128]{2,1,0:T(8,128)S(1)}, u32[]{:S(2)}, u32[]{:S(2)}) collective-permute-start(f32[2,256,128]{2,1,0:T(8,128)S(1)} %collective-permute-done.5.refs_2_.refs_4_), channel_id=1, source_target_pairs={{0,224},{32,0},{64,32},{96,64},{128,96},{160,128},{192,160},{224,1... | collective-permute-start | bytes 786440 | tf_op jit(solution)/shard_map/ppermute | solution.py:336
  47.6 9.0 %collective-permute-start.6 = (f32[2,256,128]{2,1,0:T(8,128)S(1)}, f32[2,256,128]{2,1,0:T(8,128)S(1)}, u32[]{:S(2)}, u32[]{:S(2)}) collective-permute-start(f32[2,256,128]{2,1,0:T(8,128)S(1)} %collective-permute-done.4.refs_1_.refs_3_), channel_id=1, source_target_pairs={{0,32},{32,64},{64,96},{96,128},{128,160},{160,192},{192,224},{224... | collective-permute-start | bytes 786440 | tf_op jit(solution)/shard_map/ppermute | solution.py:336
  51.5 16.1 %collective-permute-start.9 = (f32[2,256,128]{2,1,0:T(8,128)S(1)}, f32[2,256,128]{2,1,0:T(8,128)S(1)}, u32[]{:S(2)}, u32[]{:S(2)}) collective-permute-start(f32[2,256,128]{2,1,0:T(8,128)S(1)} %collective-permute-done.7.refs_4_.refs_6_), channel_id=1, source_target_pairs={{0,224},{32,0},{64,32},{96,64},{128,96},{160,128},{192,160},{224,1... | collective-permute-start | bytes 786440 | tf_op jit(solution)/shard_map/ppermute | solution.py:336
  56.6 13.0 %collective-permute-start.8 = (f32[2,256,128]{2,1,0:T(8,128)S(1)}, f32[2,256,128]{2,1,0:T(8,128)S(1)}, u32[]{:S(2)}, u32[]{:S(2)}) collective-permute-start(f32[2,256,128]{2,1,0:T(8,128)S(1)} %collective-permute-done.6.refs_3_.refs_5_), channel_id=1, source_target_pairs={{0,32},{32,64},{64,96},{96,128},{128,160},{160,192},{192,224},{224... | collective-permute-start | bytes 786440 | tf_op jit(solution)/shard_map/ppermute | solution.py:336
  67.6 12.2 %collective-permute-start.13 = (f32[1,256,128]{2,1,0:T(8,128)S(1)}, f32[1,256,128]{2,1,0:T(8,128)S(1)}, u32[]{:S(2)}, u32[]{:S(2)}) collective-permute-start(f32[1,256,128]{2,1,0:T(8,128)S(1)} %slice.39), channel_id=1, source_target_pairs={{0,224},{32,0},{64,32},{96,64},{128,96},{160,128},{192,160},{224,1... | collective-permute-start | bytes 393224 | tf_op jit(solution)/shard_map/ppermute | solution.py:336
  69.5 10.3 %collective-permute-start.12 = (f32[1,256,128]{2,1,0:T(8,128)S(1)}, f32[1,256,128]{2,1,0:T(8,128)S(1)}, u32[]{:S(2)}, u32[]{:S(2)}) collective-permute-start(f32[1,256,128]{2,1,0:T(8,128)S(1)} %slice.41), channel_id=1, source_target_pairs={{0,32},{32,64},{64,96},{96,128},{128,160},{160,192},{192,224},{224... | collective-permute-start | bytes 393224 | tf_op jit(solution)/shard_map/ppermute | solution.py:336
  76.0 3.8 %collective-permute-start.14 = (f32[8,128]{1,0:T(8,128)S(1)}, f32[8,128]{1,0:T(8,128)S(1)}, u32[]{:S(2)}, u32[]{:S(2)}) collective-permute-start(f32[8,128]{1,0:T(8,128)S(1)} %shard_map.45.refs_11_), channel_id=1, source_target_pairs={{0,256},{32,288},{1,257},{33,289},{2,258},{34,290},{3,259},{35,291... | collective-permute-start | bytes 12296 | tf_op jit(solution)/shard_map/ppermute | solution.py:408
  114.2 17.4 %collective-permute-start.15 = (f32[8,256,128]{2,1,0:T(8,128)}, f32[8,256,128]{2,1,0:T(8,128)S(1)}, u32[]{:S(2)}, u32[]{:S(2)}) collective-permute-start(f32[8,256,128]{2,1,0:T(8,128)} %get-tuple-element.36.f_ref), channel_id=1, source_target_pairs={{0,1},{1,2},{2,3},{3,4},{4,5},{5,6},{6,7},{7,8},{8,9},{9,10},{10,1... | collective-permute-start | bytes 3145736 | tf_op jit(solution)/shard_map/ppermute | solution.py:341
  116.3 27.3 %collective-permute-start.16 = (f32[8,256,128]{2,1,0:T(8,128)}, f32[8,256,128]{2,1,0:T(8,128)}, u32[]{:S(2)}, u32[]{:S(2)}) collective-permute-start(f32[8,256,128]{2,1,0:T(8,128)} %get-tuple-element.36.f_ref), channel_id=1, source_target_pairs={{1,0},{2,1},{3,2},{4,3},{5,4},{6,5},{7,6},{8,7},{9,8},{10,9},{11,1... | collective-permute-start | bytes 3145736 | tf_op jit(solution)/shard_map/ppermute | solution.py:342
  118.5 10.5 %all-to-all-start.1 = ((f32[8,8,128]{2,1,0:T(8,128)}), f32[8,8,128]{2,1,0:T(8,128)S(1)}, u32[]{:S(2)}, u32[]{:S(2)}) async-start(f32[8,8,128]{2,1,0:T(8,128)} %get-tuple-element.39), calls=%async_computation.1 | async-start | bytes 65536 | tf_op jit(solution)/shard_map/all_to_all | solution.py:423
  122.6 1.2 copy-start.1
  123.8 19.8 %copy-start.2 = (f32[8,256,128]{2,1,0:T(8,128)S(1)}, f32[8,256,128]{2,1,0:T(8,128)}, u32[]{:S(2)}) copy-start(f32[8,256,128]{2,1,0:T(8,128)} %get-tuple-element.36.f_ref) | copy-start | bytes 3145732

commit v3 on v2

--- a/solution.py
+++ b/solution.py
@@ -112,25 +112,24 @@
     jobs += split([(q, r) for q in fresh for r in range(q + 1)])
     jobs += split([(q, r) for q in IMAGE for r in imaged])
     total = pair_sums(jobs, load, chunks)
-    for part in before[: len(before) - last]:
+    for part in before:
         total = total + part[...]
     if last:
-        for n in range(3):
-            total = total + move(before[-1][...], 32 * n + 24, 96 + 8 * n)
         for n in range(out.shape[0]):
             out[n] = total
     else:
         out[...] = total
 
 
-def combine_kernel(cells_total, band_ref, sums_ref, *refs):
-    *pieces, own, out, weights_ref, gram_ref, shared, splat = refs
+def total_kernel(cells_total, parts_ref, out):
+    out[...] = jnp.sum(parts_ref[...], axis=0) / cells_total
+
+
+def combine_kernel(band_ref, sums_ref, *refs):
+    *pieces, own, out, weights_ref, gram_ref, splat = refs
     band = band_ref[0]
     lane, sub = lanes(), subs()
-    sums = jnp.sum(sums_ref[...], axis=0) / cells_total
-    for n in range(shared.shape[0]):
-        shared[n] = sums
-    tiles = unpacked(sums)
+    tiles = unpacked(sums_ref[...])
     turned = jnp.transpose(tall(tiles))
     w0, w1, w2 = (
         jnp.where(lane < 24, tile + jnp.where(lane == sub + 8 * n, 0.0, turned[8 * n : 8 * n + 8]), 0.0)
@@ -285,11 +284,7 @@
         return jnp.where((wide >= target) & (wide < target + 8), columns, 0.0)
 
     def visiting(n):
-        packed = shared_ref[n]
-        home = tall([move(packed, 32 * k + 24, 0) for k in range(3)])
-        away = tall([move(packed, 96 + 8 * k, 0) for k in range(3)])
-        matrix = jnp.where(band_ref[0] < RING, home, away)
-        return image_columns(matrix, places(n, n), 0, 8 * n)
+        return image_columns(tall(unpacked(shared_ref[n])), places(n, n), 24, 8 * n)
 
     block0, block1 = visiting(0), visiting(1)
     block = image_columns(tall(unpacked(own_ref[...])), place, 24, 16)
@@ -378,12 +373,11 @@
     crossed = lax.ppermute(piece, "band", [(y, y + RING) for y in range(RING)])
     piece = jnp.where(band < RING, piece, crossed)
 
-    def stage(fresh, imaged, pieces, *sums, guest=None):
+    def stage(fresh, imaged, pieces, *sums, last=False):
         sources = (*pieces, own, *((image,) if imaged else ()), *sums)
-        sources += () if guest is None else (guest,)
         return call(
-            lambda *refs: stage_kernel(len(pieces), fresh, imaged, guest is not None, *refs),
-            tile if guest is None else jax.ShapeDtypeStruct((domain, 8, 128), F32),
+            lambda *refs: stage_kernel(len(pieces), fresh, imaged, last, *refs),
+            jax.ShapeDtypeStruct((domain, 8, 128), F32) if last else tile,
             specs=[VMEM] * len(sources),
             flops=20 * big,
             bytes_moved=10 * big,
@@ -405,26 +399,34 @@
     pieces += [up, down]
     up, down = ring_shift(up[:1], 1), ring_shift(down[1:], -1)
     sums = stage(range(10, 14), range(14), pieces, sums, image_sums)
+    pieces += [up, down]
+    sums = stage(range(14, 16), range(14, 16), pieces, sums, last=True)
+    sums = call(
+        lambda *refs: total_kernel(cells_total, *refs),
+        tile,
+        specs=[VMEM],
+        flops=40 * 1024,
+        bytes_moved=160 * 1024,
+    )(domain_parts(sums))
     guest = lax.ppermute(sums, "band", [(0, RING), (1, RING + 1)])
-    pieces += [up, down]
-    sums = stage(range(14, 16), range(14, 16), pieces, sums, guest=guest)
-    sums = domain_parts(sums)
-    basis, weights, gram, shared = call(
-        lambda *refs: combine_kernel(cells_total, *refs),
-        (slab, tile, tile, jax.ShapeDtypeStruct((RING, 8, 128), F32)),
+    basis, weights, gram = call(
+        combine_kernel,
+        (slab, tile, tile),
         scratch=[pltpu.VMEM((24, 8, 128), F32)],
         specs=[SMEM] + [VMEM] * 11,
         flops=48 * big,
         bytes_moved=16 * big,
     )(band_word, sums, *pieces, own)
+    basis, guest = lax.optimization_barrier((basis, guest))
     left, right = neighbours(basis)
-    own_sums = shared[0]
+    shared = jnp.where((band == RING) | (band == RING + 1), guest, sums)
+    shared = jnp.broadcast_to(shared, (RING, 8, 128))
     rings = [list(range(RING)), list(range(RING, bands))]
     shared = lax.all_to_all(shared, "band", 0, 0, axis_index_groups=rings)
     inner = inner_part(basis.reshape(orbitals.shape))[0].reshape(flat)
     splat = call(
         coeff_kernel, jax.ShapeDtypeStruct((8, 8, 128), F32), specs=[SMEM] + [VMEM] * 4
-    )(band_word, weights, gram, own_sums, shared)
+    )(band_word, weights, gram, sums, shared)
     residual = call(
         residual_kernel, slab, specs=[VMEM] * 5, flops=30 * big, bytes_moved=20 * big
     )(basis, inner, left, right, splat)

time: 148 us -> 150 us (1.014)
  starting transfers between devices: 51.8 us -> 58.4 us
  blocking collectives: 28 us -> 21.5 us
  waiting for transfers between devices: 37.8 us -> 39.4 us
    ppermute x1, starting transfers between devices: 3.09 us -> 9.55 us  [local(): guest = lax.ppermute(sums, 'band', [(0, RING), (1, RING + 1)])]
    all_to_all x1, blocking collectives: 28 us -> 21.5 us  [domain_parts(): return lax.all_to_all(copies, 'domain', 0, 0)]
    ppermute x8, waiting for transfers between devices: 4.54 us -> 6.75 us  [ring_shift(): return lax.ppermute(block, 'band', pairs)]
    pallas_call x5 -> x6, Pallas kernels: 11.6 us -> 11.6 us  [the longest x4 6.18 us: stage(): call(lambda *refs: stage_kernel(len(pieces), fresh, imaged, last, *refs),...]
  transfers between devices with their start and end apart: 18 -> 18, of which waited for: 10 -> 10; matrix products, arithmetic and copies ran while one was open for 1% -> 0% of each run, Pallas kernels for 10% -> 14%
where the time goes in v3:
time: 150 us; the launch traced here: 149 us
  starting transfers between devices  58.4 us (39%)
  waiting for transfers between devices  39.4 us (26%)
  Pallas kernels  25.2 us (17%)
  blocking collectives  21.5 us (14%)
  local copies, waits for them, and re-layouts  1.87 us (1%)
    ppermute x8, starting transfers between devices, ring_shift(): return lax.ppermute(block, 'band', pairs)  23 us
    all_to_all x1, blocking collectives, domain_parts(): return lax.all_to_all(copies, 'domain', 0, 0)  21.5 us
    ppermute x2, waiting for transfers between devices, neighbours(): lax.ppermute(block, 'domain', [((i + 1) % count, i) for i in range(count)])  17.5 us
    ppermute x3, waiting for transfers between devices, local(): lax.ppermute(quarters[k], 'band', [(0, 2 * k), (1, 2 * k + 1)])  11.5 us
    ppermute x3, starting transfers between devices, local(): lax.ppermute(quarters[k], 'band', [(0, 2 * k), (1, 2 * k + 1)])  9.65 us
    ppermute x1, starting transfers between devices, local(): guest = lax.ppermute(sums, 'band', [(0, RING), (1, RING + 1)])  9.55 us
    ppermute x2, starting transfers between devices, neighbours(): lax.ppermute(block, 'domain', [(i, (i + 1) % count) for i in range(count)])  6.86 us
    ppermute x8, waiting for transfers between devices, ring_shift(): return lax.ppermute(block, 'band', pairs)  6.75 us
  transfers between devices with their start and end apart: 18, of which 10 were waited for; matrix products, arithmetic and copies ran while one was open for 0% of the time, Pallas kernels for 14%

profile of v3, /device:TPU:1, one launch (start us, length us, event | category | flops | bytes accessed | tf_op | source)
XLA Modules:
  0.0 148.8 jit_solution(14688555340603820624)
XLA Ops:
  2.0 5.1 %collective-permute-start = (f32[2,256,128]{2,1,0:T(8,128)S(1)}, f32[2,256,128]{2,1,0:T(8,128)S(1)}, u32[]{:S(2)}, u32[]{:S(2)}) collective-permute-start(f32[2,256,128]{2,1,0:T(8,128)S(1)} %bitcast.30), channel_id=1, source_target_pairs={{0,64},{32,96},{1,65},{33,97},{2,66},{34,98},{3,67},{35,99},{4,68}... | collective-permute-start | bytes 786440 | tf_op jit(solution)/shard_map/ppermute | solution.py:365
  7.1 2.3 %collective-permute-start.1 = (f32[2,256,128]{2,1,0:T(8,128)S(1)}, f32[2,256,128]{2,1,0:T(8,128)S(1)}, u32[]{:S(2)}, u32[]{:S(2)}) collective-permute-start(f32[2,256,128]{2,1,0:T(8,128)S(1)} %bitcast.29), channel_id=1, source_target_pairs={{0,192},{32,224},{1,193},{33,225},{2,194},{34,226},{3,195},{35,227... | collective-permute-start | bytes 786440 | tf_op jit(solution)/shard_map/ppermute | solution.py:365
  9.5 2.2 %collective-permute-start.2 = (f32[2,256,128]{2,1,0:T(8,128)S(1)}, f32[2,256,128]{2,1,0:T(8,128)S(1)}, u32[]{:S(2)}, u32[]{:S(2)}) collective-permute-start(f32[2,256,128]{2,1,0:T(8,128)S(1)} %bitcast.28), channel_id=1, source_target_pairs={{0,128},{32,160},{1,129},{33,161},{2,130},{34,162},{3,131},{35,163... | collective-permute-start | bytes 786440 | tf_op jit(solution)/shard_map/ppermute | solution.py:365
  11.7 3.3 %shard_map.41 = (f32[8,4,64,128]{3,2,1,0:T(8,128)S(1)}, f32[8,128]{1,0:T(8,128)S(1)}) custom-call(f32[8,4,64,128]{3,2,1,0:T(8,128)S(1)} %copy-done, f32[4,64,128]{2,1,0:T(8,128)S(1)} %copy-done.3), custom_call_target="tpu_custom_call" | custom-call | flops 15728640 | bytes 2097152 | tf_op jit(solution)/shard_map/pallas_call | solution.py:354
  15.0 11.5 %collective-permute-done.1 = f32[2,256,128]{2,1,0:T(8,128)S(1)} collective-permute-done((f32[2,256,128]{2,1,0:T(8,128)S(1)}, f32[2,256,128]{2,1,0:T(8,128)S(1)}, u32[]{:S(2)}, u32[]{:S(2)}) %collective-permute-start.1) | collective-permute-done | bytes 262176 | tf_op jit(solution)/shard_map/ppermute | solution.py:365
  28.6 4.5 %collective-permute-start.10 = (f32[8,256,128]{2,1,0:T(8,128)S(1)}, f32[8,256,128]{2,1,0:T(8,128)S(1)}, u32[]{:S(2)}, u32[]{:S(2)}) collective-permute-start(f32[8,256,128]{2,1,0:T(8,128)S(1)} %bitcast.15), channel_id=1, source_target_pairs={{0,1},{1,2},{2,3},{3,4},{4,5},{5,6},{6,7},{7,8},{8,9},{9,10},{10,1... | collective-permute-start | bytes 3145736 | tf_op jit(solution)/shard_map/ppermute | solution.py:336
  37.0 3.4 %collective-permute-start.4 = (f32[2,256,128]{2,1,0:T(8,128)S(1)}, f32[2,256,128]{2,1,0:T(8,128)S(1)}, u32[]{:S(2)}, u32[]{:S(2)}) collective-permute-start(f32[2,256,128]{2,1,0:T(8,128)S(1)} %broadcast_select_fusion.refs_0_), channel_id=1, source_target_pairs={{0,32},{32,64},{64,96},{96,128},{128,160},{160,192},{192,224},{224... | collective-permute-start | bytes 786440 | tf_op jit(solution)/shard_map/ppermute | solution.py:331
  42.5 4.3 %collective-permute-start.7 = (f32[2,256,128]{2,1,0:T(8,128)S(1)}, f32[2,256,128]{2,1,0:T(8,128)S(1)}, u32[]{:S(2)}, u32[]{:S(2)}) collective-permute-start(f32[2,256,128]{2,1,0:T(8,128)S(1)} %collective-permute-done.5.refs_2_), channel_id=1, source_target_pairs={{0,224},{32,0},{64,32},{96,64},{128,96},{160,128},{192,160},{224,1... | collective-permute-start | bytes 786440 | tf_op jit(solution)/shard_map/ppermute | solution.py:331
  51.5 4.3 %collective-permute-start.9 = (f32[2,256,128]{2,1,0:T(8,128)S(1)}, f32[2,256,128]{2,1,0:T(8,128)S(1)}, u32[]{:S(2)}, u32[]{:S(2)}) collective-permute-start(f32[2,256,128]{2,1,0:T(8,128)S(1)} %collective-permute-done.7.refs_4_), channel_id=1, source_target_pairs={{0,224},{32,0},{64,32},{96,64},{128,96},{160,128},{192,160},{224,1... | collective-permute-start | bytes 786440 | tf_op jit(solution)/shard_map/ppermute | solution.py:331
  59.5 5.5 %collective-permute-done.11.right = f32[8,256,128]{2,1,0:T(8,128)} collective-permute-done((f32[8,256,128]{2,1,0:T(8,128)S(1)}, f32[8,256,128]{2,1,0:T(8,128)}, u32[]{:S(2)}, u32[]{:S(2)}) %collective-permute-start.11) | collective-permute-done | bytes 1048608 | tf_op jit(solution)/shard_map/ppermute | solution.py:337
  64.9 2.6 %shard_map.44 = (f32[8,256,128]{2,1,0:T(8,128)S(1)}, f32[8,128]{1,0:T(8,128)S(1)}) custom-call(f32[8,256,128]{2,1,0:T(8,128)S(1)} %bitcast.19, f32[8,256,128]{2,1,0:T(8,128)S(1)} %bitcast.26, f32[8,256,128]{2,1,0:T(8,128)S(1)} %collective-permute-done.10.left, f32[8,256,128]{2,1,0:T(8,128)} %collective-permute-done.11.right), custom_call_target="tpu_custom_call" | custom-call | flops 13107200 | bytes 5242880 | tf_op jit(solution)/shard_map/pallas_call | solution.py:395
  69.5 3.4 %collective-permute-start.12 = (f32[1,256,128]{2,1,0:T(8,128)S(1)}, f32[1,256,128]{2,1,0:T(8,128)S(1)}, u32[]{:S(2)}, u32[]{:S(2)}) collective-permute-start(f32[1,256,128]{2,1,0:T(8,128)S(1)} %slice.37), channel_id=1, source_target_pairs={{0,32},{32,64},{64,96},{96,128},{128,160},{160,192},{192,224},{224... | collective-permute-start | bytes 393224 | tf_op jit(solution)/shard_map/ppermute | solution.py:331
  72.9 3.1 %shard_map.45.refs_11_ = f32[8,128]{1,0:T(8,128)S(1)} custom-call(f32[2,256,128]{2,1,0:T(8,128)S(1)} %broadcast_select_fusion.refs_0_, f32[2,256,128]{2,1,0:T(8,128)S(1)} %collective-permute-done.4.refs_1_, f32[2,256,128]{2,1,0:T(8,128)S(1)} %collective-permute-done.5.refs_2_, f32[2,256,128]{2,1,0:T(8,128)S(1)} %collective-permute-done.6.refs_3_, ...), custom_call_target="tpu_custom_call" | custom-call | flops 5242880 | bytes 2621440 | tf_op jit(solution)/shard_map/pallas_call | solution.py:378
  76.0 2.2 %collective-permute-done.12.refs_7_ = f32[1,256,128]{2,1,0:T(8,128)S(1)} collective-permute-done((f32[1,256,128]{2,1,0:T(8,128)S(1)}, f32[1,256,128]{2,1,0:T(8,128)S(1)}, u32[]{:S(2)}, u32[]{:S(2)}) %collective-permute-start.12) | collective-permute-done | bytes 131104 | tf_op jit(solution)/shard_map/ppermute | solution.py:331
  79.2 21.5 %all_to_all.10.refs_0_ = f32[32,8,128]{2,1,0:T(8,128)S(1)} all-to-all(f32[32,8,128]{2,1,0:T(8,128)S(1)} %shard_map.46), channel_id=1, replica_groups=mesh['band'=16,'domain'=32] {'domain'}, dimensions={0} | all-to-all | bytes 262144 | tf_op jit(solution)/shard_map/all_to_all | solution.py:326
  100.8 9.6 %collective-permute-start.14 = (f32[8,128]{1,0:T(8,128)S(1)}, f32[8,128]{1,0:T(8,128)S(1)}, u32[]{:S(2)}, u32[]{:S(2)}) collective-permute-start(f32[8,128]{1,0:T(8,128)S(1)} %shard_map.47.sums_ref.own_ref), channel_id=1, source_target_pairs={{0,256},{32,288},{1,257},{33,289},{2,258},{34,290},{3,259},{35,291... | collective-permute-start | bytes 12296 | tf_op jit(solution)/shard_map/ppermute | solution.py:411
  110.3 5.4 %shard_map.48 = (f32[8,256,128]{2,1,0:T(8,128)}, f32[8,128]{1,0:T(8,128)S(1)}, f32[8,128]{1,0:T(8,128)S(1)}) custom-call(s32[1]{0:T(128)} %bitcast.band_ref, f32[8,128]{1,0:T(8,128)S(1)} %shard_map.47.sums_ref.own_ref, f32[2,256,128]{2,1,0:T(8,128)S(1)} %broadcast_select_fusion.refs_0_, f32[2,256,128]{2,1,0:T(8,128)S(1)} %collective-permute-done.4.refs_1_, ...), custom_call_target="tpu_custom_call" | custom-call | flops 12582912 | bytes 4194304 | tf_op jit(solution)/shard_map/pallas_call | solution.py:412
  115.7 2.4 %collective-permute-start.15 = (f32[8,256,128]{2,1,0:T(8,128)}, f32[8,256,128]{2,1,0:T(8,128)S(1)}, u32[]{:S(2)}, u32[]{:S(2)}) collective-permute-start(f32[8,256,128]{2,1,0:T(8,128)} %get-tuple-element.38.f_ref), channel_id=1, source_target_pairs={{0,1},{1,2},{2,3},{3,4},{4,5},{5,6},{6,7},{7,8},{8,9},{9,10},{10,1... | collective-permute-start | bytes 3145736 | tf_op jit(solution)/shard_map/ppermute | solution.py:336
  118.1 2.1 %collective-permute-start.16 = (f32[8,256,128]{2,1,0:T(8,128)}, f32[8,256,128]{2,1,0:T(8,128)}, u32[]{:S(2)}, u32[]{:S(2)}) collective-permute-start(f32[8,256,128]{2,1,0:T(8,128)} %get-tuple-element.38.f_ref), channel_id=1, source_target_pairs={{1,0},{2,1},{3,2},{4,3},{5,4},{6,5},{7,6},{8,7},{9,8},{10,9},{11,1... | collective-permute-start | bytes 3145736 | tf_op jit(solution)/shard_map/ppermute | solution.py:337
  120.9 3.3 %all-to-all-start.1 = ((f32[8,8,128]{2,1,0:T(8,128)}), f32[8,8,128]{2,1,0:T(8,128)S(1)}, u32[]{:S(2)}, u32[]{:S(2)}) async-start(f32[8,8,128]{2,1,0:T(8,128)} %broadcast_in_dim.8), calls=%async_computation.1 | async-start | bytes 65536 | tf_op jit(solution)/shard_map/all_to_all | solution.py:425
  125.5 2.7 %shard_map.49 = f32[8,4,64,128]{3,2,1,0:T(8,128)S(1)} custom-call(f32[8,4,64,128]{3,2,1,0:T(8,128)S(1)} %bitcast.24, f32[4,64,128]{2,1,0:T(8,128)S(1)} %copy-done.3), custom_call_target="tpu_custom_call" | custom-call | flops 15728640 | bytes 2097152 | tf_op jit(solution)/shard_map/pallas_call | solution.py:354
  128.2 3.1 %all-to-all-done.1.shared_ref = f32[8,8,128]{2,1,0:T(8,128)S(1)} async-done(((f32[8,8,128]{2,1,0:T(8,128)}), f32[8,8,128]{2,1,0:T(8,128)S(1)}, u32[]{:S(2)}, u32[]{:S(2)}) %all-to-all-start.1) | async-done | bytes 32800 | tf_op jit(solution)/shard_map/all_to_all | solution.py:425
  133.4 12.0 %collective-permute-done.16.right_ref = f32[8,256,128]{2,1,0:T(8,128)} collective-permute-done((f32[8,256,128]{2,1,0:T(8,128)}, f32[8,256,128]{2,1,0:T(8,128)}, u32[]{:S(2)}, u32[]{:S(2)}) %collective-permute-start.16) | collective-permute-done | bytes 1048608 | tf_op jit(solution)/shard_map/ppermute | solution.py:337
  145.4 3.4 %shard_map.51 = f32[8,256,128]{2,1,0:T(8,128)} custom-call(f32[8,256,128]{2,1,0:T(8,128)S(1)} %copy-done.2, f32[8,256,128]{2,1,0:T(8,128)S(1)} %bitcast.25, f32[8,256,128]{2,1,0:T(8,128)S(1)} %collective-permute-done.15.left_ref, f32[8,256,128]{2,1,0:T(8,128)} %collective-permute-done.16.right_ref, f32[8,8,128]{2,1,0:T(8,128)S(1)} %shard_map.50.splat), custom_call_target="tpu_custom_call" | custom-call | flops 7864320 | bytes 5242880 | tf_op jit(solution)/shard_map/pallas_call | solution.py:430
  (39 shorter events, 24.7 us)
Async XLA Ops:
  0.6 11.1 %copy-start = (f32[8,4,64,128]{3,2,1,0:T(8,128)S(1)}, f32[8,4,64,128]{3,2,1,0:T(8,128)}, u32[]{:S(2)}) copy-start(f32[8,4,64,128]{3,2,1,0:T(8,128)} %f_ref.1) | copy-start | bytes 3145732
  0.6 11.1 %copy-start.3 = (f32[4,64,128]{2,1,0:T(8,128)S(1)}, f32[4,64,128]{2,1,0:T(8,128)}, u32[]{:S(2)}) copy-start(f32[4,64,128]{2,1,0:T(8,128)} %v_ref.3) | copy-start | bytes 393220
  2.0 13.0 %collective-permute-start = (f32[2,256,128]{2,1,0:T(8,128)S(1)}, f32[2,256,128]{2,1,0:T(8,128)S(1)}, u32[]{:S(2)}, u32[]{:S(2)}) collective-permute-start(f32[2,256,128]{2,1,0:T(8,128)S(1)} %bitcast.30), channel_id=1, source_target_pairs={{0,64},{32,96},{1,65},{33,97},{2,66},{34,98},{3,67},{35,99},{4,68}... | collective-permute-start | bytes 786440 | tf_op jit(solution)/shard_map/ppermute | solution.py:365
  7.1 19.5 %collective-permute-start.1 = (f32[2,256,128]{2,1,0:T(8,128)S(1)}, f32[2,256,128]{2,1,0:T(8,128)S(1)}, u32[]{:S(2)}, u32[]{:S(2)}) collective-permute-start(f32[2,256,128]{2,1,0:T(8,128)S(1)} %bitcast.29), channel_id=1, source_target_pairs={{0,192},{32,224},{1,193},{33,225},{2,194},{34,226},{3,195},{35,227... | collective-permute-start | bytes 786440 | tf_op jit(solution)/shard_map/ppermute | solution.py:365
  9.5 17.1 %collective-permute-start.2 = (f32[2,256,128]{2,1,0:T(8,128)S(1)}, f32[2,256,128]{2,1,0:T(8,128)S(1)}, u32[]{:S(2)}, u32[]{:S(2)}) collective-permute-start(f32[2,256,128]{2,1,0:T(8,128)S(1)} %bitcast.28), channel_id=1, source_target_pairs={{0,128},{32,160},{1,129},{33,161},{2,130},{34,162},{3,131},{35,163... | collective-permute-start | bytes 786440 | tf_op jit(solution)/shard_map/ppermute | solution.py:365
  26.6 8.4 %collective-permute-start.3 = (f32[2,256,128]{2,1,0:T(8,128)S(1)}, f32[2,256,128]{2,1,0:T(8,128)}, u32[]{:S(2)}, u32[]{:S(2)}) collective-permute-start(f32[2,256,128]{2,1,0:T(8,128)S(1)} %fusion.1), channel_id=1, source_target_pairs={{0,256},{32,288},{64,320},{96,352},{128,384},{160,416},{192,448},{... | collective-permute-start | bytes 786440 | tf_op jit(solution)/shard_map/ppermute | solution.py:373
  28.6 30.8 %collective-permute-start.10 = (f32[8,256,128]{2,1,0:T(8,128)S(1)}, f32[8,256,128]{2,1,0:T(8,128)S(1)}, u32[]{:S(2)}, u32[]{:S(2)}) collective-permute-start(f32[8,256,128]{2,1,0:T(8,128)S(1)} %bitcast.15), channel_id=1, source_target_pairs={{0,1},{1,2},{2,3},{3,4},{4,5},{5,6},{6,7},{7,8},{8,9},{9,10},{10,1... | collective-permute-start | bytes 3145736 | tf_op jit(solution)/shard_map/ppermute | solution.py:336
  33.1 31.8 %collective-permute-start.11 = (f32[8,256,128]{2,1,0:T(8,128)S(1)}, f32[8,256,128]{2,1,0:T(8,128)}, u32[]{:S(2)}, u32[]{:S(2)}) collective-permute-start(f32[8,256,128]{2,1,0:T(8,128)S(1)} %bitcast.16), channel_id=1, source_target_pairs={{1,0},{2,1},{3,2},{4,3},{5,4},{6,5},{7,6},{8,7},{9,8},{10,9},{11,1... | collective-permute-start | bytes 3145736 | tf_op jit(solution)/shard_map/ppermute | solution.py:337
  35.1 7.4 %collective-permute-start.5 = (f32[2,256,128]{2,1,0:T(8,128)S(1)}, f32[2,256,128]{2,1,0:T(8,128)S(1)}, u32[]{:S(2)}, u32[]{:S(2)}) collective-permute-start(f32[2,256,128]{2,1,0:T(8,128)S(1)} %broadcast_select_fusion.refs_0_), channel_id=1, source_target_pairs={{0,224},{32,0},{64,32},{96,64},{128,96},{160,128},{192,160},{224,1... | collective-permute-start | bytes 786440 | tf_op jit(solution)/shard_map/ppermute | solution.py:331
  37.0 10.5 %collective-permute-start.4 = (f32[2,256,128]{2,1,0:T(8,128)S(1)}, f32[2,256,128]{2,1,0:T(8,128)S(1)}, u32[]{:S(2)}, u32[]{:S(2)}) collective-permute-start(f32[2,256,128]{2,1,0:T(8,128)S(1)} %broadcast_select_fusion.refs_0_), channel_id=1, source_target_pairs={{0,32},{32,64},{64,96},{96,128},{128,160},{160,192},{192,224},{224... | collective-permute-start | bytes 786440 | tf_op jit(solution)/shard_map/ppermute | solution.py:331
  42.5 9.0 %collective-permute-start.7 = (f32[2,256,128]{2,1,0:T(8,128)S(1)}, f32[2,256,128]{2,1,0:T(8,128)S(1)}, u32[]{:S(2)}, u32[]{:S(2)}) collective-permute-start(f32[2,256,128]{2,1,0:T(8,128)S(1)} %collective-permute-done.5.refs_2_), channel_id=1, source_target_pairs={{0,224},{32,0},{64,32},{96,64},{128,96},{160,128},{192,160},{224,1... | collective-permute-start | bytes 786440 | tf_op jit(solution)/shard_map/ppermute | solution.py:331
  47.6 9.0 %collective-permute-start.6 = (f32[2,256,128]{2,1,0:T(8,128)S(1)}, f32[2,256,128]{2,1,0:T(8,128)S(1)}, u32[]{:S(2)}, u32[]{:S(2)}) collective-permute-start(f32[2,256,128]{2,1,0:T(8,128)S(1)} %collective-permute-done.4.refs_1_), channel_id=1, source_target_pairs={{0,32},{32,64},{64,96},{96,128},{128,160},{160,192},{192,224},{224... | collective-permute-start | bytes 786440 | tf_op jit(solution)/shard_map/ppermute | solution.py:331
  51.5 16.1 %collective-permute-start.9 = (f32[2,256,128]{2,1,0:T(8,128)S(1)}, f32[2,256,128]{2,1,0:T(8,128)S(1)}, u32[]{:S(2)}, u32[]{:S(2)}) collective-permute-start(f32[2,256,128]{2,1,0:T(8,128)S(1)} %collective-permute-done.7.refs_4_), channel_id=1, source_target_pairs={{0,224},{32,0},{64,32},{96,64},{128,96},{160,128},{192,160},{224,1... | collective-permute-start | bytes 786440 | tf_op jit(solution)/shard_map/ppermute | solution.py:331
  56.6 13.0 %collective-permute-start.8 = (f32[2,256,128]{2,1,0:T(8,128)S(1)}, f32[2,256,128]{2,1,0:T(8,128)S(1)}, u32[]{:S(2)}, u32[]{:S(2)}) collective-permute-start(f32[2,256,128]{2,1,0:T(8,128)S(1)} %collective-permute-done.6.refs_3_), channel_id=1, source_target_pairs={{0,32},{32,64},{64,96},{96,128},{128,160},{160,192},{192,224},{224... | collective-permute-start | bytes 786440 | tf_op jit(solution)/shard_map/ppermute | solution.py:331
  67.6 8.4 %collective-permute-start.13 = (f32[1,256,128]{2,1,0:T(8,128)S(1)}, f32[1,256,128]{2,1,0:T(8,128)S(1)}, u32[]{:S(2)}, u32[]{:S(2)}) collective-permute-start(f32[1,256,128]{2,1,0:T(8,128)S(1)} %slice.36), channel_id=1, source_target_pairs={{0,224},{32,0},{64,32},{96,64},{128,96},{160,128},{192,160},{224,1... | collective-permute-start | bytes 393224 | tf_op jit(solution)/shard_map/ppermute | solution.py:331
  69.5 8.7 %collective-permute-start.12 = (f32[1,256,128]{2,1,0:T(8,128)S(1)}, f32[1,256,128]{2,1,0:T(8,128)S(1)}, u32[]{:S(2)}, u32[]{:S(2)}) collective-permute-start(f32[1,256,128]{2,1,0:T(8,128)S(1)} %slice.37), channel_id=1, source_target_pairs={{0,32},{32,64},{64,96},{96,128},{128,160},{160,192},{192,224},{224... | collective-permute-start | bytes 393224 | tf_op jit(solution)/shard_map/ppermute | solution.py:331
  100.8 15.0 %collective-permute-start.14 = (f32[8,128]{1,0:T(8,128)S(1)}, f32[8,128]{1,0:T(8,128)S(1)}, u32[]{:S(2)}, u32[]{:S(2)}) collective-permute-start(f32[8,128]{1,0:T(8,128)S(1)} %shard_map.47.sums_ref.own_ref), channel_id=1, source_target_pairs={{0,256},{32,288},{1,257},{33,289},{2,258},{34,290},{3,259},{35,291... | collective-permute-start | bytes 12296 | tf_op jit(solution)/shard_map/ppermute | solution.py:411
  115.7 17.6 %collective-permute-start.15 = (f32[8,256,128]{2,1,0:T(8,128)}, f32[8,256,128]{2,1,0:T(8,128)S(1)}, u32[]{:S(2)}, u32[]{:S(2)}) collective-permute-start(f32[8,256,128]{2,1,0:T(8,128)} %get-tuple-element.38.f_ref), channel_id=1, source_target_pairs={{0,1},{1,2},{2,3},{3,4},{4,5},{5,6},{6,7},{7,8},{8,9},{9,10},{10,1... | collective-permute-start | bytes 3145736 | tf_op jit(solution)/shard_map/ppermute | solution.py:336
  118.1 27.3 %collective-permute-start.16 = (f32[8,256,128]{2,1,0:T(8,128)}, f32[8,256,128]{2,1,0:T(8,128)}, u32[]{:S(2)}, u32[]{:S(2)}) collective-permute-start(f32[8,256,128]{2,1,0:T(8,128)} %get-tuple-element.38.f_ref), channel_id=1, source_target_pairs={{1,0},{2,1},{3,2},{4,3},{5,4},{6,5},{7,6},{8,7},{9,8},{10,9},{11,1... | collective-permute-start | bytes 3145736 | tf_op jit(solution)/shard_map/ppermute | solution.py:337
  120.9 10.4 %all-to-all-start.1 = ((f32[8,8,128]{2,1,0:T(8,128)}), f32[8,8,128]{2,1,0:T(8,128)S(1)}, u32[]{:S(2)}, u32[]{:S(2)}) async-start(f32[8,8,128]{2,1,0:T(8,128)} %broadcast_in_dim.8), calls=%async_computation.1 | async-start | bytes 65536 | tf_op jit(solution)/shard_map/all_to_all | solution.py:425
  124.2 1.2 copy-start.1
  125.5 20.0 %copy-start.2 = (f32[8,256,128]{2,1,0:T(8,128)S(1)}, f32[8,256,128]{2,1,0:T(8,128)}, u32[]{:S(2)}) copy-start(f32[8,256,128]{2,1,0:T(8,128)} %get-tuple-element.38.f_ref) | copy-start | bytes 3145732

commit v4 on v3

--- a/solution.py
+++ b/solution.py
@@ -408,7 +408,6 @@
         flops=40 * 1024,
         bytes_moved=160 * 1024,
     )(domain_parts(sums))
-    guest = lax.ppermute(sums, "band", [(0, RING), (1, RING + 1)])
     basis, weights, gram = call(
         combine_kernel,
         (slab, tile, tile),
@@ -417,8 +416,9 @@
         flops=48 * big,
         bytes_moved=16 * big,
     )(band_word, sums, *pieces, own)
-    basis, guest = lax.optimization_barrier((basis, guest))
     left, right = neighbours(basis)
+    sums, weights = lax.optimization_barrier((sums, weights))
+    guest = lax.ppermute(sums, "band", [(0, RING), (1, RING + 1)])
     shared = jnp.where((band == RING) | (band == RING + 1), guest, sums)
     shared = jnp.broadcast_to(shared, (RING, 8, 128))
     rings = [list(range(RING)), list(range(RING, bands))]

time: 150 us -> 150 us (level)
  the two profiles are of different devices: /device:TPU:1 before, /device:TPU:64 now
where the time goes in v4:
time: 150 us; the launch traced here: 149 us
  starting transfers between devices  62.3 us (42%)
  waiting for transfers between devices  44.2 us (29%)
  Pallas kernels  25.2 us (17%)
  blocking collectives  13 us (9%)
  local copies, waits for them, and re-layouts  1.87 us (1%)
    ppermute x8, starting transfers between devices, ring_shift(): return lax.ppermute(block, 'band', pairs)  26.9 us
    ppermute x1, waiting for transfers between devices, local(): guest = lax.ppermute(sums, 'band', [(0, RING), (1, RING + 1)])  13.7 us
    all_to_all x1, blocking collectives, domain_parts(): return lax.all_to_all(copies, 'domain', 0, 0)  13 us
    ppermute x3, waiting for transfers between devices, local(): lax.ppermute(quarters[k], 'band', [(0, 2 * k), (1, 2 * k + 1)])  11.2 us
    ppermute x1, starting transfers between devices, local(): guest = lax.ppermute(sums, 'band', [(0, RING), (1, RING + 1)])  9.84 us
    ppermute x3, starting transfers between devices, local(): lax.ppermute(quarters[k], 'band', [(0, 2 * k), (1, 2 * k + 1)])  9.1 us
    ppermute x1, waiting for transfers between devices, local(): crossed = lax.ppermute(piece, 'band', [(y, y + RING) for y in range(RING)])  8.43 us
    ppermute x8, waiting for transfers between devices, ring_shift(): return lax.ppermute(block, 'band', pairs)  6.91 us
  transfers between devices with their start and end apart: 18, of which 10 were waited for; matrix products, arithmetic and copies ran while one was open for 0% of the time, Pallas kernels for 10%

profile of v4, /device:TPU:64, one launch (start us, length us, event | category | flops | bytes accessed | tf_op | source)
XLA Modules:
  0.0 149.0 jit_solution(8143962780704914531)
XLA Ops:
  2.0 4.5 %collective-permute-start = (f32[2,256,128]{2,1,0:T(8,128)S(1)}, f32[2,256,128]{2,1,0:T(8,128)S(1)}, u32[]{:S(2)}, u32[]{:S(2)}) collective-permute-start(f32[2,256,128]{2,1,0:T(8,128)S(1)} %bitcast.30), channel_id=1, source_target_pairs={{0,64},{32,96},{1,65},{33,97},{2,66},{34,98},{3,67},{35,99},{4,68}... | collective-permute-start | bytes 786440 | tf_op jit(solution)/shard_map/ppermute | solution.py:365
  6.6 2.3 %collective-permute-start.1 = (f32[2,256,128]{2,1,0:T(8,128)S(1)}, f32[2,256,128]{2,1,0:T(8,128)S(1)}, u32[]{:S(2)}, u32[]{:S(2)}) collective-permute-start(f32[2,256,128]{2,1,0:T(8,128)S(1)} %bitcast.29), channel_id=1, source_target_pairs={{0,192},{32,224},{1,193},{33,225},{2,194},{34,226},{3,195},{35,227... | collective-permute-start | bytes 786440 | tf_op jit(solution)/shard_map/ppermute | solution.py:365
  11.2 3.3 %shard_map.41 = (f32[8,4,64,128]{3,2,1,0:T(8,128)S(1)}, f32[8,128]{1,0:T(8,128)S(1)}) custom-call(f32[8,4,64,128]{3,2,1,0:T(8,128)S(1)} %copy-done, f32[4,64,128]{2,1,0:T(8,128)S(1)} %copy-done.3), custom_call_target="tpu_custom_call" | custom-call | flops 15728640 | bytes 2097152 | tf_op jit(solution)/shard_map/pallas_call | solution.py:354
  14.5 11.2 %collective-permute-done.1 = f32[2,256,128]{2,1,0:T(8,128)S(1)} collective-permute-done((f32[2,256,128]{2,1,0:T(8,128)S(1)}, f32[2,256,128]{2,1,0:T(8,128)S(1)}, u32[]{:S(2)}, u32[]{:S(2)}) %collective-permute-start.1) | collective-permute-done | bytes 262176 | tf_op jit(solution)/shard_map/ppermute | solution.py:365
  29.7 3.6 %collective-permute-start.11 = (f32[8,256,128]{2,1,0:T(8,128)S(1)}, f32[8,256,128]{2,1,0:T(8,128)}, u32[]{:S(2)}, u32[]{:S(2)}) collective-permute-start(f32[8,256,128]{2,1,0:T(8,128)S(1)} %bitcast.16), channel_id=1, source_target_pairs={{1,0},{2,1},{3,2},{4,3},{5,4},{6,5},{7,6},{8,7},{9,8},{10,9},{11,1... | collective-permute-start | bytes 3145736 | tf_op jit(solution)/shard_map/ppermute | solution.py:337
  33.3 8.4 %collective-permute-done.3 = f32[2,256,128]{2,1,0:T(8,128)} collective-permute-done((f32[2,256,128]{2,1,0:T(8,128)S(1)}, f32[2,256,128]{2,1,0:T(8,128)}, u32[]{:S(2)}, u32[]{:S(2)}) %collective-permute-start.3) | collective-permute-done | bytes 262176 | tf_op jit(solution)/shard_map/ppermute | solution.py:373
  43.7 3.9 %collective-permute-start.4 = (f32[2,256,128]{2,1,0:T(8,128)S(1)}, f32[2,256,128]{2,1,0:T(8,128)S(1)}, u32[]{:S(2)}, u32[]{:S(2)}) collective-permute-start(f32[2,256,128]{2,1,0:T(8,128)S(1)} %broadcast_select_fusion.refs_0_), channel_id=1, source_target_pairs={{0,32},{32,64},{64,96},{96,128},{128,160},{160,192},{192,224},{224... | collective-permute-start | bytes 786440 | tf_op jit(solution)/shard_map/ppermute | solution.py:331
  47.6 2.5 %collective-permute-done.5.refs_2_ = f32[2,256,128]{2,1,0:T(8,128)S(1)} collective-permute-done((f32[2,256,128]{2,1,0:T(8,128)S(1)}, f32[2,256,128]{2,1,0:T(8,128)S(1)}, u32[]{:S(2)}, u32[]{:S(2)}) %collective-permute-start.5) | collective-permute-done | bytes 262176 | tf_op jit(solution)/shard_map/ppermute | solution.py:331
  50.1 4.6 %collective-permute-start.7 = (f32[2,256,128]{2,1,0:T(8,128)S(1)}, f32[2,256,128]{2,1,0:T(8,128)S(1)}, u32[]{:S(2)}, u32[]{:S(2)}) collective-permute-start(f32[2,256,128]{2,1,0:T(8,128)S(1)} %collective-permute-done.5.refs_2_), channel_id=1, source_target_pairs={{0,224},{32,0},{64,32},{96,64},{128,96},{160,128},{192,160},{224,1... | collective-permute-start | bytes 786440 | tf_op jit(solution)/shard_map/ppermute | solution.py:331
  58.6 5.6 %collective-permute-start.9 = (f32[2,256,128]{2,1,0:T(8,128)S(1)}, f32[2,256,128]{2,1,0:T(8,128)S(1)}, u32[]{:S(2)}, u32[]{:S(2)}) collective-permute-start(f32[2,256,128]{2,1,0:T(8,128)S(1)} %collective-permute-done.7.refs_4_), channel_id=1, source_target_pairs={{0,224},{32,0},{64,32},{96,64},{128,96},{160,128},{192,160},{224,1... | collective-permute-start | bytes 786440 | tf_op jit(solution)/shard_map/ppermute | solution.py:331
  67.6 2.6 %shard_map.44 = (f32[8,256,128]{2,1,0:T(8,128)S(1)}, f32[8,128]{1,0:T(8,128)S(1)}) custom-call(f32[8,256,128]{2,1,0:T(8,128)S(1)} %bitcast.19, f32[8,256,128]{2,1,0:T(8,128)S(1)} %bitcast.26, f32[8,256,128]{2,1,0:T(8,128)S(1)} %collective-permute-done.10.left, f32[8,256,128]{2,1,0:T(8,128)} %collective-permute-done.11.right), custom_call_target="tpu_custom_call" | custom-call | flops 13107200 | bytes 5242880 | tf_op jit(solution)/shard_map/pallas_call | solution.py:395
  70.2 5.1 %collective-permute-start.13 = (f32[1,256,128]{2,1,0:T(8,128)S(1)}, f32[1,256,128]{2,1,0:T(8,128)S(1)}, u32[]{:S(2)}, u32[]{:S(2)}) collective-permute-start(f32[1,256,128]{2,1,0:T(8,128)S(1)} %slice.36), channel_id=1, source_target_pairs={{0,224},{32,0},{64,32},{96,64},{128,96},{160,128},{192,160},{224,1... | collective-permute-start | bytes 393224 | tf_op jit(solution)/shard_map/ppermute | solution.py:331
  77.3 3.1 %shard_map.45.refs_11_ = f32[8,128]{1,0:T(8,128)S(1)} custom-call(f32[2,256,128]{2,1,0:T(8,128)S(1)} %broadcast_select_fusion.refs_0_, f32[2,256,128]{2,1,0:T(8,128)S(1)} %collective-permute-done.4.refs_1_, f32[2,256,128]{2,1,0:T(8,128)S(1)} %collective-permute-done.5.refs_2_, f32[2,256,128]{2,1,0:T(8,128)S(1)} %collective-permute-done.6.refs_3_, ...), custom_call_target="tpu_custom_call" | custom-call | flops 5242880 | bytes 2621440 | tf_op jit(solution)/shard_map/pallas_call | solution.py:378
  80.4 3.1 %collective-permute-done.12.refs_7_ = f32[1,256,128]{2,1,0:T(8,128)S(1)} collective-permute-done((f32[1,256,128]{2,1,0:T(8,128)S(1)}, f32[1,256,128]{2,1,0:T(8,128)S(1)}, u32[]{:S(2)}, u32[]{:S(2)}) %collective-permute-start.12) | collective-permute-done | bytes 131104 | tf_op jit(solution)/shard_map/ppermute | solution.py:331
  84.5 13.0 %all_to_all.10.refs_0_ = f32[32,8,128]{2,1,0:T(8,128)S(1)} all-to-all(f32[32,8,128]{2,1,0:T(8,128)S(1)} %shard_map.46), channel_id=1, replica_groups=mesh['band'=16,'domain'=32] {'domain'}, dimensions={0} | all-to-all | bytes 262144 | tf_op jit(solution)/shard_map/all_to_all | solution.py:326
  97.5 5.4 %shard_map.48 = (f32[8,256,128]{2,1,0:T(8,128)}, f32[8,128]{1,0:T(8,128)S(1)}, f32[8,128]{1,0:T(8,128)S(1)}) custom-call(s32[1]{0:T(128)} %bitcast.band_ref, f32[8,128]{1,0:T(8,128)S(1)} %shard_map.47.sums_ref.own_ref, f32[2,256,128]{2,1,0:T(8,128)S(1)} %broadcast_select_fusion.refs_0_, f32[2,256,128]{2,1,0:T(8,128)S(1)} %collective-permute-done.4.refs_1_, ...), custom_call_target="tpu_custom_call" | custom-call | flops 12582912 | bytes 4194304 | tf_op jit(solution)/shard_map/pallas_call | solution.py:411
  102.9 2.3 %collective-permute-start.14 = (f32[8,256,128]{2,1,0:T(8,128)}, f32[8,256,128]{2,1,0:T(8,128)S(1)}, u32[]{:S(2)}, u32[]{:S(2)}) collective-permute-start(f32[8,256,128]{2,1,0:T(8,128)} %get-tuple-element.37.f_ref), channel_id=1, source_target_pairs={{0,1},{1,2},{2,3},{3,4},{4,5},{5,6},{6,7},{7,8},{8,9},{9,10},{10,1... | collective-permute-start | bytes 3145736 | tf_op jit(solution)/shard_map/ppermute | solution.py:336
  105.2 3.3 %collective-permute-start.15 = (f32[8,256,128]{2,1,0:T(8,128)}, f32[8,256,128]{2,1,0:T(8,128)}, u32[]{:S(2)}, u32[]{:S(2)}) collective-permute-start(f32[8,256,128]{2,1,0:T(8,128)} %get-tuple-element.37.f_ref), channel_id=1, source_target_pairs={{1,0},{2,1},{3,2},{4,3},{5,4},{6,5},{7,6},{8,7},{9,8},{10,9},{11,1... | collective-permute-start | bytes 3145736 | tf_op jit(solution)/shard_map/ppermute | solution.py:337
  108.5 9.8 %collective-permute-start.16 = (f32[8,128]{1,0:T(8,128)S(1)}, f32[8,128]{1,0:T(8,128)S(1)}, u32[]{:S(2)}, u32[]{:S(2)}) collective-permute-start(f32[8,128]{1,0:T(8,128)S(1)} %shard_map.47.sums_ref.own_ref), channel_id=1, source_target_pairs={{0,256},{32,288},{1,257},{33,289},{2,258},{34,290},{3,259},{35,291... | collective-permute-start | bytes 12296 | tf_op jit(solution)/shard_map/ppermute | solution.py:421
  118.3 13.7 %collective-permute-done.16 = f32[8,128]{1,0:T(8,128)S(1)} collective-permute-done((f32[8,128]{1,0:T(8,128)S(1)}, f32[8,128]{1,0:T(8,128)S(1)}, u32[]{:S(2)}, u32[]{:S(2)}) %collective-permute-start.16) | collective-permute-done | bytes 4128 | tf_op jit(solution)/shard_map/ppermute | solution.py:421
  132.6 3.3 %all-to-all-start.1 = ((f32[8,8,128]{2,1,0:T(8,128)}), f32[8,8,128]{2,1,0:T(8,128)S(1)}, u32[]{:S(2)}, u32[]{:S(2)}) async-start(f32[8,8,128]{2,1,0:T(8,128)} %broadcast_in_dim.8), calls=%async_computation.1 | async-start | bytes 65536 | tf_op jit(solution)/shard_map/all_to_all | solution.py:425
  137.2 2.7 %shard_map.49 = f32[8,4,64,128]{3,2,1,0:T(8,128)S(1)} custom-call(f32[8,4,64,128]{3,2,1,0:T(8,128)S(1)} %bitcast.24, f32[4,64,128]{2,1,0:T(8,128)S(1)} %copy-done.3), custom_call_target="tpu_custom_call" | custom-call | flops 15728640 | bytes 2097152 | tf_op jit(solution)/shard_map/pallas_call | solution.py:354
  140.0 4.0 %all-to-all-done.1.shared_ref = f32[8,8,128]{2,1,0:T(8,128)S(1)} async-done(((f32[8,8,128]{2,1,0:T(8,128)}), f32[8,8,128]{2,1,0:T(8,128)S(1)}, u32[]{:S(2)}, u32[]{:S(2)}) %all-to-all-start.1) | async-done | bytes 32800 | tf_op jit(solution)/shard_map/all_to_all | solution.py:425
  145.6 3.4 %shard_map.51 = f32[8,256,128]{2,1,0:T(8,128)} custom-call(f32[8,256,128]{2,1,0:T(8,128)S(1)} %copy-done.2, f32[8,256,128]{2,1,0:T(8,128)S(1)} %bitcast.25, f32[8,256,128]{2,1,0:T(8,128)S(1)} %collective-permute-done.14.left_ref, f32[8,256,128]{2,1,0:T(8,128)} %collective-permute-done.15.right_ref, f32[8,8,128]{2,1,0:T(8,128)S(1)} %shard_map.50.splat), custom_call_target="tpu_custom_call" | custom-call | flops 7864320 | bytes 5242880 | tf_op jit(solution)/shard_map/pallas_call | solution.py:430
  (39 shorter events, 23.3 us)
Async XLA Ops:
  0.6 10.5 %copy-start = (f32[8,4,64,128]{3,2,1,0:T(8,128)S(1)}, f32[8,4,64,128]{3,2,1,0:T(8,128)}, u32[]{:S(2)}) copy-start(f32[8,4,64,128]{3,2,1,0:T(8,128)} %f_ref.1) | copy-start | bytes 3145732
  0.6 10.5 %copy-start.3 = (f32[4,64,128]{2,1,0:T(8,128)S(1)}, f32[4,64,128]{2,1,0:T(8,128)}, u32[]{:S(2)}) copy-start(f32[4,64,128]{2,1,0:T(8,128)} %v_ref.3) | copy-start | bytes 393220
  2.0 12.4 %collective-permute-start = (f32[2,256,128]{2,1,0:T(8,128)S(1)}, f32[2,256,128]{2,1,0:T(8,128)S(1)}, u32[]{:S(2)}, u32[]{:S(2)}) collective-permute-start(f32[2,256,128]{2,1,0:T(8,128)S(1)} %bitcast.30), channel_id=1, source_target_pairs={{0,64},{32,96},{1,65},{33,97},{2,66},{34,98},{3,67},{35,99},{4,68}... | collective-permute-start | bytes 786440 | tf_op jit(solution)/shard_map/ppermute | solution.py:365
  6.6 19.1 %collective-permute-start.1 = (f32[2,256,128]{2,1,0:T(8,128)S(1)}, f32[2,256,128]{2,1,0:T(8,128)S(1)}, u32[]{:S(2)}, u32[]{:S(2)}) collective-permute-start(f32[2,256,128]{2,1,0:T(8,128)S(1)} %bitcast.29), channel_id=1, source_target_pairs={{0,192},{32,224},{1,193},{33,225},{2,194},{34,226},{3,195},{35,227... | collective-permute-start | bytes 786440 | tf_op jit(solution)/shard_map/ppermute | solution.py:365
  8.9 16.8 %collective-permute-start.2 = (f32[2,256,128]{2,1,0:T(8,128)S(1)}, f32[2,256,128]{2,1,0:T(8,128)S(1)}, u32[]{:S(2)}, u32[]{:S(2)}) collective-permute-start(f32[2,256,128]{2,1,0:T(8,128)S(1)} %bitcast.28), channel_id=1, source_target_pairs={{0,128},{32,160},{1,129},{33,161},{2,130},{34,162},{3,131},{35,163... | collective-permute-start | bytes 786440 | tf_op jit(solution)/shard_map/ppermute | solution.py:365
  25.7 16.0 %collective-permute-start.3 = (f32[2,256,128]{2,1,0:T(8,128)S(1)}, f32[2,256,128]{2,1,0:T(8,128)}, u32[]{:S(2)}, u32[]{:S(2)}) collective-permute-start(f32[2,256,128]{2,1,0:T(8,128)S(1)} %fusion.1), channel_id=1, source_target_pairs={{0,256},{32,288},{64,320},{96,352},{128,384},{160,416},{192,448},{... | collective-permute-start | bytes 786440 | tf_op jit(solution)/shard_map/ppermute | solution.py:373
  27.7 39.8 %collective-permute-start.10 = (f32[8,256,128]{2,1,0:T(8,128)S(1)}, f32[8,256,128]{2,1,0:T(8,128)S(1)}, u32[]{:S(2)}, u32[]{:S(2)}) collective-permute-start(f32[8,256,128]{2,1,0:T(8,128)S(1)} %bitcast.15), channel_id=1, source_target_pairs={{0,1},{1,2},{2,3},{3,4},{4,5},{5,6},{6,7},{7,8},{8,9},{9,10},{10,1... | collective-permute-start | bytes 3145736 | tf_op jit(solution)/shard_map/ppermute | solution.py:336
  29.7 37.9 %collective-permute-start.11 = (f32[8,256,128]{2,1,0:T(8,128)S(1)}, f32[8,256,128]{2,1,0:T(8,128)}, u32[]{:S(2)}, u32[]{:S(2)}) collective-permute-start(f32[8,256,128]{2,1,0:T(8,128)S(1)} %bitcast.16), channel_id=1, source_target_pairs={{1,0},{2,1},{3,2},{4,3},{5,4},{6,5},{7,6},{8,7},{9,8},{10,9},{11,1... | collective-permute-start | bytes 3145736 | tf_op jit(solution)/shard_map/ppermute | solution.py:337
  41.8 8.4 %collective-permute-start.5 = (f32[2,256,128]{2,1,0:T(8,128)S(1)}, f32[2,256,128]{2,1,0:T(8,128)S(1)}, u32[]{:S(2)}, u32[]{:S(2)}) collective-permute-start(f32[2,256,128]{2,1,0:T(8,128)S(1)} %broadcast_select_fusion.refs_0_), channel_id=1, source_target_pairs={{0,224},{32,0},{64,32},{96,64},{128,96},{160,128},{192,160},{224,1... | collective-permute-start | bytes 786440 | tf_op jit(solution)/shard_map/ppermute | solution.py:331
  43.7 11.5 %collective-permute-start.4 = (f32[2,256,128]{2,1,0:T(8,128)S(1)}, f32[2,256,128]{2,1,0:T(8,128)S(1)}, u32[]{:S(2)}, u32[]{:S(2)}) collective-permute-start(f32[2,256,128]{2,1,0:T(8,128)S(1)} %broadcast_select_fusion.refs_0_), channel_id=1, source_target_pairs={{0,32},{32,64},{64,96},{96,128},{128,160},{160,192},{192,224},{224... | collective-permute-start | bytes 786440 | tf_op jit(solution)/shard_map/ppermute | solution.py:331
  50.1 8.4 %collective-permute-start.7 = (f32[2,256,128]{2,1,0:T(8,128)S(1)}, f32[2,256,128]{2,1,0:T(8,128)S(1)}, u32[]{:S(2)}, u32[]{:S(2)}) collective-permute-start(f32[2,256,128]{2,1,0:T(8,128)S(1)} %collective-permute-done.5.refs_2_), channel_id=1, source_target_pairs={{0,224},{32,0},{64,32},{96,64},{128,96},{160,128},{192,160},{224,1... | collective-permute-start | bytes 786440 | tf_op jit(solution)/shard_map/ppermute | solution.py:331
  55.2 9.5 %collective-permute-start.6 = (f32[2,256,128]{2,1,0:T(8,128)S(1)}, f32[2,256,128]{2,1,0:T(8,128)S(1)}, u32[]{:S(2)}, u32[]{:S(2)}) collective-permute-start(f32[2,256,128]{2,1,0:T(8,128)S(1)} %collective-permute-done.4.refs_1_), channel_id=1, source_target_pairs={{0,32},{32,64},{64,96},{96,128},{128,160},{160,192},{192,224},{224... | collective-permute-start | bytes 786440 | tf_op jit(solution)/shard_map/ppermute | solution.py:331
  58.6 11.6 %collective-permute-start.9 = (f32[2,256,128]{2,1,0:T(8,128)S(1)}, f32[2,256,128]{2,1,0:T(8,128)S(1)}, u32[]{:S(2)}, u32[]{:S(2)}) collective-permute-start(f32[2,256,128]{2,1,0:T(8,128)S(1)} %collective-permute-done.7.refs_4_), channel_id=1, source_target_pairs={{0,224},{32,0},{64,32},{96,64},{128,96},{160,128},{192,160},{224,1... | collective-permute-start | bytes 786440 | tf_op jit(solution)/shard_map/ppermute | solution.py:331
  64.7 10.7 %collective-permute-start.8 = (f32[2,256,128]{2,1,0:T(8,128)S(1)}, f32[2,256,128]{2,1,0:T(8,128)S(1)}, u32[]{:S(2)}, u32[]{:S(2)}) collective-permute-start(f32[2,256,128]{2,1,0:T(8,128)S(1)} %collective-permute-done.6.refs_3_), channel_id=1, source_target_pairs={{0,32},{32,64},{64,96},{96,128},{128,160},{160,192},{192,224},{224... | collective-permute-start | bytes 786440 | tf_op jit(solution)/shard_map/ppermute | solution.py:331
  70.2 10.2 %collective-permute-start.13 = (f32[1,256,128]{2,1,0:T(8,128)S(1)}, f32[1,256,128]{2,1,0:T(8,128)S(1)}, u32[]{:S(2)}, u32[]{:S(2)}) collective-permute-start(f32[1,256,128]{2,1,0:T(8,128)S(1)} %slice.36), channel_id=1, source_target_pairs={{0,224},{32,0},{64,32},{96,64},{128,96},{160,128},{192,160},{224,1... | collective-permute-start | bytes 393224 | tf_op jit(solution)/shard_map/ppermute | solution.py:331
  75.4 8.1 %collective-permute-start.12 = (f32[1,256,128]{2,1,0:T(8,128)S(1)}, f32[1,256,128]{2,1,0:T(8,128)S(1)}, u32[]{:S(2)}, u32[]{:S(2)}) collective-permute-start(f32[1,256,128]{2,1,0:T(8,128)S(1)} %slice.37), channel_id=1, source_target_pairs={{0,32},{32,64},{64,96},{96,128},{128,160},{160,192},{192,224},{224... | collective-permute-start | bytes 393224 | tf_op jit(solution)/shard_map/ppermute | solution.py:331
  102.9 42.6 %collective-permute-start.14 = (f32[8,256,128]{2,1,0:T(8,128)}, f32[8,256,128]{2,1,0:T(8,128)S(1)}, u32[]{:S(2)}, u32[]{:S(2)}) collective-permute-start(f32[8,256,128]{2,1,0:T(8,128)} %get-tuple-element.37.f_ref), channel_id=1, source_target_pairs={{0,1},{1,2},{2,3},{3,4},{4,5},{5,6},{6,7},{7,8},{8,9},{9,10},{10,1... | collective-permute-start | bytes 3145736 | tf_op jit(solution)/shard_map/ppermute | solution.py:336
  105.2 40.3 %collective-permute-start.15 = (f32[8,256,128]{2,1,0:T(8,128)}, f32[8,256,128]{2,1,0:T(8,128)}, u32[]{:S(2)}, u32[]{:S(2)}) collective-permute-start(f32[8,256,128]{2,1,0:T(8,128)} %get-tuple-element.37.f_ref), channel_id=1, source_target_pairs={{1,0},{2,1},{3,2},{4,3},{5,4},{6,5},{7,6},{8,7},{9,8},{10,9},{11,1... | collective-permute-start | bytes 3145736 | tf_op jit(solution)/shard_map/ppermute | solution.py:337
  108.5 23.5 %collective-permute-start.16 = (f32[8,128]{1,0:T(8,128)S(1)}, f32[8,128]{1,0:T(8,128)S(1)}, u32[]{:S(2)}, u32[]{:S(2)}) collective-permute-start(f32[8,128]{1,0:T(8,128)S(1)} %shard_map.47.sums_ref.own_ref), channel_id=1, source_target_pairs={{0,256},{32,288},{1,257},{33,289},{2,258},{34,290},{3,259},{35,291... | collective-permute-start | bytes 12296 | tf_op jit(solution)/shard_map/ppermute | solution.py:421
  132.6 11.3 %all-to-all-start.1 = ((f32[8,8,128]{2,1,0:T(8,128)}), f32[8,8,128]{2,1,0:T(8,128)S(1)}, u32[]{:S(2)}, u32[]{:S(2)}) async-start(f32[8,8,128]{2,1,0:T(8,128)} %broadcast_in_dim.8), calls=%async_computation.1 | async-start | bytes 65536 | tf_op jit(solution)/shard_map/all_to_all | solution.py:425
  136.0 1.2 copy-start.1
  137.2 8.3 %copy-start.2 = (f32[8,256,128]{2,1,0:T(8,128)S(1)}, f32[8,256,128]{2,1,0:T(8,128)}, u32[]{:S(2)}) copy-start(f32[8,256,128]{2,1,0:T(8,128)} %get-tuple-element.37.f_ref) | copy-start | bytes 3145732

commit v5 on v4

--- a/solution.py
+++ b/solution.py
@@ -270,7 +270,7 @@
     return jnp.where((lane == target) & (row < 24), 1.0, 0.0)
 
 
-def coeff_kernel(band_ref, weights_ref, gram_ref, own_ref, shared_ref, out):
+def coeff_kernel(band_ref, weights_ref, gram_ref, own_ref, near_ref, far_ref, out):
     lane, sub = lanes(), subs()
     wide = lax.broadcasted_iota(jnp.int32, (128, 128), 1)
     row = lax.broadcasted_iota(jnp.int32, (128, 128), 0)
@@ -284,7 +284,8 @@
         return jnp.where((wide >= target) & (wide < target + 8), columns, 0.0)
 
     def visiting(n):
-        return image_columns(tall(unpacked(shared_ref[n])), places(n, n), 24, 8 * n)
+        packed = jnp.where(band_ref[0] < RING, near_ref[n], far_ref[n])
+        return image_columns(tall(unpacked(packed)), places(n, n), 24, 8 * n)
 
     block0, block1 = visiting(0), visiting(1)
     block = image_columns(tall(unpacked(own_ref[...])), place, 24, 16)
@@ -417,16 +418,15 @@
         bytes_moved=16 * big,
     )(band_word, sums, *pieces, own)
     left, right = neighbours(basis)
-    sums, weights = lax.optimization_barrier((sums, weights))
-    guest = lax.ppermute(sums, "band", [(0, RING), (1, RING + 1)])
-    shared = jnp.where((band == RING) | (band == RING + 1), guest, sums)
-    shared = jnp.broadcast_to(shared, (RING, 8, 128))
+    inner = inner_part(basis.reshape(orbitals.shape))[0].reshape(flat)
     rings = [list(range(RING)), list(range(RING, bands))]
-    shared = lax.all_to_all(shared, "band", 0, 0, axis_index_groups=rings)
-    inner = inner_part(basis.reshape(orbitals.shape))[0].reshape(flat)
+    shared, inner = lax.optimization_barrier((sums, inner))
+    near = jnp.broadcast_to(shared, (RING, 8, 128))
+    near = lax.all_to_all(near, "band", 0, 0, axis_index_groups=rings)
+    far = lax.ppermute(near[:2], "band", [(y, y + RING) for y in range(RING)])
     splat = call(
-        coeff_kernel, jax.ShapeDtypeStruct((8, 8, 128), F32), specs=[SMEM] + [VMEM] * 4
-    )(band_word, weights, gram, sums, shared)
+        coeff_kernel, jax.ShapeDtypeStruct((8, 8, 128), F32), specs=[SMEM] + [VMEM] * 5
+    )(band_word, weights, gram, sums, near, far)
     residual = call(
         residual_kernel, slab, specs=[VMEM] * 5, flops=30 * big, bytes_moved=20 * big
     )(basis, inner, left, right, splat)

time: 150 us -> 145 us (0.967)
  the two profiles are of different devices: /device:TPU:64 before, /device:TPU:8 now
where the time goes in v5:
time: 145 us
  starting transfers between devices  68 us (47%)
  blocking collectives  27.9 us (19%)
  Pallas kernels  24 us (17%)
  waiting for transfers between devices  20.9 us (14%)
  other arithmetic  1.47 us (1%)
    ppermute x8, starting transfers between devices, ring_shift(): return lax.ppermute(block, 'band', pairs)  26.9 us
    ppermute x2, starting transfers between devices, neighbours(): lax.ppermute(block, 'domain', [((i + 1) % count, i) for i in range(count)])  17.2 us
    all_to_all x1, blocking collectives, domain_parts(): return lax.all_to_all(copies, 'domain', 0, 0)  14.1 us
    all_to_all x1, blocking collectives, local(): near = lax.all_to_all(near, 'band', 0, 0, axis_index_groups=rings)  13.8 us
    ppermute x8, waiting for transfers between devices, ring_shift(): return lax.ppermute(block, 'band', pairs)  9.9 us
    ppermute x1, starting transfers between devices, local(): far = lax.ppermute(near[:2], 'band', [(y, y + RING) for y in range(RING)])  9.83 us
    ppermute x3, waiting for transfers between devices, local(): lax.ppermute(quarters[k], 'band', [(0, 2 * k), (1, 2 * k + 1)])  9.64 us
    ppermute x3, starting transfers between devices, local(): lax.ppermute(quarters[k], 'band', [(0, 2 * k), (1, 2 * k + 1)])  8.2 us
  transfers between devices with their start and end apart: 17, of which 6 were waited for; matrix products, arithmetic and copies ran while one was open for 0% of the time, Pallas kernels for 11%

profile of v5, /device:TPU:8, one launch (start us, length us, event | category | flops | bytes accessed | tf_op | source)
XLA Modules:
  0.0 144.6 jit_solution(11244372841766368486)
XLA Ops:
  2.0 4.5 %collective-permute-start = (f32[2,256,128]{2,1,0:T(8,128)S(1)}, f32[2,256,128]{2,1,0:T(8,128)S(1)}, u32[]{:S(2)}, u32[]{:S(2)}) collective-permute-start(f32[2,256,128]{2,1,0:T(8,128)S(1)} %bitcast.30), channel_id=1, source_target_pairs={{0,64},{32,96},{1,65},{33,97},{2,66},{34,98},{3,67},{35,99},{4,68}... | collective-permute-start | bytes 786440 | tf_op jit(solution)/shard_map/ppermute | solution.py:366
  8.0 2.2 %collective-permute-start.2 = (f32[2,256,128]{2,1,0:T(8,128)S(1)}, f32[2,256,128]{2,1,0:T(8,128)S(1)}, u32[]{:S(2)}, u32[]{:S(2)}) collective-permute-start(f32[2,256,128]{2,1,0:T(8,128)S(1)} %bitcast.28), channel_id=1, source_target_pairs={{0,128},{32,160},{1,129},{33,161},{2,130},{34,162},{3,131},{35,163... | collective-permute-start | bytes 786440 | tf_op jit(solution)/shard_map/ppermute | solution.py:366
  10.3 3.3 %shard_map.41 = (f32[8,4,64,128]{3,2,1,0:T(8,128)S(1)}, f32[8,128]{1,0:T(8,128)S(1)}) custom-call(f32[8,4,64,128]{3,2,1,0:T(8,128)S(1)} %copy-done, f32[4,64,128]{2,1,0:T(8,128)S(1)} %copy-done.3), custom_call_target="tpu_custom_call" | custom-call | flops 15728640 | bytes 2097152 | tf_op jit(solution)/shard_map/pallas_call | solution.py:355
  13.6 9.6 %collective-permute-done = f32[2,256,128]{2,1,0:T(8,128)S(1)} collective-permute-done((f32[2,256,128]{2,1,0:T(8,128)S(1)}, f32[2,256,128]{2,1,0:T(8,128)S(1)}, u32[]{:S(2)}, u32[]{:S(2)}) %collective-permute-start) | collective-permute-done | bytes 262176 | tf_op jit(solution)/shard_map/ppermute | solution.py:366
  23.3 2.0 %collective-permute-start.3 = (f32[2,256,128]{2,1,0:T(8,128)S(1)}, f32[2,256,128]{2,1,0:T(8,128)}, u32[]{:S(2)}, u32[]{:S(2)}) collective-permute-start(f32[2,256,128]{2,1,0:T(8,128)S(1)} %fusion.1), channel_id=1, source_target_pairs={{0,256},{32,288},{64,320},{96,352},{128,384},{160,416},{192,448},{... | collective-permute-start | bytes 786440 | tf_op jit(solution)/shard_map/ppermute | solution.py:374
  27.2 9.7 %collective-permute-start.11 = (f32[8,256,128]{2,1,0:T(8,128)S(1)}, f32[8,256,128]{2,1,0:T(8,128)}, u32[]{:S(2)}, u32[]{:S(2)}) collective-permute-start(f32[8,256,128]{2,1,0:T(8,128)S(1)} %bitcast.16), channel_id=1, source_target_pairs={{1,0},{2,1},{3,2},{4,3},{5,4},{6,5},{7,6},{8,7},{9,8},{10,9},{11,1... | collective-permute-start | bytes 3145736 | tf_op jit(solution)/shard_map/ppermute | solution.py:338
  37.0 4.7 %collective-permute-start.5 = (f32[2,256,128]{2,1,0:T(8,128)S(1)}, f32[2,256,128]{2,1,0:T(8,128)S(1)}, u32[]{:S(2)}, u32[]{:S(2)}) collective-permute-start(f32[2,256,128]{2,1,0:T(8,128)S(1)} %broadcast_select_fusion.refs_0_), channel_id=1, source_target_pairs={{0,224},{32,0},{64,32},{96,64},{128,96},{160,128},{192,160},{224,1... | collective-permute-start | bytes 786440 | tf_op jit(solution)/shard_map/ppermute | solution.py:332
  43.6 3.5 %collective-permute-done.5.refs_2_ = f32[2,256,128]{2,1,0:T(8,128)S(1)} collective-permute-done((f32[2,256,128]{2,1,0:T(8,128)S(1)}, f32[2,256,128]{2,1,0:T(8,128)S(1)}, u32[]{:S(2)}, u32[]{:S(2)}) %collective-permute-start.5) | collective-permute-done | bytes 262176 | tf_op jit(solution)/shard_map/ppermute | solution.py:332
  47.1 4.4 %collective-permute-start.7 = (f32[2,256,128]{2,1,0:T(8,128)S(1)}, f32[2,256,128]{2,1,0:T(8,128)S(1)}, u32[]{:S(2)}, u32[]{:S(2)}) collective-permute-start(f32[2,256,128]{2,1,0:T(8,128)S(1)} %collective-permute-done.5.refs_2_), channel_id=1, source_target_pairs={{0,224},{32,0},{64,32},{96,64},{128,96},{160,128},{192,160},{224,1... | collective-permute-start | bytes 786440 | tf_op jit(solution)/shard_map/ppermute | solution.py:332
  54.5 3.3 %collective-permute-done.7.refs_4_ = f32[2,256,128]{2,1,0:T(8,128)S(1)} collective-permute-done((f32[2,256,128]{2,1,0:T(8,128)S(1)}, f32[2,256,128]{2,1,0:T(8,128)S(1)}, u32[]{:S(2)}, u32[]{:S(2)}) %collective-permute-start.7) | collective-permute-done | bytes 262176 | tf_op jit(solution)/shard_map/ppermute | solution.py:332
  57.8 4.6 %collective-permute-start.9 = (f32[2,256,128]{2,1,0:T(8,128)S(1)}, f32[2,256,128]{2,1,0:T(8,128)S(1)}, u32[]{:S(2)}, u32[]{:S(2)}) collective-permute-start(f32[2,256,128]{2,1,0:T(8,128)S(1)} %collective-permute-done.7.refs_4_), channel_id=1, source_target_pairs={{0,224},{32,0},{64,32},{96,64},{128,96},{160,128},{192,160},{224,1... | collective-permute-start | bytes 786440 | tf_op jit(solution)/shard_map/ppermute | solution.py:332
  62.4 1.9 %collective-permute-start.8 = (f32[2,256,128]{2,1,0:T(8,128)S(1)}, f32[2,256,128]{2,1,0:T(8,128)S(1)}, u32[]{:S(2)}, u32[]{:S(2)}) collective-permute-start(f32[2,256,128]{2,1,0:T(8,128)S(1)} %collective-permute-done.6.refs_3_), channel_id=1, source_target_pairs={{0,32},{32,64},{64,96},{96,128},{128,160},{160,192},{192,224},{224... | collective-permute-start | bytes 786440 | tf_op jit(solution)/shard_map/ppermute | solution.py:332
  65.3 2.6 %shard_map.44 = (f32[8,256,128]{2,1,0:T(8,128)S(1)}, f32[8,128]{1,0:T(8,128)S(1)}) custom-call(f32[8,256,128]{2,1,0:T(8,128)S(1)} %bitcast.19, f32[8,256,128]{2,1,0:T(8,128)S(1)} %bitcast.26, f32[8,256,128]{2,1,0:T(8,128)S(1)} %collective-permute-done.10.left, f32[8,256,128]{2,1,0:T(8,128)} %collective-permute-done.11.right), custom_call_target="tpu_custom_call" | custom-call | flops 13107200 | bytes 5242880 | tf_op jit(solution)/shard_map/pallas_call | solution.py:396
  68.0 5.6 %collective-permute-start.13 = (f32[1,256,128]{2,1,0:T(8,128)S(1)}, f32[1,256,128]{2,1,0:T(8,128)S(1)}, u32[]{:S(2)}, u32[]{:S(2)}) collective-permute-start(f32[1,256,128]{2,1,0:T(8,128)S(1)} %slice.39), channel_id=1, source_target_pairs={{0,224},{32,0},{64,32},{96,64},{128,96},{160,128},{192,160},{224,1... | collective-permute-start | bytes 393224 | tf_op jit(solution)/shard_map/ppermute | solution.py:332
  75.6 3.1 %shard_map.45.refs_11_ = f32[8,128]{1,0:T(8,128)S(1)} custom-call(f32[2,256,128]{2,1,0:T(8,128)S(1)} %broadcast_select_fusion.refs_0_, f32[2,256,128]{2,1,0:T(8,128)S(1)} %collective-permute-done.4.refs_1_, f32[2,256,128]{2,1,0:T(8,128)S(1)} %collective-permute-done.5.refs_2_, f32[2,256,128]{2,1,0:T(8,128)S(1)} %collective-permute-done.6.refs_3_, ...), custom_call_target="tpu_custom_call" | custom-call | flops 5242880 | bytes 2621440 | tf_op jit(solution)/shard_map/pallas_call | solution.py:379
  78.6 3.1 %collective-permute-done.12.refs_7_ = f32[1,256,128]{2,1,0:T(8,128)S(1)} collective-permute-done((f32[1,256,128]{2,1,0:T(8,128)S(1)}, f32[1,256,128]{2,1,0:T(8,128)S(1)}, u32[]{:S(2)}, u32[]{:S(2)}) %collective-permute-start.12) | collective-permute-done | bytes 131104 | tf_op jit(solution)/shard_map/ppermute | solution.py:332
  82.7 14.1 %all_to_all.10.refs_0_ = f32[32,8,128]{2,1,0:T(8,128)S(1)} all-to-all(f32[32,8,128]{2,1,0:T(8,128)S(1)} %shard_map.46), channel_id=1, replica_groups=mesh['band'=16,'domain'=32] {'domain'}, dimensions={0} | all-to-all | bytes 262144 | tf_op jit(solution)/shard_map/all_to_all | solution.py:327
  96.9 5.4 %shard_map.48 = (f32[8,256,128]{2,1,0:T(8,128)}, f32[8,128]{1,0:T(8,128)S(1)}, f32[8,128]{1,0:T(8,128)S(1)}) custom-call(s32[1]{0:T(128)} %bitcast.band_ref, f32[8,128]{1,0:T(8,128)S(1)} %shard_map.47.sums_ref.own_ref, f32[2,256,128]{2,1,0:T(8,128)S(1)} %broadcast_select_fusion.refs_0_, f32[2,256,128]{2,1,0:T(8,128)S(1)} %collective-permute-done.4.refs_1_, ...), custom_call_target="tpu_custom_call" | custom-call | flops 12582912 | bytes 4194304 | tf_op jit(solution)/shard_map/pallas_call | solution.py:412
  102.3 2.0 %collective-permute-start.14 = (f32[8,256,128]{2,1,0:T(8,128)}, f32[8,256,128]{2,1,0:T(8,128)S(1)}, u32[]{:S(2)}, u32[]{:S(2)}) collective-permute-start(f32[8,256,128]{2,1,0:T(8,128)} %get-tuple-element.37.f_ref), channel_id=1, source_target_pairs={{0,1},{1,2},{2,3},{3,4},{4,5},{5,6},{6,7},{7,8},{8,9},{9,10},{10,1... | collective-permute-start | bytes 3145736 | tf_op jit(solution)/shard_map/ppermute | solution.py:337
  104.3 7.4 %collective-permute-start.15 = (f32[8,256,128]{2,1,0:T(8,128)}, f32[8,256,128]{2,1,0:T(8,128)S(1)}, u32[]{:S(2)}, u32[]{:S(2)}) collective-permute-start(f32[8,256,128]{2,1,0:T(8,128)} %get-tuple-element.37.f_ref), channel_id=1, source_target_pairs={{1,0},{2,1},{3,2},{4,3},{5,4},{6,5},{7,6},{8,7},{9,8},{10,9},{11,1... | collective-permute-start | bytes 3145736 | tf_op jit(solution)/shard_map/ppermute | solution.py:338
  113.0 2.7 %shard_map.49 = f32[8,4,64,128]{3,2,1,0:T(8,128)S(1)} custom-call(f32[8,4,64,128]{3,2,1,0:T(8,128)S(1)} %bitcast.24, f32[4,64,128]{2,1,0:T(8,128)S(1)} %copy-done.3), custom_call_target="tpu_custom_call" | custom-call | flops 15728640 | bytes 2097152 | tf_op jit(solution)/shard_map/pallas_call | solution.py:355
  115.8 13.8 %all_to_all.11.near_ref = f32[8,8,128]{2,1,0:T(8,128)S(1)} all-to-all(f32[8,8,128]{2,1,0:T(8,128)S(1)} %broadcast_in_dim.8), channel_id=1, replica_groups={{0,32,64,96,128,160,192,224},{256,288,320,352,384,416,448,480},{1,33,65..., dimensions={0} | all-to-all | bytes 65536 | tf_op jit(solution)/shard_map/all_to_all | solution.py:425
  129.6 9.8 %collective-permute-start.16 = (f32[2,8,128]{2,1,0:T(8,128)S(1)}, f32[2,8,128]{2,1,0:T(8,128)S(1)}, u32[]{:S(2)}, u32[]{:S(2)}) collective-permute-start(f32[2,8,128]{2,1,0:T(8,128)S(1)} %slice.42), channel_id=1, source_target_pairs={{0,256},{32,288},{64,320},{96,352},{128,384},{160,416},{192,448},{... | collective-permute-start | bytes 24584 | tf_op jit(solution)/shard_map/ppermute | solution.py:426
  142.4 2.2 %shard_map.51 = f32[8,256,128]{2,1,0:T(8,128)} custom-call(f32[8,256,128]{2,1,0:T(8,128)S(1)} %copy-done.2, f32[8,256,128]{2,1,0:T(8,128)S(1)} %bitcast.25, f32[8,256,128]{2,1,0:T(8,128)S(1)} %collective-permute-done.14.left_ref, f32[8,256,128]{2,1,0:T(8,128)S(1)} %collective-permute-done.15.right_ref, f32[8,8,128]{2,1,0:T(8,128)S(1)} %shard_map.50.splat), custom_call_target="tpu_custom_call" | custom-call | flops 7864320 | bytes 5242880 | tf_op jit(solution)/shard_map/pallas_call | solution.py:430
  (38 shorter events, 18.0 us)
Async XLA Ops:
  0.6 9.6 %copy-start = (f32[8,4,64,128]{3,2,1,0:T(8,128)S(1)}, f32[8,4,64,128]{3,2,1,0:T(8,128)}, u32[]{:S(2)}) copy-start(f32[8,4,64,128]{3,2,1,0:T(8,128)} %f_ref.1) | copy-start | bytes 3145732
  0.6 9.6 %copy-start.3 = (f32[4,64,128]{2,1,0:T(8,128)S(1)}, f32[4,64,128]{2,1,0:T(8,128)}, u32[]{:S(2)}) copy-start(f32[4,64,128]{2,1,0:T(8,128)} %v_ref.3) | copy-start | bytes 393220
  2.0 21.2 %collective-permute-start = (f32[2,256,128]{2,1,0:T(8,128)S(1)}, f32[2,256,128]{2,1,0:T(8,128)S(1)}, u32[]{:S(2)}, u32[]{:S(2)}) collective-permute-start(f32[2,256,128]{2,1,0:T(8,128)S(1)} %bitcast.30), channel_id=1, source_target_pairs={{0,64},{32,96},{1,65},{33,97},{2,66},{34,98},{3,67},{35,99},{4,68}... | collective-permute-start | bytes 786440 | tf_op jit(solution)/shard_map/ppermute | solution.py:366
  6.6 16.7 %collective-permute-start.1 = (f32[2,256,128]{2,1,0:T(8,128)S(1)}, f32[2,256,128]{2,1,0:T(8,128)S(1)}, u32[]{:S(2)}, u32[]{:S(2)}) collective-permute-start(f32[2,256,128]{2,1,0:T(8,128)S(1)} %bitcast.29), channel_id=1, source_target_pairs={{0,192},{32,224},{1,193},{33,225},{2,194},{34,226},{3,195},{35,227... | collective-permute-start | bytes 786440 | tf_op jit(solution)/shard_map/ppermute | solution.py:366
  8.0 15.2 %collective-permute-start.2 = (f32[2,256,128]{2,1,0:T(8,128)S(1)}, f32[2,256,128]{2,1,0:T(8,128)S(1)}, u32[]{:S(2)}, u32[]{:S(2)}) collective-permute-start(f32[2,256,128]{2,1,0:T(8,128)S(1)} %bitcast.28), channel_id=1, source_target_pairs={{0,128},{32,160},{1,129},{33,161},{2,130},{34,162},{3,131},{35,163... | collective-permute-start | bytes 786440 | tf_op jit(solution)/shard_map/ppermute | solution.py:366
  23.3 13.6 %collective-permute-start.3 = (f32[2,256,128]{2,1,0:T(8,128)S(1)}, f32[2,256,128]{2,1,0:T(8,128)}, u32[]{:S(2)}, u32[]{:S(2)}) collective-permute-start(f32[2,256,128]{2,1,0:T(8,128)S(1)} %fusion.1), channel_id=1, source_target_pairs={{0,256},{32,288},{64,320},{96,352},{128,384},{160,416},{192,448},{... | collective-permute-start | bytes 786440 | tf_op jit(solution)/shard_map/ppermute | solution.py:374
  25.3 40.1 %collective-permute-start.10 = (f32[8,256,128]{2,1,0:T(8,128)S(1)}, f32[8,256,128]{2,1,0:T(8,128)S(1)}, u32[]{:S(2)}, u32[]{:S(2)}) collective-permute-start(f32[8,256,128]{2,1,0:T(8,128)S(1)} %bitcast.15), channel_id=1, source_target_pairs={{0,1},{1,2},{2,3},{3,4},{4,5},{5,6},{6,7},{7,8},{8,9},{9,10},{10,1... | collective-permute-start | bytes 3145736 | tf_op jit(solution)/shard_map/ppermute | solution.py:337
  27.2 38.2 %collective-permute-start.11 = (f32[8,256,128]{2,1,0:T(8,128)S(1)}, f32[8,256,128]{2,1,0:T(8,128)}, u32[]{:S(2)}, u32[]{:S(2)}) collective-permute-start(f32[8,256,128]{2,1,0:T(8,128)S(1)} %bitcast.16), channel_id=1, source_target_pairs={{1,0},{2,1},{3,2},{4,3},{5,4},{6,5},{7,6},{8,7},{9,8},{10,9},{11,1... | collective-permute-start | bytes 3145736 | tf_op jit(solution)/shard_map/ppermute | solution.py:338
  37.0 10.1 %collective-permute-start.5 = (f32[2,256,128]{2,1,0:T(8,128)S(1)}, f32[2,256,128]{2,1,0:T(8,128)S(1)}, u32[]{:S(2)}, u32[]{:S(2)}) collective-permute-start(f32[2,256,128]{2,1,0:T(8,128)S(1)} %broadcast_select_fusion.refs_0_), channel_id=1, source_target_pairs={{0,224},{32,0},{64,32},{96,64},{128,96},{160,128},{192,160},{224,1... | collective-permute-start | bytes 786440 | tf_op jit(solution)/shard_map/ppermute | solution.py:332
  41.7 9.8 %collective-permute-start.4 = (f32[2,256,128]{2,1,0:T(8,128)S(1)}, f32[2,256,128]{2,1,0:T(8,128)S(1)}, u32[]{:S(2)}, u32[]{:S(2)}) collective-permute-start(f32[2,256,128]{2,1,0:T(8,128)S(1)} %broadcast_select_fusion.refs_0_), channel_id=1, source_target_pairs={{0,32},{32,64},{64,96},{96,128},{128,160},{160,192},{192,224},{224... | collective-permute-start | bytes 786440 | tf_op jit(solution)/shard_map/ppermute | solution.py:332
  47.1 10.7 %collective-permute-start.7 = (f32[2,256,128]{2,1,0:T(8,128)S(1)}, f32[2,256,128]{2,1,0:T(8,128)S(1)}, u32[]{:S(2)}, u32[]{:S(2)}) collective-permute-start(f32[2,256,128]{2,1,0:T(8,128)S(1)} %collective-permute-done.5.refs_2_), channel_id=1, source_target_pairs={{0,224},{32,0},{64,32},{96,64},{128,96},{160,128},{192,160},{224,1... | collective-permute-start | bytes 786440 | tf_op jit(solution)/shard_map/ppermute | solution.py:332
  51.5 10.9 %collective-permute-start.6 = (f32[2,256,128]{2,1,0:T(8,128)S(1)}, f32[2,256,128]{2,1,0:T(8,128)S(1)}, u32[]{:S(2)}, u32[]{:S(2)}) collective-permute-start(f32[2,256,128]{2,1,0:T(8,128)S(1)} %collective-permute-done.4.refs_1_), channel_id=1, source_target_pairs={{0,32},{32,64},{64,96},{96,128},{128,160},{160,192},{192,224},{224... | collective-permute-start | bytes 786440 | tf_op jit(solution)/shard_map/ppermute | solution.py:332
  57.8 10.1 %collective-permute-start.9 = (f32[2,256,128]{2,1,0:T(8,128)S(1)}, f32[2,256,128]{2,1,0:T(8,128)S(1)}, u32[]{:S(2)}, u32[]{:S(2)}) collective-permute-start(f32[2,256,128]{2,1,0:T(8,128)S(1)} %collective-permute-done.7.refs_4_), channel_id=1, source_target_pairs={{0,224},{32,0},{64,32},{96,64},{128,96},{160,128},{192,160},{224,1... | collective-permute-start | bytes 786440 | tf_op jit(solution)/shard_map/ppermute | solution.py:332
  62.4 11.2 %collective-permute-start.8 = (f32[2,256,128]{2,1,0:T(8,128)S(1)}, f32[2,256,128]{2,1,0:T(8,128)S(1)}, u32[]{:S(2)}, u32[]{:S(2)}) collective-permute-start(f32[2,256,128]{2,1,0:T(8,128)S(1)} %collective-permute-done.6.refs_3_), channel_id=1, source_target_pairs={{0,32},{32,64},{64,96},{96,128},{128,160},{160,192},{192,224},{224... | collective-permute-start | bytes 786440 | tf_op jit(solution)/shard_map/ppermute | solution.py:332
  68.0 10.6 %collective-permute-start.13 = (f32[1,256,128]{2,1,0:T(8,128)S(1)}, f32[1,256,128]{2,1,0:T(8,128)S(1)}, u32[]{:S(2)}, u32[]{:S(2)}) collective-permute-start(f32[1,256,128]{2,1,0:T(8,128)S(1)} %slice.39), channel_id=1, source_target_pairs={{0,224},{32,0},{64,32},{96,64},{128,96},{160,128},{192,160},{224,1... | collective-permute-start | bytes 393224 | tf_op jit(solution)/shard_map/ppermute | solution.py:332
  73.6 8.1 %collective-permute-start.12 = (f32[1,256,128]{2,1,0:T(8,128)S(1)}, f32[1,256,128]{2,1,0:T(8,128)S(1)}, u32[]{:S(2)}, u32[]{:S(2)}) collective-permute-start(f32[1,256,128]{2,1,0:T(8,128)S(1)} %slice.41), channel_id=1, source_target_pairs={{0,32},{32,64},{64,96},{96,128},{128,160},{160,192},{192,224},{224... | collective-permute-start | bytes 393224 | tf_op jit(solution)/shard_map/ppermute | solution.py:332
  102.3 40.0 %collective-permute-start.14 = (f32[8,256,128]{2,1,0:T(8,128)}, f32[8,256,128]{2,1,0:T(8,128)S(1)}, u32[]{:S(2)}, u32[]{:S(2)}) collective-permute-start(f32[8,256,128]{2,1,0:T(8,128)} %get-tuple-element.37.f_ref), channel_id=1, source_target_pairs={{0,1},{1,2},{2,3},{3,4},{4,5},{5,6},{6,7},{7,8},{8,9},{9,10},{10,1... | collective-permute-start | bytes 3145736 | tf_op jit(solution)/shard_map/ppermute | solution.py:337
  104.3 38.1 %collective-permute-start.15 = (f32[8,256,128]{2,1,0:T(8,128)}, f32[8,256,128]{2,1,0:T(8,128)S(1)}, u32[]{:S(2)}, u32[]{:S(2)}) collective-permute-start(f32[8,256,128]{2,1,0:T(8,128)} %get-tuple-element.37.f_ref), channel_id=1, source_target_pairs={{1,0},{2,1},{3,2},{4,3},{5,4},{6,5},{7,6},{8,7},{9,8},{10,9},{11,1... | collective-permute-start | bytes 3145736 | tf_op jit(solution)/shard_map/ppermute | solution.py:338
  111.8 1.2 copy-start.1
  113.0 29.4 %copy-start.2 = (f32[8,256,128]{2,1,0:T(8,128)S(1)}, f32[8,256,128]{2,1,0:T(8,128)}, u32[]{:S(2)}) copy-start(f32[8,256,128]{2,1,0:T(8,128)} %get-tuple-element.37.f_ref) | copy-start | bytes 3145732
  129.6 11.2 %collective-permute-start.16 = (f32[2,8,128]{2,1,0:T(8,128)S(1)}, f32[2,8,128]{2,1,0:T(8,128)S(1)}, u32[]{:S(2)}, u32[]{:S(2)}) collective-permute-start(f32[2,8,128]{2,1,0:T(8,128)S(1)} %slice.42), channel_id=1, source_target_pairs={{0,256},{32,288},{64,320},{96,352},{128,384},{160,416},{192,448},{... | collective-permute-start | bytes 24584 | tf_op jit(solution)/shard_map/ppermute | solution.py:426

commit v6 on v5

--- a/solution.py
+++ b/solution.py
@@ -327,8 +327,8 @@
     return lax.all_to_all(copies, "domain", 0, 0)
 
 
-def ring_shift(block, step):
-    pairs = [(z * RING + y, z * RING + (y + step) % RING) for z in range(2) for y in range(RING)]
+def ring_shift(block, step, rings=(0, 1)):
+    pairs = [(z * RING + y, z * RING + (y + step) % RING) for z in rings for y in range(RING)]
     return lax.ppermute(block, "band", pairs)
 
 
@@ -371,8 +371,12 @@
     for part in arrived:
         piece = piece + part
     left, right = neighbours(own)
+    near = band < RING
     crossed = lax.ppermute(piece, "band", [(y, y + RING) for y in range(RING)])
-    piece = jnp.where(band < RING, piece, crossed)
+    first = [ring_shift(piece, 1, (0,)), ring_shift(piece, -1, (0,))]
+    second = [ring_shift(crossed, 1, (1,)), ring_shift(crossed, -1, (1,))]
+    up, down = (jnp.where(near, a, b) for a, b in zip(first, second))
+    piece = jnp.where(near, piece, crossed)
 
     def stage(fresh, imaged, pieces, *sums, last=False):
         sources = (*pieces, own, *((image,) if imaged else ()), *sums)
@@ -384,9 +388,7 @@
             bytes_moved=10 * big,
         )(*sources)
 
-    pieces = [piece]
-    up, down = ring_shift(piece, 1), ring_shift(piece, -1)
-    pieces += [up, down]
+    pieces = [piece, up, down]
     up, down = ring_shift(up, 1), ring_shift(down, -1)
     sums = stage(range(6), (), pieces, sums)
     down, sums = lax.optimization_barrier((down, sums))
@@ -419,14 +421,16 @@
     )(band_word, sums, *pieces, own)
     left, right = neighbours(basis)
     inner = inner_part(basis.reshape(orbitals.shape))[0].reshape(flat)
-    rings = [list(range(RING)), list(range(RING, bands))]
     shared, inner = lax.optimization_barrier((sums, inner))
-    near = jnp.broadcast_to(shared, (RING, 8, 128))
-    near = lax.all_to_all(near, "band", 0, 0, axis_index_groups=rings)
-    far = lax.ppermute(near[:2], "band", [(y, y + RING) for y in range(RING)])
+    other = lax.ppermute(shared, "band", [(0, 1), (1, 0)])
+    shared = jnp.stack([jnp.where(band == 0, shared, other), jnp.where(band == 0, other, shared)])
+    shared = jnp.where(band < 2, shared, 0.0)
+    shared = shared + lax.ppermute(shared, "band", [(0, 4), (1, 5)])
+    shared = shared + lax.ppermute(shared, "band", [(0, 2), (1, 3), (4, 6), (5, 7)])
+    far = lax.ppermute(shared, "band", [(y, y + RING) for y in range(RING)])
     splat = call(
         coeff_kernel, jax.ShapeDtypeStruct((8, 8, 128), F32), specs=[SMEM] + [VMEM] * 5
-    )(band_word, weights, gram, sums, near, far)
+    )(band_word, weights, gram, sums, shared, far)
     residual = call(
         residual_kernel, slab, specs=[VMEM] * 5, flops=30 * big, bytes_moved=20 * big
     )(basis, inner, left, right, splat)

time: 145 us -> 145 us (level)
  the two profiles are of different devices: /device:TPU:8 before, /device:TPU:256 now
where the time goes in v6:
time: 145 us; the launch traced here: 144 us
  starting transfers between devices  55.6 us (38%)
  waiting for transfers between devices  43.8 us (30%)
  Pallas kernels  25.2 us (17%)
  blocking collectives  12.3 us (8%)
  other arithmetic  4.42 us (3%)
  local copies, waits for them, and re-layouts  1.96 us (1%)
    ppermute x10, starting transfers between devices, ring_shift(): return lax.ppermute(block, 'band', pairs)  28.7 us
    ppermute x1, waiting for transfers between devices, local(): crossed = lax.ppermute(piece, 'band', [(y, y + RING) for y in range(RING)])  21 us
    ppermute x2, starting transfers between devices, neighbours(): lax.ppermute(block, 'domain', [((i + 1) % count, i) for i in range(count)])  16.4 us
    all_to_all x1, blocking collectives, domain_parts(): return lax.all_to_all(copies, 'domain', 0, 0)  12.3 us
    ppermute x10, waiting for transfers between devices, ring_shift(): return lax.ppermute(block, 'band', pairs)  9.67 us
    ppermute x1, waiting for transfers between devices, local(): far = lax.ppermute(shared, 'band', [(y, y + RING) for y in range(RING)])  8.15 us
    pallas_call x4, Pallas kernels, stage(): call(lambda *refs: stage_kernel(len(pieces), fresh, imaged, last, *refs),...  6.19 us
    pallas_call x2, Pallas kernels, inner_part(): call(inner_kernel, (field, *sums), specs=[VMEM] * 2, flops=60 * big, byte...  6.04 us
  transfers between devices with their start and end apart: 22, of which 7 were waited for; matrix products, arithmetic and copies ran while one was open for 2% of the time, Pallas kernels for 11%

profile of v6, /device:TPU:256, one launch (start us, length us, event | category | flops | bytes accessed | tf_op | source)
XLA Modules:
  0.0 144.2 jit_solution(3146029715155093274)
XLA Ops:
  4.1 3.3 %shard_map.41 = (f32[8,4,64,128]{3,2,1,0:T(8,128)S(1)}, f32[8,128]{1,0:T(8,128)S(1)}) custom-call(f32[8,4,64,128]{3,2,1,0:T(8,128)S(1)} %copy-done, f32[4,64,128]{2,1,0:T(8,128)S(1)} %copy-done.3), custom_call_target="tpu_custom_call" | custom-call | flops 15728640 | bytes 2097152 | tf_op jit(solution)/shard_map/pallas_call | solution.py:355
  9.5 21.0 %collective-permute-done.3 = f32[2,256,128]{2,1,0:T(8,128)} collective-permute-done((f32[2,256,128]{2,1,0:T(8,128)S(1)}, f32[2,256,128]{2,1,0:T(8,128)}, u32[]{:S(2)}, u32[]{:S(2)}) %collective-permute-start.3) | collective-permute-done | bytes 262176 | tf_op jit(solution)/shard_map/ppermute | solution.py:375
  30.5 1.9 %collective-permute-start.7 = (f32[2,256,128]{2,1,0:T(8,128)}, f32[2,256,128]{2,1,0:T(8,128)}, u32[]{:S(2)}, u32[]{:S(2)}) collective-permute-start(f32[2,256,128]{2,1,0:T(8,128)} %collective-permute-done.3), channel_id=1, source_target_pairs={{256,480},{288,256},{320,288},{352,320},{384,352},{416,384},{448,4... | collective-permute-start | bytes 786440 | tf_op jit(solution)/shard_map/ppermute | solution.py:332
  32.4 1.9 %collective-permute-start.12 = (f32[8,256,128]{2,1,0:T(8,128)S(1)}, f32[8,256,128]{2,1,0:T(8,128)S(1)}, u32[]{:S(2)}, u32[]{:S(2)}) collective-permute-start(f32[8,256,128]{2,1,0:T(8,128)S(1)} %bitcast.19), channel_id=1, source_target_pairs={{0,1},{1,2},{2,3},{3,4},{4,5},{5,6},{6,7},{7,8},{8,9},{9,10},{10,1... | collective-permute-start | bytes 3145736 | tf_op jit(solution)/shard_map/ppermute | solution.py:337
  34.4 9.0 %collective-permute-start.13 = (f32[8,256,128]{2,1,0:T(8,128)S(1)}, f32[8,256,128]{2,1,0:T(8,128)}, u32[]{:S(2)}, u32[]{:S(2)}) collective-permute-start(f32[8,256,128]{2,1,0:T(8,128)S(1)} %bitcast.20), channel_id=1, source_target_pairs={{1,0},{2,1},{3,2},{4,3},{5,4},{6,5},{7,6},{8,7},{9,8},{10,9},{11,1... | collective-permute-start | bytes 3145736 | tf_op jit(solution)/shard_map/ppermute | solution.py:338
  45.4 3.6 %collective-permute-start.5 = (f32[2,256,128]{2,1,0:T(8,128)}, f32[2,256,128]{2,1,0:T(8,128)}, u32[]{:S(2)}, u32[]{:S(2)}) collective-permute-start(f32[2,256,128]{2,1,0:T(8,128)} %collective-permute-done.3), channel_id=1, source_target_pairs={{256,288},{288,320},{320,352},{352,384},{384,416},{416,448},{448,4... | collective-permute-start | bytes 786440 | tf_op jit(solution)/shard_map/ppermute | solution.py:332
  50.1 5.0 %collective-permute-start.9 = (f32[2,256,128]{2,1,0:T(8,128)S(1)}, f32[2,256,128]{2,1,0:T(8,128)S(1)}, u32[]{:S(2)}, u32[]{:S(2)}) collective-permute-start(f32[2,256,128]{2,1,0:T(8,128)S(1)} %broadcast_select_fusion.refs_2_), channel_id=1, source_target_pairs={{0,224},{32,0},{64,32},{96,64},{128,96},{160,128},{192,160},{224,1... | collective-permute-start | bytes 786440 | tf_op jit(solution)/shard_map/ppermute | solution.py:332
  55.1 4.0 %collective-permute-done.5 = f32[2,256,128]{2,1,0:T(8,128)} collective-permute-done((f32[2,256,128]{2,1,0:T(8,128)}, f32[2,256,128]{2,1,0:T(8,128)}, u32[]{:S(2)}, u32[]{:S(2)}) %collective-permute-start.5) | collective-permute-done | bytes 262176 | tf_op jit(solution)/shard_map/ppermute | solution.py:332
  60.1 1.9 %collective-permute-start.8 = (f32[2,256,128]{2,1,0:T(8,128)S(1)}, f32[2,256,128]{2,1,0:T(8,128)S(1)}, u32[]{:S(2)}, u32[]{:S(2)}) collective-permute-start(f32[2,256,128]{2,1,0:T(8,128)S(1)} %broadcast_select_fusion.1.refs_1_), channel_id=1, source_target_pairs={{0,32},{32,64},{64,96},{96,128},{128,160},{160,192},{192,224},{224... | collective-permute-start | bytes 786440 | tf_op jit(solution)/shard_map/ppermute | solution.py:332
  64.2 5.1 %collective-permute-start.11 = (f32[2,256,128]{2,1,0:T(8,128)S(1)}, f32[2,256,128]{2,1,0:T(8,128)S(1)}, u32[]{:S(2)}, u32[]{:S(2)}) collective-permute-start(f32[2,256,128]{2,1,0:T(8,128)S(1)} %collective-permute-done.9.refs_4_), channel_id=1, source_target_pairs={{0,224},{32,0},{64,32},{96,64},{128,96},{160,128},{192,160},{224,1... | collective-permute-start | bytes 786440 | tf_op jit(solution)/shard_map/ppermute | solution.py:332
  69.3 2.4 %collective-permute-done.8.refs_3_ = f32[2,256,128]{2,1,0:T(8,128)S(1)} collective-permute-done((f32[2,256,128]{2,1,0:T(8,128)S(1)}, f32[2,256,128]{2,1,0:T(8,128)S(1)}, u32[]{:S(2)}, u32[]{:S(2)}) %collective-permute-start.8) | collective-permute-done | bytes 262176 | tf_op jit(solution)/shard_map/ppermute | solution.py:332
  74.7 2.6 %shard_map.44 = (f32[8,256,128]{2,1,0:T(8,128)S(1)}, f32[8,128]{1,0:T(8,128)S(1)}) custom-call(f32[8,256,128]{2,1,0:T(8,128)S(1)} %bitcast.23, f32[8,256,128]{2,1,0:T(8,128)S(1)} %bitcast.30, f32[8,256,128]{2,1,0:T(8,128)S(1)} %collective-permute-done.12.left, f32[8,256,128]{2,1,0:T(8,128)} %collective-permute-done.13.right), custom_call_target="tpu_custom_call" | custom-call | flops 13107200 | bytes 5242880 | tf_op jit(solution)/shard_map/pallas_call | solution.py:398
  77.3 5.1 %collective-permute-start.15 = (f32[1,256,128]{2,1,0:T(8,128)S(1)}, f32[1,256,128]{2,1,0:T(8,128)S(1)}, u32[]{:S(2)}, u32[]{:S(2)}) collective-permute-start(f32[1,256,128]{2,1,0:T(8,128)S(1)} %slice.36), channel_id=1, source_target_pairs={{0,224},{32,0},{64,32},{96,64},{128,96},{160,128},{192,160},{224,1... | collective-permute-start | bytes 393224 | tf_op jit(solution)/shard_map/ppermute | solution.py:332
  82.6 1.9 %collective-permute-start.14 = (f32[1,256,128]{2,1,0:T(8,128)S(1)}, f32[1,256,128]{2,1,0:T(8,128)S(1)}, u32[]{:S(2)}, u32[]{:S(2)}) collective-permute-start(f32[1,256,128]{2,1,0:T(8,128)S(1)} %slice.37), channel_id=1, source_target_pairs={{0,32},{32,64},{64,96},{96,128},{128,160},{160,192},{192,224},{224... | collective-permute-start | bytes 393224 | tf_op jit(solution)/shard_map/ppermute | solution.py:332
  84.5 3.1 %shard_map.45.refs_11_ = f32[8,128]{1,0:T(8,128)S(1)} custom-call(f32[2,256,128]{2,1,0:T(8,128)S(1)} %broadcast_select_fusion.2.refs_0_, f32[2,256,128]{2,1,0:T(8,128)S(1)} %broadcast_select_fusion.1.refs_1_, f32[2,256,128]{2,1,0:T(8,128)S(1)} %broadcast_select_fusion.refs_2_, f32[2,256,128]{2,1,0:T(8,128)S(1)} %collective-permute-done.8.refs_3_, ...), custom_call_target="tpu_custom_call" | custom-call | flops 5242880 | bytes 2621440 | tf_op jit(solution)/shard_map/pallas_call | solution.py:383
  87.6 3.1 %collective-permute-done.14.refs_7_ = f32[1,256,128]{2,1,0:T(8,128)S(1)} collective-permute-done((f32[1,256,128]{2,1,0:T(8,128)S(1)}, f32[1,256,128]{2,1,0:T(8,128)S(1)}, u32[]{:S(2)}, u32[]{:S(2)}) %collective-permute-start.14) | collective-permute-done | bytes 131104 | tf_op jit(solution)/shard_map/ppermute | solution.py:332
  91.7 12.3 %all_to_all.5.refs_0_ = f32[32,8,128]{2,1,0:T(8,128)S(1)} all-to-all(f32[32,8,128]{2,1,0:T(8,128)S(1)} %shard_map.46), channel_id=1, replica_groups=mesh['band'=16,'domain'=32] {'domain'}, dimensions={0} | all-to-all | bytes 262144 | tf_op jit(solution)/shard_map/all_to_all | solution.py:327
  104.0 5.3 %shard_map.48 = (f32[8,256,128]{2,1,0:T(8,128)}, f32[8,128]{1,0:T(8,128)S(1)}, f32[8,128]{1,0:T(8,128)S(1)}) custom-call(s32[1]{0:T(128)} %bitcast.band_ref, f32[8,128]{1,0:T(8,128)S(1)} %shard_map.47.sums_ref.own_ref, f32[2,256,128]{2,1,0:T(8,128)S(1)} %broadcast_select_fusion.2.refs_0_, f32[2,256,128]{2,1,0:T(8,128)S(1)} %broadcast_select_fusion.1.refs_1_, ...), custom_call_target="tpu_custom_call" | custom-call | flops 12582912 | bytes 4194304 | tf_op jit(solution)/shard_map/pallas_call | solution.py:414
  109.4 2.0 %collective-permute-start.16 = (f32[8,256,128]{2,1,0:T(8,128)}, f32[8,256,128]{2,1,0:T(8,128)S(1)}, u32[]{:S(2)}, u32[]{:S(2)}) collective-permute-start(f32[8,256,128]{2,1,0:T(8,128)} %get-tuple-element.37.f_ref), channel_id=1, source_target_pairs={{0,1},{1,2},{2,3},{3,4},{4,5},{5,6},{6,7},{7,8},{8,9},{9,10},{10,1... | collective-permute-start | bytes 3145736 | tf_op jit(solution)/shard_map/ppermute | solution.py:337
  111.4 7.4 %collective-permute-start.17 = (f32[8,256,128]{2,1,0:T(8,128)}, f32[8,256,128]{2,1,0:T(8,128)}, u32[]{:S(2)}, u32[]{:S(2)}) collective-permute-start(f32[8,256,128]{2,1,0:T(8,128)} %get-tuple-element.37.f_ref), channel_id=1, source_target_pairs={{1,0},{2,1},{3,2},{4,3},{5,4},{6,5},{7,6},{8,7},{9,8},{10,9},{11,1... | collective-permute-start | bytes 3145736 | tf_op jit(solution)/shard_map/ppermute | solution.py:338
  120.1 2.7 %shard_map.49 = f32[8,4,64,128]{3,2,1,0:T(8,128)S(1)} custom-call(f32[8,4,64,128]{3,2,1,0:T(8,128)S(1)} %bitcast.28, f32[4,64,128]{2,1,0:T(8,128)S(1)} %copy-done.3), custom_call_target="tpu_custom_call" | custom-call | flops 15728640 | bytes 2097152 | tf_op jit(solution)/shard_map/pallas_call | solution.py:355
  126.2 8.2 %collective-permute-done.21.far_ref = f32[2,8,128]{2,1,0:T(8,128)S(1)} collective-permute-done((f32[2,8,128]{2,1,0:T(8,128)S(1)}, f32[2,8,128]{2,1,0:T(8,128)S(1)}, u32[]{:S(2)}, u32[]{:S(2)}) %collective-permute-start.21) | collective-permute-done | bytes 8224 | tf_op jit(solution)/shard_map/ppermute | solution.py:430
  136.0 4.9 %collective-permute-done.16.left_ref = f32[8,256,128]{2,1,0:T(8,128)S(1)} collective-permute-done((f32[8,256,128]{2,1,0:T(8,128)}, f32[8,256,128]{2,1,0:T(8,128)S(1)}, u32[]{:S(2)}, u32[]{:S(2)}) %collective-permute-start.16) | collective-permute-done | bytes 1048608 | tf_op jit(solution)/shard_map/ppermute | solution.py:337
  140.9 3.4 %shard_map.51 = f32[8,256,128]{2,1,0:T(8,128)} custom-call(f32[8,256,128]{2,1,0:T(8,128)S(1)} %copy-done.2, f32[8,256,128]{2,1,0:T(8,128)S(1)} %bitcast.29, f32[8,256,128]{2,1,0:T(8,128)S(1)} %collective-permute-done.16.left_ref, f32[8,256,128]{2,1,0:T(8,128)} %collective-permute-done.17.right_ref, f32[8,8,128]{2,1,0:T(8,128)S(1)} %shard_map.50.splat), custom_call_target="tpu_custom_call" | custom-call | flops 7864320 | bytes 5242880 | tf_op jit(solution)/shard_map/pallas_call | solution.py:434
  (53 shorter events, 21.8 us)
Async XLA Ops:
  0.6 3.5 %copy-start = (f32[8,4,64,128]{3,2,1,0:T(8,128)S(1)}, f32[8,4,64,128]{3,2,1,0:T(8,128)}, u32[]{:S(2)}) copy-start(f32[8,4,64,128]{3,2,1,0:T(8,128)} %f_ref.1) | copy-start | bytes 3145732
  2.0 5.4 %collective-permute-start = (f32[2,256,128]{2,1,0:T(8,128)S(1)}, f32[2,256,128]{2,1,0:T(8,128)S(1)}, u32[]{:S(2)}, u32[]{:S(2)}) collective-permute-start(f32[2,256,128]{2,1,0:T(8,128)S(1)} %bitcast.34), channel_id=1, source_target_pairs={{0,64},{32,96},{1,65},{33,97},{2,66},{34,98},{3,67},{35,99},{4,68}... | collective-permute-start | bytes 786440 | tf_op jit(solution)/shard_map/ppermute | solution.py:366
  2.7 4.7 %collective-permute-start.1 = (f32[2,256,128]{2,1,0:T(8,128)S(1)}, f32[2,256,128]{2,1,0:T(8,128)S(1)}, u32[]{:S(2)}, u32[]{:S(2)}) collective-permute-start(f32[2,256,128]{2,1,0:T(8,128)S(1)} %bitcast.33), channel_id=1, source_target_pairs={{0,192},{32,224},{1,193},{33,225},{2,194},{34,226},{3,195},{35,227... | collective-permute-start | bytes 786440 | tf_op jit(solution)/shard_map/ppermute | solution.py:366
  3.4 4.0 %collective-permute-start.2 = (f32[2,256,128]{2,1,0:T(8,128)S(1)}, f32[2,256,128]{2,1,0:T(8,128)S(1)}, u32[]{:S(2)}, u32[]{:S(2)}) collective-permute-start(f32[2,256,128]{2,1,0:T(8,128)S(1)} %bitcast.32), channel_id=1, source_target_pairs={{0,128},{32,160},{1,129},{33,161},{2,130},{34,162},{3,131},{35,163... | collective-permute-start | bytes 786440 | tf_op jit(solution)/shard_map/ppermute | solution.py:366
  7.5 23.0 %collective-permute-start.3 = (f32[2,256,128]{2,1,0:T(8,128)S(1)}, f32[2,256,128]{2,1,0:T(8,128)}, u32[]{:S(2)}, u32[]{:S(2)}) collective-permute-start(f32[2,256,128]{2,1,0:T(8,128)S(1)} %fusion.1), channel_id=1, source_target_pairs={{0,256},{32,288},{64,320},{96,352},{128,384},{160,416},{192,448},{... | collective-permute-start | bytes 786440 | tf_op jit(solution)/shard_map/ppermute | solution.py:375
  8.8 35.9 %collective-permute-start.6 = (f32[2,256,128]{2,1,0:T(8,128)S(1)}, f32[2,256,128]{2,1,0:T(8,128)S(1)}, u32[]{:S(2)}, u32[]{:S(2)}) collective-permute-start(f32[2,256,128]{2,1,0:T(8,128)S(1)} %fusion.1), channel_id=1, source_target_pairs={{0,224},{32,0},{64,32},{96,64},{128,96},{160,128},{192,160},{224,1... | collective-permute-start | bytes 786440 | tf_op jit(solution)/shard_map/ppermute | solution.py:332
  30.5 18.6 %collective-permute-start.7 = (f32[2,256,128]{2,1,0:T(8,128)}, f32[2,256,128]{2,1,0:T(8,128)}, u32[]{:S(2)}, u32[]{:S(2)}) collective-permute-start(f32[2,256,128]{2,1,0:T(8,128)} %collective-permute-done.3), channel_id=1, source_target_pairs={{256,480},{288,256},{320,288},{352,320},{384,352},{416,384},{448,4... | collective-permute-start | bytes 786440 | tf_op jit(solution)/shard_map/ppermute | solution.py:332
  32.4 42.2 %collective-permute-start.12 = (f32[8,256,128]{2,1,0:T(8,128)S(1)}, f32[8,256,128]{2,1,0:T(8,128)S(1)}, u32[]{:S(2)}, u32[]{:S(2)}) collective-permute-start(f32[8,256,128]{2,1,0:T(8,128)S(1)} %bitcast.19), channel_id=1, source_target_pairs={{0,1},{1,2},{2,3},{3,4},{4,5},{5,6},{6,7},{7,8},{8,9},{9,10},{10,1... | collective-permute-start | bytes 3145736 | tf_op jit(solution)/shard_map/ppermute | solution.py:337
  34.4 40.3 %collective-permute-start.13 = (f32[8,256,128]{2,1,0:T(8,128)S(1)}, f32[8,256,128]{2,1,0:T(8,128)}, u32[]{:S(2)}, u32[]{:S(2)}) collective-permute-start(f32[8,256,128]{2,1,0:T(8,128)S(1)} %bitcast.20), channel_id=1, source_target_pairs={{1,0},{2,1},{3,2},{4,3},{5,4},{6,5},{7,6},{8,7},{9,8},{10,9},{11,1... | collective-permute-start | bytes 3145736 | tf_op jit(solution)/shard_map/ppermute | solution.py:338
  43.3 11.8 %collective-permute-start.4 = (f32[2,256,128]{2,1,0:T(8,128)S(1)}, f32[2,256,128]{2,1,0:T(8,128)}, u32[]{:S(2)}, u32[]{:S(2)}) collective-permute-start(f32[2,256,128]{2,1,0:T(8,128)S(1)} %fusion.1), channel_id=1, source_target_pairs={{0,32},{32,64},{64,96},{96,128},{128,160},{160,192},{192,224},{224... | collective-permute-start | bytes 786440 | tf_op jit(solution)/shard_map/ppermute | solution.py:332
  45.4 13.7 %collective-permute-start.5 = (f32[2,256,128]{2,1,0:T(8,128)}, f32[2,256,128]{2,1,0:T(8,128)}, u32[]{:S(2)}, u32[]{:S(2)}) collective-permute-start(f32[2,256,128]{2,1,0:T(8,128)} %collective-permute-done.3), channel_id=1, source_target_pairs={{256,288},{288,320},{320,352},{352,384},{384,416},{416,448},{448,4... | collective-permute-start | bytes 786440 | tf_op jit(solution)/shard_map/ppermute | solution.py:332
  50.1 14.1 %collective-permute-start.9 = (f32[2,256,128]{2,1,0:T(8,128)S(1)}, f32[2,256,128]{2,1,0:T(8,128)S(1)}, u32[]{:S(2)}, u32[]{:S(2)}) collective-permute-start(f32[2,256,128]{2,1,0:T(8,128)S(1)} %broadcast_select_fusion.refs_2_), channel_id=1, source_target_pairs={{0,224},{32,0},{64,32},{96,64},{128,96},{160,128},{192,160},{224,1... | collective-permute-start | bytes 786440 | tf_op jit(solution)/shard_map/ppermute | solution.py:332
  60.1 11.6 %collective-permute-start.8 = (f32[2,256,128]{2,1,0:T(8,128)S(1)}, f32[2,256,128]{2,1,0:T(8,128)S(1)}, u32[]{:S(2)}, u32[]{:S(2)}) collective-permute-start(f32[2,256,128]{2,1,0:T(8,128)S(1)} %broadcast_select_fusion.1.refs_1_), channel_id=1, source_target_pairs={{0,32},{32,64},{64,96},{96,128},{128,160},{160,192},{192,224},{224... | collective-permute-start | bytes 786440 | tf_op jit(solution)/shard_map/ppermute | solution.py:332
  64.2 13.1 %collective-permute-start.11 = (f32[2,256,128]{2,1,0:T(8,128)S(1)}, f32[2,256,128]{2,1,0:T(8,128)S(1)}, u32[]{:S(2)}, u32[]{:S(2)}) collective-permute-start(f32[2,256,128]{2,1,0:T(8,128)S(1)} %collective-permute-done.9.refs_4_), channel_id=1, source_target_pairs={{0,224},{32,0},{64,32},{96,64},{128,96},{160,128},{192,160},{224,1... | collective-permute-start | bytes 786440 | tf_op jit(solution)/shard_map/ppermute | solution.py:332
  71.8 10.8 %collective-permute-start.10 = (f32[2,256,128]{2,1,0:T(8,128)S(1)}, f32[2,256,128]{2,1,0:T(8,128)S(1)}, u32[]{:S(2)}, u32[]{:S(2)}) collective-permute-start(f32[2,256,128]{2,1,0:T(8,128)S(1)} %collective-permute-done.8.refs_3_), channel_id=1, source_target_pairs={{0,32},{32,64},{64,96},{96,128},{128,160},{160,192},{192,224},{224... | collective-permute-start | bytes 786440 | tf_op jit(solution)/shard_map/ppermute | solution.py:332
  77.3 10.2 %collective-permute-start.15 = (f32[1,256,128]{2,1,0:T(8,128)S(1)}, f32[1,256,128]{2,1,0:T(8,128)S(1)}, u32[]{:S(2)}, u32[]{:S(2)}) collective-permute-start(f32[1,256,128]{2,1,0:T(8,128)S(1)} %slice.36), channel_id=1, source_target_pairs={{0,224},{32,0},{64,32},{96,64},{128,96},{160,128},{192,160},{224,1... | collective-permute-start | bytes 393224 | tf_op jit(solution)/shard_map/ppermute | solution.py:332
  82.6 8.1 %collective-permute-start.14 = (f32[1,256,128]{2,1,0:T(8,128)S(1)}, f32[1,256,128]{2,1,0:T(8,128)S(1)}, u32[]{:S(2)}, u32[]{:S(2)}) collective-permute-start(f32[1,256,128]{2,1,0:T(8,128)S(1)} %slice.37), channel_id=1, source_target_pairs={{0,32},{32,64},{64,96},{96,128},{128,160},{160,192},{192,224},{224... | collective-permute-start | bytes 393224 | tf_op jit(solution)/shard_map/ppermute | solution.py:332
  109.4 31.5 %collective-permute-start.16 = (f32[8,256,128]{2,1,0:T(8,128)}, f32[8,256,128]{2,1,0:T(8,128)S(1)}, u32[]{:S(2)}, u32[]{:S(2)}) collective-permute-start(f32[8,256,128]{2,1,0:T(8,128)} %get-tuple-element.37.f_ref), channel_id=1, source_target_pairs={{0,1},{1,2},{2,3},{3,4},{4,5},{5,6},{6,7},{7,8},{8,9},{9,10},{10,1... | collective-permute-start | bytes 3145736 | tf_op jit(solution)/shard_map/ppermute | solution.py:337
  111.4 29.5 %collective-permute-start.17 = (f32[8,256,128]{2,1,0:T(8,128)}, f32[8,256,128]{2,1,0:T(8,128)}, u32[]{:S(2)}, u32[]{:S(2)}) collective-permute-start(f32[8,256,128]{2,1,0:T(8,128)} %get-tuple-element.37.f_ref), channel_id=1, source_target_pairs={{1,0},{2,1},{3,2},{4,3},{5,4},{6,5},{7,6},{8,7},{9,8},{10,9},{11,1... | collective-permute-start | bytes 3145736 | tf_op jit(solution)/shard_map/ppermute | solution.py:338
  120.1 20.8 %copy-start.2 = (f32[8,256,128]{2,1,0:T(8,128)S(1)}, f32[8,256,128]{2,1,0:T(8,128)}, u32[]{:S(2)}) copy-start(f32[8,256,128]{2,1,0:T(8,128)} %get-tuple-element.37.f_ref) | copy-start | bytes 3145732
  122.8 0.7 collective-permute-start.18
  123.6 0.7 collective-permute-start.19
  124.2 0.7 collective-permute-start.20
  124.9 9.5 %collective-permute-start.21 = (f32[2,8,128]{2,1,0:T(8,128)S(1)}, f32[2,8,128]{2,1,0:T(8,128)S(1)}, u32[]{:S(2)}, u32[]{:S(2)}) collective-permute-start(f32[2,8,128]{2,1,0:T(8,128)S(1)} %fusion.3.near_ref), channel_id=1, source_target_pairs={{0,256},{32,288},{64,320},{96,352},{128,384},{160,416},{192,448},{... | collective-permute-start | bytes 24584 | tf_op jit(solution)/shard_map/ppermute | solution.py:430
  (3 other events, 5.4 us)

commit v7 on v5

--- a/solution.py
+++ b/solution.py
@@ -341,7 +341,7 @@
 
 def local(orbitals, potential):
     blocks, slab_width, rows_y, rows_z = orbitals.shape
-    domain, bands = lax.axis_size("domain"), lax.axis_size("band")
+    domain = lax.axis_size("domain")
     cells_total = float(slab_width * rows_y * rows_z * domain)
     band = lax.axis_index("band")
     band_word = band.reshape(1).astype(jnp.int32)
@@ -419,14 +419,16 @@
     )(band_word, sums, *pieces, own)
     left, right = neighbours(basis)
     inner = inner_part(basis.reshape(orbitals.shape))[0].reshape(flat)
-    rings = [list(range(RING)), list(range(RING, bands))]
     shared, inner = lax.optimization_barrier((sums, inner))
-    near = jnp.broadcast_to(shared, (RING, 8, 128))
-    near = lax.all_to_all(near, "band", 0, 0, axis_index_groups=rings)
-    far = lax.ppermute(near[:2], "band", [(y, y + RING) for y in range(RING)])
+    other = lax.ppermute(shared, "band", [(0, 1), (1, 0)])
+    shared = jnp.stack([jnp.where(band == 0, shared, other), jnp.where(band == 0, other, shared)])
+    shared = jnp.where(band < 2, shared, 0.0)
+    shared = shared + lax.ppermute(shared, "band", [(0, 4), (1, 5)])
+    shared = shared + lax.ppermute(shared, "band", [(0, 2), (1, 3), (4, 6), (5, 7)])
+    far = lax.ppermute(shared, "band", [(y, y + RING) for y in range(RING)])
     splat = call(
         coeff_kernel, jax.ShapeDtypeStruct((8, 8, 128), F32), specs=[SMEM] + [VMEM] * 5
-    )(band_word, weights, gram, sums, near, far)
+    )(band_word, weights, gram, sums, shared, far)
     residual = call(
         residual_kernel, slab, specs=[VMEM] * 5, flops=30 * big, bytes_moved=20 * big
     )(basis, inner, left, right, splat)

time: 145 us -> 141 us (0.972)
  the two profiles are of different devices: /device:TPU:8 before, /device:TPU:1 now
where the time goes in v7:
time: 141 us; the launch traced here: 139 us
  starting transfers between devices  52.7 us (37%)
  waiting for transfers between devices  36.1 us (26%)
  Pallas kernels  25.2 us (18%)
  blocking collectives  21.5 us (15%)
  other arithmetic  1.49 us (1%)
    ppermute x8, starting transfers between devices, ring_shift(): return lax.ppermute(block, 'band', pairs)  23 us
    all_to_all x1, blocking collectives, domain_parts(): return lax.all_to_all(copies, 'domain', 0, 0)  21.5 us
    ppermute x2, waiting for transfers between devices, neighbours(): lax.ppermute(block, 'domain', [((i + 1) % count, i) for i in range(count)])  12.8 us
    ppermute x3, waiting for transfers between devices, local(): lax.ppermute(quarters[k], 'band', [(0, 2 * k), (1, 2 * k + 1)])  11.5 us
    ppermute x3, starting transfers between devices, local(): lax.ppermute(quarters[k], 'band', [(0, 2 * k), (1, 2 * k + 1)])  9.65 us
    ppermute x8, waiting for transfers between devices, ring_shift(): return lax.ppermute(block, 'band', pairs)  6.75 us
    ppermute x2, starting transfers between devices, neighbours(): lax.ppermute(block, 'domain', [(i, (i + 1) % count) for i in range(count)])  6.58 us
    pallas_call x4, Pallas kernels, stage(): call(lambda *refs: stage_kernel(len(pieces), fresh, imaged, last, *refs),...  6.18 us
  transfers between devices with their start and end apart: 20, of which 12 were waited for; matrix products, arithmetic and copies ran while one was open for 0% of the time, Pallas kernels for 11%

profile of v7, /device:TPU:1, one launch (start us, length us, event | category | flops | bytes accessed | tf_op | source)
XLA Modules:
  0.0 139.2 jit_solution(1166407132655829772)
XLA Ops:
  2.0 5.1 %collective-permute-start = (f32[2,256,128]{2,1,0:T(8,128)S(1)}, f32[2,256,128]{2,1,0:T(8,128)S(1)}, u32[]{:S(2)}, u32[]{:S(2)}) collective-permute-start(f32[2,256,128]{2,1,0:T(8,128)S(1)} %bitcast.34), channel_id=1, source_target_pairs={{0,64},{32,96},{1,65},{33,97},{2,66},{34,98},{3,67},{35,99},{4,68}... | collective-permute-start | bytes 786440 | tf_op jit(solution)/shard_map/ppermute | solution.py:366
  7.1 2.3 %collective-permute-start.1 = (f32[2,256,128]{2,1,0:T(8,128)S(1)}, f32[2,256,128]{2,1,0:T(8,128)S(1)}, u32[]{:S(2)}, u32[]{:S(2)}) collective-permute-start(f32[2,256,128]{2,1,0:T(8,128)S(1)} %bitcast.33), channel_id=1, source_target_pairs={{0,192},{32,224},{1,193},{33,225},{2,194},{34,226},{3,195},{35,227... | collective-permute-start | bytes 786440 | tf_op jit(solution)/shard_map/ppermute | solution.py:366
  9.5 2.2 %collective-permute-start.2 = (f32[2,256,128]{2,1,0:T(8,128)S(1)}, f32[2,256,128]{2,1,0:T(8,128)S(1)}, u32[]{:S(2)}, u32[]{:S(2)}) collective-permute-start(f32[2,256,128]{2,1,0:T(8,128)S(1)} %bitcast.32), channel_id=1, source_target_pairs={{0,128},{32,160},{1,129},{33,161},{2,130},{34,162},{3,131},{35,163... | collective-permute-start | bytes 786440 | tf_op jit(solution)/shard_map/ppermute | solution.py:366
  11.7 3.3 %shard_map.41 = (f32[8,4,64,128]{3,2,1,0:T(8,128)S(1)}, f32[8,128]{1,0:T(8,128)S(1)}) custom-call(f32[8,4,64,128]{3,2,1,0:T(8,128)S(1)} %copy-done, f32[4,64,128]{2,1,0:T(8,128)S(1)} %copy-done.3), custom_call_target="tpu_custom_call" | custom-call | flops 15728640 | bytes 2097152 | tf_op jit(solution)/shard_map/pallas_call | solution.py:355
  15.0 11.5 %collective-permute-done.1 = f32[2,256,128]{2,1,0:T(8,128)S(1)} collective-permute-done((f32[2,256,128]{2,1,0:T(8,128)S(1)}, f32[2,256,128]{2,1,0:T(8,128)S(1)}, u32[]{:S(2)}, u32[]{:S(2)}) %collective-permute-start.1) | collective-permute-done | bytes 262176 | tf_op jit(solution)/shard_map/ppermute | solution.py:366
  28.6 4.5 %collective-permute-start.10 = (f32[8,256,128]{2,1,0:T(8,128)S(1)}, f32[8,256,128]{2,1,0:T(8,128)S(1)}, u32[]{:S(2)}, u32[]{:S(2)}) collective-permute-start(f32[8,256,128]{2,1,0:T(8,128)S(1)} %bitcast.19), channel_id=1, source_target_pairs={{0,1},{1,2},{2,3},{3,4},{4,5},{5,6},{6,7},{7,8},{8,9},{9,10},{10,1... | collective-permute-start | bytes 3145736 | tf_op jit(solution)/shard_map/ppermute | solution.py:337
  37.0 3.4 %collective-permute-start.4 = (f32[2,256,128]{2,1,0:T(8,128)S(1)}, f32[2,256,128]{2,1,0:T(8,128)S(1)}, u32[]{:S(2)}, u32[]{:S(2)}) collective-permute-start(f32[2,256,128]{2,1,0:T(8,128)S(1)} %broadcast_select_fusion.refs_0_), channel_id=1, source_target_pairs={{0,32},{32,64},{64,96},{96,128},{128,160},{160,192},{192,224},{224... | collective-permute-start | bytes 786440 | tf_op jit(solution)/shard_map/ppermute | solution.py:332
  40.4 2.1 %collective-permute-done.5.refs_2_ = f32[2,256,128]{2,1,0:T(8,128)S(1)} collective-permute-done((f32[2,256,128]{2,1,0:T(8,128)S(1)}, f32[2,256,128]{2,1,0:T(8,128)S(1)}, u32[]{:S(2)}, u32[]{:S(2)}) %collective-permute-start.5) | collective-permute-done | bytes 262176 | tf_op jit(solution)/shard_map/ppermute | solution.py:332
  42.5 4.3 %collective-permute-start.7 = (f32[2,256,128]{2,1,0:T(8,128)S(1)}, f32[2,256,128]{2,1,0:T(8,128)S(1)}, u32[]{:S(2)}, u32[]{:S(2)}) collective-permute-start(f32[2,256,128]{2,1,0:T(8,128)S(1)} %collective-permute-done.5.refs_2_), channel_id=1, source_target_pairs={{0,224},{32,0},{64,32},{96,64},{128,96},{160,128},{192,160},{224,1... | collective-permute-start | bytes 786440 | tf_op jit(solution)/shard_map/ppermute | solution.py:332
  51.5 4.3 %collective-permute-start.9 = (f32[2,256,128]{2,1,0:T(8,128)S(1)}, f32[2,256,128]{2,1,0:T(8,128)S(1)}, u32[]{:S(2)}, u32[]{:S(2)}) collective-permute-start(f32[2,256,128]{2,1,0:T(8,128)S(1)} %collective-permute-done.7.refs_4_), channel_id=1, source_target_pairs={{0,224},{32,0},{64,32},{96,64},{128,96},{160,128},{192,160},{224,1... | collective-permute-start | bytes 786440 | tf_op jit(solution)/shard_map/ppermute | solution.py:332
  59.5 5.5 %collective-permute-done.11.right = f32[8,256,128]{2,1,0:T(8,128)} collective-permute-done((f32[8,256,128]{2,1,0:T(8,128)S(1)}, f32[8,256,128]{2,1,0:T(8,128)}, u32[]{:S(2)}, u32[]{:S(2)}) %collective-permute-start.11) | collective-permute-done | bytes 1048608 | tf_op jit(solution)/shard_map/ppermute | solution.py:338
  64.9 2.6 %shard_map.44 = (f32[8,256,128]{2,1,0:T(8,128)S(1)}, f32[8,128]{1,0:T(8,128)S(1)}) custom-call(f32[8,256,128]{2,1,0:T(8,128)S(1)} %bitcast.23, f32[8,256,128]{2,1,0:T(8,128)S(1)} %bitcast.30, f32[8,256,128]{2,1,0:T(8,128)S(1)} %collective-permute-done.10.left, f32[8,256,128]{2,1,0:T(8,128)} %collective-permute-done.11.right), custom_call_target="tpu_custom_call" | custom-call | flops 13107200 | bytes 5242880 | tf_op jit(solution)/shard_map/pallas_call | solution.py:396
  69.5 3.4 %collective-permute-start.12 = (f32[1,256,128]{2,1,0:T(8,128)S(1)}, f32[1,256,128]{2,1,0:T(8,128)S(1)}, u32[]{:S(2)}, u32[]{:S(2)}) collective-permute-start(f32[1,256,128]{2,1,0:T(8,128)S(1)} %slice.37), channel_id=1, source_target_pairs={{0,32},{32,64},{64,96},{96,128},{128,160},{160,192},{192,224},{224... | collective-permute-start | bytes 393224 | tf_op jit(solution)/shard_map/ppermute | solution.py:332
  72.9 3.1 %shard_map.45.refs_11_ = f32[8,128]{1,0:T(8,128)S(1)} custom-call(f32[2,256,128]{2,1,0:T(8,128)S(1)} %broadcast_select_fusion.refs_0_, f32[2,256,128]{2,1,0:T(8,128)S(1)} %collective-permute-done.4.refs_1_, f32[2,256,128]{2,1,0:T(8,128)S(1)} %collective-permute-done.5.refs_2_, f32[2,256,128]{2,1,0:T(8,128)S(1)} %collective-permute-done.6.refs_3_, ...), custom_call_target="tpu_custom_call" | custom-call | flops 5242880 | bytes 2621440 | tf_op jit(solution)/shard_map/pallas_call | solution.py:379
  76.0 2.2 %collective-permute-done.12.refs_7_ = f32[1,256,128]{2,1,0:T(8,128)S(1)} collective-permute-done((f32[1,256,128]{2,1,0:T(8,128)S(1)}, f32[1,256,128]{2,1,0:T(8,128)S(1)}, u32[]{:S(2)}, u32[]{:S(2)}) %collective-permute-start.12) | collective-permute-done | bytes 131104 | tf_op jit(solution)/shard_map/ppermute | solution.py:332
  79.2 21.5 %all_to_all.5.refs_0_ = f32[32,8,128]{2,1,0:T(8,128)S(1)} all-to-all(f32[32,8,128]{2,1,0:T(8,128)S(1)} %shard_map.46), channel_id=1, replica_groups=mesh['band'=16,'domain'=32] {'domain'}, dimensions={0} | all-to-all | bytes 262144 | tf_op jit(solution)/shard_map/all_to_all | solution.py:327
  100.8 5.4 %shard_map.48 = (f32[8,256,128]{2,1,0:T(8,128)}, f32[8,128]{1,0:T(8,128)S(1)}, f32[8,128]{1,0:T(8,128)S(1)}) custom-call(s32[1]{0:T(128)} %bitcast.band_ref, f32[8,128]{1,0:T(8,128)S(1)} %shard_map.47.sums_ref.own_ref, f32[2,256,128]{2,1,0:T(8,128)S(1)} %broadcast_select_fusion.refs_0_, f32[2,256,128]{2,1,0:T(8,128)S(1)} %collective-permute-done.4.refs_1_, ...), custom_call_target="tpu_custom_call" | custom-call | flops 12582912 | bytes 4194304 | tf_op jit(solution)/shard_map/pallas_call | solution.py:412
  106.2 2.1 %collective-permute-start.14 = (f32[8,256,128]{2,1,0:T(8,128)}, f32[8,256,128]{2,1,0:T(8,128)S(1)}, u32[]{:S(2)}, u32[]{:S(2)}) collective-permute-start(f32[8,256,128]{2,1,0:T(8,128)} %get-tuple-element.37.f_ref), channel_id=1, source_target_pairs={{0,1},{1,2},{2,3},{3,4},{4,5},{5,6},{6,7},{7,8},{8,9},{9,10},{10,1... | collective-permute-start | bytes 3145736 | tf_op jit(solution)/shard_map/ppermute | solution.py:337
  108.3 2.2 %collective-permute-start.15 = (f32[8,256,128]{2,1,0:T(8,128)}, f32[8,256,128]{2,1,0:T(8,128)}, u32[]{:S(2)}, u32[]{:S(2)}) collective-permute-start(f32[8,256,128]{2,1,0:T(8,128)} %get-tuple-element.37.f_ref), channel_id=1, source_target_pairs={{1,0},{2,1},{3,2},{4,3},{5,4},{6,5},{7,6},{8,7},{9,8},{10,9},{11,1... | collective-permute-start | bytes 3145736 | tf_op jit(solution)/shard_map/ppermute | solution.py:338
  111.7 2.7 %shard_map.49 = f32[8,4,64,128]{3,2,1,0:T(8,128)S(1)} custom-call(f32[8,4,64,128]{3,2,1,0:T(8,128)S(1)} %bitcast.28, f32[4,64,128]{2,1,0:T(8,128)S(1)} %copy-done.3), custom_call_target="tpu_custom_call" | custom-call | flops 15728640 | bytes 2097152 | tf_op jit(solution)/shard_map/pallas_call | solution.py:355
  116.4 2.7 %collective-permute-done.16 = f32[8,128]{1,0:T(8,128)S(1)} collective-permute-done((f32[8,128]{1,0:T(8,128)S(1)}, f32[8,128]{1,0:T(8,128)S(1)}, u32[]{:S(2)}, u32[]{:S(2)}) %collective-permute-start.16) | collective-permute-done | bytes 4128 | tf_op jit(solution)/shard_map/ppermute | solution.py:423
  123.3 2.9 %collective-permute-start.19 = (f32[2,8,128]{2,1,0:T(8,128)S(1)}, f32[2,8,128]{2,1,0:T(8,128)S(1)}, u32[]{:S(2)}, u32[]{:S(2)}) collective-permute-start(f32[2,8,128]{2,1,0:T(8,128)S(1)} %fusion.3.near_ref), channel_id=1, source_target_pairs={{0,256},{32,288},{64,320},{96,352},{128,384},{160,416},{192,448},{... | collective-permute-start | bytes 24584 | tf_op jit(solution)/shard_map/ppermute | solution.py:428
  128.5 7.3 %collective-permute-done.15.right_ref = f32[8,256,128]{2,1,0:T(8,128)} collective-permute-done((f32[8,256,128]{2,1,0:T(8,128)}, f32[8,256,128]{2,1,0:T(8,128)}, u32[]{:S(2)}, u32[]{:S(2)}) %collective-permute-start.15) | collective-permute-done | bytes 1048608 | tf_op jit(solution)/shard_map/ppermute | solution.py:338
  135.8 3.4 %shard_map.51 = f32[8,256,128]{2,1,0:T(8,128)} custom-call(f32[8,256,128]{2,1,0:T(8,128)S(1)} %copy-done.2, f32[8,256,128]{2,1,0:T(8,128)S(1)} %bitcast.29, f32[8,256,128]{2,1,0:T(8,128)S(1)} %collective-permute-done.14.left_ref, f32[8,256,128]{2,1,0:T(8,128)} %collective-permute-done.15.right_ref, f32[8,8,128]{2,1,0:T(8,128)S(1)} %shard_map.50.splat), custom_call_target="tpu_custom_call" | custom-call | flops 7864320 | bytes 5242880 | tf_op jit(solution)/shard_map/pallas_call | solution.py:432
  (45 shorter events, 28.3 us)
Async XLA Ops:
  0.6 11.1 %copy-start = (f32[8,4,64,128]{3,2,1,0:T(8,128)S(1)}, f32[8,4,64,128]{3,2,1,0:T(8,128)}, u32[]{:S(2)}) copy-start(f32[8,4,64,128]{3,2,1,0:T(8,128)} %f_ref.1) | copy-start | bytes 3145732
  0.6 11.1 %copy-start.3 = (f32[4,64,128]{2,1,0:T(8,128)S(1)}, f32[4,64,128]{2,1,0:T(8,128)}, u32[]{:S(2)}) copy-start(f32[4,64,128]{2,1,0:T(8,128)} %v_ref.3) | copy-start | bytes 393220
  2.0 13.0 %collective-permute-start = (f32[2,256,128]{2,1,0:T(8,128)S(1)}, f32[2,256,128]{2,1,0:T(8,128)S(1)}, u32[]{:S(2)}, u32[]{:S(2)}) collective-permute-start(f32[2,256,128]{2,1,0:T(8,128)S(1)} %bitcast.34), channel_id=1, source_target_pairs={{0,64},{32,96},{1,65},{33,97},{2,66},{34,98},{3,67},{35,99},{4,68}... | collective-permute-start | bytes 786440 | tf_op jit(solution)/shard_map/ppermute | solution.py:366
  7.1 19.5 %collective-permute-start.1 = (f32[2,256,128]{2,1,0:T(8,128)S(1)}, f32[2,256,128]{2,1,0:T(8,128)S(1)}, u32[]{:S(2)}, u32[]{:S(2)}) collective-permute-start(f32[2,256,128]{2,1,0:T(8,128)S(1)} %bitcast.33), channel_id=1, source_target_pairs={{0,192},{32,224},{1,193},{33,225},{2,194},{34,226},{3,195},{35,227... | collective-permute-start | bytes 786440 | tf_op jit(solution)/shard_map/ppermute | solution.py:366
  9.5 17.1 %collective-permute-start.2 = (f32[2,256,128]{2,1,0:T(8,128)S(1)}, f32[2,256,128]{2,1,0:T(8,128)S(1)}, u32[]{:S(2)}, u32[]{:S(2)}) collective-permute-start(f32[2,256,128]{2,1,0:T(8,128)S(1)} %bitcast.32), channel_id=1, source_target_pairs={{0,128},{32,160},{1,129},{33,161},{2,130},{34,162},{3,131},{35,163... | collective-permute-start | bytes 786440 | tf_op jit(solution)/shard_map/ppermute | solution.py:366
  26.6 8.4 %collective-permute-start.3 = (f32[2,256,128]{2,1,0:T(8,128)S(1)}, f32[2,256,128]{2,1,0:T(8,128)}, u32[]{:S(2)}, u32[]{:S(2)}) collective-permute-start(f32[2,256,128]{2,1,0:T(8,128)S(1)} %fusion.1), channel_id=1, source_target_pairs={{0,256},{32,288},{64,320},{96,352},{128,384},{160,416},{192,448},{... | collective-permute-start | bytes 786440 | tf_op jit(solution)/shard_map/ppermute | solution.py:374
  28.6 30.8 %collective-permute-start.10 = (f32[8,256,128]{2,1,0:T(8,128)S(1)}, f32[8,256,128]{2,1,0:T(8,128)S(1)}, u32[]{:S(2)}, u32[]{:S(2)}) collective-permute-start(f32[8,256,128]{2,1,0:T(8,128)S(1)} %bitcast.19), channel_id=1, source_target_pairs={{0,1},{1,2},{2,3},{3,4},{4,5},{5,6},{6,7},{7,8},{8,9},{9,10},{10,1... | collective-permute-start | bytes 3145736 | tf_op jit(solution)/shard_map/ppermute | solution.py:337
  33.1 31.8 %collective-permute-start.11 = (f32[8,256,128]{2,1,0:T(8,128)S(1)}, f32[8,256,128]{2,1,0:T(8,128)}, u32[]{:S(2)}, u32[]{:S(2)}) collective-permute-start(f32[8,256,128]{2,1,0:T(8,128)S(1)} %bitcast.20), channel_id=1, source_target_pairs={{1,0},{2,1},{3,2},{4,3},{5,4},{6,5},{7,6},{8,7},{9,8},{10,9},{11,1... | collective-permute-start | bytes 3145736 | tf_op jit(solution)/shard_map/ppermute | solution.py:338
  35.1 7.4 %collective-permute-start.5 = (f32[2,256,128]{2,1,0:T(8,128)S(1)}, f32[2,256,128]{2,1,0:T(8,128)S(1)}, u32[]{:S(2)}, u32[]{:S(2)}) collective-permute-start(f32[2,256,128]{2,1,0:T(8,128)S(1)} %broadcast_select_fusion.refs_0_), channel_id=1, source_target_pairs={{0,224},{32,0},{64,32},{96,64},{128,96},{160,128},{192,160},{224,1... | collective-permute-start | bytes 786440 | tf_op jit(solution)/shard_map/ppermute | solution.py:332
  37.0 10.5 %collective-permute-start.4 = (f32[2,256,128]{2,1,0:T(8,128)S(1)}, f32[2,256,128]{2,1,0:T(8,128)S(1)}, u32[]{:S(2)}, u32[]{:S(2)}) collective-permute-start(f32[2,256,128]{2,1,0:T(8,128)S(1)} %broadcast_select_fusion.refs_0_), channel_id=1, source_target_pairs={{0,32},{32,64},{64,96},{96,128},{128,160},{160,192},{192,224},{224... | collective-permute-start | bytes 786440 | tf_op jit(solution)/shard_map/ppermute | solution.py:332
  42.5 9.0 %collective-permute-start.7 = (f32[2,256,128]{2,1,0:T(8,128)S(1)}, f32[2,256,128]{2,1,0:T(8,128)S(1)}, u32[]{:S(2)}, u32[]{:S(2)}) collective-permute-start(f32[2,256,128]{2,1,0:T(8,128)S(1)} %collective-permute-done.5.refs_2_), channel_id=1, source_target_pairs={{0,224},{32,0},{64,32},{96,64},{128,96},{160,128},{192,160},{224,1... | collective-permute-start | bytes 786440 | tf_op jit(solution)/shard_map/ppermute | solution.py:332
  47.6 9.0 %collective-permute-start.6 = (f32[2,256,128]{2,1,0:T(8,128)S(1)}, f32[2,256,128]{2,1,0:T(8,128)S(1)}, u32[]{:S(2)}, u32[]{:S(2)}) collective-permute-start(f32[2,256,128]{2,1,0:T(8,128)S(1)} %collective-permute-done.4.refs_1_), channel_id=1, source_target_pairs={{0,32},{32,64},{64,96},{96,128},{128,160},{160,192},{192,224},{224... | collective-permute-start | bytes 786440 | tf_op jit(solution)/shard_map/ppermute | solution.py:332
  51.5 16.1 %collective-permute-start.9 = (f32[2,256,128]{2,1,0:T(8,128)S(1)}, f32[2,256,128]{2,1,0:T(8,128)S(1)}, u32[]{:S(2)}, u32[]{:S(2)}) collective-permute-start(f32[2,256,128]{2,1,0:T(8,128)S(1)} %collective-permute-done.7.refs_4_), channel_id=1, source_target_pairs={{0,224},{32,0},{64,32},{96,64},{128,96},{160,128},{192,160},{224,1... | collective-permute-start | bytes 786440 | tf_op jit(solution)/shard_map/ppermute | solution.py:332
  56.6 13.0 %collective-permute-start.8 = (f32[2,256,128]{2,1,0:T(8,128)S(1)}, f32[2,256,128]{2,1,0:T(8,128)S(1)}, u32[]{:S(2)}, u32[]{:S(2)}) collective-permute-start(f32[2,256,128]{2,1,0:T(8,128)S(1)} %collective-permute-done.6.refs_3_), channel_id=1, source_target_pairs={{0,32},{32,64},{64,96},{96,128},{128,160},{160,192},{192,224},{224... | collective-permute-start | bytes 786440 | tf_op jit(solution)/shard_map/ppermute | solution.py:332
  67.6 8.4 %collective-permute-start.13 = (f32[1,256,128]{2,1,0:T(8,128)S(1)}, f32[1,256,128]{2,1,0:T(8,128)S(1)}, u32[]{:S(2)}, u32[]{:S(2)}) collective-permute-start(f32[1,256,128]{2,1,0:T(8,128)S(1)} %slice.36), channel_id=1, source_target_pairs={{0,224},{32,0},{64,32},{96,64},{128,96},{160,128},{192,160},{224,1... | collective-permute-start | bytes 393224 | tf_op jit(solution)/shard_map/ppermute | solution.py:332
  69.5 8.7 %collective-permute-start.12 = (f32[1,256,128]{2,1,0:T(8,128)S(1)}, f32[1,256,128]{2,1,0:T(8,128)S(1)}, u32[]{:S(2)}, u32[]{:S(2)}) collective-permute-start(f32[1,256,128]{2,1,0:T(8,128)S(1)} %slice.37), channel_id=1, source_target_pairs={{0,32},{32,64},{64,96},{96,128},{128,160},{160,192},{192,224},{224... | collective-permute-start | bytes 393224 | tf_op jit(solution)/shard_map/ppermute | solution.py:332
  106.2 22.3 %collective-permute-start.14 = (f32[8,256,128]{2,1,0:T(8,128)}, f32[8,256,128]{2,1,0:T(8,128)S(1)}, u32[]{:S(2)}, u32[]{:S(2)}) collective-permute-start(f32[8,256,128]{2,1,0:T(8,128)} %get-tuple-element.37.f_ref), channel_id=1, source_target_pairs={{0,1},{1,2},{2,3},{3,4},{4,5},{5,6},{6,7},{7,8},{8,9},{9,10},{10,1... | collective-permute-start | bytes 3145736 | tf_op jit(solution)/shard_map/ppermute | solution.py:337
  108.3 27.5 %collective-permute-start.15 = (f32[8,256,128]{2,1,0:T(8,128)}, f32[8,256,128]{2,1,0:T(8,128)}, u32[]{:S(2)}, u32[]{:S(2)}) collective-permute-start(f32[8,256,128]{2,1,0:T(8,128)} %get-tuple-element.37.f_ref), channel_id=1, source_target_pairs={{1,0},{2,1},{3,2},{4,3},{5,4},{6,5},{7,6},{8,7},{9,8},{10,9},{11,1... | collective-permute-start | bytes 3145736 | tf_op jit(solution)/shard_map/ppermute | solution.py:338
  110.5 1.2 copy-start.1
  111.7 24.0 %copy-start.2 = (f32[8,256,128]{2,1,0:T(8,128)S(1)}, f32[8,256,128]{2,1,0:T(8,128)}, u32[]{:S(2)}) copy-start(f32[8,256,128]{2,1,0:T(8,128)} %get-tuple-element.37.f_ref) | copy-start | bytes 3145732
  114.5 4.6 %collective-permute-start.16 = (f32[8,128]{1,0:T(8,128)S(1)}, f32[8,128]{1,0:T(8,128)S(1)}, u32[]{:S(2)}, u32[]{:S(2)}) collective-permute-start(f32[8,128]{1,0:T(8,128)S(1)} %shard_map.47.sums_ref.own_ref), channel_id=1, source_target_pairs={{0,32},{32,0},{1,33},{33,1},{2,34},{34,2},{3,35},{35,3},{4,36},{36... | collective-permute-start | bytes 12296 | tf_op jit(solution)/shard_map/ppermute | solution.py:423
  119.2 2.1 %collective-permute-start.17 = (f32[2,8,128]{2,1,0:T(8,128)S(1)}, f32[2,8,128]{2,1,0:T(8,128)S(1)}, u32[]{:S(2)}, u32[]{:S(2)}) collective-permute-start(f32[2,8,128]{2,1,0:T(8,128)S(1)} %maximum_select_fusion), channel_id=1, source_target_pairs={{0,128},{32,160},{1,129},{33,161},{2,130},{34,162},{3,131},{35,163... | collective-permute-start | bytes 24584 | tf_op jit(solution)/shard_map/ppermute | solution.py:426
  121.2 2.1 %collective-permute-start.18 = (f32[2,8,128]{2,1,0:T(8,128)S(1)}, f32[2,8,128]{2,1,0:T(8,128)S(1)}, u32[]{:S(2)}, u32[]{:S(2)}) collective-permute-start(f32[2,8,128]{2,1,0:T(8,128)S(1)} %fusion.2), channel_id=1, source_target_pairs={{0,64},{32,96},{128,192},{160,224},{1,65},{33,97},{129,193},{161,2... | collective-permute-start | bytes 24584 | tf_op jit(solution)/shard_map/ppermute | solution.py:427
  123.3 3.6 %collective-permute-start.19 = (f32[2,8,128]{2,1,0:T(8,128)S(1)}, f32[2,8,128]{2,1,0:T(8,128)S(1)}, u32[]{:S(2)}, u32[]{:S(2)}) collective-permute-start(f32[2,8,128]{2,1,0:T(8,128)S(1)} %fusion.3.near_ref), channel_id=1, source_target_pairs={{0,256},{32,288},{64,320},{96,352},{128,384},{160,416},{192,448},{... | collective-permute-start | bytes 24584 | tf_op jit(solution)/shard_map/ppermute | solution.py:428

commit v8 on v7

--- a/solution.py
+++ b/solution.py
@@ -393,12 +393,12 @@
     pieces += [up, down]
     up, down = ring_shift(up, 1), ring_shift(down, -1)
     sums = stage(range(6, 10), (), pieces, sums)
+    down, sums, left, right = lax.optimization_barrier((down, sums, left, right))
+    pieces += [up, down]
+    up, down = ring_shift(up[:1], 1), ring_shift(down[1:], -1)
     image, image_sums = call(
         image_kernel, (slab, tile), specs=[VMEM] * 4, flops=50 * big, bytes_moved=20 * big
     )(own, inner.reshape(flat), left, right)
-    down, sums, image, image_sums = lax.optimization_barrier((down, sums, image, image_sums))
-    pieces += [up, down]
-    up, down = ring_shift(up[:1], 1), ring_shift(down[1:], -1)
     sums = stage(range(10, 14), range(14), pieces, sums, image_sums)
     pieces += [up, down]
     sums = stage(range(14, 16), range(14, 16), pieces, sums, last=True)

time: 141 us -> 139 us (0.986)
  no operation moved by 1% of the time
where the time goes in v8:
time: 139 us; the launch traced here: 138 us
  starting transfers between devices  52.7 us (38%)
  waiting for transfers between devices  35.2 us (25%)
  Pallas kernels  25.2 us (18%)
  blocking collectives  21.2 us (15%)
  other arithmetic  1.49 us (1%)
    ppermute x8, starting transfers between devices, ring_shift(): return lax.ppermute(block, 'band', pairs)  23 us
    all_to_all x1, blocking collectives, domain_parts(): return lax.all_to_all(copies, 'domain', 0, 0)  21.2 us
    ppermute x2, waiting for transfers between devices, neighbours(): lax.ppermute(block, 'domain', [((i + 1) % count, i) for i in range(count)])  12.8 us
    ppermute x3, waiting for transfers between devices, local(): lax.ppermute(quarters[k], 'band', [(0, 2 * k), (1, 2 * k + 1)])  11.5 us
    ppermute x3, starting transfers between devices, local(): lax.ppermute(quarters[k], 'band', [(0, 2 * k), (1, 2 * k + 1)])  9.65 us
    ppermute x2, starting transfers between devices, neighbours(): lax.ppermute(block, 'domain', [(i, (i + 1) % count) for i in range(count)])  6.58 us
    pallas_call x4, Pallas kernels, stage(): call(lambda *refs: stage_kernel(len(pieces), fresh, imaged, last, *refs),...  6.17 us
    pallas_call x2, Pallas kernels, inner_part(): call(inner_kernel, (field, *sums), specs=[VMEM] * 2, flops=60 * big, byte...  6.04 us
  transfers between devices with their start and end apart: 20, of which 12 were waited for; matrix products, arithmetic and copies ran while one was open for 0% of the time, Pallas kernels for 11%

profile of v8, /device:TPU:1, one launch (start us, length us, event | category | flops | bytes accessed | tf_op | source)
XLA Modules:
  0.0 137.9 jit_solution(9716316245754249912)
XLA Ops:
  2.0 5.1 %collective-permute-start = (f32[2,256,128]{2,1,0:T(8,128)S(1)}, f32[2,256,128]{2,1,0:T(8,128)S(1)}, u32[]{:S(2)}, u32[]{:S(2)}) collective-permute-start(f32[2,256,128]{2,1,0:T(8,128)S(1)} %bitcast.34), channel_id=1, source_target_pairs={{0,64},{32,96},{1,65},{33,97},{2,66},{34,98},{3,67},{35,99},{4,68}... | collective-permute-start | bytes 786440 | tf_op jit(solution)/shard_map/ppermute | solution.py:366
  7.1 2.3 %collective-permute-start.1 = (f32[2,256,128]{2,1,0:T(8,128)S(1)}, f32[2,256,128]{2,1,0:T(8,128)S(1)}, u32[]{:S(2)}, u32[]{:S(2)}) collective-permute-start(f32[2,256,128]{2,1,0:T(8,128)S(1)} %bitcast.33), channel_id=1, source_target_pairs={{0,192},{32,224},{1,193},{33,225},{2,194},{34,226},{3,195},{35,227... | collective-permute-start | bytes 786440 | tf_op jit(solution)/shard_map/ppermute | solution.py:366
  9.5 2.2 %collective-permute-start.2 = (f32[2,256,128]{2,1,0:T(8,128)S(1)}, f32[2,256,128]{2,1,0:T(8,128)S(1)}, u32[]{:S(2)}, u32[]{:S(2)}) collective-permute-start(f32[2,256,128]{2,1,0:T(8,128)S(1)} %bitcast.32), channel_id=1, source_target_pairs={{0,128},{32,160},{1,129},{33,161},{2,130},{34,162},{3,131},{35,163... | collective-permute-start | bytes 786440 | tf_op jit(solution)/shard_map/ppermute | solution.py:366
  11.7 3.3 %shard_map.41 = (f32[8,4,64,128]{3,2,1,0:T(8,128)S(1)}, f32[8,128]{1,0:T(8,128)S(1)}) custom-call(f32[8,4,64,128]{3,2,1,0:T(8,128)S(1)} %copy-done, f32[4,64,128]{2,1,0:T(8,128)S(1)} %copy-done.3), custom_call_target="tpu_custom_call" | custom-call | flops 15728640 | bytes 2097152 | tf_op jit(solution)/shard_map/pallas_call | solution.py:355
  15.0 11.5 %collective-permute-done.1 = f32[2,256,128]{2,1,0:T(8,128)S(1)} collective-permute-done((f32[2,256,128]{2,1,0:T(8,128)S(1)}, f32[2,256,128]{2,1,0:T(8,128)S(1)}, u32[]{:S(2)}, u32[]{:S(2)}) %collective-permute-start.1) | collective-permute-done | bytes 262176 | tf_op jit(solution)/shard_map/ppermute | solution.py:366
  26.6 2.0 %collective-permute-start.3 = (f32[2,256,128]{2,1,0:T(8,128)S(1)}, f32[2,256,128]{2,1,0:T(8,128)}, u32[]{:S(2)}, u32[]{:S(2)}) collective-permute-start(f32[2,256,128]{2,1,0:T(8,128)S(1)} %fusion.1), channel_id=1, source_target_pairs={{0,256},{32,288},{64,320},{96,352},{128,384},{160,416},{192,448},{... | collective-permute-start | bytes 786440 | tf_op jit(solution)/shard_map/ppermute | solution.py:374
  28.6 4.5 %collective-permute-start.10 = (f32[8,256,128]{2,1,0:T(8,128)S(1)}, f32[8,256,128]{2,1,0:T(8,128)S(1)}, u32[]{:S(2)}, u32[]{:S(2)}) collective-permute-start(f32[8,256,128]{2,1,0:T(8,128)S(1)} %bitcast.19), channel_id=1, source_target_pairs={{0,1},{1,2},{2,3},{3,4},{4,5},{5,6},{6,7},{7,8},{8,9},{9,10},{10,1... | collective-permute-start | bytes 3145736 | tf_op jit(solution)/shard_map/ppermute | solution.py:337
  37.0 3.4 %collective-permute-start.4 = (f32[2,256,128]{2,1,0:T(8,128)S(1)}, f32[2,256,128]{2,1,0:T(8,128)S(1)}, u32[]{:S(2)}, u32[]{:S(2)}) collective-permute-start(f32[2,256,128]{2,1,0:T(8,128)S(1)} %broadcast_select_fusion.refs_0_), channel_id=1, source_target_pairs={{0,32},{32,64},{64,96},{96,128},{128,160},{160,192},{192,224},{224... | collective-permute-start | bytes 786440 | tf_op jit(solution)/shard_map/ppermute | solution.py:332
  40.4 2.1 %collective-permute-done.5.refs_2_ = f32[2,256,128]{2,1,0:T(8,128)S(1)} collective-permute-done((f32[2,256,128]{2,1,0:T(8,128)S(1)}, f32[2,256,128]{2,1,0:T(8,128)S(1)}, u32[]{:S(2)}, u32[]{:S(2)}) %collective-permute-start.5) | collective-permute-done | bytes 262176 | tf_op jit(solution)/shard_map/ppermute | solution.py:332
  42.5 4.3 %collective-permute-start.7 = (f32[2,256,128]{2,1,0:T(8,128)S(1)}, f32[2,256,128]{2,1,0:T(8,128)S(1)}, u32[]{:S(2)}, u32[]{:S(2)}) collective-permute-start(f32[2,256,128]{2,1,0:T(8,128)S(1)} %collective-permute-done.5.refs_2_), channel_id=1, source_target_pairs={{0,224},{32,0},{64,32},{96,64},{128,96},{160,128},{192,160},{224,1... | collective-permute-start | bytes 786440 | tf_op jit(solution)/shard_map/ppermute | solution.py:332
  51.5 4.3 %collective-permute-start.9 = (f32[2,256,128]{2,1,0:T(8,128)S(1)}, f32[2,256,128]{2,1,0:T(8,128)S(1)}, u32[]{:S(2)}, u32[]{:S(2)}) collective-permute-start(f32[2,256,128]{2,1,0:T(8,128)S(1)} %collective-permute-done.7.refs_4_), channel_id=1, source_target_pairs={{0,224},{32,0},{64,32},{96,64},{128,96},{160,128},{192,160},{224,1... | collective-permute-start | bytes 786440 | tf_op jit(solution)/shard_map/ppermute | solution.py:332
  59.5 5.5 %collective-permute-done.11.right = f32[8,256,128]{2,1,0:T(8,128)} collective-permute-done((f32[8,256,128]{2,1,0:T(8,128)S(1)}, f32[8,256,128]{2,1,0:T(8,128)}, u32[]{:S(2)}, u32[]{:S(2)}) %collective-permute-start.11) | collective-permute-done | bytes 1048608 | tf_op jit(solution)/shard_map/ppermute | solution.py:338
  66.9 3.4 %collective-permute-start.12 = (f32[1,256,128]{2,1,0:T(8,128)S(1)}, f32[1,256,128]{2,1,0:T(8,128)S(1)}, u32[]{:S(2)}, u32[]{:S(2)}) collective-permute-start(f32[1,256,128]{2,1,0:T(8,128)S(1)} %slice.37), channel_id=1, source_target_pairs={{0,32},{32,64},{64,96},{96,128},{128,160},{160,192},{192,224},{224... | collective-permute-start | bytes 393224 | tf_op jit(solution)/shard_map/ppermute | solution.py:332
  70.3 2.6 %shard_map.44 = (f32[8,256,128]{2,1,0:T(8,128)S(1)}, f32[8,128]{1,0:T(8,128)S(1)}) custom-call(f32[8,256,128]{2,1,0:T(8,128)S(1)} %bitcast.23, f32[8,256,128]{2,1,0:T(8,128)S(1)} %bitcast.30, f32[8,256,128]{2,1,0:T(8,128)S(1)} %collective-permute-done.10.left, f32[8,256,128]{2,1,0:T(8,128)} %collective-permute-done.11.right), custom_call_target="tpu_custom_call" | custom-call | flops 13107200 | bytes 5242880 | tf_op jit(solution)/shard_map/pallas_call | solution.py:399
  72.9 3.1 %shard_map.45.refs_11_ = f32[8,128]{1,0:T(8,128)S(1)} custom-call(f32[2,256,128]{2,1,0:T(8,128)S(1)} %broadcast_select_fusion.refs_0_, f32[2,256,128]{2,1,0:T(8,128)S(1)} %collective-permute-done.4.refs_1_, f32[2,256,128]{2,1,0:T(8,128)S(1)} %collective-permute-done.5.refs_2_, f32[2,256,128]{2,1,0:T(8,128)S(1)} %collective-permute-done.6.refs_3_, ...), custom_call_target="tpu_custom_call" | custom-call | flops 5242880 | bytes 2621440 | tf_op jit(solution)/shard_map/pallas_call | solution.py:379
  78.3 21.2 %all_to_all.5.refs_0_ = f32[32,8,128]{2,1,0:T(8,128)S(1)} all-to-all(f32[32,8,128]{2,1,0:T(8,128)S(1)} %shard_map.46), channel_id=1, replica_groups=mesh['band'=16,'domain'=32] {'domain'}, dimensions={0} | all-to-all | bytes 262144 | tf_op jit(solution)/shard_map/all_to_all | solution.py:327
  99.5 5.4 %shard_map.48 = (f32[8,256,128]{2,1,0:T(8,128)}, f32[8,128]{1,0:T(8,128)S(1)}, f32[8,128]{1,0:T(8,128)S(1)}) custom-call(s32[1]{0:T(128)} %bitcast.band_ref, f32[8,128]{1,0:T(8,128)S(1)} %shard_map.47.sums_ref.own_ref, f32[2,256,128]{2,1,0:T(8,128)S(1)} %broadcast_select_fusion.refs_0_, f32[2,256,128]{2,1,0:T(8,128)S(1)} %collective-permute-done.4.refs_1_, ...), custom_call_target="tpu_custom_call" | custom-call | flops 12582912 | bytes 4194304 | tf_op jit(solution)/shard_map/pallas_call | solution.py:412
  104.9 2.1 %collective-permute-start.14 = (f32[8,256,128]{2,1,0:T(8,128)}, f32[8,256,128]{2,1,0:T(8,128)S(1)}, u32[]{:S(2)}, u32[]{:S(2)}) collective-permute-start(f32[8,256,128]{2,1,0:T(8,128)} %get-tuple-element.37.f_ref), channel_id=1, source_target_pairs={{0,1},{1,2},{2,3},{3,4},{4,5},{5,6},{6,7},{7,8},{8,9},{9,10},{10,1... | collective-permute-start | bytes 3145736 | tf_op jit(solution)/shard_map/ppermute | solution.py:337
  107.0 2.2 %collective-permute-start.15 = (f32[8,256,128]{2,1,0:T(8,128)}, f32[8,256,128]{2,1,0:T(8,128)}, u32[]{:S(2)}, u32[]{:S(2)}) collective-permute-start(f32[8,256,128]{2,1,0:T(8,128)} %get-tuple-element.37.f_ref), channel_id=1, source_target_pairs={{1,0},{2,1},{3,2},{4,3},{5,4},{6,5},{7,6},{8,7},{9,8},{10,9},{11,1... | collective-permute-start | bytes 3145736 | tf_op jit(solution)/shard_map/ppermute | solution.py:338
  110.5 2.7 %shard_map.49 = f32[8,4,64,128]{3,2,1,0:T(8,128)S(1)} custom-call(f32[8,4,64,128]{3,2,1,0:T(8,128)S(1)} %bitcast.28, f32[4,64,128]{2,1,0:T(8,128)S(1)} %copy-done.3), custom_call_target="tpu_custom_call" | custom-call | flops 15728640 | bytes 2097152 | tf_op jit(solution)/shard_map/pallas_call | solution.py:355
  115.2 2.7 %collective-permute-done.16 = f32[8,128]{1,0:T(8,128)S(1)} collective-permute-done((f32[8,128]{1,0:T(8,128)S(1)}, f32[8,128]{1,0:T(8,128)S(1)}, u32[]{:S(2)}, u32[]{:S(2)}) %collective-permute-start.16) | collective-permute-done | bytes 4128 | tf_op jit(solution)/shard_map/ppermute | solution.py:423
  122.1 2.9 %collective-permute-start.19 = (f32[2,8,128]{2,1,0:T(8,128)S(1)}, f32[2,8,128]{2,1,0:T(8,128)S(1)}, u32[]{:S(2)}, u32[]{:S(2)}) collective-permute-start(f32[2,8,128]{2,1,0:T(8,128)S(1)} %fusion.3.near_ref), channel_id=1, source_target_pairs={{0,256},{32,288},{64,320},{96,352},{128,384},{160,416},{192,448},{... | collective-permute-start | bytes 24584 | tf_op jit(solution)/shard_map/ppermute | solution.py:428
  127.3 7.3 %collective-permute-done.15.right_ref = f32[8,256,128]{2,1,0:T(8,128)} collective-permute-done((f32[8,256,128]{2,1,0:T(8,128)}, f32[8,256,128]{2,1,0:T(8,128)}, u32[]{:S(2)}, u32[]{:S(2)}) %collective-permute-start.15) | collective-permute-done | bytes 1048608 | tf_op jit(solution)/shard_map/ppermute | solution.py:338
  134.5 3.4 %shard_map.51 = f32[8,256,128]{2,1,0:T(8,128)} custom-call(f32[8,256,128]{2,1,0:T(8,128)S(1)} %copy-done.2, f32[8,256,128]{2,1,0:T(8,128)S(1)} %bitcast.29, f32[8,256,128]{2,1,0:T(8,128)S(1)} %collective-permute-done.14.left_ref, f32[8,256,128]{2,1,0:T(8,128)} %collective-permute-done.15.right_ref, f32[8,8,128]{2,1,0:T(8,128)S(1)} %shard_map.50.splat), custom_call_target="tpu_custom_call" | custom-call | flops 7864320 | bytes 5242880 | tf_op jit(solution)/shard_map/pallas_call | solution.py:432
  (45 shorter events, 27.6 us)
Async XLA Ops:
  0.6 11.1 %copy-start = (f32[8,4,64,128]{3,2,1,0:T(8,128)S(1)}, f32[8,4,64,128]{3,2,1,0:T(8,128)}, u32[]{:S(2)}) copy-start(f32[8,4,64,128]{3,2,1,0:T(8,128)} %f_ref.1) | copy-start | bytes 3145732
  0.6 11.1 %copy-start.3 = (f32[4,64,128]{2,1,0:T(8,128)S(1)}, f32[4,64,128]{2,1,0:T(8,128)}, u32[]{:S(2)}) copy-start(f32[4,64,128]{2,1,0:T(8,128)} %v_ref.3) | copy-start | bytes 393220
  2.0 13.0 %collective-permute-start = (f32[2,256,128]{2,1,0:T(8,128)S(1)}, f32[2,256,128]{2,1,0:T(8,128)S(1)}, u32[]{:S(2)}, u32[]{:S(2)}) collective-permute-start(f32[2,256,128]{2,1,0:T(8,128)S(1)} %bitcast.34), channel_id=1, source_target_pairs={{0,64},{32,96},{1,65},{33,97},{2,66},{34,98},{3,67},{35,99},{4,68}... | collective-permute-start | bytes 786440 | tf_op jit(solution)/shard_map/ppermute | solution.py:366
  7.1 19.5 %collective-permute-start.1 = (f32[2,256,128]{2,1,0:T(8,128)S(1)}, f32[2,256,128]{2,1,0:T(8,128)S(1)}, u32[]{:S(2)}, u32[]{:S(2)}) collective-permute-start(f32[2,256,128]{2,1,0:T(8,128)S(1)} %bitcast.33), channel_id=1, source_target_pairs={{0,192},{32,224},{1,193},{33,225},{2,194},{34,226},{3,195},{35,227... | collective-permute-start | bytes 786440 | tf_op jit(solution)/shard_map/ppermute | solution.py:366
  9.5 17.1 %collective-permute-start.2 = (f32[2,256,128]{2,1,0:T(8,128)S(1)}, f32[2,256,128]{2,1,0:T(8,128)S(1)}, u32[]{:S(2)}, u32[]{:S(2)}) collective-permute-start(f32[2,256,128]{2,1,0:T(8,128)S(1)} %bitcast.32), channel_id=1, source_target_pairs={{0,128},{32,160},{1,129},{33,161},{2,130},{34,162},{3,131},{35,163... | collective-permute-start | bytes 786440 | tf_op jit(solution)/shard_map/ppermute | solution.py:366
  26.6 8.4 %collective-permute-start.3 = (f32[2,256,128]{2,1,0:T(8,128)S(1)}, f32[2,256,128]{2,1,0:T(8,128)}, u32[]{:S(2)}, u32[]{:S(2)}) collective-permute-start(f32[2,256,128]{2,1,0:T(8,128)S(1)} %fusion.1), channel_id=1, source_target_pairs={{0,256},{32,288},{64,320},{96,352},{128,384},{160,416},{192,448},{... | collective-permute-start | bytes 786440 | tf_op jit(solution)/shard_map/ppermute | solution.py:374
  28.6 30.8 %collective-permute-start.10 = (f32[8,256,128]{2,1,0:T(8,128)S(1)}, f32[8,256,128]{2,1,0:T(8,128)S(1)}, u32[]{:S(2)}, u32[]{:S(2)}) collective-permute-start(f32[8,256,128]{2,1,0:T(8,128)S(1)} %bitcast.19), channel_id=1, source_target_pairs={{0,1},{1,2},{2,3},{3,4},{4,5},{5,6},{6,7},{7,8},{8,9},{9,10},{10,1... | collective-permute-start | bytes 3145736 | tf_op jit(solution)/shard_map/ppermute | solution.py:337
  33.1 31.8 %collective-permute-start.11 = (f32[8,256,128]{2,1,0:T(8,128)S(1)}, f32[8,256,128]{2,1,0:T(8,128)}, u32[]{:S(2)}, u32[]{:S(2)}) collective-permute-start(f32[8,256,128]{2,1,0:T(8,128)S(1)} %bitcast.20), channel_id=1, source_target_pairs={{1,0},{2,1},{3,2},{4,3},{5,4},{6,5},{7,6},{8,7},{9,8},{10,9},{11,1... | collective-permute-start | bytes 3145736 | tf_op jit(solution)/shard_map/ppermute | solution.py:338
  35.1 7.4 %collective-permute-start.5 = (f32[2,256,128]{2,1,0:T(8,128)S(1)}, f32[2,256,128]{2,1,0:T(8,128)S(1)}, u32[]{:S(2)}, u32[]{:S(2)}) collective-permute-start(f32[2,256,128]{2,1,0:T(8,128)S(1)} %broadcast_select_fusion.refs_0_), channel_id=1, source_target_pairs={{0,224},{32,0},{64,32},{96,64},{128,96},{160,128},{192,160},{224,1... | collective-permute-start | bytes 786440 | tf_op jit(solution)/shard_map/ppermute | solution.py:332
  37.0 10.5 %collective-permute-start.4 = (f32[2,256,128]{2,1,0:T(8,128)S(1)}, f32[2,256,128]{2,1,0:T(8,128)S(1)}, u32[]{:S(2)}, u32[]{:S(2)}) collective-permute-start(f32[2,256,128]{2,1,0:T(8,128)S(1)} %broadcast_select_fusion.refs_0_), channel_id=1, source_target_pairs={{0,32},{32,64},{64,96},{96,128},{128,160},{160,192},{192,224},{224... | collective-permute-start | bytes 786440 | tf_op jit(solution)/shard_map/ppermute | solution.py:332
  42.5 9.0 %collective-permute-start.7 = (f32[2,256,128]{2,1,0:T(8,128)S(1)}, f32[2,256,128]{2,1,0:T(8,128)S(1)}, u32[]{:S(2)}, u32[]{:S(2)}) collective-permute-start(f32[2,256,128]{2,1,0:T(8,128)S(1)} %collective-permute-done.5.refs_2_), channel_id=1, source_target_pairs={{0,224},{32,0},{64,32},{96,64},{128,96},{160,128},{192,160},{224,1... | collective-permute-start | bytes 786440 | tf_op jit(solution)/shard_map/ppermute | solution.py:332
  47.6 9.0 %collective-permute-start.6 = (f32[2,256,128]{2,1,0:T(8,128)S(1)}, f32[2,256,128]{2,1,0:T(8,128)S(1)}, u32[]{:S(2)}, u32[]{:S(2)}) collective-permute-start(f32[2,256,128]{2,1,0:T(8,128)S(1)} %collective-permute-done.4.refs_1_), channel_id=1, source_target_pairs={{0,32},{32,64},{64,96},{96,128},{128,160},{160,192},{192,224},{224... | collective-permute-start | bytes 786440 | tf_op jit(solution)/shard_map/ppermute | solution.py:332
  51.5 13.4 %collective-permute-start.9 = (f32[2,256,128]{2,1,0:T(8,128)S(1)}, f32[2,256,128]{2,1,0:T(8,128)S(1)}, u32[]{:S(2)}, u32[]{:S(2)}) collective-permute-start(f32[2,256,128]{2,1,0:T(8,128)S(1)} %collective-permute-done.7.refs_4_), channel_id=1, source_target_pairs={{0,224},{32,0},{64,32},{96,64},{128,96},{160,128},{192,160},{224,1... | collective-permute-start | bytes 786440 | tf_op jit(solution)/shard_map/ppermute | solution.py:332
  56.6 10.3 %collective-permute-start.8 = (f32[2,256,128]{2,1,0:T(8,128)S(1)}, f32[2,256,128]{2,1,0:T(8,128)S(1)}, u32[]{:S(2)}, u32[]{:S(2)}) collective-permute-start(f32[2,256,128]{2,1,0:T(8,128)S(1)} %collective-permute-done.6.refs_3_), channel_id=1, source_target_pairs={{0,32},{32,64},{64,96},{96,128},{128,160},{160,192},{192,224},{224... | collective-permute-start | bytes 786440 | tf_op jit(solution)/shard_map/ppermute | solution.py:332
  65.0 11.0 %collective-permute-start.13 = (f32[1,256,128]{2,1,0:T(8,128)S(1)}, f32[1,256,128]{2,1,0:T(8,128)S(1)}, u32[]{:S(2)}, u32[]{:S(2)}) collective-permute-start(f32[1,256,128]{2,1,0:T(8,128)S(1)} %slice.36), channel_id=1, source_target_pairs={{0,224},{32,0},{64,32},{96,64},{128,96},{160,128},{192,160},{224,1... | collective-permute-start | bytes 393224 | tf_op jit(solution)/shard_map/ppermute | solution.py:332
  66.9 10.3 %collective-permute-start.12 = (f32[1,256,128]{2,1,0:T(8,128)S(1)}, f32[1,256,128]{2,1,0:T(8,128)S(1)}, u32[]{:S(2)}, u32[]{:S(2)}) collective-permute-start(f32[1,256,128]{2,1,0:T(8,128)S(1)} %slice.37), channel_id=1, source_target_pairs={{0,32},{32,64},{64,96},{96,128},{128,160},{160,192},{192,224},{224... | collective-permute-start | bytes 393224 | tf_op jit(solution)/shard_map/ppermute | solution.py:332
  104.9 22.3 %collective-permute-start.14 = (f32[8,256,128]{2,1,0:T(8,128)}, f32[8,256,128]{2,1,0:T(8,128)S(1)}, u32[]{:S(2)}, u32[]{:S(2)}) collective-permute-start(f32[8,256,128]{2,1,0:T(8,128)} %get-tuple-element.37.f_ref), channel_id=1, source_target_pairs={{0,1},{1,2},{2,3},{3,4},{4,5},{5,6},{6,7},{7,8},{8,9},{9,10},{10,1... | collective-permute-start | bytes 3145736 | tf_op jit(solution)/shard_map/ppermute | solution.py:337
  107.0 27.5 %collective-permute-start.15 = (f32[8,256,128]{2,1,0:T(8,128)}, f32[8,256,128]{2,1,0:T(8,128)}, u32[]{:S(2)}, u32[]{:S(2)}) collective-permute-start(f32[8,256,128]{2,1,0:T(8,128)} %get-tuple-element.37.f_ref), channel_id=1, source_target_pairs={{1,0},{2,1},{3,2},{4,3},{5,4},{6,5},{7,6},{8,7},{9,8},{10,9},{11,1... | collective-permute-start | bytes 3145736 | tf_op jit(solution)/shard_map/ppermute | solution.py:338
  109.3 1.2 copy-start.1
  110.5 24.0 %copy-start.2 = (f32[8,256,128]{2,1,0:T(8,128)S(1)}, f32[8,256,128]{2,1,0:T(8,128)}, u32[]{:S(2)}) copy-start(f32[8,256,128]{2,1,0:T(8,128)} %get-tuple-element.37.f_ref) | copy-start | bytes 3145732
  113.3 4.6 %collective-permute-start.16 = (f32[8,128]{1,0:T(8,128)S(1)}, f32[8,128]{1,0:T(8,128)S(1)}, u32[]{:S(2)}, u32[]{:S(2)}) collective-permute-start(f32[8,128]{1,0:T(8,128)S(1)} %shard_map.47.sums_ref.own_ref), channel_id=1, source_target_pairs={{0,32},{32,0},{1,33},{33,1},{2,34},{34,2},{3,35},{35,3},{4,36},{36... | collective-permute-start | bytes 12296 | tf_op jit(solution)/shard_map/ppermute | solution.py:423
  117.9 2.1 %collective-permute-start.17 = (f32[2,8,128]{2,1,0:T(8,128)S(1)}, f32[2,8,128]{2,1,0:T(8,128)S(1)}, u32[]{:S(2)}, u32[]{:S(2)}) collective-permute-start(f32[2,8,128]{2,1,0:T(8,128)S(1)} %maximum_select_fusion), channel_id=1, source_target_pairs={{0,128},{32,160},{1,129},{33,161},{2,130},{34,162},{3,131},{35,163... | collective-permute-start | bytes 24584 | tf_op jit(solution)/shard_map/ppermute | solution.py:426
  120.0 2.1 %collective-permute-start.18 = (f32[2,8,128]{2,1,0:T(8,128)S(1)}, f32[2,8,128]{2,1,0:T(8,128)S(1)}, u32[]{:S(2)}, u32[]{:S(2)}) collective-permute-start(f32[2,8,128]{2,1,0:T(8,128)S(1)} %fusion.2), channel_id=1, source_target_pairs={{0,64},{32,96},{128,192},{160,224},{1,65},{33,97},{129,193},{161,2... | collective-permute-start | bytes 24584 | tf_op jit(solution)/shard_map/ppermute | solution.py:427
  122.1 3.6 %collective-permute-start.19 = (f32[2,8,128]{2,1,0:T(8,128)S(1)}, f32[2,8,128]{2,1,0:T(8,128)S(1)}, u32[]{:S(2)}, u32[]{:S(2)}) collective-permute-start(f32[2,8,128]{2,1,0:T(8,128)S(1)} %fusion.3.near_ref), channel_id=1, source_target_pairs={{0,256},{32,288},{64,320},{96,352},{128,384},{160,416},{192,448},{... | collective-permute-start | bytes 24584 | tf_op jit(solution)/shard_map/ppermute | solution.py:428

commit v9 on v8

--- a/solution.py
+++ b/solution.py
@@ -363,7 +363,8 @@
     own = orbitals.reshape(flat)
     quarters = [own[2 * k : 2 * k + 2] for k in range(4)]
     arrived = [
-        lax.ppermute(quarters[k], "band", [(0, 2 * k), (1, 2 * k + 1)]) for k in (1, 3, 2)
+        lax.ppermute(quarters[k], "band", [(0, place), (1, place + 1)])
+        for k, place in ((2, RING + 4), (1, 2), (3, 6))
     ]
     inner, sums = inner_part(orbitals, tile)
     arrived, inner, sums = lax.optimization_barrier((arrived, inner, sums))
@@ -371,8 +372,11 @@
     for part in arrived:
         piece = piece + part
     left, right = neighbours(own)
-    crossed = lax.ppermute(piece, "band", [(y, y + RING) for y in range(RING)])
-    piece = jnp.where(band < RING, piece, crossed)
+    far_first = (4, 5)
+    pairs = [(y + RING, y) if y in far_first else (y, y + RING) for y in range(RING)]
+    crossed = lax.ppermute(piece, "band", pairs)
+    at_first = (band < RING) != (((band & 7) == 4) | ((band & 7) == 5))
+    piece = jnp.where(at_first, piece, crossed)
 
     def stage(fresh, imaged, pieces, *sums, last=False):
         sources = (*pieces, own, *((image,) if imaged else ()), *sums)

time: 139 us -> 152 us (1.094); the launches traced: 138 us -> 149 us
  starting transfers between devices: 52.7 us -> 62.3 us
  blocking collectives: 21.2 us -> 24.8 us
  waiting for transfers between devices: 35.2 us -> 33.1 us
    ppermute x4, starting transfers between devices: 11.7 us -> 21.4 us  [the longest x3 19.4 us: local(): lax.ppermute(quarters[k], 'band', [(0, place), (1, place + 1)])]
    all_to_all x1, blocking collectives: 21.2 us -> 24.8 us  [domain_parts(): return lax.all_to_all(copies, 'domain', 0, 0)]
    ppermute x8, waiting for transfers between devices: 5.83 us -> 3.64 us  [ring_shift(): return lax.ppermute(block, 'band', pairs)]
  transfers between devices with their start and end apart: 20 -> 20, of which waited for: 12 -> 11; matrix products, arithmetic and copies ran while one was open for 0% -> 0% of each run, Pallas kernels for 11% -> 10%
where the time goes in v9:
time: 152 us; the launch traced here: 149 us
  starting transfers between devices  62.3 us (41%)
  waiting for transfers between devices  33.1 us (22%)
  Pallas kernels  25.2 us (17%)
  blocking collectives  24.8 us (16%)
    all_to_all x1, blocking collectives, domain_parts(): return lax.all_to_all(copies, 'domain', 0, 0)  24.8 us
    ppermute x8, starting transfers between devices, ring_shift(): return lax.ppermute(block, 'band', pairs)  23.5 us
    ppermute x3, starting transfers between devices, local(): lax.ppermute(quarters[k], 'band', [(0, place), (1, place + 1)])  19.4 us
    ppermute x2, waiting for transfers between devices, neighbours(): lax.ppermute(block, 'domain', [((i + 1) % count, i) for i in range(count)])  13 us
    ppermute x3, waiting for transfers between devices, local(): lax.ppermute(quarters[k], 'band', [(0, place), (1, place + 1)])  11.4 us
    pallas_call x4, Pallas kernels, stage(): call(lambda *refs: stage_kernel(len(pieces), fresh, imaged, last, *refs),...  6.18 us
    pallas_call x2, Pallas kernels, inner_part(): call(inner_kernel, (field, *sums), specs=[VMEM] * 2, flops=60 * big, byte...  6.04 us
    ppermute x2, starting transfers between devices, neighbours(): lax.ppermute(block, 'domain', [(i, (i + 1) % count) for i in range(count)])  5.97 us
  transfers between devices with their start and end apart: 20, of which 11 were waited for; matrix products, arithmetic and copies ran while one was open for 0% of the time, Pallas kernels for 10%

profile of v9, /device:TPU:1, one launch (start us, length us, event | category | flops | bytes accessed | tf_op | source)
XLA Modules:
  0.0 149.1 jit_solution(2641169810371739402)
XLA Ops:
  2.0 16.7 %collective-permute-start = (f32[2,256,128]{2,1,0:T(8,128)S(1)}, f32[2,256,128]{2,1,0:T(8,128)S(1)}, u32[]{:S(2)}, u32[]{:S(2)}) collective-permute-start(f32[2,256,128]{2,1,0:T(8,128)S(1)} %bitcast.34), channel_id=1, source_target_pairs={{0,384},{32,416},{1,385},{33,417},{2,386},{34,418},{3,387},{35,419... | collective-permute-start | bytes 786440 | tf_op jit(solution)/shard_map/ppermute | solution.py:366
  21.4 3.3 %shard_map.41 = (f32[8,4,64,128]{3,2,1,0:T(8,128)S(1)}, f32[8,128]{1,0:T(8,128)S(1)}) custom-call(f32[8,4,64,128]{3,2,1,0:T(8,128)S(1)} %copy-done, f32[4,64,128]{2,1,0:T(8,128)S(1)} %copy-done.3), custom_call_target="tpu_custom_call" | custom-call | flops 15728640 | bytes 2097152 | tf_op jit(solution)/shard_map/pallas_call | solution.py:355
  24.7 4.7 %collective-permute-done.1 = f32[2,256,128]{2,1,0:T(8,128)S(1)} collective-permute-done((f32[2,256,128]{2,1,0:T(8,128)S(1)}, f32[2,256,128]{2,1,0:T(8,128)S(1)}, u32[]{:S(2)}, u32[]{:S(2)}) %collective-permute-start.1) | collective-permute-done | bytes 262176 | tf_op jit(solution)/shard_map/ppermute | solution.py:366
  29.4 6.7 %collective-permute-done.2 = f32[2,256,128]{2,1,0:T(8,128)S(1)} collective-permute-done((f32[2,256,128]{2,1,0:T(8,128)S(1)}, f32[2,256,128]{2,1,0:T(8,128)S(1)}, u32[]{:S(2)}, u32[]{:S(2)}) %collective-permute-start.2) | collective-permute-done | bytes 262176 | tf_op jit(solution)/shard_map/ppermute | solution.py:366
  36.2 2.0 %collective-permute-start.3 = (f32[2,256,128]{2,1,0:T(8,128)S(1)}, f32[2,256,128]{2,1,0:T(8,128)}, u32[]{:S(2)}, u32[]{:S(2)}) collective-permute-start(f32[2,256,128]{2,1,0:T(8,128)S(1)} %fusion.1), channel_id=1, source_target_pairs={{0,256},{32,288},{64,320},{96,352},{384,128},{416,160},{192,448},{... | collective-permute-start | bytes 786440 | tf_op jit(solution)/shard_map/ppermute | solution.py:377
  38.2 3.9 %collective-permute-start.10 = (f32[8,256,128]{2,1,0:T(8,128)S(1)}, f32[8,256,128]{2,1,0:T(8,128)S(1)}, u32[]{:S(2)}, u32[]{:S(2)}) collective-permute-start(f32[8,256,128]{2,1,0:T(8,128)S(1)} %bitcast.19), channel_id=1, source_target_pairs={{0,1},{1,2},{2,3},{3,4},{4,5},{5,6},{6,7},{7,8},{8,9},{9,10},{10,1... | collective-permute-start | bytes 3145736 | tf_op jit(solution)/shard_map/ppermute | solution.py:337
  46.0 3.4 %collective-permute-start.4 = (f32[2,256,128]{2,1,0:T(8,128)S(1)}, f32[2,256,128]{2,1,0:T(8,128)S(1)}, u32[]{:S(2)}, u32[]{:S(2)}) collective-permute-start(f32[2,256,128]{2,1,0:T(8,128)S(1)} %broadcast_select_fusion.refs_0_), channel_id=1, source_target_pairs={{0,32},{32,64},{64,96},{96,128},{128,160},{160,192},{192,224},{224... | collective-permute-start | bytes 786440 | tf_op jit(solution)/shard_map/ppermute | solution.py:332
  49.4 2.1 %collective-permute-done.5.refs_2_ = f32[2,256,128]{2,1,0:T(8,128)S(1)} collective-permute-done((f32[2,256,128]{2,1,0:T(8,128)S(1)}, f32[2,256,128]{2,1,0:T(8,128)S(1)}, u32[]{:S(2)}, u32[]{:S(2)}) %collective-permute-start.5) | collective-permute-done | bytes 262176 | tf_op jit(solution)/shard_map/ppermute | solution.py:332
  51.5 4.3 %collective-permute-start.7 = (f32[2,256,128]{2,1,0:T(8,128)S(1)}, f32[2,256,128]{2,1,0:T(8,128)S(1)}, u32[]{:S(2)}, u32[]{:S(2)}) collective-permute-start(f32[2,256,128]{2,1,0:T(8,128)S(1)} %collective-permute-done.5.refs_2_), channel_id=1, source_target_pairs={{0,224},{32,0},{64,32},{96,64},{128,96},{160,128},{192,160},{224,1... | collective-permute-start | bytes 786440 | tf_op jit(solution)/shard_map/ppermute | solution.py:332
  59.6 4.8 %collective-permute-start.9 = (f32[2,256,128]{2,1,0:T(8,128)S(1)}, f32[2,256,128]{2,1,0:T(8,128)S(1)}, u32[]{:S(2)}, u32[]{:S(2)}) collective-permute-start(f32[2,256,128]{2,1,0:T(8,128)S(1)} %collective-permute-done.7.refs_4_), channel_id=1, source_target_pairs={{0,224},{32,0},{64,32},{96,64},{128,96},{160,128},{192,160},{224,1... | collective-permute-start | bytes 786440 | tf_op jit(solution)/shard_map/ppermute | solution.py:332
  68.0 5.8 %collective-permute-done.11.right = f32[8,256,128]{2,1,0:T(8,128)} collective-permute-done((f32[8,256,128]{2,1,0:T(8,128)S(1)}, f32[8,256,128]{2,1,0:T(8,128)}, u32[]{:S(2)}, u32[]{:S(2)}) %collective-permute-start.11) | collective-permute-done | bytes 1048608 | tf_op jit(solution)/shard_map/ppermute | solution.py:338
  75.8 3.4 %collective-permute-start.12 = (f32[1,256,128]{2,1,0:T(8,128)S(1)}, f32[1,256,128]{2,1,0:T(8,128)S(1)}, u32[]{:S(2)}, u32[]{:S(2)}) collective-permute-start(f32[1,256,128]{2,1,0:T(8,128)S(1)} %slice.37), channel_id=1, source_target_pairs={{0,32},{32,64},{64,96},{96,128},{128,160},{160,192},{192,224},{224... | collective-permute-start | bytes 393224 | tf_op jit(solution)/shard_map/ppermute | solution.py:332
  79.2 2.6 %shard_map.44 = (f32[8,256,128]{2,1,0:T(8,128)S(1)}, f32[8,128]{1,0:T(8,128)S(1)}) custom-call(f32[8,256,128]{2,1,0:T(8,128)S(1)} %bitcast.23, f32[8,256,128]{2,1,0:T(8,128)S(1)} %bitcast.30, f32[8,256,128]{2,1,0:T(8,128)S(1)} %collective-permute-done.10.left, f32[8,256,128]{2,1,0:T(8,128)} %collective-permute-done.11.right), custom_call_target="tpu_custom_call" | custom-call | flops 13107200 | bytes 5242880 | tf_op jit(solution)/shard_map/pallas_call | solution.py:403
  81.8 3.1 %shard_map.45.refs_11_ = f32[8,128]{1,0:T(8,128)S(1)} custom-call(f32[2,256,128]{2,1,0:T(8,128)S(1)} %broadcast_select_fusion.refs_0_, f32[2,256,128]{2,1,0:T(8,128)S(1)} %collective-permute-done.4.refs_1_, f32[2,256,128]{2,1,0:T(8,128)S(1)} %collective-permute-done.5.refs_2_, f32[2,256,128]{2,1,0:T(8,128)S(1)} %collective-permute-done.6.refs_3_, ...), custom_call_target="tpu_custom_call" | custom-call | flops 5242880 | bytes 2621440 | tf_op jit(solution)/shard_map/pallas_call | solution.py:383
  85.9 24.8 %all_to_all.5.refs_0_ = f32[32,8,128]{2,1,0:T(8,128)S(1)} all-to-all(f32[32,8,128]{2,1,0:T(8,128)S(1)} %shard_map.46), channel_id=1, replica_groups=mesh['band'=16,'domain'=32] {'domain'}, dimensions={0} | all-to-all | bytes 262144 | tf_op jit(solution)/shard_map/all_to_all | solution.py:327
  110.7 5.4 %shard_map.48 = (f32[8,256,128]{2,1,0:T(8,128)}, f32[8,128]{1,0:T(8,128)S(1)}, f32[8,128]{1,0:T(8,128)S(1)}) custom-call(s32[1]{0:T(128)} %bitcast.band_ref, f32[8,128]{1,0:T(8,128)S(1)} %shard_map.47.sums_ref.own_ref, f32[2,256,128]{2,1,0:T(8,128)S(1)} %broadcast_select_fusion.refs_0_, f32[2,256,128]{2,1,0:T(8,128)S(1)} %collective-permute-done.4.refs_1_, ...), custom_call_target="tpu_custom_call" | custom-call | flops 12582912 | bytes 4194304 | tf_op jit(solution)/shard_map/pallas_call | solution.py:416
  116.1 2.1 %collective-permute-start.14 = (f32[8,256,128]{2,1,0:T(8,128)}, f32[8,256,128]{2,1,0:T(8,128)S(1)}, u32[]{:S(2)}, u32[]{:S(2)}) collective-permute-start(f32[8,256,128]{2,1,0:T(8,128)} %get-tuple-element.37.f_ref), channel_id=1, source_target_pairs={{0,1},{1,2},{2,3},{3,4},{4,5},{5,6},{6,7},{7,8},{8,9},{9,10},{10,1... | collective-permute-start | bytes 3145736 | tf_op jit(solution)/shard_map/ppermute | solution.py:337
  118.2 2.2 %collective-permute-start.15 = (f32[8,256,128]{2,1,0:T(8,128)}, f32[8,256,128]{2,1,0:T(8,128)}, u32[]{:S(2)}, u32[]{:S(2)}) collective-permute-start(f32[8,256,128]{2,1,0:T(8,128)} %get-tuple-element.37.f_ref), channel_id=1, source_target_pairs={{1,0},{2,1},{3,2},{4,3},{5,4},{6,5},{7,6},{8,7},{9,8},{10,9},{11,1... | collective-permute-start | bytes 3145736 | tf_op jit(solution)/shard_map/ppermute | solution.py:338
  121.7 2.7 %shard_map.49 = f32[8,4,64,128]{3,2,1,0:T(8,128)S(1)} custom-call(f32[8,4,64,128]{3,2,1,0:T(8,128)S(1)} %bitcast.28, f32[4,64,128]{2,1,0:T(8,128)S(1)} %copy-done.3), custom_call_target="tpu_custom_call" | custom-call | flops 15728640 | bytes 2097152 | tf_op jit(solution)/shard_map/pallas_call | solution.py:355
  126.4 2.7 %collective-permute-done.16 = f32[8,128]{1,0:T(8,128)S(1)} collective-permute-done((f32[8,128]{1,0:T(8,128)S(1)}, f32[8,128]{1,0:T(8,128)S(1)}, u32[]{:S(2)}, u32[]{:S(2)}) %collective-permute-start.16) | collective-permute-done | bytes 4128 | tf_op jit(solution)/shard_map/ppermute | solution.py:427
  129.1 2.2 %collective-permute-start.17 = (f32[2,8,128]{2,1,0:T(8,128)S(1)}, f32[2,8,128]{2,1,0:T(8,128)S(1)}, u32[]{:S(2)}, u32[]{:S(2)}) collective-permute-start(f32[2,8,128]{2,1,0:T(8,128)S(1)} %maximum_select_fusion), channel_id=1, source_target_pairs={{0,128},{32,160},{1,129},{33,161},{2,130},{34,162},{3,131},{35,163... | collective-permute-start | bytes 24584 | tf_op jit(solution)/shard_map/ppermute | solution.py:430
  134.1 2.0 %collective-permute-start.19 = (f32[2,8,128]{2,1,0:T(8,128)S(1)}, f32[2,8,128]{2,1,0:T(8,128)S(1)}, u32[]{:S(2)}, u32[]{:S(2)}) collective-permute-start(f32[2,8,128]{2,1,0:T(8,128)S(1)} %fusion.3.near_ref), channel_id=1, source_target_pairs={{0,256},{32,288},{64,320},{96,352},{128,384},{160,416},{192,448},{... | collective-permute-start | bytes 24584 | tf_op jit(solution)/shard_map/ppermute | solution.py:432
  138.4 7.3 %collective-permute-done.15.right_ref = f32[8,256,128]{2,1,0:T(8,128)} collective-permute-done((f32[8,256,128]{2,1,0:T(8,128)}, f32[8,256,128]{2,1,0:T(8,128)}, u32[]{:S(2)}, u32[]{:S(2)}) %collective-permute-start.15) | collective-permute-done | bytes 1048608 | tf_op jit(solution)/shard_map/ppermute | solution.py:338
  145.7 3.4 %shard_map.51 = f32[8,256,128]{2,1,0:T(8,128)} custom-call(f32[8,256,128]{2,1,0:T(8,128)S(1)} %copy-done.2, f32[8,256,128]{2,1,0:T(8,128)S(1)} %bitcast.29, f32[8,256,128]{2,1,0:T(8,128)S(1)} %collective-permute-done.14.left_ref, f32[8,256,128]{2,1,0:T(8,128)} %collective-permute-done.15.right_ref, f32[8,8,128]{2,1,0:T(8,128)S(1)} %shard_map.50.splat), custom_call_target="tpu_custom_call" | custom-call | flops 7864320 | bytes 5242880 | tf_op jit(solution)/shard_map/pallas_call | solution.py:436
  (45 shorter events, 26.7 us)
Async XLA Ops:
  0.6 20.8 %copy-start = (f32[8,4,64,128]{3,2,1,0:T(8,128)S(1)}, f32[8,4,64,128]{3,2,1,0:T(8,128)}, u32[]{:S(2)}) copy-start(f32[8,4,64,128]{3,2,1,0:T(8,128)} %f_ref.1) | copy-start | bytes 3145732
  0.6 20.8 %copy-start.3 = (f32[4,64,128]{2,1,0:T(8,128)S(1)}, f32[4,64,128]{2,1,0:T(8,128)}, u32[]{:S(2)}) copy-start(f32[4,64,128]{2,1,0:T(8,128)} %v_ref.3) | copy-start | bytes 393220
  2.0 22.7 %collective-permute-start = (f32[2,256,128]{2,1,0:T(8,128)S(1)}, f32[2,256,128]{2,1,0:T(8,128)S(1)}, u32[]{:S(2)}, u32[]{:S(2)}) collective-permute-start(f32[2,256,128]{2,1,0:T(8,128)S(1)} %bitcast.34), channel_id=1, source_target_pairs={{0,384},{32,416},{1,385},{33,417},{2,386},{34,418},{3,387},{35,419... | collective-permute-start | bytes 786440 | tf_op jit(solution)/shard_map/ppermute | solution.py:366
  18.8 10.6 %collective-permute-start.1 = (f32[2,256,128]{2,1,0:T(8,128)S(1)}, f32[2,256,128]{2,1,0:T(8,128)S(1)}, u32[]{:S(2)}, u32[]{:S(2)}) collective-permute-start(f32[2,256,128]{2,1,0:T(8,128)S(1)} %bitcast.33), channel_id=1, source_target_pairs={{0,64},{32,96},{1,65},{33,97},{2,66},{34,98},{3,67},{35,99},{4,68}... | collective-permute-start | bytes 786440 | tf_op jit(solution)/shard_map/ppermute | solution.py:366
  20.1 16.0 %collective-permute-start.2 = (f32[2,256,128]{2,1,0:T(8,128)S(1)}, f32[2,256,128]{2,1,0:T(8,128)S(1)}, u32[]{:S(2)}, u32[]{:S(2)}) collective-permute-start(f32[2,256,128]{2,1,0:T(8,128)S(1)} %bitcast.32), channel_id=1, source_target_pairs={{0,192},{32,224},{1,193},{33,225},{2,194},{34,226},{3,195},{35,227... | collective-permute-start | bytes 786440 | tf_op jit(solution)/shard_map/ppermute | solution.py:366
  36.2 7.8 %collective-permute-start.3 = (f32[2,256,128]{2,1,0:T(8,128)S(1)}, f32[2,256,128]{2,1,0:T(8,128)}, u32[]{:S(2)}, u32[]{:S(2)}) collective-permute-start(f32[2,256,128]{2,1,0:T(8,128)S(1)} %fusion.1), channel_id=1, source_target_pairs={{0,256},{32,288},{64,320},{96,352},{384,128},{416,160},{192,448},{... | collective-permute-start | bytes 786440 | tf_op jit(solution)/shard_map/ppermute | solution.py:377
  38.2 29.9 %collective-permute-start.10 = (f32[8,256,128]{2,1,0:T(8,128)S(1)}, f32[8,256,128]{2,1,0:T(8,128)S(1)}, u32[]{:S(2)}, u32[]{:S(2)}) collective-permute-start(f32[8,256,128]{2,1,0:T(8,128)S(1)} %bitcast.19), channel_id=1, source_target_pairs={{0,1},{1,2},{2,3},{3,4},{4,5},{5,6},{6,7},{7,8},{8,9},{9,10},{10,1... | collective-permute-start | bytes 3145736 | tf_op jit(solution)/shard_map/ppermute | solution.py:337
  42.1 31.8 %collective-permute-start.11 = (f32[8,256,128]{2,1,0:T(8,128)S(1)}, f32[8,256,128]{2,1,0:T(8,128)}, u32[]{:S(2)}, u32[]{:S(2)}) collective-permute-start(f32[8,256,128]{2,1,0:T(8,128)S(1)} %bitcast.20), channel_id=1, source_target_pairs={{1,0},{2,1},{3,2},{4,3},{5,4},{6,5},{7,6},{8,7},{9,8},{10,9},{11,1... | collective-permute-start | bytes 3145736 | tf_op jit(solution)/shard_map/ppermute | solution.py:338
  44.1 7.4 %collective-permute-start.5 = (f32[2,256,128]{2,1,0:T(8,128)S(1)}, f32[2,256,128]{2,1,0:T(8,128)S(1)}, u32[]{:S(2)}, u32[]{:S(2)}) collective-permute-start(f32[2,256,128]{2,1,0:T(8,128)S(1)} %broadcast_select_fusion.refs_0_), channel_id=1, source_target_pairs={{0,224},{32,0},{64,32},{96,64},{128,96},{160,128},{192,160},{224,1... | collective-permute-start | bytes 786440 | tf_op jit(solution)/shard_map/ppermute | solution.py:332
  46.0 10.5 %collective-permute-start.4 = (f32[2,256,128]{2,1,0:T(8,128)S(1)}, f32[2,256,128]{2,1,0:T(8,128)S(1)}, u32[]{:S(2)}, u32[]{:S(2)}) collective-permute-start(f32[2,256,128]{2,1,0:T(8,128)S(1)} %broadcast_select_fusion.refs_0_), channel_id=1, source_target_pairs={{0,32},{32,64},{64,96},{96,128},{128,160},{160,192},{192,224},{224... | collective-permute-start | bytes 786440 | tf_op jit(solution)/shard_map/ppermute | solution.py:332
  51.5 8.1 %collective-permute-start.7 = (f32[2,256,128]{2,1,0:T(8,128)S(1)}, f32[2,256,128]{2,1,0:T(8,128)S(1)}, u32[]{:S(2)}, u32[]{:S(2)}) collective-permute-start(f32[2,256,128]{2,1,0:T(8,128)S(1)} %collective-permute-done.5.refs_2_), channel_id=1, source_target_pairs={{0,224},{32,0},{64,32},{96,64},{128,96},{160,128},{192,160},{224,1... | collective-permute-start | bytes 786440 | tf_op jit(solution)/shard_map/ppermute | solution.py:332
  56.5 8.6 %collective-permute-start.6 = (f32[2,256,128]{2,1,0:T(8,128)S(1)}, f32[2,256,128]{2,1,0:T(8,128)S(1)}, u32[]{:S(2)}, u32[]{:S(2)}) collective-permute-start(f32[2,256,128]{2,1,0:T(8,128)S(1)} %collective-permute-done.4.refs_1_), channel_id=1, source_target_pairs={{0,32},{32,64},{64,96},{96,128},{128,160},{160,192},{192,224},{224... | collective-permute-start | bytes 786440 | tf_op jit(solution)/shard_map/ppermute | solution.py:332
  59.6 14.3 %collective-permute-start.9 = (f32[2,256,128]{2,1,0:T(8,128)S(1)}, f32[2,256,128]{2,1,0:T(8,128)S(1)}, u32[]{:S(2)}, u32[]{:S(2)}) collective-permute-start(f32[2,256,128]{2,1,0:T(8,128)S(1)} %collective-permute-done.7.refs_4_), channel_id=1, source_target_pairs={{0,224},{32,0},{64,32},{96,64},{128,96},{160,128},{192,160},{224,1... | collective-permute-start | bytes 786440 | tf_op jit(solution)/shard_map/ppermute | solution.py:332
  65.1 10.6 %collective-permute-start.8 = (f32[2,256,128]{2,1,0:T(8,128)S(1)}, f32[2,256,128]{2,1,0:T(8,128)S(1)}, u32[]{:S(2)}, u32[]{:S(2)}) collective-permute-start(f32[2,256,128]{2,1,0:T(8,128)S(1)} %collective-permute-done.6.refs_3_), channel_id=1, source_target_pairs={{0,32},{32,64},{64,96},{96,128},{128,160},{160,192},{192,224},{224... | collective-permute-start | bytes 786440 | tf_op jit(solution)/shard_map/ppermute | solution.py:332
  73.8 11.0 %collective-permute-start.13 = (f32[1,256,128]{2,1,0:T(8,128)S(1)}, f32[1,256,128]{2,1,0:T(8,128)S(1)}, u32[]{:S(2)}, u32[]{:S(2)}) collective-permute-start(f32[1,256,128]{2,1,0:T(8,128)S(1)} %slice.36), channel_id=1, source_target_pairs={{0,224},{32,0},{64,32},{96,64},{128,96},{160,128},{192,160},{224,1... | collective-permute-start | bytes 393224 | tf_op jit(solution)/shard_map/ppermute | solution.py:332
  75.8 9.1 %collective-permute-start.12 = (f32[1,256,128]{2,1,0:T(8,128)S(1)}, f32[1,256,128]{2,1,0:T(8,128)S(1)}, u32[]{:S(2)}, u32[]{:S(2)}) collective-permute-start(f32[1,256,128]{2,1,0:T(8,128)S(1)} %slice.37), channel_id=1, source_target_pairs={{0,32},{32,64},{64,96},{96,128},{128,160},{160,192},{192,224},{224... | collective-permute-start | bytes 393224 | tf_op jit(solution)/shard_map/ppermute | solution.py:332
  116.1 22.3 %collective-permute-start.14 = (f32[8,256,128]{2,1,0:T(8,128)}, f32[8,256,128]{2,1,0:T(8,128)S(1)}, u32[]{:S(2)}, u32[]{:S(2)}) collective-permute-start(f32[8,256,128]{2,1,0:T(8,128)} %get-tuple-element.37.f_ref), channel_id=1, source_target_pairs={{0,1},{1,2},{2,3},{3,4},{4,5},{5,6},{6,7},{7,8},{8,9},{9,10},{10,1... | collective-permute-start | bytes 3145736 | tf_op jit(solution)/shard_map/ppermute | solution.py:337
  118.2 27.5 %collective-permute-start.15 = (f32[8,256,128]{2,1,0:T(8,128)}, f32[8,256,128]{2,1,0:T(8,128)}, u32[]{:S(2)}, u32[]{:S(2)}) collective-permute-start(f32[8,256,128]{2,1,0:T(8,128)} %get-tuple-element.37.f_ref), channel_id=1, source_target_pairs={{1,0},{2,1},{3,2},{4,3},{5,4},{6,5},{7,6},{8,7},{9,8},{10,9},{11,1... | collective-permute-start | bytes 3145736 | tf_op jit(solution)/shard_map/ppermute | solution.py:338
  120.5 1.2 copy-start.1
  121.7 24.0 %copy-start.2 = (f32[8,256,128]{2,1,0:T(8,128)S(1)}, f32[8,256,128]{2,1,0:T(8,128)}, u32[]{:S(2)}) copy-start(f32[8,256,128]{2,1,0:T(8,128)} %get-tuple-element.37.f_ref) | copy-start | bytes 3145732
  124.4 4.6 %collective-permute-start.16 = (f32[8,128]{1,0:T(8,128)S(1)}, f32[8,128]{1,0:T(8,128)S(1)}, u32[]{:S(2)}, u32[]{:S(2)}) collective-permute-start(f32[8,128]{1,0:T(8,128)S(1)} %shard_map.47.sums_ref.own_ref), channel_id=1, source_target_pairs={{0,32},{32,0},{1,33},{33,1},{2,34},{34,2},{3,35},{35,3},{4,36},{36... | collective-permute-start | bytes 12296 | tf_op jit(solution)/shard_map/ppermute | solution.py:427
  129.1 2.9 %collective-permute-start.17 = (f32[2,8,128]{2,1,0:T(8,128)S(1)}, f32[2,8,128]{2,1,0:T(8,128)S(1)}, u32[]{:S(2)}, u32[]{:S(2)}) collective-permute-start(f32[2,8,128]{2,1,0:T(8,128)S(1)} %maximum_select_fusion), channel_id=1, source_target_pairs={{0,128},{32,160},{1,129},{33,161},{2,130},{34,162},{3,131},{35,163... | collective-permute-start | bytes 24584 | tf_op jit(solution)/shard_map/ppermute | solution.py:430
  132.0 2.1 %collective-permute-start.18 = (f32[2,8,128]{2,1,0:T(8,128)S(1)}, f32[2,8,128]{2,1,0:T(8,128)S(1)}, u32[]{:S(2)}, u32[]{:S(2)}) collective-permute-start(f32[2,8,128]{2,1,0:T(8,128)S(1)} %fusion.2), channel_id=1, source_target_pairs={{0,64},{32,96},{128,192},{160,224},{1,65},{33,97},{129,193},{161,2... | collective-permute-start | bytes 24584 | tf_op jit(solution)/shard_map/ppermute | solution.py:431
  134.1 2.8 %collective-permute-start.19 = (f32[2,8,128]{2,1,0:T(8,128)S(1)}, f32[2,8,128]{2,1,0:T(8,128)S(1)}, u32[]{:S(2)}, u32[]{:S(2)}) collective-permute-start(f32[2,8,128]{2,1,0:T(8,128)S(1)} %fusion.3.near_ref), channel_id=1, source_target_pairs={{0,256},{32,288},{64,320},{96,352},{128,384},{160,416},{192,448},{... | collective-permute-start | bytes 24584 | tf_op jit(solution)/shard_map/ppermute | solution.py:432

commit v10 on v8

--- a/solution.py
+++ b/solution.py
@@ -33,10 +33,31 @@
     return lax.broadcasted_iota(jnp.int32, (8, 128), 0)
 
 
+def folded(rows):
+    sub = subs()
+    step = 4
+    while step:
+        lower = (sub & step) == 0
+        merged = []
+        for first, second in zip(rows[:step], rows[step:]):
+            if first is not None:
+                first = first + pltpu.roll(first, 8 - step, 0)
+            if second is not None:
+                second = second + pltpu.roll(second, step, 0)
+            if first is None and second is None:
+                merged.append(None)
+            else:
+                merged.append(
+                    jnp.where(lower, 0.0 if first is None else first, 0.0 if second is None else second)
+                )
+        rows = merged
+        step //= 2
+    return rows[0]
+
+
 def pair_sums(jobs, load, chunks):
     lane = lanes()
     result = jnp.zeros((8, 128), F32)
-    zero_row = jnp.zeros((1, 128), F32)
     for pairs in jobs:
         used = sorted({n for pair in pairs for n in pair})
 
@@ -50,10 +71,9 @@
         sums = lax.fori_loop(0, chunks // 4, body, (zero,) * len(pairs))
         columns = {}
         for s, (q, r) in zip(sums, pairs):
-            rows = columns.setdefault(32 * (r // 8) + q, [zero_row] * 8)
-            rows[r % 8] = jnp.sum(s, axis=0, keepdims=True)
+            columns.setdefault(32 * (r // 8) + q, [None] * 8)[r % 8] = s
         for place, rows in columns.items():
-            column = jnp.sum(jnp.concatenate(rows, axis=0), axis=1, keepdims=True)
+            column = jnp.sum(folded(rows), axis=1, keepdims=True)
             result = result + jnp.where(lane == place, column, 0.0)
     return result
 
@@ -177,17 +197,29 @@
         splat[c] = spread_lane(weights, 24 + c)
     rows = rows_of(pieces) + [(own, i) for i in range(BLK)]
 
-    def body(c, carry):
-        part = pl.ds(pl.multiple_of(c * 16, 16), 16)
-        inputs = [r[i, part, :] for r, i in rows]
-        for i in range(BLK):
-            total = splat[0, pl.ds(i, 1), :] * inputs[0]
-            for n in range(1, 24):
-                total = total + splat[n, pl.ds(i, 1), :] * inputs[n]
-            out[i, part, :] = total
-        return carry
-
-    lax.fori_loop(0, own.shape[1] // 16, body, 0)
+    def combine(places, plus_own):
+        def body(c, carry):
+            part = pl.ds(pl.multiple_of(c * 32, 32), 32)
+            for low in (0, 4):
+                if plus_own:
+                    totals = [own[low + k, part, :] for k in range(4)]
+                else:
+                    totals = [jnp.zeros((32, 128), F32)] * 4
+                for n in places:
+                    r, i = rows[n]
+                    cells = r[i, part, :]
+                    totals = [
+                        t + splat[n, pl.ds(low + k, 1), :] * cells for k, t in enumerate(totals)
+                    ]
+                for k in range(4):
+                    out[low + k, part, :] = totals[k]
+            return carry
+
+        lax.fori_loop(0, own.shape[1] // 32, body, 0)
+
+    pl.when(later)(lambda: combine(range(16), True))
+    pl.when(second)(lambda: combine((2, 3, 4, 5, 10, 11, 12, 13, *OWN), False))
+    pl.when(band == 0)(lambda: combine(OWN, False))
 
 
 def inner_kernel(f_ref, v_ref, out, *sums):
@@ -244,7 +276,7 @@
     lax.fori_loop(0, BLK, body, 0)
     load = {n: loader(own, n - 16) for n in OWN}
     load |= {n: loader(out, n - 24) for n in IMAGE}
-    jobs = split([(q, r) for q in IMAGE for r in OWN], 32)
+    jobs = [[(q, r) for q in IMAGE for r in OWN if r <= q - 8]]
     sums[...] = pair_sums(jobs, load, own.shape[1] // 8)
 
 
@@ -278,6 +310,12 @@
     weights = jnp.where(lane < 24, pltpu.roll(weights_ref[...], 104, 1), 0.0)
     weights = dot(weights, place)
 
+    def with_mirror(packed):
+        tiles = unpacked(packed)
+        mirror = jnp.transpose(tall([move(tiles[2], 24, 0)]))[0:8]
+        tiles[2] = tiles[2] + move(jnp.where(lane == sub, 0.0, mirror), 0, 24)
+        return tall(tiles)
+
     def image_columns(matrix, place, source, target):
         columns = dot(place, matrix, turn_left=True)
         columns = pltpu.roll(columns, (target - source) % 128, 1)
@@ -285,10 +323,10 @@
 
     def visiting(n):
         packed = jnp.where(band_ref[0] < RING, near_ref[n], far_ref[n])
-        return image_columns(tall(unpacked(packed)), places(n, n), 24, 8 * n)
+        return image_columns(with_mirror(packed), places(n, n), 24, 8 * n)
 
     block0, block1 = visiting(0), visiting(1)
-    block = image_columns(tall(unpacked(own_ref[...])), place, 24, 16)
+    block = image_columns(with_mirror(own_ref[...]), place, 24, 16)
     half = dot(weights, block0 + block1 + block)
     half = half + dot(weights, jnp.where(row < 16, block, 0.0), turn_right=True)
     theta = dot(half, tall([weights]), turn_right=True)
@@ -301,26 +339,36 @@
         out[j] = spread_lane(work, 8 + j)
 
 
-def residual_kernel(f_ref, inner_ref, left_ref, right_ref, splat, out):
+def partial_kernel(f_ref, inner_ref, splat, out):
     def body(c, carry):
-        def part(x):
-            return pl.ds(pl.multiple_of(64 * x + 8 * c, 8), 8)
-
+        part = pl.ds(pl.multiple_of(c * 32, 32), 32)
+        for low in (0, 4):
+            totals = [inner_ref[low + k, part, :] for k in range(4)]
+            for i in range(BLK):
+                cells = f_ref[i, part, :]
+                totals = [
+                    t - splat[low + k, pl.ds(i, 1), :] * cells for k, t in enumerate(totals)
+                ]
+            for k in range(4):
+                out[low + k, part, :] = totals[k]
+        return carry
+
+    lax.fori_loop(0, f_ref.shape[1] // 32, body, 0)
+
+
+def edge_kernel(partial_ref, left_ref, right_ref, out):
+    def body(i, carry):
         for x in range(4):
-            inputs = [f_ref[i, part(x), :] for i in range(BLK)]
-            for j in range(BLK):
-                total = edged(
-                    inner_ref[j, part(x), :],
-                    x,
-                    lambda n: left_ref[j, part(n), :],
-                    lambda n: right_ref[j, part(n), :],
-                )
-                for i in range(BLK):
-                    total = total - splat[j, pl.ds(i, 1), :] * inputs[i]
-                out[j, part(x), :] = total
+            part = pl.ds(64 * x, 64)
+            out[i, part, :] = edged(
+                partial_ref[i, part, :],
+                x,
+                lambda n: left_ref[i, pl.ds(64 * n, 64), :],
+                lambda n: right_ref[i, pl.ds(64 * n, 64), :],
+            )
         return carry
 
-    lax.fori_loop(0, 8, body, 0)
+    lax.fori_loop(0, BLK, body, 0)
 
 
 def domain_parts(copies):
@@ -419,19 +467,23 @@
     )(band_word, sums, *pieces, own)
     left, right = neighbours(basis)
     inner = inner_part(basis.reshape(orbitals.shape))[0].reshape(flat)
-    shared, inner = lax.optimization_barrier((sums, inner))
+    shared = sums
     other = lax.ppermute(shared, "band", [(0, 1), (1, 0)])
     shared = jnp.stack([jnp.where(band == 0, shared, other), jnp.where(band == 0, other, shared)])
     shared = jnp.where(band < 2, shared, 0.0)
     shared = shared + lax.ppermute(shared, "band", [(0, 4), (1, 5)])
     shared = shared + lax.ppermute(shared, "band", [(0, 2), (1, 3), (4, 6), (5, 7)])
+    shared, inner = lax.optimization_barrier((shared, inner))
     far = lax.ppermute(shared, "band", [(y, y + RING) for y in range(RING)])
     splat = call(
         coeff_kernel, jax.ShapeDtypeStruct((8, 8, 128), F32), specs=[SMEM] + [VMEM] * 5
     )(band_word, weights, gram, sums, shared, far)
+    partial = call(
+        partial_kernel, slab, specs=[VMEM] * 3, flops=16 * big, bytes_moved=12 * big
+    )(basis, inner, splat)
     residual = call(
-        residual_kernel, slab, specs=[VMEM] * 5, flops=30 * big, bytes_moved=20 * big
-    )(basis, inner, left, right, splat)
+        edge_kernel, slab, specs=[VMEM] * 3, flops=20 * big, bytes_moved=16 * big
+    )(partial, left, right)
     return (basis.reshape(orbitals.shape), residual.reshape(orbitals.shape))
 
 

time: 139 us -> 136 us (0.978)
  Pallas kernels: 25.2 us -> 22 us
  waiting for transfers between devices: 35.2 us -> 32.8 us
  starting transfers between devices: 52.7 us -> 54.6 us
    ppermute x2, waiting for transfers between devices: 12.8 us -> 10.9 us  [neighbours(): lax.ppermute(block, 'domain', [((i + 1) % count, i) for i in range(count)])]
    pallas_call x1, Pallas kernels: 5.4 us -> 3.79 us  [local(): call(combine_kernel, (slab, tile, tile), scratch=[pltpu.VMEM((24, 8, 128)...]
    ppermute x1, starting transfers between devices: 2.86 us -> 4.25 us  [local(): far = lax.ppermute(shared, 'band', [(y, y + RING) for y in range(RING)])]
    pallas_call x1 -> x2, Pallas kernels: 3.39 us -> 2.07 us  [the longest x1 1.41 us: local(): call(edge_kernel, slab, specs=[VMEM] * 3, flops=20 * big, bytes_moved=16...]
  transfers between devices with their start and end apart: 20 -> 20, of which waited for: 12 -> 11; matrix products, arithmetic and copies ran while one was open for 0% -> 0% of each run, Pallas kernels for 11% -> 12%
where the time goes in v10:
time: 136 us; the launch traced here: 134 us
  starting transfers between devices  54.6 us (40%)
  waiting for transfers between devices  32.8 us (24%)
  Pallas kernels  22 us (16%)
  blocking collectives  21.2 us (16%)
  other arithmetic  1.49 us (1%)
    ppermute x8, starting transfers between devices, ring_shift(): return lax.ppermute(block, 'band', pairs)  23 us
    all_to_all x1, blocking collectives, domain_parts(): return lax.all_to_all(copies, 'domain', 0, 0)  21.2 us
    ppermute x3, waiting for transfers between devices, local(): lax.ppermute(quarters[k], 'band', [(0, 2 * k), (1, 2 * k + 1)])  11.6 us
    ppermute x2, waiting for transfers between devices, neighbours(): lax.ppermute(block, 'domain', [((i + 1) % count, i) for i in range(count)])  10.9 us
    ppermute x3, starting transfers between devices, local(): lax.ppermute(quarters[k], 'band', [(0, 2 * k), (1, 2 * k + 1)])  9.65 us
    ppermute x2, starting transfers between devices, neighbours(): lax.ppermute(block, 'domain', [(i, (i + 1) % count) for i in range(count)])  6.58 us
    ppermute x8, waiting for transfers between devices, ring_shift(): return lax.ppermute(block, 'band', pairs)  6.34 us
    pallas_call x4, Pallas kernels, stage(): call(lambda *refs: stage_kernel(len(pieces), fresh, imaged, last, *refs),...  6.12 us
  transfers between devices with their start and end apart: 20, of which 11 were waited for; matrix products, arithmetic and copies ran while one was open for 0% of the time, Pallas kernels for 12%

profile of v10, /device:TPU:1, one launch (start us, length us, event | category | flops | bytes accessed | tf_op | source)
XLA Modules:
  0.0 134.3 jit_solution(14854276234250061633)
XLA Ops:
  2.0 5.1 %collective-permute-start = (f32[2,256,128]{2,1,0:T(8,128)S(1)}, f32[2,256,128]{2,1,0:T(8,128)S(1)}, u32[]{:S(2)}, u32[]{:S(2)}) collective-permute-start(f32[2,256,128]{2,1,0:T(8,128)S(1)} %bitcast.34), channel_id=1, source_target_pairs={{0,64},{32,96},{1,65},{33,97},{2,66},{34,98},{3,67},{35,99},{4,68}... | collective-permute-start | bytes 786440 | tf_op jit(solution)/shard_map/ppermute | solution.py:414
  7.1 2.3 %collective-permute-start.1 = (f32[2,256,128]{2,1,0:T(8,128)S(1)}, f32[2,256,128]{2,1,0:T(8,128)S(1)}, u32[]{:S(2)}, u32[]{:S(2)}) collective-permute-start(f32[2,256,128]{2,1,0:T(8,128)S(1)} %bitcast.33), channel_id=1, source_target_pairs={{0,192},{32,224},{1,193},{33,225},{2,194},{34,226},{3,195},{35,227... | collective-permute-start | bytes 786440 | tf_op jit(solution)/shard_map/ppermute | solution.py:414
  9.5 2.2 %collective-permute-start.2 = (f32[2,256,128]{2,1,0:T(8,128)S(1)}, f32[2,256,128]{2,1,0:T(8,128)S(1)}, u32[]{:S(2)}, u32[]{:S(2)}) collective-permute-start(f32[2,256,128]{2,1,0:T(8,128)S(1)} %bitcast.32), channel_id=1, source_target_pairs={{0,128},{32,160},{1,129},{33,161},{2,130},{34,162},{3,131},{35,163... | collective-permute-start | bytes 786440 | tf_op jit(solution)/shard_map/ppermute | solution.py:414
  11.7 3.3 %shard_map.41 = (f32[8,4,64,128]{3,2,1,0:T(8,128)S(1)}, f32[8,128]{1,0:T(8,128)S(1)}) custom-call(f32[8,4,64,128]{3,2,1,0:T(8,128)S(1)} %copy-done, f32[4,64,128]{2,1,0:T(8,128)S(1)} %copy-done.3), custom_call_target="tpu_custom_call" | custom-call | flops 15728640 | bytes 2097152 | tf_op jit(solution)/shard_map/pallas_call | solution.py:403
  15.0 11.5 %collective-permute-done.1 = f32[2,256,128]{2,1,0:T(8,128)S(1)} collective-permute-done((f32[2,256,128]{2,1,0:T(8,128)S(1)}, f32[2,256,128]{2,1,0:T(8,128)S(1)}, u32[]{:S(2)}, u32[]{:S(2)}) %collective-permute-start.1) | collective-permute-done | bytes 262176 | tf_op jit(solution)/shard_map/ppermute | solution.py:414
  26.6 2.0 %collective-permute-start.3 = (f32[2,256,128]{2,1,0:T(8,128)S(1)}, f32[2,256,128]{2,1,0:T(8,128)}, u32[]{:S(2)}, u32[]{:S(2)}) collective-permute-start(f32[2,256,128]{2,1,0:T(8,128)S(1)} %fusion.1), channel_id=1, source_target_pairs={{0,256},{32,288},{64,320},{96,352},{128,384},{160,416},{192,448},{... | collective-permute-start | bytes 786440 | tf_op jit(solution)/shard_map/ppermute | solution.py:422
  28.6 4.5 %collective-permute-start.10 = (f32[8,256,128]{2,1,0:T(8,128)S(1)}, f32[8,256,128]{2,1,0:T(8,128)S(1)}, u32[]{:S(2)}, u32[]{:S(2)}) collective-permute-start(f32[8,256,128]{2,1,0:T(8,128)S(1)} %bitcast.19), channel_id=1, source_target_pairs={{0,1},{1,2},{2,3},{3,4},{4,5},{5,6},{6,7},{7,8},{8,9},{9,10},{10,1... | collective-permute-start | bytes 3145736 | tf_op jit(solution)/shard_map/ppermute | solution.py:385
  33.1 1.9 %collective-permute-start.11 = (f32[8,256,128]{2,1,0:T(8,128)S(1)}, f32[8,256,128]{2,1,0:T(8,128)}, u32[]{:S(2)}, u32[]{:S(2)}) collective-permute-start(f32[8,256,128]{2,1,0:T(8,128)S(1)} %bitcast.20), channel_id=1, source_target_pairs={{1,0},{2,1},{3,2},{4,3},{5,4},{6,5},{7,6},{8,7},{9,8},{10,9},{11,1... | collective-permute-start | bytes 3145736 | tf_op jit(solution)/shard_map/ppermute | solution.py:386
  37.0 3.4 %collective-permute-start.4 = (f32[2,256,128]{2,1,0:T(8,128)S(1)}, f32[2,256,128]{2,1,0:T(8,128)S(1)}, u32[]{:S(2)}, u32[]{:S(2)}) collective-permute-start(f32[2,256,128]{2,1,0:T(8,128)S(1)} %broadcast_select_fusion.refs_0_), channel_id=1, source_target_pairs={{0,32},{32,64},{64,96},{96,128},{128,160},{160,192},{192,224},{224... | collective-permute-start | bytes 786440 | tf_op jit(solution)/shard_map/ppermute | solution.py:380
  40.4 2.1 %collective-permute-done.5.refs_2_ = f32[2,256,128]{2,1,0:T(8,128)S(1)} collective-permute-done((f32[2,256,128]{2,1,0:T(8,128)S(1)}, f32[2,256,128]{2,1,0:T(8,128)S(1)}, u32[]{:S(2)}, u32[]{:S(2)}) %collective-permute-start.5) | collective-permute-done | bytes 262176 | tf_op jit(solution)/shard_map/ppermute | solution.py:380
  42.5 4.3 %collective-permute-start.7 = (f32[2,256,128]{2,1,0:T(8,128)S(1)}, f32[2,256,128]{2,1,0:T(8,128)S(1)}, u32[]{:S(2)}, u32[]{:S(2)}) collective-permute-start(f32[2,256,128]{2,1,0:T(8,128)S(1)} %collective-permute-done.5.refs_2_), channel_id=1, source_target_pairs={{0,224},{32,0},{64,32},{96,64},{128,96},{160,128},{192,160},{224,1... | collective-permute-start | bytes 786440 | tf_op jit(solution)/shard_map/ppermute | solution.py:380
  51.5 4.3 %collective-permute-start.9 = (f32[2,256,128]{2,1,0:T(8,128)S(1)}, f32[2,256,128]{2,1,0:T(8,128)S(1)}, u32[]{:S(2)}, u32[]{:S(2)}) collective-permute-start(f32[2,256,128]{2,1,0:T(8,128)S(1)} %collective-permute-done.7.refs_4_), channel_id=1, source_target_pairs={{0,224},{32,0},{64,32},{96,64},{128,96},{160,128},{192,160},{224,1... | collective-permute-start | bytes 786440 | tf_op jit(solution)/shard_map/ppermute | solution.py:380
  59.4 5.5 %collective-permute-done.11.right = f32[8,256,128]{2,1,0:T(8,128)} collective-permute-done((f32[8,256,128]{2,1,0:T(8,128)S(1)}, f32[8,256,128]{2,1,0:T(8,128)}, u32[]{:S(2)}, u32[]{:S(2)}) %collective-permute-start.11) | collective-permute-done | bytes 1048608 | tf_op jit(solution)/shard_map/ppermute | solution.py:386
  66.9 3.4 %collective-permute-start.12 = (f32[1,256,128]{2,1,0:T(8,128)S(1)}, f32[1,256,128]{2,1,0:T(8,128)S(1)}, u32[]{:S(2)}, u32[]{:S(2)}) collective-permute-start(f32[1,256,128]{2,1,0:T(8,128)S(1)} %slice.37), channel_id=1, source_target_pairs={{0,32},{32,64},{64,96},{96,128},{128,160},{160,192},{192,224},{224... | collective-permute-start | bytes 393224 | tf_op jit(solution)/shard_map/ppermute | solution.py:380
  70.3 2.2 %shard_map.44 = (f32[8,256,128]{2,1,0:T(8,128)S(1)}, f32[8,128]{1,0:T(8,128)S(1)}) custom-call(f32[8,256,128]{2,1,0:T(8,128)S(1)} %bitcast.23, f32[8,256,128]{2,1,0:T(8,128)S(1)} %bitcast.30, f32[8,256,128]{2,1,0:T(8,128)S(1)} %collective-permute-done.10.left, f32[8,256,128]{2,1,0:T(8,128)} %collective-permute-done.11.right), custom_call_target="tpu_custom_call" | custom-call | flops 13107200 | bytes 5242880 | tf_op jit(solution)/shard_map/pallas_call | solution.py:447
  72.5 3.0 %shard_map.45.refs_11_ = f32[8,128]{1,0:T(8,128)S(1)} custom-call(f32[2,256,128]{2,1,0:T(8,128)S(1)} %broadcast_select_fusion.refs_0_, f32[2,256,128]{2,1,0:T(8,128)S(1)} %collective-permute-done.4.refs_1_, f32[2,256,128]{2,1,0:T(8,128)S(1)} %collective-permute-done.5.refs_2_, f32[2,256,128]{2,1,0:T(8,128)S(1)} %collective-permute-done.6.refs_3_, ...), custom_call_target="tpu_custom_call" | custom-call | flops 5242880 | bytes 2621440 | tf_op jit(solution)/shard_map/pallas_call | solution.py:427
  78.3 21.2 %all_to_all.5.refs_0_ = f32[32,8,128]{2,1,0:T(8,128)S(1)} all-to-all(f32[32,8,128]{2,1,0:T(8,128)S(1)} %shard_map.46), channel_id=1, replica_groups=mesh['band'=16,'domain'=32] {'domain'}, dimensions={0} | all-to-all | bytes 262144 | tf_op jit(solution)/shard_map/all_to_all | solution.py:375
  99.6 3.8 %shard_map.48 = (f32[8,256,128]{2,1,0:T(8,128)}, f32[8,128]{1,0:T(8,128)S(1)}, f32[8,128]{1,0:T(8,128)S(1)}) custom-call(s32[1]{0:T(128)} %bitcast.band_ref, f32[8,128]{1,0:T(8,128)S(1)} %shard_map.47.sums_ref.own_ref, f32[2,256,128]{2,1,0:T(8,128)S(1)} %broadcast_select_fusion.refs_0_, f32[2,256,128]{2,1,0:T(8,128)S(1)} %collective-permute-done.4.refs_1_, ...), custom_call_target="tpu_custom_call" | custom-call | flops 12582912 | bytes 4194304 | tf_op jit(solution)/shard_map/pallas_call | solution.py:460
  103.3 2.1 %collective-permute-start.18 = (f32[8,256,128]{2,1,0:T(8,128)}, f32[8,256,128]{2,1,0:T(8,128)S(1)}, u32[]{:S(2)}, u32[]{:S(2)}) collective-permute-start(f32[8,256,128]{2,1,0:T(8,128)} %get-tuple-element.37.f_ref), channel_id=1, source_target_pairs={{0,1},{1,2},{2,3},{3,4},{4,5},{5,6},{6,7},{7,8},{8,9},{9,10},{10,1... | collective-permute-start | bytes 3145736 | tf_op jit(solution)/shard_map/ppermute | solution.py:385
  105.4 2.2 %collective-permute-start.19 = (f32[8,256,128]{2,1,0:T(8,128)}, f32[8,256,128]{2,1,0:T(8,128)S(1)}, u32[]{:S(2)}, u32[]{:S(2)}) collective-permute-start(f32[8,256,128]{2,1,0:T(8,128)} %get-tuple-element.37.f_ref), channel_id=1, source_target_pairs={{1,0},{2,1},{3,2},{4,3},{5,4},{6,5},{7,6},{8,7},{9,8},{10,9},{11,1... | collective-permute-start | bytes 3145736 | tf_op jit(solution)/shard_map/ppermute | solution.py:386
  109.6 2.4 %collective-permute-done.14 = f32[8,128]{1,0:T(8,128)S(1)} collective-permute-done((f32[8,128]{1,0:T(8,128)S(1)}, f32[8,128]{1,0:T(8,128)S(1)}, u32[]{:S(2)}, u32[]{:S(2)}) %collective-permute-start.14) | collective-permute-done | bytes 4128 | tf_op jit(solution)/shard_map/ppermute | solution.py:471
  117.2 2.7 %shard_map.49 = f32[8,4,64,128]{3,2,1,0:T(8,128)S(1)} custom-call(f32[8,4,64,128]{3,2,1,0:T(8,128)S(1)} %bitcast.28, f32[4,64,128]{2,1,0:T(8,128)S(1)} %copy-done.3), custom_call_target="tpu_custom_call" | custom-call | flops 15728640 | bytes 2097152 | tf_op jit(solution)/shard_map/pallas_call | solution.py:403
  120.0 4.3 %collective-permute-start.17 = (f32[2,8,128]{2,1,0:T(8,128)S(1)}, f32[2,8,128]{2,1,0:T(8,128)S(1)}, u32[]{:S(2)}, u32[]{:S(2)}) collective-permute-start(f32[2,8,128]{2,1,0:T(8,128)S(1)} %fusion.3.near_ref), channel_id=1, source_target_pairs={{0,256},{32,288},{64,320},{96,352},{128,384},{160,416},{192,448},{... | collective-permute-start | bytes 24584 | tf_op jit(solution)/shard_map/ppermute | solution.py:477
  127.5 5.4 %collective-permute-done.19.right_ref = f32[8,256,128]{2,1,0:T(8,128)S(1)} collective-permute-done((f32[8,256,128]{2,1,0:T(8,128)}, f32[8,256,128]{2,1,0:T(8,128)S(1)}, u32[]{:S(2)}, u32[]{:S(2)}) %collective-permute-start.19) | collective-permute-done | bytes 1048608 | tf_op jit(solution)/shard_map/ppermute | solution.py:386
  (46 shorter events, 28.3 us)
Async XLA Ops:
  0.6 11.1 %copy-start = (f32[8,4,64,128]{3,2,1,0:T(8,128)S(1)}, f32[8,4,64,128]{3,2,1,0:T(8,128)}, u32[]{:S(2)}) copy-start(f32[8,4,64,128]{3,2,1,0:T(8,128)} %f_ref.1) | copy-start | bytes 3145732
  0.6 11.1 %copy-start.3 = (f32[4,64,128]{2,1,0:T(8,128)S(1)}, f32[4,64,128]{2,1,0:T(8,128)}, u32[]{:S(2)}) copy-start(f32[4,64,128]{2,1,0:T(8,128)} %v_ref.3) | copy-start | bytes 393220
  2.0 13.0 %collective-permute-start = (f32[2,256,128]{2,1,0:T(8,128)S(1)}, f32[2,256,128]{2,1,0:T(8,128)S(1)}, u32[]{:S(2)}, u32[]{:S(2)}) collective-permute-start(f32[2,256,128]{2,1,0:T(8,128)S(1)} %bitcast.34), channel_id=1, source_target_pairs={{0,64},{32,96},{1,65},{33,97},{2,66},{34,98},{3,67},{35,99},{4,68}... | collective-permute-start | bytes 786440 | tf_op jit(solution)/shard_map/ppermute | solution.py:414
  7.1 19.5 %collective-permute-start.1 = (f32[2,256,128]{2,1,0:T(8,128)S(1)}, f32[2,256,128]{2,1,0:T(8,128)S(1)}, u32[]{:S(2)}, u32[]{:S(2)}) collective-permute-start(f32[2,256,128]{2,1,0:T(8,128)S(1)} %bitcast.33), channel_id=1, source_target_pairs={{0,192},{32,224},{1,193},{33,225},{2,194},{34,226},{3,195},{35,227... | collective-permute-start | bytes 786440 | tf_op jit(solution)/shard_map/ppermute | solution.py:414
  9.5 17.1 %collective-permute-start.2 = (f32[2,256,128]{2,1,0:T(8,128)S(1)}, f32[2,256,128]{2,1,0:T(8,128)S(1)}, u32[]{:S(2)}, u32[]{:S(2)}) collective-permute-start(f32[2,256,128]{2,1,0:T(8,128)S(1)} %bitcast.32), channel_id=1, source_target_pairs={{0,128},{32,160},{1,129},{33,161},{2,130},{34,162},{3,131},{35,163... | collective-permute-start | bytes 786440 | tf_op jit(solution)/shard_map/ppermute | solution.py:414
  26.6 8.4 %collective-permute-start.3 = (f32[2,256,128]{2,1,0:T(8,128)S(1)}, f32[2,256,128]{2,1,0:T(8,128)}, u32[]{:S(2)}, u32[]{:S(2)}) collective-permute-start(f32[2,256,128]{2,1,0:T(8,128)S(1)} %fusion.1), channel_id=1, source_target_pairs={{0,256},{32,288},{64,320},{96,352},{128,384},{160,416},{192,448},{... | collective-permute-start | bytes 786440 | tf_op jit(solution)/shard_map/ppermute | solution.py:422
  28.6 30.8 %collective-permute-start.10 = (f32[8,256,128]{2,1,0:T(8,128)S(1)}, f32[8,256,128]{2,1,0:T(8,128)S(1)}, u32[]{:S(2)}, u32[]{:S(2)}) collective-permute-start(f32[8,256,128]{2,1,0:T(8,128)S(1)} %bitcast.19), channel_id=1, source_target_pairs={{0,1},{1,2},{2,3},{3,4},{4,5},{5,6},{6,7},{7,8},{8,9},{9,10},{10,1... | collective-permute-start | bytes 3145736 | tf_op jit(solution)/shard_map/ppermute | solution.py:385
  33.1 31.8 %collective-permute-start.11 = (f32[8,256,128]{2,1,0:T(8,128)S(1)}, f32[8,256,128]{2,1,0:T(8,128)}, u32[]{:S(2)}, u32[]{:S(2)}) collective-permute-start(f32[8,256,128]{2,1,0:T(8,128)S(1)} %bitcast.20), channel_id=1, source_target_pairs={{1,0},{2,1},{3,2},{4,3},{5,4},{6,5},{7,6},{8,7},{9,8},{10,9},{11,1... | collective-permute-start | bytes 3145736 | tf_op jit(solution)/shard_map/ppermute | solution.py:386
  35.1 7.4 %collective-permute-start.5 = (f32[2,256,128]{2,1,0:T(8,128)S(1)}, f32[2,256,128]{2,1,0:T(8,128)S(1)}, u32[]{:S(2)}, u32[]{:S(2)}) collective-permute-start(f32[2,256,128]{2,1,0:T(8,128)S(1)} %broadcast_select_fusion.refs_0_), channel_id=1, source_target_pairs={{0,224},{32,0},{64,32},{96,64},{128,96},{160,128},{192,160},{224,1... | collective-permute-start | bytes 786440 | tf_op jit(solution)/shard_map/ppermute | solution.py:380
  37.0 10.5 %collective-permute-start.4 = (f32[2,256,128]{2,1,0:T(8,128)S(1)}, f32[2,256,128]{2,1,0:T(8,128)S(1)}, u32[]{:S(2)}, u32[]{:S(2)}) collective-permute-start(f32[2,256,128]{2,1,0:T(8,128)S(1)} %broadcast_select_fusion.refs_0_), channel_id=1, source_target_pairs={{0,32},{32,64},{64,96},{96,128},{128,160},{160,192},{192,224},{224... | collective-permute-start | bytes 786440 | tf_op jit(solution)/shard_map/ppermute | solution.py:380
  42.5 9.0 %collective-permute-start.7 = (f32[2,256,128]{2,1,0:T(8,128)S(1)}, f32[2,256,128]{2,1,0:T(8,128)S(1)}, u32[]{:S(2)}, u32[]{:S(2)}) collective-permute-start(f32[2,256,128]{2,1,0:T(8,128)S(1)} %collective-permute-done.5.refs_2_), channel_id=1, source_target_pairs={{0,224},{32,0},{64,32},{96,64},{128,96},{160,128},{192,160},{224,1... | collective-permute-start | bytes 786440 | tf_op jit(solution)/shard_map/ppermute | solution.py:380
  47.6 9.0 %collective-permute-start.6 = (f32[2,256,128]{2,1,0:T(8,128)S(1)}, f32[2,256,128]{2,1,0:T(8,128)S(1)}, u32[]{:S(2)}, u32[]{:S(2)}) collective-permute-start(f32[2,256,128]{2,1,0:T(8,128)S(1)} %collective-permute-done.4.refs_1_), channel_id=1, source_target_pairs={{0,32},{32,64},{64,96},{96,128},{128,160},{160,192},{192,224},{224... | collective-permute-start | bytes 786440 | tf_op jit(solution)/shard_map/ppermute | solution.py:380
  51.5 13.4 %collective-permute-start.9 = (f32[2,256,128]{2,1,0:T(8,128)S(1)}, f32[2,256,128]{2,1,0:T(8,128)S(1)}, u32[]{:S(2)}, u32[]{:S(2)}) collective-permute-start(f32[2,256,128]{2,1,0:T(8,128)S(1)} %collective-permute-done.7.refs_4_), channel_id=1, source_target_pairs={{0,224},{32,0},{64,32},{96,64},{128,96},{160,128},{192,160},{224,1... | collective-permute-start | bytes 786440 | tf_op jit(solution)/shard_map/ppermute | solution.py:380
  56.6 10.3 %collective-permute-start.8 = (f32[2,256,128]{2,1,0:T(8,128)S(1)}, f32[2,256,128]{2,1,0:T(8,128)S(1)}, u32[]{:S(2)}, u32[]{:S(2)}) collective-permute-start(f32[2,256,128]{2,1,0:T(8,128)S(1)} %collective-permute-done.6.refs_3_), channel_id=1, source_target_pairs={{0,32},{32,64},{64,96},{96,128},{128,160},{160,192},{192,224},{224... | collective-permute-start | bytes 786440 | tf_op jit(solution)/shard_map/ppermute | solution.py:380
  65.0 10.5 %collective-permute-start.13 = (f32[1,256,128]{2,1,0:T(8,128)S(1)}, f32[1,256,128]{2,1,0:T(8,128)S(1)}, u32[]{:S(2)}, u32[]{:S(2)}) collective-permute-start(f32[1,256,128]{2,1,0:T(8,128)S(1)} %slice.36), channel_id=1, source_target_pairs={{0,224},{32,0},{64,32},{96,64},{128,96},{160,128},{192,160},{224,1... | collective-permute-start | bytes 393224 | tf_op jit(solution)/shard_map/ppermute | solution.py:380
  66.9 10.3 %collective-permute-start.12 = (f32[1,256,128]{2,1,0:T(8,128)S(1)}, f32[1,256,128]{2,1,0:T(8,128)S(1)}, u32[]{:S(2)}, u32[]{:S(2)}) collective-permute-start(f32[1,256,128]{2,1,0:T(8,128)S(1)} %slice.37), channel_id=1, source_target_pairs={{0,32},{32,64},{64,96},{96,128},{128,160},{160,192},{192,224},{224... | collective-permute-start | bytes 393224 | tf_op jit(solution)/shard_map/ppermute | solution.py:380
  103.3 24.2 %collective-permute-start.18 = (f32[8,256,128]{2,1,0:T(8,128)}, f32[8,256,128]{2,1,0:T(8,128)S(1)}, u32[]{:S(2)}, u32[]{:S(2)}) collective-permute-start(f32[8,256,128]{2,1,0:T(8,128)} %get-tuple-element.37.f_ref), channel_id=1, source_target_pairs={{0,1},{1,2},{2,3},{3,4},{4,5},{5,6},{6,7},{7,8},{8,9},{9,10},{10,1... | collective-permute-start | bytes 3145736 | tf_op jit(solution)/shard_map/ppermute | solution.py:385
  105.4 27.5 %collective-permute-start.19 = (f32[8,256,128]{2,1,0:T(8,128)}, f32[8,256,128]{2,1,0:T(8,128)S(1)}, u32[]{:S(2)}, u32[]{:S(2)}) collective-permute-start(f32[8,256,128]{2,1,0:T(8,128)} %get-tuple-element.37.f_ref), channel_id=1, source_target_pairs={{1,0},{2,1},{3,2},{4,3},{5,4},{6,5},{7,6},{8,7},{9,8},{10,9},{11,1... | collective-permute-start | bytes 3145736 | tf_op jit(solution)/shard_map/ppermute | solution.py:386
  107.7 4.4 %collective-permute-start.14 = (f32[8,128]{1,0:T(8,128)S(1)}, f32[8,128]{1,0:T(8,128)S(1)}, u32[]{:S(2)}, u32[]{:S(2)}) collective-permute-start(f32[8,128]{1,0:T(8,128)S(1)} %shard_map.47.sums_ref.own_ref), channel_id=1, source_target_pairs={{0,32},{32,0},{1,33},{33,1},{2,34},{34,2},{3,35},{35,3},{4,36},{36... | collective-permute-start | bytes 12296 | tf_op jit(solution)/shard_map/ppermute | solution.py:471
  112.0 2.6 %collective-permute-start.15 = (f32[2,8,128]{2,1,0:T(8,128)S(1)}, f32[2,8,128]{2,1,0:T(8,128)S(1)}, u32[]{:S(2)}, u32[]{:S(2)}) collective-permute-start(f32[2,8,128]{2,1,0:T(8,128)S(1)} %maximum_select_fusion), channel_id=1, source_target_pairs={{0,128},{32,160},{1,129},{33,161},{2,130},{34,162},{3,131},{35,163... | collective-permute-start | bytes 24584 | tf_op jit(solution)/shard_map/ppermute | solution.py:474
  114.7 5.3 %collective-permute-start.16 = (f32[2,8,128]{2,1,0:T(8,128)S(1)}, f32[2,8,128]{2,1,0:T(8,128)S(1)}, u32[]{:S(2)}, u32[]{:S(2)}) collective-permute-start(f32[2,8,128]{2,1,0:T(8,128)S(1)} %fusion.2), channel_id=1, source_target_pairs={{0,64},{32,96},{128,192},{160,224},{1,65},{33,97},{129,193},{161,2... | collective-permute-start | bytes 24584 | tf_op jit(solution)/shard_map/ppermute | solution.py:475
  116.0 1.2 copy-start.1
  117.2 9.6 %copy-start.2 = (f32[8,256,128]{2,1,0:T(8,128)S(1)}, f32[8,256,128]{2,1,0:T(8,128)}, u32[]{:S(2)}) copy-start(f32[8,256,128]{2,1,0:T(8,128)} %get-tuple-element.37.f_ref) | copy-start | bytes 3145732
  120.0 5.0 %collective-permute-start.17 = (f32[2,8,128]{2,1,0:T(8,128)S(1)}, f32[2,8,128]{2,1,0:T(8,128)S(1)}, u32[]{:S(2)}, u32[]{:S(2)}) collective-permute-start(f32[2,8,128]{2,1,0:T(8,128)S(1)} %fusion.3.near_ref), channel_id=1, source_target_pairs={{0,256},{32,288},{64,320},{96,352},{128,384},{160,416},{192,448},{... | collective-permute-start | bytes 24584 | tf_op jit(solution)/shard_map/ppermute | solution.py:477

commit v11 on v10

--- a/solution.py
+++ b/solution.py
@@ -261,19 +261,27 @@
     return inner - 0.5 * total
 
 
-def image_kernel(own, inner, left, right, out, sums):
-    def body(i, carry):
-        for x in range(4):
-            part = pl.ds(64 * x, 64)
-            out[i, part, :] = edged(
-                inner[i, part, :],
-                x,
-                lambda n: left[i, pl.ds(64 * n, 64), :],
-                lambda n: right[i, pl.ds(64 * n, 64), :],
-            )
-        return carry
-
-    lax.fori_loop(0, BLK, body, 0)
+def add_edges(inner, across, beside, odd, out):
+    def run(left, right):
+        def body(i, carry):
+            for x in range(4):
+                part = pl.ds(64 * x, 64)
+                out[i, part, :] = edged(
+                    inner[i, part, :],
+                    x,
+                    lambda n: left[i, pl.ds(64 * n, 64), :],
+                    lambda n: right[i, pl.ds(64 * n, 64), :],
+                )
+            return carry
+
+        lax.fori_loop(0, BLK, body, 0)
+
+    pl.when(odd == 0)(lambda: run(across, beside))
+    pl.when(odd == 1)(lambda: run(beside, across))
+
+
+def image_kernel(words, own, inner, across, beside, out, sums):
+    add_edges(inner, across, beside, words[1], out)
     load = {n: loader(own, n - 16) for n in OWN}
     load |= {n: loader(out, n - 24) for n in IMAGE}
     jobs = [[(q, r) for q in IMAGE for r in OWN if r <= q - 8]]
@@ -291,7 +299,7 @@
     row = lax.broadcasted_iota(jnp.int32, (128, 128), 0)
     lane = lax.broadcasted_iota(jnp.int32, (128, 128), 1)
     distance = (row + 2) >> 2
-    distance = jnp.where(((row + 2) & 2) == 0, -distance, distance)
+    distance = jnp.where((((row + 2) >> 1) & 1) == (y & 1), distance, -distance)
     piece = (y + distance) & 7
     target = (piece & 1) * 8 + (piece >> 1) * 2 + (row & 1)
     if home is None:
@@ -356,35 +364,28 @@
     lax.fori_loop(0, f_ref.shape[1] // 32, body, 0)
 
 
-def edge_kernel(partial_ref, left_ref, right_ref, out):
-    def body(i, carry):
-        for x in range(4):
-            part = pl.ds(64 * x, 64)
-            out[i, part, :] = edged(
-                partial_ref[i, part, :],
-                x,
-                lambda n: left_ref[i, pl.ds(64 * n, 64), :],
-                lambda n: right_ref[i, pl.ds(64 * n, 64), :],
-            )
-        return carry
-
-    lax.fori_loop(0, BLK, body, 0)
+def edge_kernel(words, partial, across, beside, out):
+    add_edges(partial, across, beside, words[1], out)
 
 
 def domain_parts(copies):
     return lax.all_to_all(copies, "domain", 0, 0)
 
 
-def ring_shift(block, step):
-    pairs = [(z * RING + y, z * RING + (y + step) % RING) for z in range(2) for y in range(RING)]
+def ring_exchange(block, odd):
+    pairs = []
+    for z in range(2):
+        for y in range(odd, RING, 2):
+            here, there = z * RING + y, z * RING + (y + 1) % RING
+            pairs += [(here, there), (there, here)]
     return lax.ppermute(block, "band", pairs)
 
 
 def neighbours(block):
     count = lax.axis_size("domain")
-    left = lax.ppermute(block, "domain", [(i, (i + 1) % count) for i in range(count)])
-    right = lax.ppermute(block, "domain", [((i + 1) % count, i) for i in range(count)])
-    return left, right
+    across = [(i, (i + 1 if i % 2 else i - 1) % count) for i in range(count)]
+    beside = [(i, i ^ 1) for i in range(count)]
+    return lax.ppermute(block, "domain", across), lax.ppermute(block, "domain", beside)
 
 
 def local(orbitals, potential):
@@ -392,7 +393,7 @@
     domain = lax.axis_size("domain")
     cells_total = float(slab_width * rows_y * rows_z * domain)
     band = lax.axis_index("band")
-    band_word = band.reshape(1).astype(jnp.int32)
+    words = jnp.stack([band, lax.axis_index("domain") & 1]).astype(jnp.int32)
     flat = (blocks, slab_width * rows_y, rows_z)
     big = flat[0] * flat[1] * flat[2]
     slab = jax.ShapeDtypeStruct(flat, F32)
@@ -414,11 +415,11 @@
         lax.ppermute(quarters[k], "band", [(0, 2 * k), (1, 2 * k + 1)]) for k in (1, 3, 2)
     ]
     inner, sums = inner_part(orbitals, tile)
-    arrived, inner, sums = lax.optimization_barrier((arrived, inner, sums))
+    arrived, inner, sums, words = lax.optimization_barrier((arrived, inner, sums, words))
     piece = jnp.where(band < 2, quarters[0], 0.0)
     for part in arrived:
         piece = piece + part
-    left, right = neighbours(own)
+    across, beside = neighbours(own)
     crossed = lax.ppermute(piece, "band", [(y, y + RING) for y in range(RING)])
     piece = jnp.where(band < RING, piece, crossed)
 
@@ -433,20 +434,24 @@
         )(*sources)
 
     pieces = [piece]
-    up, down = ring_shift(piece, 1), ring_shift(piece, -1)
+    up, down = ring_exchange(piece, 0), ring_exchange(piece, 1)
     pieces += [up, down]
-    up, down = ring_shift(up, 1), ring_shift(down, -1)
+    up, down = ring_exchange(down, 0), ring_exchange(up, 1)
     sums = stage(range(6), (), pieces, sums)
     down, sums = lax.optimization_barrier((down, sums))
     pieces += [up, down]
-    up, down = ring_shift(up, 1), ring_shift(down, -1)
+    up, down = ring_exchange(down, 0), ring_exchange(up, 1)
     sums = stage(range(6, 10), (), pieces, sums)
-    down, sums, left, right = lax.optimization_barrier((down, sums, left, right))
+    down, sums, across, beside = lax.optimization_barrier((down, sums, across, beside))
     pieces += [up, down]
-    up, down = ring_shift(up[:1], 1), ring_shift(down[1:], -1)
+    up, down = ring_exchange(down[:1], 0), ring_exchange(up[1:], 1)
     image, image_sums = call(
-        image_kernel, (slab, tile), specs=[VMEM] * 4, flops=50 * big, bytes_moved=20 * big
-    )(own, inner.reshape(flat), left, right)
+        image_kernel,
+        (slab, tile),
+        specs=[SMEM] + [VMEM] * 4,
+        flops=50 * big,
+        bytes_moved=20 * big,
+    )(words, own, inner.reshape(flat), across, beside)
     sums = stage(range(10, 14), range(14), pieces, sums, image_sums)
     pieces += [up, down]
     sums = stage(range(14, 16), range(14, 16), pieces, sums, last=True)
@@ -464,8 +469,8 @@
         specs=[SMEM] + [VMEM] * 11,
         flops=48 * big,
         bytes_moved=16 * big,
-    )(band_word, sums, *pieces, own)
-    left, right = neighbours(basis)
+    )(words, sums, *pieces, own)
+    across, beside = neighbours(basis)
     inner = inner_part(basis.reshape(orbitals.shape))[0].reshape(flat)
     shared = sums
     other = lax.ppermute(shared, "band", [(0, 1), (1, 0)])
@@ -477,13 +482,13 @@
     far = lax.ppermute(shared, "band", [(y, y + RING) for y in range(RING)])
     splat = call(
         coeff_kernel, jax.ShapeDtypeStruct((8, 8, 128), F32), specs=[SMEM] + [VMEM] * 5
-    )(band_word, weights, gram, sums, shared, far)
+    )(words, weights, gram, sums, shared, far)
     partial = call(
         partial_kernel, slab, specs=[VMEM] * 3, flops=16 * big, bytes_moved=12 * big
     )(basis, inner, splat)
     residual = call(
-        edge_kernel, slab, specs=[VMEM] * 3, flops=20 * big, bytes_moved=16 * big
-    )(partial, left, right)
+        edge_kernel, slab, specs=[SMEM] + [VMEM] * 3, flops=20 * big, bytes_moved=16 * big
+    )(words, partial, across, beside)
     return (basis.reshape(orbitals.shape), residual.reshape(orbitals.shape))
 
 

time: 136 us -> 139 us (1.022)
  starting transfers between devices: 54.6 us -> 61.5 us
  waiting for transfers between devices: 32.8 us -> 28.3 us
  blocking collectives: 21.2 us -> 19.1 us
  Pallas kernels: 22 us -> 23.8 us
  other arithmetic: 1.49 us -> 3.2 us
    ppermute x12, starting transfers between devices: 33.7 us -> 39.8 us  [the longest x8 21.9 us: ring_exchange(): return lax.ppermute(block, 'band', pairs)]
    ppermute x12, waiting for transfers between devices: 17.2 us -> 13.2 us  [the longest x8 11.7 us: ring_exchange(): return lax.ppermute(block, 'band', pairs)]
    all_to_all x1, blocking collectives: 21.2 us -> 19.1 us  [domain_parts(): return lax.all_to_all(copies, 'domain', 0, 0)]
  transfers between devices with their start and end apart: 20 -> 20, of which waited for: 11 -> 9; matrix products, arithmetic and copies ran while one was open for 0% -> 0% of each run, Pallas kernels for 12% -> 12%
where the time goes in v11:
time: 139 us; the launch traced here: 138 us
  starting transfers between devices  61.5 us (44%)
  waiting for transfers between devices  28.3 us (20%)
  Pallas kernels  23.8 us (17%)
  blocking collectives  19.1 us (14%)
  other arithmetic  3.2 us (2%)
    ppermute x8, starting transfers between devices, ring_exchange(): return lax.ppermute(block, 'band', pairs)  21.9 us
    all_to_all x1, blocking collectives, domain_parts(): return lax.all_to_all(copies, 'domain', 0, 0)  19.1 us
    ppermute x8, waiting for transfers between devices, ring_exchange(): return lax.ppermute(block, 'band', pairs)  11.7 us
    ppermute x2, starting transfers between devices, neighbours(): lax.ppermute(block, 'domain', beside)  11.3 us
    ppermute x3, waiting for transfers between devices, local(): lax.ppermute(quarters[k], 'band', [(0, 2 * k), (1, 2 * k + 1)])  10.8 us
    ppermute x3, starting transfers between devices, local(): lax.ppermute(quarters[k], 'band', [(0, 2 * k), (1, 2 * k + 1)])  10.3 us
    ppermute x2, starting transfers between devices, neighbours(): lax.ppermute(block, 'domain', across)  6.58 us
    pallas_call x4, Pallas kernels, stage(): call(lambda *refs: stage_kernel(len(pieces), fresh, imaged, last, *refs),...  6.2 us
  transfers between devices with their start and end apart: 20, of which 9 were waited for; matrix products, arithmetic and copies ran while one was open for 0% of the time, Pallas kernels for 12%

profile of v11, /device:TPU:1, one launch (start us, length us, event | category | flops | bytes accessed | tf_op | source)
XLA Modules:
  0.0 138.1 jit_solution(1382733910114949977)
XLA Ops:
  0.7 2.1 %slice_select_fusion = (f32[2,4,64,128]{3,2,1,0:T(8,128)S(1)}, f32[2,4,64,128]{3,2,1,0:T(8,128)S(1)}, f32[2,4,64,128]{3,2,1,0:T(8,128)S(1)}, f32[2,4,64,128]{3,2,1,0:T(8,128)}) fusion(f32[8,4,64,128]{3,2,1,0:T(8,128)} %f_ref.1, pred[]{:T(512)S(6)} %lt.8), kind=kLoop, calls=%fused_computation.3 | loop fusion | flops 65536 | bytes 2097153 | tf_op jit(solution)/shard_map/jit(_where)/select_n | solution.py:419
  2.7 5.0 %collective-permute-start = (f32[2,256,128]{2,1,0:T(8,128)}, f32[2,256,128]{2,1,0:T(8,128)S(1)}, u32[]{:S(2)}, u32[]{:S(2)}) collective-permute-start(f32[2,256,128]{2,1,0:T(8,128)} %bitcast), channel_id=1, source_target_pairs={{0,64},{32,96},{1,65},{33,97},{2,66},{34,98},{3,67},{35,99},{4,68}... | collective-permute-start | bytes 786440 | tf_op jit(solution)/shard_map/ppermute | solution.py:415
  7.8 2.3 %collective-permute-start.1 = (f32[2,256,128]{2,1,0:T(8,128)S(1)}, f32[2,256,128]{2,1,0:T(8,128)S(1)}, u32[]{:S(2)}, u32[]{:S(2)}) collective-permute-start(f32[2,256,128]{2,1,0:T(8,128)S(1)} %bitcast.34), channel_id=1, source_target_pairs={{0,192},{32,224},{1,193},{33,225},{2,194},{34,226},{3,195},{35,227... | collective-permute-start | bytes 786440 | tf_op jit(solution)/shard_map/ppermute | solution.py:415
  10.1 3.0 %collective-permute-start.2 = (f32[2,256,128]{2,1,0:T(8,128)S(1)}, f32[2,256,128]{2,1,0:T(8,128)}, u32[]{:S(2)}, u32[]{:S(2)}) collective-permute-start(f32[2,256,128]{2,1,0:T(8,128)S(1)} %bitcast.33), channel_id=1, source_target_pairs={{0,128},{32,160},{1,129},{33,161},{2,130},{34,162},{3,131},{35,163... | collective-permute-start | bytes 786440 | tf_op jit(solution)/shard_map/ppermute | solution.py:415
  13.1 3.3 %shard_map.41 = (f32[8,4,64,128]{3,2,1,0:T(8,128)S(1)}, f32[8,128]{1,0:T(8,128)S(1)}) custom-call(f32[8,4,64,128]{3,2,1,0:T(8,128)S(1)} %copy-done, f32[4,64,128]{2,1,0:T(8,128)S(1)} %copy-done.3), custom_call_target="tpu_custom_call" | custom-call | flops 15728640 | bytes 2097152 | tf_op jit(solution)/shard_map/pallas_call | solution.py:404
  16.5 10.8 %collective-permute-done.1 = f32[2,256,128]{2,1,0:T(8,128)S(1)} collective-permute-done((f32[2,256,128]{2,1,0:T(8,128)S(1)}, f32[2,256,128]{2,1,0:T(8,128)S(1)}, u32[]{:S(2)}, u32[]{:S(2)}) %collective-permute-start.1) | collective-permute-done | bytes 262176 | tf_op jit(solution)/shard_map/ppermute | solution.py:415
  28.2 2.0 %collective-permute-start.3 = (f32[2,256,128]{2,1,0:T(8,128)S(1)}, f32[2,256,128]{2,1,0:T(8,128)}, u32[]{:S(2)}, u32[]{:S(2)}) collective-permute-start(f32[2,256,128]{2,1,0:T(8,128)S(1)} %fusion.1), channel_id=1, source_target_pairs={{0,256},{32,288},{64,320},{96,352},{128,384},{160,416},{192,448},{... | collective-permute-start | bytes 786440 | tf_op jit(solution)/shard_map/ppermute | solution.py:423
  30.2 4.5 %collective-permute-start.10 = (f32[8,256,128]{2,1,0:T(8,128)S(1)}, f32[8,256,128]{2,1,0:T(8,128)S(1)}, u32[]{:S(2)}, u32[]{:S(2)}) collective-permute-start(f32[8,256,128]{2,1,0:T(8,128)S(1)} %bitcast.20), channel_id=1, source_target_pairs={{0,31},{1,2},{2,1},{3,4},{4,3},{5,6},{6,5},{7,8},{8,7},{9,10},{10,... | collective-permute-start | bytes 3145736 | tf_op jit(solution)/shard_map/ppermute | solution.py:388
  34.7 7.6 %collective-permute-start.11 = (f32[8,256,128]{2,1,0:T(8,128)S(1)}, f32[8,256,128]{2,1,0:T(8,128)}, u32[]{:S(2)}, u32[]{:S(2)}) collective-permute-start(f32[8,256,128]{2,1,0:T(8,128)S(1)} %bitcast.21), channel_id=1, source_target_pairs={{0,1},{1,0},{2,3},{3,2},{4,5},{5,4},{6,7},{7,6},{8,9},{9,8},{10,11... | collective-permute-start | bytes 3145736 | tf_op jit(solution)/shard_map/ppermute | solution.py:388
  46.3 7.2 %collective-permute-done.5.refs_2_ = f32[2,256,128]{2,1,0:T(8,128)S(1)} collective-permute-done((f32[2,256,128]{2,1,0:T(8,128)S(1)}, f32[2,256,128]{2,1,0:T(8,128)S(1)}, u32[]{:S(2)}, u32[]{:S(2)}) %collective-permute-start.5) | collective-permute-done | bytes 262176 | tf_op jit(solution)/shard_map/ppermute | solution.py:381
  55.4 5.3 %collective-permute-start.7 = (f32[2,256,128]{2,1,0:T(8,128)S(1)}, f32[2,256,128]{2,1,0:T(8,128)S(1)}, u32[]{:S(2)}, u32[]{:S(2)}) collective-permute-start(f32[2,256,128]{2,1,0:T(8,128)S(1)} %collective-permute-done.4.refs_1_), channel_id=1, source_target_pairs={{32,64},{64,32},{96,128},{128,96},{160,192},{192,160},{224,0},{0,2... | collective-permute-start | bytes 786440 | tf_op jit(solution)/shard_map/ppermute | solution.py:381
  62.4 4.1 %collective-permute-start.9 = (f32[2,256,128]{2,1,0:T(8,128)S(1)}, f32[2,256,128]{2,1,0:T(8,128)S(1)}, u32[]{:S(2)}, u32[]{:S(2)}) collective-permute-start(f32[2,256,128]{2,1,0:T(8,128)S(1)} %collective-permute-done.6.refs_3_), channel_id=1, source_target_pairs={{32,64},{64,32},{96,128},{128,96},{160,192},{192,160},{224,0},{0,2... | collective-permute-start | bytes 786440 | tf_op jit(solution)/shard_map/ppermute | solution.py:381
  71.6 2.3 %collective-permute-start.12 = (f32[1,256,128]{2,1,0:T(8,128)S(1)}, f32[1,256,128]{2,1,0:T(8,128)S(1)}, u32[]{:S(2)}, u32[]{:S(2)}) collective-permute-start(f32[1,256,128]{2,1,0:T(8,128)S(1)} %slice.35), channel_id=1, source_target_pairs={{0,32},{32,0},{64,96},{96,64},{128,160},{160,128},{192,224},{224,1... | collective-permute-start | bytes 393224 | tf_op jit(solution)/shard_map/ppermute | solution.py:381
  75.7 2.5 %collective-permute-start.13 = (f32[1,256,128]{2,1,0:T(8,128)S(1)}, f32[1,256,128]{2,1,0:T(8,128)S(1)}, u32[]{:S(2)}, u32[]{:S(2)}) collective-permute-start(f32[1,256,128]{2,1,0:T(8,128)S(1)} %slice.37), channel_id=1, source_target_pairs={{32,64},{64,32},{96,128},{128,96},{160,192},{192,160},{224,0},{0,2... | collective-permute-start | bytes 393224 | tf_op jit(solution)/shard_map/ppermute | solution.py:381
  78.2 2.2 %shard_map.44 = (f32[8,256,128]{2,1,0:T(8,128)S(1)}, f32[8,128]{1,0:T(8,128)S(1)}) custom-call(s32[2]{0:T(128)S(1)} %pad_add_fusion.words.band_ref, f32[8,256,128]{2,1,0:T(8,128)S(1)} %bitcast.24, f32[8,256,128]{2,1,0:T(8,128)S(1)} %bitcast.31, f32[8,256,128]{2,1,0:T(8,128)S(1)} %collective-permute-done.10.across, f32[8,256,128]{2,1,0:T(8,128)} %collective-permute-done.11.beside), custom_call_target="tpu_custom_call" | custom-call | flops 13107200 | bytes 5242880 | tf_op jit(solution)/shard_map/pallas_call | solution.py:448
  80.4 3.1 %shard_map.45.refs_11_ = f32[8,128]{1,0:T(8,128)S(1)} custom-call(f32[2,256,128]{2,1,0:T(8,128)S(1)} %broadcast_select_fusion.refs_0_, f32[2,256,128]{2,1,0:T(8,128)S(1)} %collective-permute-done.4.refs_1_, f32[2,256,128]{2,1,0:T(8,128)S(1)} %collective-permute-done.5.refs_2_, f32[2,256,128]{2,1,0:T(8,128)S(1)} %collective-permute-done.6.refs_3_, ...), custom_call_target="tpu_custom_call" | custom-call | flops 5242880 | bytes 2621440 | tf_op jit(solution)/shard_map/pallas_call | solution.py:428
  84.5 19.1 %all_to_all.5.refs_0_ = f32[32,8,128]{2,1,0:T(8,128)S(1)} all-to-all(f32[32,8,128]{2,1,0:T(8,128)S(1)} %shard_map.46), channel_id=1, replica_groups=mesh['band'=16,'domain'=32] {'domain'}, dimensions={0} | all-to-all | bytes 262144 | tf_op jit(solution)/shard_map/all_to_all | solution.py:372
  103.7 4.3 %shard_map.48 = (f32[8,256,128]{2,1,0:T(8,128)}, f32[8,128]{1,0:T(8,128)S(1)}, f32[8,128]{1,0:T(8,128)S(1)}) custom-call(s32[2]{0:T(128)S(1)} %pad_add_fusion.words.band_ref, f32[8,128]{1,0:T(8,128)S(1)} %shard_map.47.sums_ref.own_ref, f32[2,256,128]{2,1,0:T(8,128)S(1)} %broadcast_select_fusion.refs_0_, f32[2,256,128]{2,1,0:T(8,128)S(1)} %collective-permute-done.4.refs_1_, ...), custom_call_target="tpu_custom_call" | custom-call | flops 12582912 | bytes 4194304 | tf_op jit(solution)/shard_map/pallas_call | solution.py:465
  108.0 2.1 %collective-permute-start.18 = (f32[8,256,128]{2,1,0:T(8,128)}, f32[8,256,128]{2,1,0:T(8,128)S(1)}, u32[]{:S(2)}, u32[]{:S(2)}) collective-permute-start(f32[8,256,128]{2,1,0:T(8,128)} %get-tuple-element.39.f_ref), channel_id=1, source_target_pairs={{0,31},{1,2},{2,1},{3,4},{4,3},{5,6},{6,5},{7,8},{8,7},{9,10},{10,... | collective-permute-start | bytes 3145736 | tf_op jit(solution)/shard_map/ppermute | solution.py:388
  110.1 3.7 %collective-permute-start.19 = (f32[8,256,128]{2,1,0:T(8,128)}, f32[8,256,128]{2,1,0:T(8,128)S(1)}, u32[]{:S(2)}, u32[]{:S(2)}) collective-permute-start(f32[8,256,128]{2,1,0:T(8,128)} %get-tuple-element.39.f_ref), channel_id=1, source_target_pairs={{0,1},{1,0},{2,3},{3,2},{4,5},{5,4},{6,7},{7,6},{8,9},{9,8},{10,11... | collective-permute-start | bytes 3145736 | tf_op jit(solution)/shard_map/ppermute | solution.py:388
  115.7 2.7 %collective-permute-done.14 = f32[8,128]{1,0:T(8,128)S(1)} collective-permute-done((f32[8,128]{1,0:T(8,128)S(1)}, f32[8,128]{1,0:T(8,128)S(1)}, u32[]{:S(2)}, u32[]{:S(2)}) %collective-permute-start.14) | collective-permute-done | bytes 4128 | tf_op jit(solution)/shard_map/ppermute | solution.py:476
  123.0 2.7 %shard_map.49 = f32[8,4,64,128]{3,2,1,0:T(8,128)S(1)} custom-call(f32[8,4,64,128]{3,2,1,0:T(8,128)S(1)} %bitcast.29, f32[4,64,128]{2,1,0:T(8,128)S(1)} %copy-done.3), custom_call_target="tpu_custom_call" | custom-call | flops 15728640 | bytes 2097152 | tf_op jit(solution)/shard_map/pallas_call | solution.py:404
  125.8 4.9 %collective-permute-start.17 = (f32[2,8,128]{2,1,0:T(8,128)S(1)}, f32[2,8,128]{2,1,0:T(8,128)S(1)}, u32[]{:S(2)}, u32[]{:S(2)}) collective-permute-start(f32[2,8,128]{2,1,0:T(8,128)S(1)} %fusion.3.near_ref), channel_id=1, source_target_pairs={{0,256},{32,288},{64,320},{96,352},{128,384},{160,416},{192,448},{... | collective-permute-start | bytes 24584 | tf_op jit(solution)/shard_map/ppermute | solution.py:482
  131.5 2.4 %shard_map.50.splat = f32[8,8,128]{2,1,0:T(8,128)S(1)} custom-call(s32[2]{0:T(128)S(1)} %pad_add_fusion.words.band_ref, f32[8,128]{1,0:T(8,128)S(1)} %get-tuple-element.41.weights_ref, f32[8,128]{1,0:T(8,128)S(1)} %get-tuple-element.42.gram_ref, f32[8,128]{1,0:T(8,128)S(1)} %shard_map.47.sums_ref.own_ref, f32[2,8,128]{2,1,0:T(8,128)S(1)} %fusion.3.near_ref, ...), custom_call_target="tpu_custom_call" | custom-call | tf_op jit(solution)/shard_map/pallas_call | solution.py:483
  (47 shorter events, 28.0 us)
Async XLA Ops:
  0.6 12.4 %copy-start = (f32[8,4,64,128]{3,2,1,0:T(8,128)S(1)}, f32[8,4,64,128]{3,2,1,0:T(8,128)}, u32[]{:S(2)}) copy-start(f32[8,4,64,128]{3,2,1,0:T(8,128)} %f_ref.1) | copy-start | bytes 3145732
  0.6 12.4 %copy-start.3 = (f32[4,64,128]{2,1,0:T(8,128)S(1)}, f32[4,64,128]{2,1,0:T(8,128)}, u32[]{:S(2)}) copy-start(f32[4,64,128]{2,1,0:T(8,128)} %v_ref.3) | copy-start | bytes 393220
  2.7 13.7 %collective-permute-start = (f32[2,256,128]{2,1,0:T(8,128)}, f32[2,256,128]{2,1,0:T(8,128)S(1)}, u32[]{:S(2)}, u32[]{:S(2)}) collective-permute-start(f32[2,256,128]{2,1,0:T(8,128)} %bitcast), channel_id=1, source_target_pairs={{0,64},{32,96},{1,65},{33,97},{2,66},{34,98},{3,67},{35,99},{4,68}... | collective-permute-start | bytes 786440 | tf_op jit(solution)/shard_map/ppermute | solution.py:415
  7.8 19.5 %collective-permute-start.1 = (f32[2,256,128]{2,1,0:T(8,128)S(1)}, f32[2,256,128]{2,1,0:T(8,128)S(1)}, u32[]{:S(2)}, u32[]{:S(2)}) collective-permute-start(f32[2,256,128]{2,1,0:T(8,128)S(1)} %bitcast.34), channel_id=1, source_target_pairs={{0,192},{32,224},{1,193},{33,225},{2,194},{34,226},{3,195},{35,227... | collective-permute-start | bytes 786440 | tf_op jit(solution)/shard_map/ppermute | solution.py:415
  10.1 17.1 %collective-permute-start.2 = (f32[2,256,128]{2,1,0:T(8,128)S(1)}, f32[2,256,128]{2,1,0:T(8,128)}, u32[]{:S(2)}, u32[]{:S(2)}) collective-permute-start(f32[2,256,128]{2,1,0:T(8,128)S(1)} %bitcast.33), channel_id=1, source_target_pairs={{0,128},{32,160},{1,129},{33,161},{2,130},{34,162},{3,131},{35,163... | collective-permute-start | bytes 786440 | tf_op jit(solution)/shard_map/ppermute | solution.py:415
  28.2 14.1 %collective-permute-start.3 = (f32[2,256,128]{2,1,0:T(8,128)S(1)}, f32[2,256,128]{2,1,0:T(8,128)}, u32[]{:S(2)}, u32[]{:S(2)}) collective-permute-start(f32[2,256,128]{2,1,0:T(8,128)S(1)} %fusion.1), channel_id=1, source_target_pairs={{0,256},{32,288},{64,320},{96,352},{128,384},{160,416},{192,448},{... | collective-permute-start | bytes 786440 | tf_op jit(solution)/shard_map/ppermute | solution.py:423
  30.2 40.3 %collective-permute-start.10 = (f32[8,256,128]{2,1,0:T(8,128)S(1)}, f32[8,256,128]{2,1,0:T(8,128)S(1)}, u32[]{:S(2)}, u32[]{:S(2)}) collective-permute-start(f32[8,256,128]{2,1,0:T(8,128)S(1)} %bitcast.20), channel_id=1, source_target_pairs={{0,31},{1,2},{2,1},{3,4},{4,3},{5,6},{6,5},{7,8},{8,7},{9,10},{10,... | collective-permute-start | bytes 3145736 | tf_op jit(solution)/shard_map/ppermute | solution.py:388
  34.7 35.8 %collective-permute-start.11 = (f32[8,256,128]{2,1,0:T(8,128)S(1)}, f32[8,256,128]{2,1,0:T(8,128)}, u32[]{:S(2)}, u32[]{:S(2)}) collective-permute-start(f32[8,256,128]{2,1,0:T(8,128)S(1)} %bitcast.21), channel_id=1, source_target_pairs={{0,1},{1,0},{2,3},{3,2},{4,5},{5,4},{6,7},{7,6},{8,9},{9,8},{10,11... | collective-permute-start | bytes 3145736 | tf_op jit(solution)/shard_map/ppermute | solution.py:388
  42.4 11.0 %collective-permute-start.5 = (f32[2,256,128]{2,1,0:T(8,128)S(1)}, f32[2,256,128]{2,1,0:T(8,128)S(1)}, u32[]{:S(2)}, u32[]{:S(2)}) collective-permute-start(f32[2,256,128]{2,1,0:T(8,128)S(1)} %broadcast_select_fusion.refs_0_), channel_id=1, source_target_pairs={{32,64},{64,32},{96,128},{128,96},{160,192},{192,160},{224,0},{0,2... | collective-permute-start | bytes 786440 | tf_op jit(solution)/shard_map/ppermute | solution.py:381
  44.4 11.0 %collective-permute-start.4 = (f32[2,256,128]{2,1,0:T(8,128)S(1)}, f32[2,256,128]{2,1,0:T(8,128)S(1)}, u32[]{:S(2)}, u32[]{:S(2)}) collective-permute-start(f32[2,256,128]{2,1,0:T(8,128)S(1)} %broadcast_select_fusion.refs_0_), channel_id=1, source_target_pairs={{0,32},{32,0},{64,96},{96,64},{128,160},{160,128},{192,224},{224,1... | collective-permute-start | bytes 786440 | tf_op jit(solution)/shard_map/ppermute | solution.py:381
  53.5 8.9 %collective-permute-start.6 = (f32[2,256,128]{2,1,0:T(8,128)S(1)}, f32[2,256,128]{2,1,0:T(8,128)S(1)}, u32[]{:S(2)}, u32[]{:S(2)}) collective-permute-start(f32[2,256,128]{2,1,0:T(8,128)S(1)} %collective-permute-done.5.refs_2_), channel_id=1, source_target_pairs={{0,32},{32,0},{64,96},{96,64},{128,160},{160,128},{192,224},{224,1... | collective-permute-start | bytes 786440 | tf_op jit(solution)/shard_map/ppermute | solution.py:381
  55.4 12.3 %collective-permute-start.7 = (f32[2,256,128]{2,1,0:T(8,128)S(1)}, f32[2,256,128]{2,1,0:T(8,128)S(1)}, u32[]{:S(2)}, u32[]{:S(2)}) collective-permute-start(f32[2,256,128]{2,1,0:T(8,128)S(1)} %collective-permute-done.4.refs_1_), channel_id=1, source_target_pairs={{32,64},{64,32},{96,128},{128,96},{160,192},{192,160},{224,0},{0,2... | collective-permute-start | bytes 786440 | tf_op jit(solution)/shard_map/ppermute | solution.py:381
  62.4 9.2 %collective-permute-start.9 = (f32[2,256,128]{2,1,0:T(8,128)S(1)}, f32[2,256,128]{2,1,0:T(8,128)S(1)}, u32[]{:S(2)}, u32[]{:S(2)}) collective-permute-start(f32[2,256,128]{2,1,0:T(8,128)S(1)} %collective-permute-done.6.refs_3_), channel_id=1, source_target_pairs={{32,64},{64,32},{96,128},{128,96},{160,192},{192,160},{224,0},{0,2... | collective-permute-start | bytes 786440 | tf_op jit(solution)/shard_map/ppermute | solution.py:381
  67.6 8.0 %collective-permute-start.8 = (f32[2,256,128]{2,1,0:T(8,128)S(1)}, f32[2,256,128]{2,1,0:T(8,128)S(1)}, u32[]{:S(2)}, u32[]{:S(2)}) collective-permute-start(f32[2,256,128]{2,1,0:T(8,128)S(1)} %collective-permute-done.7.refs_4_), channel_id=1, source_target_pairs={{0,32},{32,0},{64,96},{96,64},{128,160},{160,128},{192,224},{224,1... | collective-permute-start | bytes 786440 | tf_op jit(solution)/shard_map/ppermute | solution.py:381
  71.6 11.9 %collective-permute-start.12 = (f32[1,256,128]{2,1,0:T(8,128)S(1)}, f32[1,256,128]{2,1,0:T(8,128)S(1)}, u32[]{:S(2)}, u32[]{:S(2)}) collective-permute-start(f32[1,256,128]{2,1,0:T(8,128)S(1)} %slice.35), channel_id=1, source_target_pairs={{0,32},{32,0},{64,96},{96,64},{128,160},{160,128},{192,224},{224,1... | collective-permute-start | bytes 393224 | tf_op jit(solution)/shard_map/ppermute | solution.py:381
  75.7 7.8 %collective-permute-start.13 = (f32[1,256,128]{2,1,0:T(8,128)S(1)}, f32[1,256,128]{2,1,0:T(8,128)S(1)}, u32[]{:S(2)}, u32[]{:S(2)}) collective-permute-start(f32[1,256,128]{2,1,0:T(8,128)S(1)} %slice.37), channel_id=1, source_target_pairs={{32,64},{64,32},{96,128},{128,96},{160,192},{192,160},{224,0},{0,2... | collective-permute-start | bytes 393224 | tf_op jit(solution)/shard_map/ppermute | solution.py:381
  108.0 28.1 %collective-permute-start.18 = (f32[8,256,128]{2,1,0:T(8,128)}, f32[8,256,128]{2,1,0:T(8,128)S(1)}, u32[]{:S(2)}, u32[]{:S(2)}) collective-permute-start(f32[8,256,128]{2,1,0:T(8,128)} %get-tuple-element.39.f_ref), channel_id=1, source_target_pairs={{0,31},{1,2},{2,1},{3,4},{4,3},{5,6},{6,5},{7,8},{8,7},{9,10},{10,... | collective-permute-start | bytes 3145736 | tf_op jit(solution)/shard_map/ppermute | solution.py:388
  110.1 26.0 %collective-permute-start.19 = (f32[8,256,128]{2,1,0:T(8,128)}, f32[8,256,128]{2,1,0:T(8,128)S(1)}, u32[]{:S(2)}, u32[]{:S(2)}) collective-permute-start(f32[8,256,128]{2,1,0:T(8,128)} %get-tuple-element.39.f_ref), channel_id=1, source_target_pairs={{0,1},{1,0},{2,3},{3,2},{4,5},{5,4},{6,7},{7,6},{8,9},{9,8},{10,11... | collective-permute-start | bytes 3145736 | tf_op jit(solution)/shard_map/ppermute | solution.py:388
  113.8 4.6 %collective-permute-start.14 = (f32[8,128]{1,0:T(8,128)S(1)}, f32[8,128]{1,0:T(8,128)S(1)}, u32[]{:S(2)}, u32[]{:S(2)}) collective-permute-start(f32[8,128]{1,0:T(8,128)S(1)} %shard_map.47.sums_ref.own_ref), channel_id=1, source_target_pairs={{0,32},{32,0},{1,33},{33,1},{2,34},{34,2},{3,35},{35,3},{4,36},{36... | collective-permute-start | bytes 12296 | tf_op jit(solution)/shard_map/ppermute | solution.py:476
  118.5 2.1 %collective-permute-start.15 = (f32[2,8,128]{2,1,0:T(8,128)S(1)}, f32[2,8,128]{2,1,0:T(8,128)S(1)}, u32[]{:S(2)}, u32[]{:S(2)}) collective-permute-start(f32[2,8,128]{2,1,0:T(8,128)S(1)} %maximum_select_fusion), channel_id=1, source_target_pairs={{0,128},{32,160},{1,129},{33,161},{2,130},{34,162},{3,131},{35,163... | collective-permute-start | bytes 24584 | tf_op jit(solution)/shard_map/ppermute | solution.py:479
  120.5 5.3 %collective-permute-start.16 = (f32[2,8,128]{2,1,0:T(8,128)S(1)}, f32[2,8,128]{2,1,0:T(8,128)S(1)}, u32[]{:S(2)}, u32[]{:S(2)}) collective-permute-start(f32[2,8,128]{2,1,0:T(8,128)S(1)} %fusion.2), channel_id=1, source_target_pairs={{0,64},{32,96},{128,192},{160,224},{1,65},{33,97},{129,193},{161,2... | collective-permute-start | bytes 24584 | tf_op jit(solution)/shard_map/ppermute | solution.py:480
  121.8 1.2 copy-start.1
  123.0 10.8 %copy-start.2 = (f32[8,256,128]{2,1,0:T(8,128)S(1)}, f32[8,256,128]{2,1,0:T(8,128)}, u32[]{:S(2)}) copy-start(f32[8,256,128]{2,1,0:T(8,128)} %get-tuple-element.39.f_ref) | copy-start | bytes 3145732
  125.8 5.7 %collective-permute-start.17 = (f32[2,8,128]{2,1,0:T(8,128)S(1)}, f32[2,8,128]{2,1,0:T(8,128)S(1)}, u32[]{:S(2)}, u32[]{:S(2)}) collective-permute-start(f32[2,8,128]{2,1,0:T(8,128)S(1)} %fusion.3.near_ref), channel_id=1, source_target_pairs={{0,256},{32,288},{64,320},{96,352},{128,384},{160,416},{192,448},{... | collective-permute-start | bytes 24584 | tf_op jit(solution)/shard_map/ppermute | solution.py:482

commit v12 on v11

--- a/solution.py
+++ b/solution.py
@@ -299,7 +299,7 @@
     row = lax.broadcasted_iota(jnp.int32, (128, 128), 0)
     lane = lax.broadcasted_iota(jnp.int32, (128, 128), 1)
     distance = (row + 2) >> 2
-    distance = jnp.where((((row + 2) >> 1) & 1) == (y & 1), distance, -distance)
+    distance = jnp.where(((row + 2) & 2) == 0, -distance, distance)
     piece = (y + distance) & 7
     target = (piece & 1) * 8 + (piece >> 1) * 2 + (row & 1)
     if home is None:
@@ -372,12 +372,8 @@
     return lax.all_to_all(copies, "domain", 0, 0)
 
 
-def ring_exchange(block, odd):
-    pairs = []
-    for z in range(2):
-        for y in range(odd, RING, 2):
-            here, there = z * RING + y, z * RING + (y + 1) % RING
-            pairs += [(here, there), (there, here)]
+def ring_shift(block, step):
+    pairs = [(z * RING + y, z * RING + (y + step) % RING) for z in range(2) for y in range(RING)]
     return lax.ppermute(block, "band", pairs)
 
 
@@ -434,17 +430,9 @@
         )(*sources)
 
     pieces = [piece]
-    up, down = ring_exchange(piece, 0), ring_exchange(piece, 1)
+    up, down = ring_shift(piece, 1), ring_shift(piece, -1)
     pieces += [up, down]
-    up, down = ring_exchange(down, 0), ring_exchange(up, 1)
-    sums = stage(range(6), (), pieces, sums)
-    down, sums = lax.optimization_barrier((down, sums))
-    pieces += [up, down]
-    up, down = ring_exchange(down, 0), ring_exchange(up, 1)
-    sums = stage(range(6, 10), (), pieces, sums)
-    down, sums, across, beside = lax.optimization_barrier((down, sums, across, beside))
-    pieces += [up, down]
-    up, down = ring_exchange(down[:1], 0), ring_exchange(up[1:], 1)
+    up, down = ring_shift(up, 1), ring_shift(down, -1)
     image, image_sums = call(
         image_kernel,
         (slab, tile),
@@ -452,6 +440,13 @@
         flops=50 * big,
         bytes_moved=20 * big,
     )(words, own, inner.reshape(flat), across, beside)
+    down, image, image_sums = lax.optimization_barrier((down, image, image_sums))
+    pieces += [up, down]
+    up, down = ring_shift(up, 1), ring_shift(down, -1)
+    sums = stage(range(10), (), pieces, sums)
+    down, sums = lax.optimization_barrier((down, sums))
+    pieces += [up, down]
+    up, down = ring_shift(up[:1], 1), ring_shift(down[1:], -1)
     sums = stage(range(10, 14), range(14), pieces, sums, image_sums)
     pieces += [up, down]
     sums = stage(range(14, 16), range(14, 16), pieces, sums, last=True)

time: 139 us -> 147 us (1.058)
  blocking collectives: 19.1 us -> 28.4 us
  waiting for transfers between devices: 28.3 us -> 24.4 us
  local copies, waits for them, and re-layouts: 1.25 us -> 3.44 us
  other arithmetic: 3.2 us -> 5.13 us
    ppermute x3, waiting for transfers between devices: 10.8 us -> 0.01 us  [local(): lax.ppermute(quarters[k], 'band', [(0, 2 * k), (1, 2 * k + 1)])]
    all_to_all x1, blocking collectives: 19.1 us -> 28.4 us  [domain_parts(): return lax.all_to_all(copies, 'domain', 0, 0)]
    ppermute x1, waiting for transfers between devices: 0.01 us -> 8.31 us  [local(): crossed = lax.ppermute(piece, 'band', [(y, y + RING) for y in range(RING)])]
    ppermute x8, waiting for transfers between devices: 11.7 us -> 7.45 us  [ring_shift(): return lax.ppermute(block, 'band', pairs)]
    ppermute x1, starting transfers between devices: 4.87 us -> 1.57 us  [local(): far = lax.ppermute(shared, 'band', [(y, y + RING) for y in range(RING)])]
    ppermute x1, waiting for transfers between devices: 0.78 us -> 3.48 us  [local(): far = lax.ppermute(shared, 'band', [(y, y + RING) for y in range(RING)])]
    unnamed x8 -> x12, local copies, waits for them, and re-layouts: 1.23 us -> 3.42 us
    pallas_call x4 -> x3, Pallas kernels: 6.2 us -> 6.15 us  [stage(): call(lambda *refs: stage_kernel(len(pieces), fresh, imaged, last, *refs),...]
  transfers between devices with their start and end apart: 20 -> 20, of which waited for: 9 -> 10; matrix products, arithmetic and copies ran while one was open for 0% -> 2% of each run, Pallas kernels for 12% -> 11%
where the time goes in v12:
time: 147 us; the launch traced here: 146 us
  starting transfers between devices  60.7 us (41%)
  blocking collectives  28.4 us (19%)
  waiting for transfers between devices  24.4 us (17%)
  Pallas kernels  23.1 us (16%)
  other arithmetic  5.13 us (3%)
  local copies, waits for them, and re-layouts  3.44 us (2%)
    all_to_all x1, blocking collectives, domain_parts(): return lax.all_to_all(copies, 'domain', 0, 0)  28.4 us
    ppermute x8, starting transfers between devices, ring_shift(): return lax.ppermute(block, 'band', pairs)  23.1 us
    ppermute x3, starting transfers between devices, local(): lax.ppermute(quarters[k], 'band', [(0, 2 * k), (1, 2 * k + 1)])  11.7 us
    ppermute x2, starting transfers between devices, neighbours(): lax.ppermute(block, 'domain', beside)  11 us
    ppermute x1, waiting for transfers between devices, local(): crossed = lax.ppermute(piece, 'band', [(y, y + RING) for y in range(RING)])  8.31 us
    ppermute x8, waiting for transfers between devices, ring_shift(): return lax.ppermute(block, 'band', pairs)  7.45 us
    ppermute x2, starting transfers between devices, neighbours(): lax.ppermute(block, 'domain', across)  6.92 us
    pallas_call x3, Pallas kernels, stage(): call(lambda *refs: stage_kernel(len(pieces), fresh, imaged, last, *refs),...  6.15 us
  transfers between devices with their start and end apart: 20, of which 10 were waited for; matrix products, arithmetic and copies ran while one was open for 2% of the time, Pallas kernels for 11%

profile of v12, /device:TPU:1, one launch (start us, length us, event | category | flops | bytes accessed | tf_op | source)
XLA Modules:
  0.0 146.0 jit_solution(7980932172545082980)
XLA Ops:
  0.7 2.2 %slice_select_fusion = (f32[2,4,64,128]{3,2,1,0:T(8,128)S(1)}, f32[2,4,64,128]{3,2,1,0:T(8,128)}, f32[2,4,64,128]{3,2,1,0:T(8,128)}, f32[2,4,64,128]{3,2,1,0:T(8,128)}) fusion(f32[8,4,64,128]{3,2,1,0:T(8,128)} %f_ref.1, pred[]{:T(512)S(6)} %lt.8), kind=kLoop, calls=%fused_computation.3 | loop fusion | flops 65536 | bytes 2097153 | tf_op jit(solution)/shard_map/jit(_where)/select_n | solution.py:415
  2.8 5.8 %collective-permute-start = (f32[2,256,128]{2,1,0:T(8,128)}, f32[2,256,128]{2,1,0:T(8,128)}, u32[]{:S(2)}, u32[]{:S(2)}) collective-permute-start(f32[2,256,128]{2,1,0:T(8,128)} %bitcast), channel_id=1, source_target_pairs={{0,64},{32,96},{1,65},{33,97},{2,66},{34,98},{3,67},{35,99},{4,68}... | collective-permute-start | bytes 786440 | tf_op jit(solution)/shard_map/ppermute | solution.py:411
  8.6 3.0 %collective-permute-start.1 = (f32[2,256,128]{2,1,0:T(8,128)}, f32[2,256,128]{2,1,0:T(8,128)}, u32[]{:S(2)}, u32[]{:S(2)}) collective-permute-start(f32[2,256,128]{2,1,0:T(8,128)} %bitcast.1), channel_id=1, source_target_pairs={{0,192},{32,224},{1,193},{33,225},{2,194},{34,226},{3,195},{35,227... | collective-permute-start | bytes 786440 | tf_op jit(solution)/shard_map/ppermute | solution.py:411
  11.6 2.9 %collective-permute-start.2 = (f32[2,256,128]{2,1,0:T(8,128)}, f32[2,256,128]{2,1,0:T(8,128)}, u32[]{:S(2)}, u32[]{:S(2)}) collective-permute-start(f32[2,256,128]{2,1,0:T(8,128)} %bitcast.2), channel_id=1, source_target_pairs={{0,128},{32,160},{1,129},{33,161},{2,130},{34,162},{3,131},{35,163... | collective-permute-start | bytes 786440 | tf_op jit(solution)/shard_map/ppermute | solution.py:411
  14.6 4.8 %collective-permute-start.8 = (f32[8,256,128]{2,1,0:T(8,128)S(1)}, f32[8,256,128]{2,1,0:T(8,128)S(1)}, u32[]{:S(2)}, u32[]{:S(2)}) collective-permute-start(f32[8,256,128]{2,1,0:T(8,128)S(1)} %bitcast.20), channel_id=1, source_target_pairs={{0,31},{1,2},{2,1},{3,4},{4,3},{5,6},{6,5},{7,8},{8,7},{9,10},{10,... | collective-permute-start | bytes 3145736 | tf_op jit(solution)/shard_map/ppermute | solution.py:384
  19.4 7.3 %collective-permute-start.9 = (f32[8,256,128]{2,1,0:T(8,128)S(1)}, f32[8,256,128]{2,1,0:T(8,128)S(1)}, u32[]{:S(2)}, u32[]{:S(2)}) collective-permute-start(f32[8,256,128]{2,1,0:T(8,128)S(1)} %bitcast.21), channel_id=1, source_target_pairs={{0,1},{1,0},{2,3},{3,2},{4,5},{5,4},{6,7},{7,6},{8,9},{9,8},{10,11... | collective-permute-start | bytes 3145736 | tf_op jit(solution)/shard_map/ppermute | solution.py:384
  26.7 3.3 %shard_map.41 = (f32[8,4,64,128]{3,2,1,0:T(8,128)S(1)}, f32[8,128]{1,0:T(8,128)S(1)}) custom-call(f32[8,4,64,128]{3,2,1,0:T(8,128)S(1)} %copy-done, f32[4,64,128]{2,1,0:T(8,128)S(1)} %copy-done.5), custom_call_target="tpu_custom_call" | custom-call | flops 15728640 | bytes 2097152 | tf_op jit(solution)/shard_map/pallas_call | solution.py:400
  34.2 8.3 %collective-permute-done.3 = f32[2,256,128]{2,1,0:T(8,128)S(1)} collective-permute-done((f32[2,256,128]{2,1,0:T(8,128)}, f32[2,256,128]{2,1,0:T(8,128)S(1)}, u32[]{:S(2)}, u32[]{:S(2)}) %collective-permute-start.3) | collective-permute-done | bytes 262176 | tf_op jit(solution)/shard_map/ppermute | solution.py:419
  43.5 3.1 %collective-permute-start.5 = (f32[2,256,128]{2,1,0:T(8,128)S(1)}, f32[2,256,128]{2,1,0:T(8,128)S(1)}, u32[]{:S(2)}, u32[]{:S(2)}) collective-permute-start(f32[2,256,128]{2,1,0:T(8,128)S(1)} %broadcast_select_fusion.refs_0_), channel_id=1, source_target_pairs={{0,224},{32,0},{64,32},{96,64},{128,96},{160,128},{192,160},{224,1... | collective-permute-start | bytes 786440 | tf_op jit(solution)/shard_map/ppermute | solution.py:377
  46.7 2.2 %collective-permute-start.4 = (f32[2,256,128]{2,1,0:T(8,128)S(1)}, f32[2,256,128]{2,1,0:T(8,128)S(1)}, u32[]{:S(2)}, u32[]{:S(2)}) collective-permute-start(f32[2,256,128]{2,1,0:T(8,128)S(1)} %broadcast_select_fusion.refs_0_), channel_id=1, source_target_pairs={{0,32},{32,64},{64,96},{96,128},{128,160},{160,192},{192,224},{224... | collective-permute-start | bytes 786440 | tf_op jit(solution)/shard_map/ppermute | solution.py:377
  50.7 4.3 %collective-permute-start.7 = (f32[2,256,128]{2,1,0:T(8,128)S(1)}, f32[2,256,128]{2,1,0:T(8,128)S(1)}, u32[]{:S(2)}, u32[]{:S(2)}) collective-permute-start(f32[2,256,128]{2,1,0:T(8,128)S(1)} %collective-permute-done.5.refs_2_), channel_id=1, source_target_pairs={{0,224},{32,0},{64,32},{96,64},{128,96},{160,128},{192,160},{224,1... | collective-permute-start | bytes 786440 | tf_op jit(solution)/shard_map/ppermute | solution.py:377
  60.2 4.0 %collective-permute-start.11 = (f32[2,256,128]{2,1,0:T(8,128)S(1)}, f32[2,256,128]{2,1,0:T(8,128)S(1)}, u32[]{:S(2)}, u32[]{:S(2)}) collective-permute-start(f32[2,256,128]{2,1,0:T(8,128)S(1)} %collective-permute-done.7.refs_4_), channel_id=1, source_target_pairs={{0,224},{32,0},{64,32},{96,64},{128,96},{160,128},{192,160},{224,1... | collective-permute-start | bytes 786440 | tf_op jit(solution)/shard_map/ppermute | solution.py:377
  70.2 3.1 %collective-permute-start.13 = (f32[1,256,128]{2,1,0:T(8,128)S(1)}, f32[1,256,128]{2,1,0:T(8,128)S(1)}, u32[]{:S(2)}, u32[]{:S(2)}) collective-permute-start(f32[1,256,128]{2,1,0:T(8,128)S(1)} %slice.36), channel_id=1, source_target_pairs={{0,224},{32,0},{64,32},{96,64},{128,96},{160,128},{192,160},{224,1... | collective-permute-start | bytes 393224 | tf_op jit(solution)/shard_map/ppermute | solution.py:377
  73.6 2.6 %collective-permute-start.12 = (f32[1,256,128]{2,1,0:T(8,128)S(1)}, f32[1,256,128]{2,1,0:T(8,128)S(1)}, u32[]{:S(2)}, u32[]{:S(2)}) collective-permute-start(f32[1,256,128]{2,1,0:T(8,128)S(1)} %slice.37), channel_id=1, source_target_pairs={{0,32},{32,64},{64,96},{96,128},{128,160},{160,192},{192,224},{224... | collective-permute-start | bytes 393224 | tf_op jit(solution)/shard_map/ppermute | solution.py:377
  76.2 3.0 %shard_map.44.refs_11_ = f32[8,128]{1,0:T(8,128)S(1)} custom-call(f32[2,256,128]{2,1,0:T(8,128)S(1)} %broadcast_select_fusion.refs_0_, f32[2,256,128]{2,1,0:T(8,128)S(1)} %collective-permute-done.4.refs_1_, f32[2,256,128]{2,1,0:T(8,128)S(1)} %collective-permute-done.5.refs_2_, f32[2,256,128]{2,1,0:T(8,128)S(1)} %collective-permute-done.6.refs_3_, ...), custom_call_target="tpu_custom_call" | custom-call | flops 5242880 | bytes 2621440 | tf_op jit(solution)/shard_map/pallas_call | solution.py:424
  79.2 2.9 %collective-permute-done.12.refs_7_ = f32[1,256,128]{2,1,0:T(8,128)S(1)} collective-permute-done((f32[1,256,128]{2,1,0:T(8,128)S(1)}, f32[1,256,128]{2,1,0:T(8,128)S(1)}, u32[]{:S(2)}, u32[]{:S(2)}) %collective-permute-start.12) | collective-permute-done | bytes 131104 | tf_op jit(solution)/shard_map/ppermute | solution.py:377
  83.1 28.4 %all_to_all.5.refs_0_ = f32[32,8,128]{2,1,0:T(8,128)S(1)} all-to-all(f32[32,8,128]{2,1,0:T(8,128)S(1)} %shard_map.45), channel_id=1, replica_groups=mesh['band'=16,'domain'=32] {'domain'}, dimensions={0} | all-to-all | bytes 262144 | tf_op jit(solution)/shard_map/all_to_all | solution.py:372
  111.6 4.3 %shard_map.47 = (f32[8,256,128]{2,1,0:T(8,128)}, f32[8,128]{1,0:T(8,128)S(1)}, f32[8,128]{1,0:T(8,128)S(1)}) custom-call(s32[2]{0:T(128)S(1)} %pad_add_fusion.words.band_ref, f32[8,128]{1,0:T(8,128)S(1)} %shard_map.46.sums_ref.own_ref, f32[2,256,128]{2,1,0:T(8,128)S(1)} %broadcast_select_fusion.refs_0_, f32[2,256,128]{2,1,0:T(8,128)S(1)} %collective-permute-done.4.refs_1_, ...), custom_call_target="tpu_custom_call" | custom-call | flops 12582912 | bytes 4194304 | tf_op jit(solution)/shard_map/pallas_call | solution.py:460
  115.9 2.1 %collective-permute-start.18 = (f32[8,256,128]{2,1,0:T(8,128)}, f32[8,256,128]{2,1,0:T(8,128)S(1)}, u32[]{:S(2)}, u32[]{:S(2)}) collective-permute-start(f32[8,256,128]{2,1,0:T(8,128)} %get-tuple-element.37.f_ref), channel_id=1, source_target_pairs={{0,31},{1,2},{2,1},{3,4},{4,3},{5,6},{6,5},{7,8},{8,7},{9,10},{10,... | collective-permute-start | bytes 3145736 | tf_op jit(solution)/shard_map/ppermute | solution.py:384
  118.0 3.7 %collective-permute-start.19 = (f32[8,256,128]{2,1,0:T(8,128)}, f32[8,256,128]{2,1,0:T(8,128)S(1)}, u32[]{:S(2)}, u32[]{:S(2)}) collective-permute-start(f32[8,256,128]{2,1,0:T(8,128)} %get-tuple-element.37.f_ref), channel_id=1, source_target_pairs={{0,1},{1,0},{2,3},{3,2},{4,5},{5,4},{6,7},{7,6},{8,9},{9,8},{10,11... | collective-permute-start | bytes 3145736 | tf_op jit(solution)/shard_map/ppermute | solution.py:384
  123.6 2.7 %collective-permute-done.14 = f32[8,128]{1,0:T(8,128)S(1)} collective-permute-done((f32[8,128]{1,0:T(8,128)S(1)}, f32[8,128]{1,0:T(8,128)S(1)}, u32[]{:S(2)}, u32[]{:S(2)}) %collective-permute-start.14) | collective-permute-done | bytes 4128 | tf_op jit(solution)/shard_map/ppermute | solution.py:471
  131.5 2.7 %shard_map.48 = f32[8,4,64,128]{3,2,1,0:T(8,128)S(1)} custom-call(f32[8,4,64,128]{3,2,1,0:T(8,128)S(1)} %bitcast.28, f32[4,64,128]{2,1,0:T(8,128)S(1)} %copy-done.5), custom_call_target="tpu_custom_call" | custom-call | flops 15728640 | bytes 2097152 | tf_op jit(solution)/shard_map/pallas_call | solution.py:400
  135.9 3.5 %collective-permute-done.17.far_ref = f32[2,8,128]{2,1,0:T(8,128)S(1)} collective-permute-done((f32[2,8,128]{2,1,0:T(8,128)S(1)}, f32[2,8,128]{2,1,0:T(8,128)S(1)}, u32[]{:S(2)}, u32[]{:S(2)}) %collective-permute-start.17) | collective-permute-done | bytes 8224 | tf_op jit(solution)/shard_map/ppermute | solution.py:477
  139.3 2.4 %shard_map.49.splat = f32[8,8,128]{2,1,0:T(8,128)S(1)} custom-call(s32[2]{0:T(128)S(1)} %pad_add_fusion.words.band_ref, f32[8,128]{1,0:T(8,128)S(1)} %get-tuple-element.39.weights_ref, f32[8,128]{1,0:T(8,128)S(1)} %get-tuple-element.40.gram_ref, f32[8,128]{1,0:T(8,128)S(1)} %shard_map.46.sums_ref.own_ref, f32[2,8,128]{2,1,0:T(8,128)S(1)} %fusion.3.near_ref, ...), custom_call_target="tpu_custom_call" | custom-call | tf_op jit(solution)/shard_map/pallas_call | solution.py:478
  (50 shorter events, 32.4 us)
Async XLA Ops:
  0.6 14.0 %copy-start = (f32[8,4,64,128]{3,2,1,0:T(8,128)S(1)}, f32[8,4,64,128]{3,2,1,0:T(8,128)}, u32[]{:S(2)}) copy-start(f32[8,4,64,128]{3,2,1,0:T(8,128)} %f_ref.1) | copy-start | bytes 3145732
  0.6 26.1 %copy-start.5 = (f32[4,64,128]{2,1,0:T(8,128)S(1)}, f32[4,64,128]{2,1,0:T(8,128)}, u32[]{:S(2)}) copy-start(f32[4,64,128]{2,1,0:T(8,128)} %v_ref.3) | copy-start | bytes 393220
  2.8 28.2 %collective-permute-start = (f32[2,256,128]{2,1,0:T(8,128)}, f32[2,256,128]{2,1,0:T(8,128)}, u32[]{:S(2)}, u32[]{:S(2)}) collective-permute-start(f32[2,256,128]{2,1,0:T(8,128)} %bitcast), channel_id=1, source_target_pairs={{0,64},{32,96},{1,65},{33,97},{2,66},{34,98},{3,67},{35,99},{4,68}... | collective-permute-start | bytes 786440 | tf_op jit(solution)/shard_map/ppermute | solution.py:411
  8.6 22.5 %collective-permute-start.1 = (f32[2,256,128]{2,1,0:T(8,128)}, f32[2,256,128]{2,1,0:T(8,128)}, u32[]{:S(2)}, u32[]{:S(2)}) collective-permute-start(f32[2,256,128]{2,1,0:T(8,128)} %bitcast.1), channel_id=1, source_target_pairs={{0,192},{32,224},{1,193},{33,225},{2,194},{34,226},{3,195},{35,227... | collective-permute-start | bytes 786440 | tf_op jit(solution)/shard_map/ppermute | solution.py:411
  11.6 19.4 %collective-permute-start.2 = (f32[2,256,128]{2,1,0:T(8,128)}, f32[2,256,128]{2,1,0:T(8,128)}, u32[]{:S(2)}, u32[]{:S(2)}) collective-permute-start(f32[2,256,128]{2,1,0:T(8,128)} %bitcast.2), channel_id=1, source_target_pairs={{0,128},{32,160},{1,129},{33,161},{2,130},{34,162},{3,131},{35,163... | collective-permute-start | bytes 786440 | tf_op jit(solution)/shard_map/ppermute | solution.py:411
  14.6 42.3 %collective-permute-start.8 = (f32[8,256,128]{2,1,0:T(8,128)S(1)}, f32[8,256,128]{2,1,0:T(8,128)S(1)}, u32[]{:S(2)}, u32[]{:S(2)}) collective-permute-start(f32[8,256,128]{2,1,0:T(8,128)S(1)} %bitcast.20), channel_id=1, source_target_pairs={{0,31},{1,2},{2,1},{3,4},{4,3},{5,6},{6,5},{7,8},{8,7},{9,10},{10,... | collective-permute-start | bytes 3145736 | tf_op jit(solution)/shard_map/ppermute | solution.py:384
  19.4 37.5 %collective-permute-start.9 = (f32[8,256,128]{2,1,0:T(8,128)S(1)}, f32[8,256,128]{2,1,0:T(8,128)S(1)}, u32[]{:S(2)}, u32[]{:S(2)}) collective-permute-start(f32[8,256,128]{2,1,0:T(8,128)S(1)} %bitcast.21), channel_id=1, source_target_pairs={{0,1},{1,0},{2,3},{3,2},{4,5},{5,4},{6,7},{7,6},{8,9},{9,8},{10,11... | collective-permute-start | bytes 3145736 | tf_op jit(solution)/shard_map/ppermute | solution.py:384
  32.9 9.6 %collective-permute-start.3 = (f32[2,256,128]{2,1,0:T(8,128)}, f32[2,256,128]{2,1,0:T(8,128)S(1)}, u32[]{:S(2)}, u32[]{:S(2)}) collective-permute-start(f32[2,256,128]{2,1,0:T(8,128)} %fusion.1), channel_id=1, source_target_pairs={{0,256},{32,288},{64,320},{96,352},{128,384},{160,416},{192,448},{... | collective-permute-start | bytes 786440 | tf_op jit(solution)/shard_map/ppermute | solution.py:419
  43.5 7.1 %collective-permute-start.5 = (f32[2,256,128]{2,1,0:T(8,128)S(1)}, f32[2,256,128]{2,1,0:T(8,128)S(1)}, u32[]{:S(2)}, u32[]{:S(2)}) collective-permute-start(f32[2,256,128]{2,1,0:T(8,128)S(1)} %broadcast_select_fusion.refs_0_), channel_id=1, source_target_pairs={{0,224},{32,0},{64,32},{96,64},{128,96},{160,128},{192,160},{224,1... | collective-permute-start | bytes 786440 | tf_op jit(solution)/shard_map/ppermute | solution.py:377
  46.7 8.3 %collective-permute-start.4 = (f32[2,256,128]{2,1,0:T(8,128)S(1)}, f32[2,256,128]{2,1,0:T(8,128)S(1)}, u32[]{:S(2)}, u32[]{:S(2)}) collective-permute-start(f32[2,256,128]{2,1,0:T(8,128)S(1)} %broadcast_select_fusion.refs_0_), channel_id=1, source_target_pairs={{0,32},{32,64},{64,96},{96,128},{128,160},{160,192},{192,224},{224... | collective-permute-start | bytes 786440 | tf_op jit(solution)/shard_map/ppermute | solution.py:377
  50.7 9.6 %collective-permute-start.7 = (f32[2,256,128]{2,1,0:T(8,128)S(1)}, f32[2,256,128]{2,1,0:T(8,128)S(1)}, u32[]{:S(2)}, u32[]{:S(2)}) collective-permute-start(f32[2,256,128]{2,1,0:T(8,128)S(1)} %collective-permute-done.5.refs_2_), channel_id=1, source_target_pairs={{0,224},{32,0},{64,32},{96,64},{128,96},{160,128},{192,160},{224,1... | collective-permute-start | bytes 786440 | tf_op jit(solution)/shard_map/ppermute | solution.py:377
  55.0 9.3 %collective-permute-start.6 = (f32[2,256,128]{2,1,0:T(8,128)S(1)}, f32[2,256,128]{2,1,0:T(8,128)S(1)}, u32[]{:S(2)}, u32[]{:S(2)}) collective-permute-start(f32[2,256,128]{2,1,0:T(8,128)S(1)} %collective-permute-done.4.refs_1_), channel_id=1, source_target_pairs={{0,32},{32,64},{64,96},{96,128},{128,160},{160,192},{192,224},{224... | collective-permute-start | bytes 786440 | tf_op jit(solution)/shard_map/ppermute | solution.py:377
  56.9 1.2 copy-start.4
  60.2 9.9 %collective-permute-start.11 = (f32[2,256,128]{2,1,0:T(8,128)S(1)}, f32[2,256,128]{2,1,0:T(8,128)S(1)}, u32[]{:S(2)}, u32[]{:S(2)}) collective-permute-start(f32[2,256,128]{2,1,0:T(8,128)S(1)} %collective-permute-done.7.refs_4_), channel_id=1, source_target_pairs={{0,224},{32,0},{64,32},{96,64},{128,96},{160,128},{192,160},{224,1... | collective-permute-start | bytes 786440 | tf_op jit(solution)/shard_map/ppermute | solution.py:377
  64.3 9.3 %collective-permute-start.10 = (f32[2,256,128]{2,1,0:T(8,128)S(1)}, f32[2,256,128]{2,1,0:T(8,128)S(1)}, u32[]{:S(2)}, u32[]{:S(2)}) collective-permute-start(f32[2,256,128]{2,1,0:T(8,128)S(1)} %collective-permute-done.6.refs_3_), channel_id=1, source_target_pairs={{0,32},{32,64},{64,96},{96,128},{128,160},{160,192},{192,224},{224... | collective-permute-start | bytes 786440 | tf_op jit(solution)/shard_map/ppermute | solution.py:377
  70.2 9.0 %collective-permute-start.13 = (f32[1,256,128]{2,1,0:T(8,128)S(1)}, f32[1,256,128]{2,1,0:T(8,128)S(1)}, u32[]{:S(2)}, u32[]{:S(2)}) collective-permute-start(f32[1,256,128]{2,1,0:T(8,128)S(1)} %slice.36), channel_id=1, source_target_pairs={{0,224},{32,0},{64,32},{96,64},{128,96},{160,128},{192,160},{224,1... | collective-permute-start | bytes 393224 | tf_op jit(solution)/shard_map/ppermute | solution.py:377
  73.6 8.5 %collective-permute-start.12 = (f32[1,256,128]{2,1,0:T(8,128)S(1)}, f32[1,256,128]{2,1,0:T(8,128)S(1)}, u32[]{:S(2)}, u32[]{:S(2)}) collective-permute-start(f32[1,256,128]{2,1,0:T(8,128)S(1)} %slice.37), channel_id=1, source_target_pairs={{0,32},{32,64},{64,96},{96,128},{128,160},{160,192},{192,224},{224... | collective-permute-start | bytes 393224 | tf_op jit(solution)/shard_map/ppermute | solution.py:377
  115.9 28.1 %collective-permute-start.18 = (f32[8,256,128]{2,1,0:T(8,128)}, f32[8,256,128]{2,1,0:T(8,128)S(1)}, u32[]{:S(2)}, u32[]{:S(2)}) collective-permute-start(f32[8,256,128]{2,1,0:T(8,128)} %get-tuple-element.37.f_ref), channel_id=1, source_target_pairs={{0,31},{1,2},{2,1},{3,4},{4,3},{5,6},{6,5},{7,8},{8,7},{9,10},{10,... | collective-permute-start | bytes 3145736 | tf_op jit(solution)/shard_map/ppermute | solution.py:384
  118.0 26.0 %collective-permute-start.19 = (f32[8,256,128]{2,1,0:T(8,128)}, f32[8,256,128]{2,1,0:T(8,128)S(1)}, u32[]{:S(2)}, u32[]{:S(2)}) collective-permute-start(f32[8,256,128]{2,1,0:T(8,128)} %get-tuple-element.37.f_ref), channel_id=1, source_target_pairs={{0,1},{1,0},{2,3},{3,2},{4,5},{5,4},{6,7},{7,6},{8,9},{9,8},{10,11... | collective-permute-start | bytes 3145736 | tf_op jit(solution)/shard_map/ppermute | solution.py:384
  121.7 4.6 %collective-permute-start.14 = (f32[8,128]{1,0:T(8,128)S(1)}, f32[8,128]{1,0:T(8,128)S(1)}, u32[]{:S(2)}, u32[]{:S(2)}) collective-permute-start(f32[8,128]{1,0:T(8,128)S(1)} %shard_map.46.sums_ref.own_ref), channel_id=1, source_target_pairs={{0,32},{32,0},{1,33},{33,1},{2,34},{34,2},{3,35},{35,3},{4,36},{36... | collective-permute-start | bytes 12296 | tf_op jit(solution)/shard_map/ppermute | solution.py:471
  126.4 2.6 %collective-permute-start.15 = (f32[2,8,128]{2,1,0:T(8,128)S(1)}, f32[2,8,128]{2,1,0:T(8,128)S(1)}, u32[]{:S(2)}, u32[]{:S(2)}) collective-permute-start(f32[2,8,128]{2,1,0:T(8,128)S(1)} %maximum_select_fusion), channel_id=1, source_target_pairs={{0,128},{32,160},{1,129},{33,161},{2,130},{34,162},{3,131},{35,163... | collective-permute-start | bytes 24584 | tf_op jit(solution)/shard_map/ppermute | solution.py:474
  129.0 5.3 %collective-permute-start.16 = (f32[2,8,128]{2,1,0:T(8,128)S(1)}, f32[2,8,128]{2,1,0:T(8,128)S(1)}, u32[]{:S(2)}, u32[]{:S(2)}) collective-permute-start(f32[2,8,128]{2,1,0:T(8,128)S(1)} %fusion.2), channel_id=1, source_target_pairs={{0,64},{32,96},{128,192},{160,224},{1,65},{33,97},{129,193},{161,2... | collective-permute-start | bytes 24584 | tf_op jit(solution)/shard_map/ppermute | solution.py:475
  131.5 10.2 %copy-start.2 = (f32[8,256,128]{2,1,0:T(8,128)S(1)}, f32[8,256,128]{2,1,0:T(8,128)}, u32[]{:S(2)}) copy-start(f32[8,256,128]{2,1,0:T(8,128)} %get-tuple-element.37.f_ref) | copy-start | bytes 3145732
  134.3 5.1 %collective-permute-start.17 = (f32[2,8,128]{2,1,0:T(8,128)S(1)}, f32[2,8,128]{2,1,0:T(8,128)S(1)}, u32[]{:S(2)}, u32[]{:S(2)}) collective-permute-start(f32[2,8,128]{2,1,0:T(8,128)S(1)} %fusion.3.near_ref), channel_id=1, source_target_pairs={{0,256},{32,288},{64,320},{96,352},{128,384},{160,416},{192,448},{... | collective-permute-start | bytes 24584 | tf_op jit(solution)/shard_map/ppermute | solution.py:477
  (2 other events, 2.2 us)

commit v13 on v12

--- a/solution.py
+++ b/solution.py
@@ -415,9 +415,10 @@
     piece = jnp.where(band < 2, quarters[0], 0.0)
     for part in arrived:
         piece = piece + part
-    across, beside = neighbours(own)
     crossed = lax.ppermute(piece, "band", [(y, y + RING) for y in range(RING)])
     piece = jnp.where(band < RING, piece, crossed)
+    piece, raw = lax.optimization_barrier((piece, own))
+    across, beside = neighbours(raw)
 
     def stage(fresh, imaged, pieces, *sums, last=False):
         sources = (*pieces, own, *((image,) if imaged else ()), *sums)
@@ -433,6 +434,14 @@
     up, down = ring_shift(piece, 1), ring_shift(piece, -1)
     pieces += [up, down]
     up, down = ring_shift(up, 1), ring_shift(down, -1)
+    sums = stage(range(6), (), pieces, sums)
+    down, sums = lax.optimization_barrier((down, sums))
+    pieces += [up, down]
+    up, down = ring_shift(up, 1), ring_shift(down, -1)
+    sums = stage(range(6, 10), (), pieces, sums)
+    down, sums = lax.optimization_barrier((down, sums))
+    pieces += [up, down]
+    up, down = ring_shift(up[:1], 1), ring_shift(down[1:], -1)
     image, image_sums = call(
         image_kernel,
         (slab, tile),
@@ -440,13 +449,6 @@
         flops=50 * big,
         bytes_moved=20 * big,
     )(words, own, inner.reshape(flat), across, beside)
-    down, image, image_sums = lax.optimization_barrier((down, image, image_sums))
-    pieces += [up, down]
-    up, down = ring_shift(up, 1), ring_shift(down, -1)
-    sums = stage(range(10), (), pieces, sums)
-    down, sums = lax.optimization_barrier((down, sums))
-    pieces += [up, down]
-    up, down = ring_shift(up[:1], 1), ring_shift(down[1:], -1)
     sums = stage(range(10, 14), range(14), pieces, sums, image_sums)
     pieces += [up, down]
     sums = stage(range(14, 16), range(14, 16), pieces, sums, last=True)

time: 147 us -> 147 us (level)
  blocking collectives: 28.4 us -> 19.1 us
  starting transfers between devices: 60.7 us -> 67.6 us
  waiting for transfers between devices: 24.4 us -> 30.8 us
  local copies, waits for them, and re-layouts: 3.44 us -> 1.25 us
  other arithmetic: 5.13 us -> 3.2 us
    ppermute x3, waiting for transfers between devices: 0.01 us -> 10.8 us  [local(): lax.ppermute(quarters[k], 'band', [(0, 2 * k), (1, 2 * k + 1)])]
    ppermute x2, starting transfers between devices: 6.92 us -> 17.3 us  [neighbours(): lax.ppermute(block, 'domain', across)]
    all_to_all x1, blocking collectives: 28.4 us -> 19.1 us  [domain_parts(): return lax.all_to_all(copies, 'domain', 0, 0)]
    ppermute x2, starting transfers between devices: 11 us -> 5.6 us  [neighbours(): lax.ppermute(block, 'domain', beside)]
    ppermute x1, waiting for transfers between devices: 8.31 us -> 5.33 us  [local(): crossed = lax.ppermute(piece, 'band', [(y, y + RING) for y in range(RING)])]
    ppermute x8, starting transfers between devices: 23.1 us -> 25.6 us  [ring_shift(): return lax.ppermute(block, 'band', pairs)]
    unnamed x12 -> x8, local copies, waits for them, and re-layouts: 3.42 us -> 1.23 us
    pallas_call x3 -> x4, Pallas kernels: 6.15 us -> 6.19 us  [stage(): call(lambda *refs: stage_kernel(len(pieces), fresh, imaged, last, *refs),...]
  transfers between devices with their start and end apart: 20 -> 20, of which waited for: 10 -> 12; matrix products, arithmetic and copies ran while one was open for 2% -> 0% of each run, Pallas kernels for 11% -> 11%
where the time goes in v13:
time: 147 us; the launch traced here: 146 us
  starting transfers between devices  67.6 us (46%)
  waiting for transfers between devices  30.8 us (21%)
  Pallas kernels  23.1 us (16%)
  blocking collectives  19.1 us (13%)
  other arithmetic  3.2 us (2%)
    ppermute x8, starting transfers between devices, ring_shift(): return lax.ppermute(block, 'band', pairs)  25.6 us
    all_to_all x1, blocking collectives, domain_parts(): return lax.all_to_all(copies, 'domain', 0, 0)  19.1 us
    ppermute x2, starting transfers between devices, neighbours(): lax.ppermute(block, 'domain', across)  17.3 us
    ppermute x3, waiting for transfers between devices, local(): lax.ppermute(quarters[k], 'band', [(0, 2 * k), (1, 2 * k + 1)])  10.8 us
    ppermute x3, starting transfers between devices, local(): lax.ppermute(quarters[k], 'band', [(0, 2 * k), (1, 2 * k + 1)])  10.3 us
    ppermute x8, waiting for transfers between devices, ring_shift(): return lax.ppermute(block, 'band', pairs)  7.05 us
    pallas_call x4, Pallas kernels, stage(): call(lambda *refs: stage_kernel(len(pieces), fresh, imaged, last, *refs),...  6.19 us
    pallas_call x2, Pallas kernels, inner_part(): call(inner_kernel, (field, *sums), specs=[VMEM] * 2, flops=60 * big, byte...  6.03 us
  transfers between devices with their start and end apart: 20, of which 12 were waited for; matrix products, arithmetic and copies ran while one was open for 0% of the time, Pallas kernels for 11%

profile of v13, /device:TPU:1, one launch (start us, length us, event | category | flops | bytes accessed | tf_op | source)
XLA Modules:
  0.0 146.1 jit_solution(11198764995910220566)
XLA Ops:
  0.7 2.1 %slice_select_fusion = (f32[2,4,64,128]{3,2,1,0:T(8,128)S(1)}, f32[2,4,64,128]{3,2,1,0:T(8,128)S(1)}, f32[2,4,64,128]{3,2,1,0:T(8,128)S(1)}, f32[2,4,64,128]{3,2,1,0:T(8,128)}) fusion(f32[8,4,64,128]{3,2,1,0:T(8,128)} %f_ref.1, pred[]{:T(512)S(6)} %lt.8), kind=kLoop, calls=%fused_computation.3 | loop fusion | flops 65536 | bytes 2097153 | tf_op jit(solution)/shard_map/jit(_where)/select_n | solution.py:415
  2.7 5.0 %collective-permute-start = (f32[2,256,128]{2,1,0:T(8,128)}, f32[2,256,128]{2,1,0:T(8,128)S(1)}, u32[]{:S(2)}, u32[]{:S(2)}) collective-permute-start(f32[2,256,128]{2,1,0:T(8,128)} %bitcast), channel_id=1, source_target_pairs={{0,64},{32,96},{1,65},{33,97},{2,66},{34,98},{3,67},{35,99},{4,68}... | collective-permute-start | bytes 786440 | tf_op jit(solution)/shard_map/ppermute | solution.py:411
  7.8 2.3 %collective-permute-start.1 = (f32[2,256,128]{2,1,0:T(8,128)S(1)}, f32[2,256,128]{2,1,0:T(8,128)S(1)}, u32[]{:S(2)}, u32[]{:S(2)}) collective-permute-start(f32[2,256,128]{2,1,0:T(8,128)S(1)} %bitcast.34), channel_id=1, source_target_pairs={{0,192},{32,224},{1,193},{33,225},{2,194},{34,226},{3,195},{35,227... | collective-permute-start | bytes 786440 | tf_op jit(solution)/shard_map/ppermute | solution.py:411
  10.1 3.0 %collective-permute-start.2 = (f32[2,256,128]{2,1,0:T(8,128)S(1)}, f32[2,256,128]{2,1,0:T(8,128)}, u32[]{:S(2)}, u32[]{:S(2)}) collective-permute-start(f32[2,256,128]{2,1,0:T(8,128)S(1)} %bitcast.33), channel_id=1, source_target_pairs={{0,128},{32,160},{1,129},{33,161},{2,130},{34,162},{3,131},{35,163... | collective-permute-start | bytes 786440 | tf_op jit(solution)/shard_map/ppermute | solution.py:411
  13.1 3.3 %shard_map.41 = (f32[8,4,64,128]{3,2,1,0:T(8,128)S(1)}, f32[8,128]{1,0:T(8,128)S(1)}) custom-call(f32[8,4,64,128]{3,2,1,0:T(8,128)S(1)} %copy-done, f32[4,64,128]{2,1,0:T(8,128)S(1)} %copy-done.3), custom_call_target="tpu_custom_call" | custom-call | flops 15728640 | bytes 2097152 | tf_op jit(solution)/shard_map/pallas_call | solution.py:400
  16.4 10.8 %collective-permute-done.1 = f32[2,256,128]{2,1,0:T(8,128)S(1)} collective-permute-done((f32[2,256,128]{2,1,0:T(8,128)S(1)}, f32[2,256,128]{2,1,0:T(8,128)S(1)}, u32[]{:S(2)}, u32[]{:S(2)}) %collective-permute-start.1) | collective-permute-done | bytes 262176 | tf_op jit(solution)/shard_map/ppermute | solution.py:411
  29.6 5.3 %collective-permute-done.3 = f32[2,256,128]{2,1,0:T(8,128)S(1)} collective-permute-done((f32[2,256,128]{2,1,0:T(8,128)S(1)}, f32[2,256,128]{2,1,0:T(8,128)S(1)}, u32[]{:S(2)}, u32[]{:S(2)}) %collective-permute-start.3) | collective-permute-done | bytes 262176 | tf_op jit(solution)/shard_map/ppermute | solution.py:418
  34.9 15.2 %collective-permute-start.12 = (f32[8,256,128]{2,1,0:T(8,128)S(1)}, f32[8,256,128]{2,1,0:T(8,128)S(1)}, u32[]{:S(2)}, u32[]{:S(2)}) collective-permute-start(f32[8,256,128]{2,1,0:T(8,128)S(1)} %bitcast.20), channel_id=1, source_target_pairs={{0,31},{1,2},{2,1},{3,4},{4,3},{5,6},{6,5},{7,8},{8,7},{9,10},{10,... | collective-permute-start | bytes 3145736 | tf_op jit(solution)/shard_map/ppermute | solution.py:384
  54.0 3.4 %collective-permute-start.4 = (f32[2,256,128]{2,1,0:T(8,128)S(1)}, f32[2,256,128]{2,1,0:T(8,128)S(1)}, u32[]{:S(2)}, u32[]{:S(2)}) collective-permute-start(f32[2,256,128]{2,1,0:T(8,128)S(1)} %broadcast_select_fusion.refs_0_), channel_id=1, source_target_pairs={{0,32},{32,64},{64,96},{96,128},{128,160},{160,192},{192,224},{224... | collective-permute-start | bytes 786440 | tf_op jit(solution)/shard_map/ppermute | solution.py:377
  57.4 4.0 %collective-permute-done.5.refs_2_ = f32[2,256,128]{2,1,0:T(8,128)S(1)} collective-permute-done((f32[2,256,128]{2,1,0:T(8,128)S(1)}, f32[2,256,128]{2,1,0:T(8,128)S(1)}, u32[]{:S(2)}, u32[]{:S(2)}) %collective-permute-start.5) | collective-permute-done | bytes 262176 | tf_op jit(solution)/shard_map/ppermute | solution.py:377
  61.3 4.3 %collective-permute-start.7 = (f32[2,256,128]{2,1,0:T(8,128)S(1)}, f32[2,256,128]{2,1,0:T(8,128)S(1)}, u32[]{:S(2)}, u32[]{:S(2)}) collective-permute-start(f32[2,256,128]{2,1,0:T(8,128)S(1)} %collective-permute-done.5.refs_2_), channel_id=1, source_target_pairs={{0,224},{32,0},{64,32},{96,64},{128,96},{160,128},{192,160},{224,1... | collective-permute-start | bytes 786440 | tf_op jit(solution)/shard_map/ppermute | solution.py:377
  69.8 5.3 %collective-permute-start.9 = (f32[2,256,128]{2,1,0:T(8,128)S(1)}, f32[2,256,128]{2,1,0:T(8,128)S(1)}, u32[]{:S(2)}, u32[]{:S(2)}) collective-permute-start(f32[2,256,128]{2,1,0:T(8,128)S(1)} %collective-permute-done.7.refs_4_), channel_id=1, source_target_pairs={{0,224},{32,0},{64,32},{96,64},{128,96},{160,128},{192,160},{224,1... | collective-permute-start | bytes 786440 | tf_op jit(solution)/shard_map/ppermute | solution.py:377
  78.8 5.0 %collective-permute-start.11 = (f32[1,256,128]{2,1,0:T(8,128)S(1)}, f32[1,256,128]{2,1,0:T(8,128)S(1)}, u32[]{:S(2)}, u32[]{:S(2)}) collective-permute-start(f32[1,256,128]{2,1,0:T(8,128)S(1)} %slice.36), channel_id=1, source_target_pairs={{0,224},{32,0},{64,32},{96,64},{128,96},{160,128},{192,160},{224,1... | collective-permute-start | bytes 393224 | tf_op jit(solution)/shard_map/ppermute | solution.py:377
  88.0 3.1 %shard_map.45.refs_11_ = f32[8,128]{1,0:T(8,128)S(1)} custom-call(f32[2,256,128]{2,1,0:T(8,128)S(1)} %broadcast_select_fusion.refs_0_, f32[2,256,128]{2,1,0:T(8,128)S(1)} %collective-permute-done.4.refs_1_, f32[2,256,128]{2,1,0:T(8,128)S(1)} %collective-permute-done.5.refs_2_, f32[2,256,128]{2,1,0:T(8,128)S(1)} %collective-permute-done.6.refs_3_, ...), custom_call_target="tpu_custom_call" | custom-call | flops 5242880 | bytes 2621440 | tf_op jit(solution)/shard_map/pallas_call | solution.py:425
  92.5 19.1 %all_to_all.5.refs_0_ = f32[32,8,128]{2,1,0:T(8,128)S(1)} all-to-all(f32[32,8,128]{2,1,0:T(8,128)S(1)} %shard_map.46), channel_id=1, replica_groups=mesh['band'=16,'domain'=32] {'domain'}, dimensions={0} | all-to-all | bytes 262144 | tf_op jit(solution)/shard_map/all_to_all | solution.py:372
  111.7 4.3 %shard_map.48 = (f32[8,256,128]{2,1,0:T(8,128)}, f32[8,128]{1,0:T(8,128)S(1)}, f32[8,128]{1,0:T(8,128)S(1)}) custom-call(s32[2]{0:T(128)S(1)} %pad_add_fusion.words.band_ref, f32[8,128]{1,0:T(8,128)S(1)} %shard_map.47.sums_ref.own_ref, f32[2,256,128]{2,1,0:T(8,128)S(1)} %broadcast_select_fusion.refs_0_, f32[2,256,128]{2,1,0:T(8,128)S(1)} %collective-permute-done.4.refs_1_, ...), custom_call_target="tpu_custom_call" | custom-call | flops 12582912 | bytes 4194304 | tf_op jit(solution)/shard_map/pallas_call | solution.py:462
  116.0 2.1 %collective-permute-start.18 = (f32[8,256,128]{2,1,0:T(8,128)}, f32[8,256,128]{2,1,0:T(8,128)S(1)}, u32[]{:S(2)}, u32[]{:S(2)}) collective-permute-start(f32[8,256,128]{2,1,0:T(8,128)} %get-tuple-element.39.f_ref), channel_id=1, source_target_pairs={{0,31},{1,2},{2,1},{3,4},{4,3},{5,6},{6,5},{7,8},{8,7},{9,10},{10,... | collective-permute-start | bytes 3145736 | tf_op jit(solution)/shard_map/ppermute | solution.py:384
  118.1 3.7 %collective-permute-start.19 = (f32[8,256,128]{2,1,0:T(8,128)}, f32[8,256,128]{2,1,0:T(8,128)S(1)}, u32[]{:S(2)}, u32[]{:S(2)}) collective-permute-start(f32[8,256,128]{2,1,0:T(8,128)} %get-tuple-element.39.f_ref), channel_id=1, source_target_pairs={{0,1},{1,0},{2,3},{3,2},{4,5},{5,4},{6,7},{7,6},{8,9},{9,8},{10,11... | collective-permute-start | bytes 3145736 | tf_op jit(solution)/shard_map/ppermute | solution.py:384
  123.7 2.7 %collective-permute-done.14 = f32[8,128]{1,0:T(8,128)S(1)} collective-permute-done((f32[8,128]{1,0:T(8,128)S(1)}, f32[8,128]{1,0:T(8,128)S(1)}, u32[]{:S(2)}, u32[]{:S(2)}) %collective-permute-start.14) | collective-permute-done | bytes 4128 | tf_op jit(solution)/shard_map/ppermute | solution.py:473
  131.0 2.7 %shard_map.49 = f32[8,4,64,128]{3,2,1,0:T(8,128)S(1)} custom-call(f32[8,4,64,128]{3,2,1,0:T(8,128)S(1)} %bitcast.29, f32[4,64,128]{2,1,0:T(8,128)S(1)} %copy-done.3), custom_call_target="tpu_custom_call" | custom-call | flops 15728640 | bytes 2097152 | tf_op jit(solution)/shard_map/pallas_call | solution.py:400
  133.8 3.0 %collective-permute-start.17 = (f32[2,8,128]{2,1,0:T(8,128)S(1)}, f32[2,8,128]{2,1,0:T(8,128)S(1)}, u32[]{:S(2)}, u32[]{:S(2)}) collective-permute-start(f32[2,8,128]{2,1,0:T(8,128)S(1)} %fusion.3.near_ref), channel_id=1, source_target_pairs={{0,256},{32,288},{64,320},{96,352},{128,384},{160,416},{192,448},{... | collective-permute-start | bytes 24584 | tf_op jit(solution)/shard_map/ppermute | solution.py:479
  136.9 2.6 %collective-permute-done.17.far_ref = f32[2,8,128]{2,1,0:T(8,128)S(1)} collective-permute-done((f32[2,8,128]{2,1,0:T(8,128)S(1)}, f32[2,8,128]{2,1,0:T(8,128)S(1)}, u32[]{:S(2)}, u32[]{:S(2)}) %collective-permute-start.17) | collective-permute-done | bytes 8224 | tf_op jit(solution)/shard_map/ppermute | solution.py:479
  139.4 2.4 %shard_map.50.splat = f32[8,8,128]{2,1,0:T(8,128)S(1)} custom-call(s32[2]{0:T(128)S(1)} %pad_add_fusion.words.band_ref, f32[8,128]{1,0:T(8,128)S(1)} %get-tuple-element.41.weights_ref, f32[8,128]{1,0:T(8,128)S(1)} %get-tuple-element.42.gram_ref, f32[8,128]{1,0:T(8,128)S(1)} %shard_map.47.sums_ref.own_ref, f32[2,8,128]{2,1,0:T(8,128)S(1)} %fusion.3.near_ref, ...), custom_call_target="tpu_custom_call" | custom-call | tf_op jit(solution)/shard_map/pallas_call | solution.py:480
  144.1 2.0 %shard_map.52 = f32[8,256,128]{2,1,0:T(8,128)} custom-call(s32[2]{0:T(128)S(1)} %pad_add_fusion.words.band_ref, f32[8,256,128]{2,1,0:T(8,128)S(1)} %shard_map.51.partial, f32[8,256,128]{2,1,0:T(8,128)S(1)} %collective-permute-done.18.across, f32[8,256,128]{2,1,0:T(8,128)S(1)} %collective-permute-done.19.beside), custom_call_target="tpu_custom_call" | custom-call | flops 5242880 | bytes 4194304 | tf_op jit(solution)/shard_map/pallas_call | solution.py:486
  (47 shorter events, 28.6 us)
Async XLA Ops:
  0.6 12.4 %copy-start = (f32[8,4,64,128]{3,2,1,0:T(8,128)S(1)}, f32[8,4,64,128]{3,2,1,0:T(8,128)}, u32[]{:S(2)}) copy-start(f32[8,4,64,128]{3,2,1,0:T(8,128)} %f_ref.1) | copy-start | bytes 3145732
  0.6 12.4 %copy-start.3 = (f32[4,64,128]{2,1,0:T(8,128)S(1)}, f32[4,64,128]{2,1,0:T(8,128)}, u32[]{:S(2)}) copy-start(f32[4,64,128]{2,1,0:T(8,128)} %v_ref.3) | copy-start | bytes 393220
  2.7 13.7 %collective-permute-start = (f32[2,256,128]{2,1,0:T(8,128)}, f32[2,256,128]{2,1,0:T(8,128)S(1)}, u32[]{:S(2)}, u32[]{:S(2)}) collective-permute-start(f32[2,256,128]{2,1,0:T(8,128)} %bitcast), channel_id=1, source_target_pairs={{0,64},{32,96},{1,65},{33,97},{2,66},{34,98},{3,67},{35,99},{4,68}... | collective-permute-start | bytes 786440 | tf_op jit(solution)/shard_map/ppermute | solution.py:411
  7.8 19.5 %collective-permute-start.1 = (f32[2,256,128]{2,1,0:T(8,128)S(1)}, f32[2,256,128]{2,1,0:T(8,128)S(1)}, u32[]{:S(2)}, u32[]{:S(2)}) collective-permute-start(f32[2,256,128]{2,1,0:T(8,128)S(1)} %bitcast.34), channel_id=1, source_target_pairs={{0,192},{32,224},{1,193},{33,225},{2,194},{34,226},{3,195},{35,227... | collective-permute-start | bytes 786440 | tf_op jit(solution)/shard_map/ppermute | solution.py:411
  10.1 17.1 %collective-permute-start.2 = (f32[2,256,128]{2,1,0:T(8,128)S(1)}, f32[2,256,128]{2,1,0:T(8,128)}, u32[]{:S(2)}, u32[]{:S(2)}) collective-permute-start(f32[2,256,128]{2,1,0:T(8,128)S(1)} %bitcast.33), channel_id=1, source_target_pairs={{0,128},{32,160},{1,129},{33,161},{2,130},{34,162},{3,131},{35,163... | collective-permute-start | bytes 786440 | tf_op jit(solution)/shard_map/ppermute | solution.py:411
  28.3 6.6 %collective-permute-start.3 = (f32[2,256,128]{2,1,0:T(8,128)S(1)}, f32[2,256,128]{2,1,0:T(8,128)S(1)}, u32[]{:S(2)}, u32[]{:S(2)}) collective-permute-start(f32[2,256,128]{2,1,0:T(8,128)S(1)} %fusion.1), channel_id=1, source_target_pairs={{0,256},{32,288},{64,320},{96,352},{128,384},{160,416},{192,448},{... | collective-permute-start | bytes 786440 | tf_op jit(solution)/shard_map/ppermute | solution.py:418
  34.9 51.6 %collective-permute-start.12 = (f32[8,256,128]{2,1,0:T(8,128)S(1)}, f32[8,256,128]{2,1,0:T(8,128)S(1)}, u32[]{:S(2)}, u32[]{:S(2)}) collective-permute-start(f32[8,256,128]{2,1,0:T(8,128)S(1)} %bitcast.20), channel_id=1, source_target_pairs={{0,31},{1,2},{2,1},{3,4},{4,3},{5,6},{6,5},{7,8},{8,7},{9,10},{10,... | collective-permute-start | bytes 3145736 | tf_op jit(solution)/shard_map/ppermute | solution.py:384
  50.1 36.4 %collective-permute-start.13 = (f32[8,256,128]{2,1,0:T(8,128)S(1)}, f32[8,256,128]{2,1,0:T(8,128)S(1)}, u32[]{:S(2)}, u32[]{:S(2)}) collective-permute-start(f32[8,256,128]{2,1,0:T(8,128)S(1)} %bitcast.21), channel_id=1, source_target_pairs={{0,1},{1,0},{2,3},{3,2},{4,5},{5,4},{6,7},{7,6},{8,9},{9,8},{10,11... | collective-permute-start | bytes 3145736 | tf_op jit(solution)/shard_map/ppermute | solution.py:384
  52.1 9.3 %collective-permute-start.5 = (f32[2,256,128]{2,1,0:T(8,128)S(1)}, f32[2,256,128]{2,1,0:T(8,128)S(1)}, u32[]{:S(2)}, u32[]{:S(2)}) collective-permute-start(f32[2,256,128]{2,1,0:T(8,128)S(1)} %broadcast_select_fusion.refs_0_), channel_id=1, source_target_pairs={{0,224},{32,0},{64,32},{96,64},{128,96},{160,128},{192,160},{224,1... | collective-permute-start | bytes 786440 | tf_op jit(solution)/shard_map/ppermute | solution.py:377
  54.0 12.4 %collective-permute-start.4 = (f32[2,256,128]{2,1,0:T(8,128)S(1)}, f32[2,256,128]{2,1,0:T(8,128)S(1)}, u32[]{:S(2)}, u32[]{:S(2)}) collective-permute-start(f32[2,256,128]{2,1,0:T(8,128)S(1)} %broadcast_select_fusion.refs_0_), channel_id=1, source_target_pairs={{0,32},{32,64},{64,96},{96,128},{128,160},{160,192},{192,224},{224... | collective-permute-start | bytes 786440 | tf_op jit(solution)/shard_map/ppermute | solution.py:377
  61.3 8.5 %collective-permute-start.7 = (f32[2,256,128]{2,1,0:T(8,128)S(1)}, f32[2,256,128]{2,1,0:T(8,128)S(1)}, u32[]{:S(2)}, u32[]{:S(2)}) collective-permute-start(f32[2,256,128]{2,1,0:T(8,128)S(1)} %collective-permute-done.5.refs_2_), channel_id=1, source_target_pairs={{0,224},{32,0},{64,32},{96,64},{128,96},{160,128},{192,160},{224,1... | collective-permute-start | bytes 786440 | tf_op jit(solution)/shard_map/ppermute | solution.py:377
  66.4 9.5 %collective-permute-start.6 = (f32[2,256,128]{2,1,0:T(8,128)S(1)}, f32[2,256,128]{2,1,0:T(8,128)S(1)}, u32[]{:S(2)}, u32[]{:S(2)}) collective-permute-start(f32[2,256,128]{2,1,0:T(8,128)S(1)} %collective-permute-done.4.refs_1_), channel_id=1, source_target_pairs={{0,32},{32,64},{64,96},{96,128},{128,160},{160,192},{192,224},{224... | collective-permute-start | bytes 786440 | tf_op jit(solution)/shard_map/ppermute | solution.py:377
  69.8 9.0 %collective-permute-start.9 = (f32[2,256,128]{2,1,0:T(8,128)S(1)}, f32[2,256,128]{2,1,0:T(8,128)S(1)}, u32[]{:S(2)}, u32[]{:S(2)}) collective-permute-start(f32[2,256,128]{2,1,0:T(8,128)S(1)} %collective-permute-done.7.refs_4_), channel_id=1, source_target_pairs={{0,224},{32,0},{64,32},{96,64},{128,96},{160,128},{192,160},{224,1... | collective-permute-start | bytes 786440 | tf_op jit(solution)/shard_map/ppermute | solution.py:377
  75.9 8.6 %collective-permute-start.8 = (f32[2,256,128]{2,1,0:T(8,128)S(1)}, f32[2,256,128]{2,1,0:T(8,128)S(1)}, u32[]{:S(2)}, u32[]{:S(2)}) collective-permute-start(f32[2,256,128]{2,1,0:T(8,128)S(1)} %collective-permute-done.6.refs_3_), channel_id=1, source_target_pairs={{0,32},{32,64},{64,96},{96,128},{128,160},{160,192},{192,224},{224... | collective-permute-start | bytes 786440 | tf_op jit(solution)/shard_map/ppermute | solution.py:377
  78.8 12.3 %collective-permute-start.11 = (f32[1,256,128]{2,1,0:T(8,128)S(1)}, f32[1,256,128]{2,1,0:T(8,128)S(1)}, u32[]{:S(2)}, u32[]{:S(2)}) collective-permute-start(f32[1,256,128]{2,1,0:T(8,128)S(1)} %slice.36), channel_id=1, source_target_pairs={{0,224},{32,0},{64,32},{96,64},{128,96},{160,128},{192,160},{224,1... | collective-permute-start | bytes 393224 | tf_op jit(solution)/shard_map/ppermute | solution.py:377
  84.6 6.9 %collective-permute-start.10 = (f32[1,256,128]{2,1,0:T(8,128)S(1)}, f32[1,256,128]{2,1,0:T(8,128)S(1)}, u32[]{:S(2)}, u32[]{:S(2)}) collective-permute-start(f32[1,256,128]{2,1,0:T(8,128)S(1)} %slice.37), channel_id=1, source_target_pairs={{0,32},{32,64},{64,96},{96,128},{128,160},{160,192},{192,224},{224... | collective-permute-start | bytes 393224 | tf_op jit(solution)/shard_map/ppermute | solution.py:377
  116.0 28.1 %collective-permute-start.18 = (f32[8,256,128]{2,1,0:T(8,128)}, f32[8,256,128]{2,1,0:T(8,128)S(1)}, u32[]{:S(2)}, u32[]{:S(2)}) collective-permute-start(f32[8,256,128]{2,1,0:T(8,128)} %get-tuple-element.39.f_ref), channel_id=1, source_target_pairs={{0,31},{1,2},{2,1},{3,4},{4,3},{5,6},{6,5},{7,8},{8,7},{9,10},{10,... | collective-permute-start | bytes 3145736 | tf_op jit(solution)/shard_map/ppermute | solution.py:384
  118.1 26.0 %collective-permute-start.19 = (f32[8,256,128]{2,1,0:T(8,128)}, f32[8,256,128]{2,1,0:T(8,128)S(1)}, u32[]{:S(2)}, u32[]{:S(2)}) collective-permute-start(f32[8,256,128]{2,1,0:T(8,128)} %get-tuple-element.39.f_ref), channel_id=1, source_target_pairs={{0,1},{1,0},{2,3},{3,2},{4,5},{5,4},{6,7},{7,6},{8,9},{9,8},{10,11... | collective-permute-start | bytes 3145736 | tf_op jit(solution)/shard_map/ppermute | solution.py:384
  121.8 4.6 %collective-permute-start.14 = (f32[8,128]{1,0:T(8,128)S(1)}, f32[8,128]{1,0:T(8,128)S(1)}, u32[]{:S(2)}, u32[]{:S(2)}) collective-permute-start(f32[8,128]{1,0:T(8,128)S(1)} %shard_map.47.sums_ref.own_ref), channel_id=1, source_target_pairs={{0,32},{32,0},{1,33},{33,1},{2,34},{34,2},{3,35},{35,3},{4,36},{36... | collective-permute-start | bytes 12296 | tf_op jit(solution)/shard_map/ppermute | solution.py:473
  126.5 2.1 %collective-permute-start.15 = (f32[2,8,128]{2,1,0:T(8,128)S(1)}, f32[2,8,128]{2,1,0:T(8,128)S(1)}, u32[]{:S(2)}, u32[]{:S(2)}) collective-permute-start(f32[2,8,128]{2,1,0:T(8,128)S(1)} %maximum_select_fusion), channel_id=1, source_target_pairs={{0,128},{32,160},{1,129},{33,161},{2,130},{34,162},{3,131},{35,163... | collective-permute-start | bytes 24584 | tf_op jit(solution)/shard_map/ppermute | solution.py:476
  128.5 5.3 %collective-permute-start.16 = (f32[2,8,128]{2,1,0:T(8,128)S(1)}, f32[2,8,128]{2,1,0:T(8,128)S(1)}, u32[]{:S(2)}, u32[]{:S(2)}) collective-permute-start(f32[2,8,128]{2,1,0:T(8,128)S(1)} %fusion.2), channel_id=1, source_target_pairs={{0,64},{32,96},{128,192},{160,224},{1,65},{33,97},{129,193},{161,2... | collective-permute-start | bytes 24584 | tf_op jit(solution)/shard_map/ppermute | solution.py:477
  129.8 1.2 copy-start.1
  131.0 10.8 %copy-start.2 = (f32[8,256,128]{2,1,0:T(8,128)S(1)}, f32[8,256,128]{2,1,0:T(8,128)}, u32[]{:S(2)}) copy-start(f32[8,256,128]{2,1,0:T(8,128)} %get-tuple-element.39.f_ref) | copy-start | bytes 3145732
  133.8 5.6 %collective-permute-start.17 = (f32[2,8,128]{2,1,0:T(8,128)S(1)}, f32[2,8,128]{2,1,0:T(8,128)S(1)}, u32[]{:S(2)}, u32[]{:S(2)}) collective-permute-start(f32[2,8,128]{2,1,0:T(8,128)S(1)} %fusion.3.near_ref), channel_id=1, source_target_pairs={{0,256},{32,288},{64,320},{96,352},{128,384},{160,416},{192,448},{... | collective-permute-start | bytes 24584 | tf_op jit(solution)/shard_map/ppermute | solution.py:479

commit v14 on v10

--- a/solution.py
+++ b/solution.py
@@ -356,19 +356,23 @@
     lax.fori_loop(0, f_ref.shape[1] // 32, body, 0)
 
 
-def edge_kernel(partial_ref, left_ref, right_ref, out):
-    def body(i, carry):
-        for x in range(4):
-            part = pl.ds(64 * x, 64)
-            out[i, part, :] = edged(
-                partial_ref[i, part, :],
-                x,
-                lambda n: left_ref[i, pl.ds(64 * n, 64), :],
-                lambda n: right_ref[i, pl.ds(64 * n, 64), :],
-            )
-        return carry
-
-    lax.fori_loop(0, BLK, body, 0)
+def edge_kernel(words, partial, across, beside, out):
+    def run(left, right):
+        def body(i, carry):
+            for x in range(4):
+                part = pl.ds(64 * x, 64)
+                out[i, part, :] = edged(
+                    partial[i, part, :],
+                    x,
+                    lambda n: left[i, pl.ds(64 * n, 64), :],
+                    lambda n: right[i, pl.ds(64 * n, 64), :],
+                )
+            return carry
+
+        lax.fori_loop(0, BLK, body, 0)
+
+    pl.when(words[1] == 0)(lambda: run(across, beside))
+    pl.when(words[1] == 1)(lambda: run(beside, across))
 
 
 def domain_parts(copies):
@@ -387,12 +391,19 @@
     return left, right
 
 
+def exchanged(block):
+    count = lax.axis_size("domain")
+    across = [(i, (i + 1 if i % 2 else i - 1) % count) for i in range(count)]
+    beside = [(i, i ^ 1) for i in range(count)]
+    return lax.ppermute(block, "domain", across), lax.ppermute(block, "domain", beside)
+
+
 def local(orbitals, potential):
     blocks, slab_width, rows_y, rows_z = orbitals.shape
     domain = lax.axis_size("domain")
     cells_total = float(slab_width * rows_y * rows_z * domain)
     band = lax.axis_index("band")
-    band_word = band.reshape(1).astype(jnp.int32)
+    words = jnp.stack([band, lax.axis_index("domain") & 1]).astype(jnp.int32)
     flat = (blocks, slab_width * rows_y, rows_z)
     big = flat[0] * flat[1] * flat[2]
     slab = jax.ShapeDtypeStruct(flat, F32)
@@ -414,7 +425,7 @@
         lax.ppermute(quarters[k], "band", [(0, 2 * k), (1, 2 * k + 1)]) for k in (1, 3, 2)
     ]
     inner, sums = inner_part(orbitals, tile)
-    arrived, inner, sums = lax.optimization_barrier((arrived, inner, sums))
+    arrived, inner, sums, words = lax.optimization_barrier((arrived, inner, sums, words))
     piece = jnp.where(band < 2, quarters[0], 0.0)
     for part in arrived:
         piece = piece + part
@@ -464,8 +475,8 @@
         specs=[SMEM] + [VMEM] * 11,
         flops=48 * big,
         bytes_moved=16 * big,
-    )(band_word, sums, *pieces, own)
-    left, right = neighbours(basis)
+    )(words, sums, *pieces, own)
+    across, beside = exchanged(basis)
     inner = inner_part(basis.reshape(orbitals.shape))[0].reshape(flat)
     shared = sums
     other = lax.ppermute(shared, "band", [(0, 1), (1, 0)])
@@ -473,17 +484,16 @@
     shared = jnp.where(band < 2, shared, 0.0)
     shared = shared + lax.ppermute(shared, "band", [(0, 4), (1, 5)])
     shared = shared + lax.ppermute(shared, "band", [(0, 2), (1, 3), (4, 6), (5, 7)])
-    shared, inner = lax.optimization_barrier((shared, inner))
     far = lax.ppermute(shared, "band", [(y, y + RING) for y in range(RING)])
     splat = call(
         coeff_kernel, jax.ShapeDtypeStruct((8, 8, 128), F32), specs=[SMEM] + [VMEM] * 5
-    )(band_word, weights, gram, sums, shared, far)
+    )(words, weights, gram, sums, shared, far)
     partial = call(
         partial_kernel, slab, specs=[VMEM] * 3, flops=16 * big, bytes_moved=12 * big
     )(basis, inner, splat)
     residual = call(
-        edge_kernel, slab, specs=[VMEM] * 3, flops=20 * big, bytes_moved=16 * big
-    )(partial, left, right)
+        edge_kernel, slab, specs=[SMEM] + [VMEM] * 3, flops=20 * big, bytes_moved=16 * big
+    )(words, partial, across, beside)
     return (basis.reshape(orbitals.shape), residual.reshape(orbitals.shape))
 
 

time: 136 us -> 136 us (level)
  waiting for transfers between devices: 32.8 us -> 29.6 us
  other arithmetic: 1.49 us -> 3.2 us
  Pallas kernels: 22 us -> 23.7 us
    ppermute x0 -> x2, starting transfers between devices: none -> 5.77 us  [the longest x1 3.68 us: exchanged(): lax.ppermute(block, 'domain', beside)]
    ppermute x2 -> x1, waiting for transfers between devices: 10.9 us -> 5.5 us  [neighbours(): lax.ppermute(block, 'domain', [((i + 1) % count, i) for i in range(count)])]
    ppermute x2 -> x1, starting transfers between devices: 4.14 us -> 1.92 us  [neighbours(): lax.ppermute(block, 'domain', [((i + 1) % count, i) for i in range(count)])]
    ppermute x2 -> x1, starting transfers between devices: 6.58 us -> 4.48 us  [neighbours(): lax.ppermute(block, 'domain', [(i, (i + 1) % count) for i in range(count)])]
    ppermute x0 -> x2, waiting for transfers between devices: none -> 1.6 us  [the longest x1 1.6 us: exchanged(): lax.ppermute(block, 'domain', across)]
  transfers between devices with their start and end apart: 20 -> 20, of which waited for: 11 -> 12; matrix products, arithmetic and copies ran while one was open for 0% -> 0% of each run, Pallas kernels for 12% -> 12%
where the time goes in v14:
time: 136 us
  starting transfers between devices  55.8 us (41%)
  waiting for transfers between devices  29.6 us (22%)
  Pallas kernels  23.7 us (17%)
  blocking collectives  21.2 us (16%)
  other arithmetic  3.2 us (2%)
    ppermute x8, starting transfers between devices, ring_shift(): return lax.ppermute(block, 'band', pairs)  23 us
    all_to_all x1, blocking collectives, domain_parts(): return lax.all_to_all(copies, 'domain', 0, 0)  21.2 us
    ppermute x3, waiting for transfers between devices, local(): lax.ppermute(quarters[k], 'band', [(0, 2 * k), (1, 2 * k + 1)])  10.8 us
    ppermute x3, starting transfers between devices, local(): lax.ppermute(quarters[k], 'band', [(0, 2 * k), (1, 2 * k + 1)])  10.3 us
    ppermute x8, waiting for transfers between devices, ring_shift(): return lax.ppermute(block, 'band', pairs)  6.34 us
    pallas_call x4, Pallas kernels, stage(): call(lambda *refs: stage_kernel(len(pieces), fresh, imaged, last, *refs),...  6.12 us
    pallas_call x2, Pallas kernels, inner_part(): call(inner_kernel, (field, *sums), specs=[VMEM] * 2, flops=60 * big, byte...  6.03 us
    ppermute x1, waiting for transfers between devices, neighbours(): lax.ppermute(block, 'domain', [((i + 1) % count, i) for i in range(count)])  5.5 us
  transfers between devices with their start and end apart: 20, of which 12 were waited for; matrix products, arithmetic and copies ran while one was open for 0% of the time, Pallas kernels for 12%

profile of v14, /device:TPU:1, one launch (start us, length us, event | category | flops | bytes accessed | tf_op | source)
XLA Modules:
  0.0 135.6 jit_solution(12172490810177868849)
XLA Ops:
  0.7 2.1 %slice_select_fusion = (f32[2,4,64,128]{3,2,1,0:T(8,128)S(1)}, f32[2,4,64,128]{3,2,1,0:T(8,128)S(1)}, f32[2,4,64,128]{3,2,1,0:T(8,128)S(1)}, f32[2,4,64,128]{3,2,1,0:T(8,128)}) fusion(f32[8,4,64,128]{3,2,1,0:T(8,128)} %f_ref.1, pred[]{:T(512)S(6)} %lt.8), kind=kLoop, calls=%fused_computation.3 | loop fusion | flops 65536 | bytes 2097153 | tf_op jit(solution)/shard_map/jit(_where)/select_n | solution.py:429
  2.7 5.0 %collective-permute-start = (f32[2,256,128]{2,1,0:T(8,128)}, f32[2,256,128]{2,1,0:T(8,128)S(1)}, u32[]{:S(2)}, u32[]{:S(2)}) collective-permute-start(f32[2,256,128]{2,1,0:T(8,128)} %bitcast), channel_id=1, source_target_pairs={{0,64},{32,96},{1,65},{33,97},{2,66},{34,98},{3,67},{35,99},{4,68}... | collective-permute-start | bytes 786440 | tf_op jit(solution)/shard_map/ppermute | solution.py:425
  7.8 2.3 %collective-permute-start.1 = (f32[2,256,128]{2,1,0:T(8,128)S(1)}, f32[2,256,128]{2,1,0:T(8,128)S(1)}, u32[]{:S(2)}, u32[]{:S(2)}) collective-permute-start(f32[2,256,128]{2,1,0:T(8,128)S(1)} %bitcast.34), channel_id=1, source_target_pairs={{0,192},{32,224},{1,193},{33,225},{2,194},{34,226},{3,195},{35,227... | collective-permute-start | bytes 786440 | tf_op jit(solution)/shard_map/ppermute | solution.py:425
  10.1 3.0 %collective-permute-start.2 = (f32[2,256,128]{2,1,0:T(8,128)S(1)}, f32[2,256,128]{2,1,0:T(8,128)}, u32[]{:S(2)}, u32[]{:S(2)}) collective-permute-start(f32[2,256,128]{2,1,0:T(8,128)S(1)} %bitcast.33), channel_id=1, source_target_pairs={{0,128},{32,160},{1,129},{33,161},{2,130},{34,162},{3,131},{35,163... | collective-permute-start | bytes 786440 | tf_op jit(solution)/shard_map/ppermute | solution.py:425
  13.1 3.3 %shard_map.41 = (f32[8,4,64,128]{3,2,1,0:T(8,128)S(1)}, f32[8,128]{1,0:T(8,128)S(1)}) custom-call(f32[8,4,64,128]{3,2,1,0:T(8,128)S(1)} %copy-done, f32[4,64,128]{2,1,0:T(8,128)S(1)} %copy-done.3), custom_call_target="tpu_custom_call" | custom-call | flops 15728640 | bytes 2097152 | tf_op jit(solution)/shard_map/pallas_call | solution.py:414
  16.5 10.8 %collective-permute-done.1 = f32[2,256,128]{2,1,0:T(8,128)S(1)} collective-permute-done((f32[2,256,128]{2,1,0:T(8,128)S(1)}, f32[2,256,128]{2,1,0:T(8,128)S(1)}, u32[]{:S(2)}, u32[]{:S(2)}) %collective-permute-start.1) | collective-permute-done | bytes 262176 | tf_op jit(solution)/shard_map/ppermute | solution.py:425
  28.2 2.0 %collective-permute-start.3 = (f32[2,256,128]{2,1,0:T(8,128)S(1)}, f32[2,256,128]{2,1,0:T(8,128)}, u32[]{:S(2)}, u32[]{:S(2)}) collective-permute-start(f32[2,256,128]{2,1,0:T(8,128)S(1)} %fusion.1), channel_id=1, source_target_pairs={{0,256},{32,288},{64,320},{96,352},{128,384},{160,416},{192,448},{... | collective-permute-start | bytes 786440 | tf_op jit(solution)/shard_map/ppermute | solution.py:433
  30.2 4.5 %collective-permute-start.10 = (f32[8,256,128]{2,1,0:T(8,128)S(1)}, f32[8,256,128]{2,1,0:T(8,128)S(1)}, u32[]{:S(2)}, u32[]{:S(2)}) collective-permute-start(f32[8,256,128]{2,1,0:T(8,128)S(1)} %bitcast.20), channel_id=1, source_target_pairs={{0,1},{1,2},{2,3},{3,4},{4,5},{5,6},{6,7},{7,8},{8,9},{9,10},{10,1... | collective-permute-start | bytes 3145736 | tf_op jit(solution)/shard_map/ppermute | solution.py:389
  38.7 3.4 %collective-permute-start.4 = (f32[2,256,128]{2,1,0:T(8,128)S(1)}, f32[2,256,128]{2,1,0:T(8,128)S(1)}, u32[]{:S(2)}, u32[]{:S(2)}) collective-permute-start(f32[2,256,128]{2,1,0:T(8,128)S(1)} %broadcast_select_fusion.refs_0_), channel_id=1, source_target_pairs={{0,32},{32,64},{64,96},{96,128},{128,160},{160,192},{192,224},{224... | collective-permute-start | bytes 786440 | tf_op jit(solution)/shard_map/ppermute | solution.py:384
  42.0 2.1 %collective-permute-done.5.refs_2_ = f32[2,256,128]{2,1,0:T(8,128)S(1)} collective-permute-done((f32[2,256,128]{2,1,0:T(8,128)S(1)}, f32[2,256,128]{2,1,0:T(8,128)S(1)}, u32[]{:S(2)}, u32[]{:S(2)}) %collective-permute-start.5) | collective-permute-done | bytes 262176 | tf_op jit(solution)/shard_map/ppermute | solution.py:384
  44.1 4.3 %collective-permute-start.7 = (f32[2,256,128]{2,1,0:T(8,128)S(1)}, f32[2,256,128]{2,1,0:T(8,128)S(1)}, u32[]{:S(2)}, u32[]{:S(2)}) collective-permute-start(f32[2,256,128]{2,1,0:T(8,128)S(1)} %collective-permute-done.5.refs_2_), channel_id=1, source_target_pairs={{0,224},{32,0},{64,32},{96,64},{128,96},{160,128},{192,160},{224,1... | collective-permute-start | bytes 786440 | tf_op jit(solution)/shard_map/ppermute | solution.py:384
  53.1 4.3 %collective-permute-start.9 = (f32[2,256,128]{2,1,0:T(8,128)S(1)}, f32[2,256,128]{2,1,0:T(8,128)S(1)}, u32[]{:S(2)}, u32[]{:S(2)}) collective-permute-start(f32[2,256,128]{2,1,0:T(8,128)S(1)} %collective-permute-done.7.refs_4_), channel_id=1, source_target_pairs={{0,224},{32,0},{64,32},{96,64},{128,96},{160,128},{192,160},{224,1... | collective-permute-start | bytes 786440 | tf_op jit(solution)/shard_map/ppermute | solution.py:384
  61.1 5.5 %collective-permute-done.11.right = f32[8,256,128]{2,1,0:T(8,128)} collective-permute-done((f32[8,256,128]{2,1,0:T(8,128)S(1)}, f32[8,256,128]{2,1,0:T(8,128)}, u32[]{:S(2)}, u32[]{:S(2)}) %collective-permute-start.11) | collective-permute-done | bytes 1048608 | tf_op jit(solution)/shard_map/ppermute | solution.py:390
  68.5 3.4 %collective-permute-start.12 = (f32[1,256,128]{2,1,0:T(8,128)S(1)}, f32[1,256,128]{2,1,0:T(8,128)S(1)}, u32[]{:S(2)}, u32[]{:S(2)}) collective-permute-start(f32[1,256,128]{2,1,0:T(8,128)S(1)} %slice.37), channel_id=1, source_target_pairs={{0,32},{32,64},{64,96},{96,128},{128,160},{160,192},{192,224},{224... | collective-permute-start | bytes 393224 | tf_op jit(solution)/shard_map/ppermute | solution.py:384
  71.9 2.2 %shard_map.44 = (f32[8,256,128]{2,1,0:T(8,128)S(1)}, f32[8,128]{1,0:T(8,128)S(1)}) custom-call(f32[8,256,128]{2,1,0:T(8,128)S(1)} %bitcast.24, f32[8,256,128]{2,1,0:T(8,128)S(1)} %bitcast.31, f32[8,256,128]{2,1,0:T(8,128)S(1)} %collective-permute-done.10.left, f32[8,256,128]{2,1,0:T(8,128)} %collective-permute-done.11.right), custom_call_target="tpu_custom_call" | custom-call | flops 13107200 | bytes 5242880 | tf_op jit(solution)/shard_map/pallas_call | solution.py:458
  74.1 3.0 %shard_map.45.refs_11_ = f32[8,128]{1,0:T(8,128)S(1)} custom-call(f32[2,256,128]{2,1,0:T(8,128)S(1)} %broadcast_select_fusion.refs_0_, f32[2,256,128]{2,1,0:T(8,128)S(1)} %collective-permute-done.4.refs_1_, f32[2,256,128]{2,1,0:T(8,128)S(1)} %collective-permute-done.5.refs_2_, f32[2,256,128]{2,1,0:T(8,128)S(1)} %collective-permute-done.6.refs_3_, ...), custom_call_target="tpu_custom_call" | custom-call | flops 5242880 | bytes 2621440 | tf_op jit(solution)/shard_map/pallas_call | solution.py:438
  79.9 21.2 %all_to_all.5.refs_0_ = f32[32,8,128]{2,1,0:T(8,128)S(1)} all-to-all(f32[32,8,128]{2,1,0:T(8,128)S(1)} %shard_map.46), channel_id=1, replica_groups=mesh['band'=16,'domain'=32] {'domain'}, dimensions={0} | all-to-all | bytes 262144 | tf_op jit(solution)/shard_map/all_to_all | solution.py:379
  101.2 4.3 %shard_map.48 = (f32[8,256,128]{2,1,0:T(8,128)}, f32[8,128]{1,0:T(8,128)S(1)}, f32[8,128]{1,0:T(8,128)S(1)}) custom-call(s32[2]{0:T(128)S(1)} %pad_add_fusion.band_ref.words, f32[8,128]{1,0:T(8,128)S(1)} %shard_map.47.sums_ref.own_ref, f32[2,256,128]{2,1,0:T(8,128)S(1)} %broadcast_select_fusion.refs_0_, f32[2,256,128]{2,1,0:T(8,128)S(1)} %collective-permute-done.4.refs_1_, ...), custom_call_target="tpu_custom_call" | custom-call | flops 12582912 | bytes 4194304 | tf_op jit(solution)/shard_map/pallas_call | solution.py:471
  105.5 2.1 %collective-permute-start.18 = (f32[8,256,128]{2,1,0:T(8,128)}, f32[8,256,128]{2,1,0:T(8,128)S(1)}, u32[]{:S(2)}, u32[]{:S(2)}) collective-permute-start(f32[8,256,128]{2,1,0:T(8,128)} %get-tuple-element.37.f_ref), channel_id=1, source_target_pairs={{0,31},{1,2},{2,1},{3,4},{4,3},{5,6},{6,5},{7,8},{8,7},{9,10},{10,... | collective-permute-start | bytes 3145736 | tf_op jit(solution)/shard_map/ppermute | solution.py:398
  107.6 3.7 %collective-permute-start.19 = (f32[8,256,128]{2,1,0:T(8,128)}, f32[8,256,128]{2,1,0:T(8,128)S(1)}, u32[]{:S(2)}, u32[]{:S(2)}) collective-permute-start(f32[8,256,128]{2,1,0:T(8,128)} %get-tuple-element.37.f_ref), channel_id=1, source_target_pairs={{0,1},{1,0},{2,3},{3,2},{4,5},{5,4},{6,7},{7,6},{8,9},{9,8},{10,11... | collective-permute-start | bytes 3145736 | tf_op jit(solution)/shard_map/ppermute | solution.py:398
  113.2 2.7 %collective-permute-done.14 = f32[8,128]{1,0:T(8,128)S(1)} collective-permute-done((f32[8,128]{1,0:T(8,128)S(1)}, f32[8,128]{1,0:T(8,128)S(1)}, u32[]{:S(2)}, u32[]{:S(2)}) %collective-permute-start.14) | collective-permute-done | bytes 4128 | tf_op jit(solution)/shard_map/ppermute | solution.py:482
  120.6 3.3 %collective-permute-start.17 = (f32[2,8,128]{2,1,0:T(8,128)S(1)}, f32[2,8,128]{2,1,0:T(8,128)S(1)}, u32[]{:S(2)}, u32[]{:S(2)}) collective-permute-start(f32[2,8,128]{2,1,0:T(8,128)S(1)} %fusion.3.near_ref), channel_id=1, source_target_pairs={{0,256},{32,288},{64,320},{96,352},{128,384},{160,416},{192,448},{... | collective-permute-start | bytes 24584 | tf_op jit(solution)/shard_map/ppermute | solution.py:487
  125.1 2.7 %shard_map.49 = f32[8,4,64,128]{3,2,1,0:T(8,128)S(1)} custom-call(f32[8,4,64,128]{3,2,1,0:T(8,128)S(1)} %bitcast.29, f32[4,64,128]{2,1,0:T(8,128)S(1)} %copy-done.3), custom_call_target="tpu_custom_call" | custom-call | flops 15728640 | bytes 2097152 | tf_op jit(solution)/shard_map/pallas_call | solution.py:414
  128.9 2.4 %shard_map.50.splat = f32[8,8,128]{2,1,0:T(8,128)S(1)} custom-call(s32[2]{0:T(128)S(1)} %pad_add_fusion.band_ref.words, f32[8,128]{1,0:T(8,128)S(1)} %get-tuple-element.38.weights_ref, f32[8,128]{1,0:T(8,128)S(1)} %get-tuple-element.39.gram_ref, f32[8,128]{1,0:T(8,128)S(1)} %shard_map.47.sums_ref.own_ref, f32[2,8,128]{2,1,0:T(8,128)S(1)} %fusion.3.near_ref, ...), custom_call_target="tpu_custom_call" | custom-call | tf_op jit(solution)/shard_map/pallas_call | solution.py:488
  (47 shorter events, 31.2 us)
Async XLA Ops:
  0.6 12.4 %copy-start = (f32[8,4,64,128]{3,2,1,0:T(8,128)S(1)}, f32[8,4,64,128]{3,2,1,0:T(8,128)}, u32[]{:S(2)}) copy-start(f32[8,4,64,128]{3,2,1,0:T(8,128)} %f_ref.1) | copy-start | bytes 3145732
  0.6 12.4 %copy-start.3 = (f32[4,64,128]{2,1,0:T(8,128)S(1)}, f32[4,64,128]{2,1,0:T(8,128)}, u32[]{:S(2)}) copy-start(f32[4,64,128]{2,1,0:T(8,128)} %v_ref.3) | copy-start | bytes 393220
  2.7 13.7 %collective-permute-start = (f32[2,256,128]{2,1,0:T(8,128)}, f32[2,256,128]{2,1,0:T(8,128)S(1)}, u32[]{:S(2)}, u32[]{:S(2)}) collective-permute-start(f32[2,256,128]{2,1,0:T(8,128)} %bitcast), channel_id=1, source_target_pairs={{0,64},{32,96},{1,65},{33,97},{2,66},{34,98},{3,67},{35,99},{4,68}... | collective-permute-start | bytes 786440 | tf_op jit(solution)/shard_map/ppermute | solution.py:425
  7.8 19.5 %collective-permute-start.1 = (f32[2,256,128]{2,1,0:T(8,128)S(1)}, f32[2,256,128]{2,1,0:T(8,128)S(1)}, u32[]{:S(2)}, u32[]{:S(2)}) collective-permute-start(f32[2,256,128]{2,1,0:T(8,128)S(1)} %bitcast.34), channel_id=1, source_target_pairs={{0,192},{32,224},{1,193},{33,225},{2,194},{34,226},{3,195},{35,227... | collective-permute-start | bytes 786440 | tf_op jit(solution)/shard_map/ppermute | solution.py:425
  10.1 17.1 %collective-permute-start.2 = (f32[2,256,128]{2,1,0:T(8,128)S(1)}, f32[2,256,128]{2,1,0:T(8,128)}, u32[]{:S(2)}, u32[]{:S(2)}) collective-permute-start(f32[2,256,128]{2,1,0:T(8,128)S(1)} %bitcast.33), channel_id=1, source_target_pairs={{0,128},{32,160},{1,129},{33,161},{2,130},{34,162},{3,131},{35,163... | collective-permute-start | bytes 786440 | tf_op jit(solution)/shard_map/ppermute | solution.py:425
  28.2 8.4 %collective-permute-start.3 = (f32[2,256,128]{2,1,0:T(8,128)S(1)}, f32[2,256,128]{2,1,0:T(8,128)}, u32[]{:S(2)}, u32[]{:S(2)}) collective-permute-start(f32[2,256,128]{2,1,0:T(8,128)S(1)} %fusion.1), channel_id=1, source_target_pairs={{0,256},{32,288},{64,320},{96,352},{128,384},{160,416},{192,448},{... | collective-permute-start | bytes 786440 | tf_op jit(solution)/shard_map/ppermute | solution.py:433
  30.2 30.8 %collective-permute-start.10 = (f32[8,256,128]{2,1,0:T(8,128)S(1)}, f32[8,256,128]{2,1,0:T(8,128)S(1)}, u32[]{:S(2)}, u32[]{:S(2)}) collective-permute-start(f32[8,256,128]{2,1,0:T(8,128)S(1)} %bitcast.20), channel_id=1, source_target_pairs={{0,1},{1,2},{2,3},{3,4},{4,5},{5,6},{6,7},{7,8},{8,9},{9,10},{10,1... | collective-permute-start | bytes 3145736 | tf_op jit(solution)/shard_map/ppermute | solution.py:389
  34.7 31.8 %collective-permute-start.11 = (f32[8,256,128]{2,1,0:T(8,128)S(1)}, f32[8,256,128]{2,1,0:T(8,128)}, u32[]{:S(2)}, u32[]{:S(2)}) collective-permute-start(f32[8,256,128]{2,1,0:T(8,128)S(1)} %bitcast.21), channel_id=1, source_target_pairs={{1,0},{2,1},{3,2},{4,3},{5,4},{6,5},{7,6},{8,7},{9,8},{10,9},{11,1... | collective-permute-start | bytes 3145736 | tf_op jit(solution)/shard_map/ppermute | solution.py:390
  36.7 7.4 %collective-permute-start.5 = (f32[2,256,128]{2,1,0:T(8,128)S(1)}, f32[2,256,128]{2,1,0:T(8,128)S(1)}, u32[]{:S(2)}, u32[]{:S(2)}) collective-permute-start(f32[2,256,128]{2,1,0:T(8,128)S(1)} %broadcast_select_fusion.refs_0_), channel_id=1, source_target_pairs={{0,224},{32,0},{64,32},{96,64},{128,96},{160,128},{192,160},{224,1... | collective-permute-start | bytes 786440 | tf_op jit(solution)/shard_map/ppermute | solution.py:384
  38.7 10.5 %collective-permute-start.4 = (f32[2,256,128]{2,1,0:T(8,128)S(1)}, f32[2,256,128]{2,1,0:T(8,128)S(1)}, u32[]{:S(2)}, u32[]{:S(2)}) collective-permute-start(f32[2,256,128]{2,1,0:T(8,128)S(1)} %broadcast_select_fusion.refs_0_), channel_id=1, source_target_pairs={{0,32},{32,64},{64,96},{96,128},{128,160},{160,192},{192,224},{224... | collective-permute-start | bytes 786440 | tf_op jit(solution)/shard_map/ppermute | solution.py:384
  44.1 9.0 %collective-permute-start.7 = (f32[2,256,128]{2,1,0:T(8,128)S(1)}, f32[2,256,128]{2,1,0:T(8,128)S(1)}, u32[]{:S(2)}, u32[]{:S(2)}) collective-permute-start(f32[2,256,128]{2,1,0:T(8,128)S(1)} %collective-permute-done.5.refs_2_), channel_id=1, source_target_pairs={{0,224},{32,0},{64,32},{96,64},{128,96},{160,128},{192,160},{224,1... | collective-permute-start | bytes 786440 | tf_op jit(solution)/shard_map/ppermute | solution.py:384
  49.2 9.0 %collective-permute-start.6 = (f32[2,256,128]{2,1,0:T(8,128)S(1)}, f32[2,256,128]{2,1,0:T(8,128)S(1)}, u32[]{:S(2)}, u32[]{:S(2)}) collective-permute-start(f32[2,256,128]{2,1,0:T(8,128)S(1)} %collective-permute-done.4.refs_1_), channel_id=1, source_target_pairs={{0,32},{32,64},{64,96},{96,128},{128,160},{160,192},{192,224},{224... | collective-permute-start | bytes 786440 | tf_op jit(solution)/shard_map/ppermute | solution.py:384
  53.1 13.4 %collective-permute-start.9 = (f32[2,256,128]{2,1,0:T(8,128)S(1)}, f32[2,256,128]{2,1,0:T(8,128)S(1)}, u32[]{:S(2)}, u32[]{:S(2)}) collective-permute-start(f32[2,256,128]{2,1,0:T(8,128)S(1)} %collective-permute-done.7.refs_4_), channel_id=1, source_target_pairs={{0,224},{32,0},{64,32},{96,64},{128,96},{160,128},{192,160},{224,1... | collective-permute-start | bytes 786440 | tf_op jit(solution)/shard_map/ppermute | solution.py:384
  58.2 10.3 %collective-permute-start.8 = (f32[2,256,128]{2,1,0:T(8,128)S(1)}, f32[2,256,128]{2,1,0:T(8,128)S(1)}, u32[]{:S(2)}, u32[]{:S(2)}) collective-permute-start(f32[2,256,128]{2,1,0:T(8,128)S(1)} %collective-permute-done.6.refs_3_), channel_id=1, source_target_pairs={{0,32},{32,64},{64,96},{96,128},{128,160},{160,192},{192,224},{224... | collective-permute-start | bytes 786440 | tf_op jit(solution)/shard_map/ppermute | solution.py:384
  66.6 10.5 %collective-permute-start.13 = (f32[1,256,128]{2,1,0:T(8,128)S(1)}, f32[1,256,128]{2,1,0:T(8,128)S(1)}, u32[]{:S(2)}, u32[]{:S(2)}) collective-permute-start(f32[1,256,128]{2,1,0:T(8,128)S(1)} %slice.36), channel_id=1, source_target_pairs={{0,224},{32,0},{64,32},{96,64},{128,96},{160,128},{192,160},{224,1... | collective-permute-start | bytes 393224 | tf_op jit(solution)/shard_map/ppermute | solution.py:384
  68.5 10.3 %collective-permute-start.12 = (f32[1,256,128]{2,1,0:T(8,128)S(1)}, f32[1,256,128]{2,1,0:T(8,128)S(1)}, u32[]{:S(2)}, u32[]{:S(2)}) collective-permute-start(f32[1,256,128]{2,1,0:T(8,128)S(1)} %slice.37), channel_id=1, source_target_pairs={{0,32},{32,64},{64,96},{96,128},{128,160},{160,192},{192,224},{224... | collective-permute-start | bytes 393224 | tf_op jit(solution)/shard_map/ppermute | solution.py:384
  105.5 28.1 %collective-permute-start.18 = (f32[8,256,128]{2,1,0:T(8,128)}, f32[8,256,128]{2,1,0:T(8,128)S(1)}, u32[]{:S(2)}, u32[]{:S(2)}) collective-permute-start(f32[8,256,128]{2,1,0:T(8,128)} %get-tuple-element.37.f_ref), channel_id=1, source_target_pairs={{0,31},{1,2},{2,1},{3,4},{4,3},{5,6},{6,5},{7,8},{8,7},{9,10},{10,... | collective-permute-start | bytes 3145736 | tf_op jit(solution)/shard_map/ppermute | solution.py:398
  107.6 26.0 %collective-permute-start.19 = (f32[8,256,128]{2,1,0:T(8,128)}, f32[8,256,128]{2,1,0:T(8,128)S(1)}, u32[]{:S(2)}, u32[]{:S(2)}) collective-permute-start(f32[8,256,128]{2,1,0:T(8,128)} %get-tuple-element.37.f_ref), channel_id=1, source_target_pairs={{0,1},{1,0},{2,3},{3,2},{4,5},{5,4},{6,7},{7,6},{8,9},{9,8},{10,11... | collective-permute-start | bytes 3145736 | tf_op jit(solution)/shard_map/ppermute | solution.py:398
  111.3 4.6 %collective-permute-start.14 = (f32[8,128]{1,0:T(8,128)S(1)}, f32[8,128]{1,0:T(8,128)S(1)}, u32[]{:S(2)}, u32[]{:S(2)}) collective-permute-start(f32[8,128]{1,0:T(8,128)S(1)} %shard_map.47.sums_ref.own_ref), channel_id=1, source_target_pairs={{0,32},{32,0},{1,33},{33,1},{2,34},{34,2},{3,35},{35,3},{4,36},{36... | collective-permute-start | bytes 12296 | tf_op jit(solution)/shard_map/ppermute | solution.py:482
  115.9 2.6 %collective-permute-start.15 = (f32[2,8,128]{2,1,0:T(8,128)S(1)}, f32[2,8,128]{2,1,0:T(8,128)S(1)}, u32[]{:S(2)}, u32[]{:S(2)}) collective-permute-start(f32[2,8,128]{2,1,0:T(8,128)S(1)} %maximum_select_fusion), channel_id=1, source_target_pairs={{0,128},{32,160},{1,129},{33,161},{2,130},{34,162},{3,131},{35,163... | collective-permute-start | bytes 24584 | tf_op jit(solution)/shard_map/ppermute | solution.py:485
  118.5 2.1 %collective-permute-start.16 = (f32[2,8,128]{2,1,0:T(8,128)S(1)}, f32[2,8,128]{2,1,0:T(8,128)S(1)}, u32[]{:S(2)}, u32[]{:S(2)}) collective-permute-start(f32[2,8,128]{2,1,0:T(8,128)S(1)} %fusion.2), channel_id=1, source_target_pairs={{0,64},{32,96},{128,192},{160,224},{1,65},{33,97},{129,193},{161,2... | collective-permute-start | bytes 24584 | tf_op jit(solution)/shard_map/ppermute | solution.py:486
  120.6 8.3 %collective-permute-start.17 = (f32[2,8,128]{2,1,0:T(8,128)S(1)}, f32[2,8,128]{2,1,0:T(8,128)S(1)}, u32[]{:S(2)}, u32[]{:S(2)}) collective-permute-start(f32[2,8,128]{2,1,0:T(8,128)S(1)} %fusion.3.near_ref), channel_id=1, source_target_pairs={{0,256},{32,288},{64,320},{96,352},{128,384},{160,416},{192,448},{... | collective-permute-start | bytes 24584 | tf_op jit(solution)/shard_map/ppermute | solution.py:487
  123.9 1.2 copy-start.1
  125.1 6.2 %copy-start.2 = (f32[8,256,128]{2,1,0:T(8,128)S(1)}, f32[8,256,128]{2,1,0:T(8,128)}, u32[]{:S(2)}) copy-start(f32[8,256,128]{2,1,0:T(8,128)} %get-tuple-element.37.f_ref) | copy-start | bytes 3145732

commit v15 on v14

--- a/solution.py
+++ b/solution.py
@@ -10,7 +10,6 @@
 RING = 8
 F32 = jnp.float32
 VMEM = pl.BlockSpec(memory_space=pltpu.VMEM)
-SMEM = pl.BlockSpec(memory_space=pltpu.SMEM)
 
 
 def call(kernel, outs, scratch=(), specs=None, flops=0, bytes_moved=0):
@@ -145,9 +144,9 @@
     out[...] = jnp.sum(parts_ref[...], axis=0) / cells_total
 
 
-def combine_kernel(band_ref, sums_ref, *refs):
+def combine_kernel(sums_ref, *refs):
     *pieces, own, out, weights_ref, gram_ref, splat = refs
-    band = band_ref[0]
+    band = lax.axis_index("band")
     lane, sub = lanes(), subs()
     tiles = unpacked(sums_ref[...])
     turned = jnp.transpose(tall(tiles))
@@ -302,33 +301,44 @@
     return jnp.where((lane == target) & (row < 24), 1.0, 0.0)
 
 
-def coeff_kernel(band_ref, weights_ref, gram_ref, own_ref, near_ref, far_ref, out):
+def with_mirror(packed):
     lane, sub = lanes(), subs()
+    tiles = unpacked(packed)
+    mirror = jnp.transpose(tall([move(tiles[2], 24, 0)]))[0:8]
+    tiles[2] = tiles[2] + move(jnp.where(lane == sub, 0.0, mirror), 0, 24)
+    return tall(tiles)
+
+
+def image_columns(packed, place, target):
     wide = lax.broadcasted_iota(jnp.int32, (128, 128), 1)
+    columns = dot(place, with_mirror(packed), turn_left=True)
+    columns = pltpu.roll(columns, (target - 24) % 128, 1)
+    return jnp.where((wide >= target) & (wide < target + 8), columns, 0.0)
+
+
+def prepare_kernel(weights_ref, own_ref, ordered_ref, half_ref):
+    lane = lanes()
     row = lax.broadcasted_iota(jnp.int32, (128, 128), 0)
-    place = places(band_ref[0] & 7)
+    place = places(lax.axis_index("band") & 7)
     weights = jnp.where(lane < 24, pltpu.roll(weights_ref[...], 104, 1), 0.0)
     weights = dot(weights, place)
-
-    def with_mirror(packed):
-        tiles = unpacked(packed)
-        mirror = jnp.transpose(tall([move(tiles[2], 24, 0)]))[0:8]
-        tiles[2] = tiles[2] + move(jnp.where(lane == sub, 0.0, mirror), 0, 24)
-        return tall(tiles)
-
-    def image_columns(matrix, place, source, target):
-        columns = dot(place, matrix, turn_left=True)
-        columns = pltpu.roll(columns, (target - source) % 128, 1)
-        return jnp.where((wide >= target) & (wide < target + 8), columns, 0.0)
+    block = image_columns(own_ref[...], place, 16)
+    half = dot(weights, block)
+    half_ref[...] = half + dot(weights, jnp.where(row < 16, block, 0.0), turn_right=True)
+    ordered_ref[...] = weights
+
+
+def coeff_kernel(weights_ref, half_ref, gram_ref, near_ref, far_ref, out):
+    lane, sub = lanes(), subs()
+    row = lax.broadcasted_iota(jnp.int32, (128, 128), 0)
+    near = lax.axis_index("band") < RING
+    weights = weights_ref[...]
 
     def visiting(n):
-        packed = jnp.where(band_ref[0] < RING, near_ref[n], far_ref[n])
-        return image_columns(with_mirror(packed), places(n, n), 24, 8 * n)
-
-    block0, block1 = visiting(0), visiting(1)
-    block = image_columns(with_mirror(own_ref[...]), place, 24, 16)
-    half = dot(weights, block0 + block1 + block)
-    half = half + dot(weights, jnp.where(row < 16, block, 0.0), turn_right=True)
+        packed = jnp.where(near, near_ref[n], far_ref[n])
+        return image_columns(packed, places(n, n), 8 * n)
+
+    half = half_ref[...] + dot(weights, jnp.where(row < 16, visiting(0) + visiting(1), 0.0))
     theta = dot(half, tall([weights]), turn_right=True)
     work = gram_ref[...] + move(theta, 0, 8)
     for k in range(8):
@@ -356,7 +366,7 @@
     lax.fori_loop(0, f_ref.shape[1] // 32, body, 0)
 
 
-def edge_kernel(words, partial, across, beside, out):
+def edge_kernel(partial, across, beside, out):
     def run(left, right):
         def body(i, carry):
             for x in range(4):
@@ -371,8 +381,9 @@
 
         lax.fori_loop(0, BLK, body, 0)
 
-    pl.when(words[1] == 0)(lambda: run(across, beside))
-    pl.when(words[1] == 1)(lambda: run(beside, across))
+    odd = lax.axis_index("domain") & 1
+    pl.when(odd == 0)(lambda: run(across, beside))
+    pl.when(odd == 1)(lambda: run(beside, across))
 
 
 def domain_parts(copies):
@@ -403,7 +414,6 @@
     domain = lax.axis_size("domain")
     cells_total = float(slab_width * rows_y * rows_z * domain)
     band = lax.axis_index("band")
-    words = jnp.stack([band, lax.axis_index("domain") & 1]).astype(jnp.int32)
     flat = (blocks, slab_width * rows_y, rows_z)
     big = flat[0] * flat[1] * flat[2]
     slab = jax.ShapeDtypeStruct(flat, F32)
@@ -425,7 +435,7 @@
         lax.ppermute(quarters[k], "band", [(0, 2 * k), (1, 2 * k + 1)]) for k in (1, 3, 2)
     ]
     inner, sums = inner_part(orbitals, tile)
-    arrived, inner, sums, words = lax.optimization_barrier((arrived, inner, sums, words))
+    arrived, inner, sums = lax.optimization_barrier((arrived, inner, sums))
     piece = jnp.where(band < 2, quarters[0], 0.0)
     for part in arrived:
         piece = piece + part
@@ -472,10 +482,10 @@
         combine_kernel,
         (slab, tile, tile),
         scratch=[pltpu.VMEM((24, 8, 128), F32)],
-        specs=[SMEM] + [VMEM] * 11,
+        specs=[VMEM] * 11,
         flops=48 * big,
         bytes_moved=16 * big,
-    )(words, sums, *pieces, own)
+    )(sums, *pieces, own)
     across, beside = exchanged(basis)
     inner = inner_part(basis.reshape(orbitals.shape))[0].reshape(flat)
     shared = sums
@@ -485,15 +495,16 @@
     shared = shared + lax.ppermute(shared, "band", [(0, 4), (1, 5)])
     shared = shared + lax.ppermute(shared, "band", [(0, 2), (1, 3), (4, 6), (5, 7)])
     far = lax.ppermute(shared, "band", [(y, y + RING) for y in range(RING)])
-    splat = call(
-        coeff_kernel, jax.ShapeDtypeStruct((8, 8, 128), F32), specs=[SMEM] + [VMEM] * 5
-    )(words, weights, gram, sums, shared, far)
+    ordered, half = call(prepare_kernel, (tile, tile), specs=[VMEM] * 2)(weights, sums)
+    splat = call(coeff_kernel, jax.ShapeDtypeStruct((8, 8, 128), F32), specs=[VMEM] * 5)(
+        ordered, half, gram, shared, far
+    )
     partial = call(
         partial_kernel, slab, specs=[VMEM] * 3, flops=16 * big, bytes_moved=12 * big
     )(basis, inner, splat)
     residual = call(
-        edge_kernel, slab, specs=[SMEM] + [VMEM] * 3, flops=20 * big, bytes_moved=16 * big
-    )(words, partial, across, beside)
+        edge_kernel, slab, specs=[VMEM] * 3, flops=20 * big, bytes_moved=16 * big
+    )(partial, across, beside)
     return (basis.reshape(orbitals.shape), residual.reshape(orbitals.shape))
 
 

time: 136 us -> 134 us (0.985)
  other arithmetic: 3.2 us -> 1.49 us
    pallas_call x2 -> x3, Pallas kernels: 4.32 us -> 3.8 us  [the longest x1 1.63 us: local(): call(coeff_kernel, jax.ShapeDtypeStruct((8, 8, 128), F32), specs=[VMEM] * 5)]
where the time goes in v15:
time: 134 us; the launch traced here: 133 us
  starting transfers between devices  55.1 us (41%)
  waiting for transfers between devices  30.3 us (23%)
  Pallas kernels  22.6 us (17%)
  blocking collectives  21.2 us (16%)
  other arithmetic  1.49 us (1%)
    ppermute x8, starting transfers between devices, ring_shift(): return lax.ppermute(block, 'band', pairs)  23 us
    all_to_all x1, blocking collectives, domain_parts(): return lax.all_to_all(copies, 'domain', 0, 0)  21.2 us
    ppermute x3, waiting for transfers between devices, local(): lax.ppermute(quarters[k], 'band', [(0, 2 * k), (1, 2 * k + 1)])  11.6 us
    ppermute x3, starting transfers between devices, local(): lax.ppermute(quarters[k], 'band', [(0, 2 * k), (1, 2 * k + 1)])  9.65 us
    ppermute x8, waiting for transfers between devices, ring_shift(): return lax.ppermute(block, 'band', pairs)  6.34 us
    pallas_call x4, Pallas kernels, stage(): call(lambda *refs: stage_kernel(len(pieces), fresh, imaged, last, *refs),...  6.12 us
    pallas_call x2, Pallas kernels, inner_part(): call(inner_kernel, (field, *sums), specs=[VMEM] * 2, flops=60 * big, byte...  6.04 us
    ppermute x1, waiting for transfers between devices, neighbours(): lax.ppermute(block, 'domain', [((i + 1) % count, i) for i in range(count)])  5.5 us
  transfers between devices with their start and end apart: 20, of which 12 were waited for; matrix products, arithmetic and copies ran while one was open for 0% of the time, Pallas kernels for 12%

profile of v15, /device:TPU:1, one launch (start us, length us, event | category | flops | bytes accessed | tf_op | source)
XLA Modules:
  0.0 132.9 jit_solution(12683755064339794301)
XLA Ops:
  2.0 5.1 %collective-permute-start = (f32[2,256,128]{2,1,0:T(8,128)S(1)}, f32[2,256,128]{2,1,0:T(8,128)S(1)}, u32[]{:S(2)}, u32[]{:S(2)}) collective-permute-start(f32[2,256,128]{2,1,0:T(8,128)S(1)} %bitcast.33), channel_id=1, source_target_pairs={{0,64},{32,96},{1,65},{33,97},{2,66},{34,98},{3,67},{35,99},{4,68}... | collective-permute-start | bytes 786440 | tf_op jit(solution)/shard_map/ppermute | solution.py:435
  7.1 2.3 %collective-permute-start.1 = (f32[2,256,128]{2,1,0:T(8,128)S(1)}, f32[2,256,128]{2,1,0:T(8,128)S(1)}, u32[]{:S(2)}, u32[]{:S(2)}) collective-permute-start(f32[2,256,128]{2,1,0:T(8,128)S(1)} %bitcast.32), channel_id=1, source_target_pairs={{0,192},{32,224},{1,193},{33,225},{2,194},{34,226},{3,195},{35,227... | collective-permute-start | bytes 786440 | tf_op jit(solution)/shard_map/ppermute | solution.py:435
  9.5 2.2 %collective-permute-start.2 = (f32[2,256,128]{2,1,0:T(8,128)S(1)}, f32[2,256,128]{2,1,0:T(8,128)S(1)}, u32[]{:S(2)}, u32[]{:S(2)}) collective-permute-start(f32[2,256,128]{2,1,0:T(8,128)S(1)} %bitcast.31), channel_id=1, source_target_pairs={{0,128},{32,160},{1,129},{33,161},{2,130},{34,162},{3,131},{35,163... | collective-permute-start | bytes 786440 | tf_op jit(solution)/shard_map/ppermute | solution.py:435
  11.7 3.3 %shard_map.41 = (f32[8,4,64,128]{3,2,1,0:T(8,128)S(1)}, f32[8,128]{1,0:T(8,128)S(1)}) custom-call(f32[8,4,64,128]{3,2,1,0:T(8,128)S(1)} %copy-done, f32[4,64,128]{2,1,0:T(8,128)S(1)} %copy-done.3), custom_call_target="tpu_custom_call" | custom-call | flops 15728640 | bytes 2097152 | tf_op jit(solution)/shard_map/pallas_call | solution.py:424
  15.0 11.5 %collective-permute-done.1 = f32[2,256,128]{2,1,0:T(8,128)S(1)} collective-permute-done((f32[2,256,128]{2,1,0:T(8,128)S(1)}, f32[2,256,128]{2,1,0:T(8,128)S(1)}, u32[]{:S(2)}, u32[]{:S(2)}) %collective-permute-start.1) | collective-permute-done | bytes 262176 | tf_op jit(solution)/shard_map/ppermute | solution.py:435
  26.6 2.0 %collective-permute-start.3 = (f32[2,256,128]{2,1,0:T(8,128)S(1)}, f32[2,256,128]{2,1,0:T(8,128)}, u32[]{:S(2)}, u32[]{:S(2)}) collective-permute-start(f32[2,256,128]{2,1,0:T(8,128)S(1)} %fusion.1), channel_id=1, source_target_pairs={{0,256},{32,288},{64,320},{96,352},{128,384},{160,416},{192,448},{... | collective-permute-start | bytes 786440 | tf_op jit(solution)/shard_map/ppermute | solution.py:443
  28.6 4.5 %collective-permute-start.10 = (f32[8,256,128]{2,1,0:T(8,128)S(1)}, f32[8,256,128]{2,1,0:T(8,128)S(1)}, u32[]{:S(2)}, u32[]{:S(2)}) collective-permute-start(f32[8,256,128]{2,1,0:T(8,128)S(1)} %bitcast.18), channel_id=1, source_target_pairs={{0,1},{1,2},{2,3},{3,4},{4,5},{5,6},{6,7},{7,8},{8,9},{9,10},{10,1... | collective-permute-start | bytes 3145736 | tf_op jit(solution)/shard_map/ppermute | solution.py:400
  33.1 1.9 %collective-permute-start.11 = (f32[8,256,128]{2,1,0:T(8,128)S(1)}, f32[8,256,128]{2,1,0:T(8,128)}, u32[]{:S(2)}, u32[]{:S(2)}) collective-permute-start(f32[8,256,128]{2,1,0:T(8,128)S(1)} %bitcast.19), channel_id=1, source_target_pairs={{1,0},{2,1},{3,2},{4,3},{5,4},{6,5},{7,6},{8,7},{9,8},{10,9},{11,1... | collective-permute-start | bytes 3145736 | tf_op jit(solution)/shard_map/ppermute | solution.py:401
  37.0 3.4 %collective-permute-start.4 = (f32[2,256,128]{2,1,0:T(8,128)S(1)}, f32[2,256,128]{2,1,0:T(8,128)S(1)}, u32[]{:S(2)}, u32[]{:S(2)}) collective-permute-start(f32[2,256,128]{2,1,0:T(8,128)S(1)} %broadcast_select_fusion.refs_0_), channel_id=1, source_target_pairs={{0,32},{32,64},{64,96},{96,128},{128,160},{160,192},{192,224},{224... | collective-permute-start | bytes 786440 | tf_op jit(solution)/shard_map/ppermute | solution.py:395
  40.4 2.1 %collective-permute-done.5.refs_2_ = f32[2,256,128]{2,1,0:T(8,128)S(1)} collective-permute-done((f32[2,256,128]{2,1,0:T(8,128)S(1)}, f32[2,256,128]{2,1,0:T(8,128)S(1)}, u32[]{:S(2)}, u32[]{:S(2)}) %collective-permute-start.5) | collective-permute-done | bytes 262176 | tf_op jit(solution)/shard_map/ppermute | solution.py:395
  42.5 4.3 %collective-permute-start.7 = (f32[2,256,128]{2,1,0:T(8,128)S(1)}, f32[2,256,128]{2,1,0:T(8,128)S(1)}, u32[]{:S(2)}, u32[]{:S(2)}) collective-permute-start(f32[2,256,128]{2,1,0:T(8,128)S(1)} %collective-permute-done.5.refs_2_), channel_id=1, source_target_pairs={{0,224},{32,0},{64,32},{96,64},{128,96},{160,128},{192,160},{224,1... | collective-permute-start | bytes 786440 | tf_op jit(solution)/shard_map/ppermute | solution.py:395
  51.5 4.3 %collective-permute-start.9 = (f32[2,256,128]{2,1,0:T(8,128)S(1)}, f32[2,256,128]{2,1,0:T(8,128)S(1)}, u32[]{:S(2)}, u32[]{:S(2)}) collective-permute-start(f32[2,256,128]{2,1,0:T(8,128)S(1)} %collective-permute-done.7.refs_4_), channel_id=1, source_target_pairs={{0,224},{32,0},{64,32},{96,64},{128,96},{160,128},{192,160},{224,1... | collective-permute-start | bytes 786440 | tf_op jit(solution)/shard_map/ppermute | solution.py:395
  59.4 5.5 %collective-permute-done.11.right = f32[8,256,128]{2,1,0:T(8,128)} collective-permute-done((f32[8,256,128]{2,1,0:T(8,128)S(1)}, f32[8,256,128]{2,1,0:T(8,128)}, u32[]{:S(2)}, u32[]{:S(2)}) %collective-permute-start.11) | collective-permute-done | bytes 1048608 | tf_op jit(solution)/shard_map/ppermute | solution.py:401
  66.9 3.4 %collective-permute-start.12 = (f32[1,256,128]{2,1,0:T(8,128)S(1)}, f32[1,256,128]{2,1,0:T(8,128)S(1)}, u32[]{:S(2)}, u32[]{:S(2)}) collective-permute-start(f32[1,256,128]{2,1,0:T(8,128)S(1)} %slice.37), channel_id=1, source_target_pairs={{0,32},{32,64},{64,96},{96,128},{128,160},{160,192},{192,224},{224... | collective-permute-start | bytes 393224 | tf_op jit(solution)/shard_map/ppermute | solution.py:395
  70.3 2.2 %shard_map.44 = (f32[8,256,128]{2,1,0:T(8,128)S(1)}, f32[8,128]{1,0:T(8,128)S(1)}) custom-call(f32[8,256,128]{2,1,0:T(8,128)S(1)} %bitcast.22, f32[8,256,128]{2,1,0:T(8,128)S(1)} %bitcast.29, f32[8,256,128]{2,1,0:T(8,128)S(1)} %collective-permute-done.10.left, f32[8,256,128]{2,1,0:T(8,128)} %collective-permute-done.11.right), custom_call_target="tpu_custom_call" | custom-call | flops 13107200 | bytes 5242880 | tf_op jit(solution)/shard_map/pallas_call | solution.py:468
  72.5 3.0 %shard_map.45.refs_11_ = f32[8,128]{1,0:T(8,128)S(1)} custom-call(f32[2,256,128]{2,1,0:T(8,128)S(1)} %broadcast_select_fusion.refs_0_, f32[2,256,128]{2,1,0:T(8,128)S(1)} %collective-permute-done.4.refs_1_, f32[2,256,128]{2,1,0:T(8,128)S(1)} %collective-permute-done.5.refs_2_, f32[2,256,128]{2,1,0:T(8,128)S(1)} %collective-permute-done.6.refs_3_, ...), custom_call_target="tpu_custom_call" | custom-call | flops 5242880 | bytes 2621440 | tf_op jit(solution)/shard_map/pallas_call | solution.py:448
  78.3 21.2 %all_to_all.5.refs_0_ = f32[32,8,128]{2,1,0:T(8,128)S(1)} all-to-all(f32[32,8,128]{2,1,0:T(8,128)S(1)} %shard_map.46), channel_id=1, replica_groups=mesh['band'=16,'domain'=32] {'domain'}, dimensions={0} | all-to-all | bytes 262144 | tf_op jit(solution)/shard_map/all_to_all | solution.py:390
  99.6 3.8 %shard_map.48 = (f32[8,256,128]{2,1,0:T(8,128)}, f32[8,128]{1,0:T(8,128)S(1)}, f32[8,128]{1,0:T(8,128)S(1)}) custom-call(f32[8,128]{1,0:T(8,128)S(1)} %shard_map.47.sums_ref.own_ref, f32[2,256,128]{2,1,0:T(8,128)S(1)} %broadcast_select_fusion.refs_0_, f32[2,256,128]{2,1,0:T(8,128)S(1)} %collective-permute-done.4.refs_1_, ...), custom_call_target="tpu_custom_call" | custom-call | flops 12582912 | bytes 4194304 | tf_op jit(solution)/shard_map/pallas_call | solution.py:481
  103.3 2.1 %collective-permute-start.18 = (f32[8,256,128]{2,1,0:T(8,128)}, f32[8,256,128]{2,1,0:T(8,128)S(1)}, u32[]{:S(2)}, u32[]{:S(2)}) collective-permute-start(f32[8,256,128]{2,1,0:T(8,128)} %get-tuple-element.37.f_ref), channel_id=1, source_target_pairs={{0,31},{1,2},{2,1},{3,4},{4,3},{5,6},{6,5},{7,8},{8,7},{9,10},{10,... | collective-permute-start | bytes 3145736 | tf_op jit(solution)/shard_map/ppermute | solution.py:409
  105.4 3.7 %collective-permute-start.19 = (f32[8,256,128]{2,1,0:T(8,128)}, f32[8,256,128]{2,1,0:T(8,128)S(1)}, u32[]{:S(2)}, u32[]{:S(2)}) collective-permute-start(f32[8,256,128]{2,1,0:T(8,128)} %get-tuple-element.37.f_ref), channel_id=1, source_target_pairs={{0,1},{1,0},{2,3},{3,2},{4,5},{5,4},{6,7},{7,6},{8,9},{9,8},{10,11... | collective-permute-start | bytes 3145736 | tf_op jit(solution)/shard_map/ppermute | solution.py:409
  111.1 2.7 %collective-permute-done.14 = f32[8,128]{1,0:T(8,128)S(1)} collective-permute-done((f32[8,128]{1,0:T(8,128)S(1)}, f32[8,128]{1,0:T(8,128)S(1)}, u32[]{:S(2)}, u32[]{:S(2)}) %collective-permute-start.14) | collective-permute-done | bytes 4128 | tf_op jit(solution)/shard_map/ppermute | solution.py:492
  118.2 3.5 %collective-permute-start.17 = (f32[2,8,128]{2,1,0:T(8,128)S(1)}, f32[2,8,128]{2,1,0:T(8,128)S(1)}, u32[]{:S(2)}, u32[]{:S(2)}) collective-permute-start(f32[2,8,128]{2,1,0:T(8,128)S(1)} %fusion.3.near_ref), channel_id=1, source_target_pairs={{0,256},{32,288},{64,320},{96,352},{128,384},{160,416},{192,448},{... | collective-permute-start | bytes 24584 | tf_op jit(solution)/shard_map/ppermute | solution.py:497
  123.7 2.7 %shard_map.49 = f32[8,4,64,128]{3,2,1,0:T(8,128)S(1)} custom-call(f32[8,4,64,128]{3,2,1,0:T(8,128)S(1)} %bitcast.27, f32[4,64,128]{2,1,0:T(8,128)S(1)} %copy-done.3), custom_call_target="tpu_custom_call" | custom-call | flops 15728640 | bytes 2097152 | tf_op jit(solution)/shard_map/pallas_call | solution.py:424
  129.0 2.4 %collective-permute-done.18.across = f32[8,256,128]{2,1,0:T(8,128)S(1)} collective-permute-done((f32[8,256,128]{2,1,0:T(8,128)}, f32[8,256,128]{2,1,0:T(8,128)S(1)}, u32[]{:S(2)}, u32[]{:S(2)}) %collective-permute-start.18) | collective-permute-done | bytes 1048608 | tf_op jit(solution)/shard_map/ppermute | solution.py:409
  (47 shorter events, 28.8 us)
Async XLA Ops:
  0.6 11.1 %copy-start = (f32[8,4,64,128]{3,2,1,0:T(8,128)S(1)}, f32[8,4,64,128]{3,2,1,0:T(8,128)}, u32[]{:S(2)}) copy-start(f32[8,4,64,128]{3,2,1,0:T(8,128)} %f_ref.1) | copy-start | bytes 3145732
  0.6 11.1 %copy-start.3 = (f32[4,64,128]{2,1,0:T(8,128)S(1)}, f32[4,64,128]{2,1,0:T(8,128)}, u32[]{:S(2)}) copy-start(f32[4,64,128]{2,1,0:T(8,128)} %v_ref.3) | copy-start | bytes 393220
  2.0 13.0 %collective-permute-start = (f32[2,256,128]{2,1,0:T(8,128)S(1)}, f32[2,256,128]{2,1,0:T(8,128)S(1)}, u32[]{:S(2)}, u32[]{:S(2)}) collective-permute-start(f32[2,256,128]{2,1,0:T(8,128)S(1)} %bitcast.33), channel_id=1, source_target_pairs={{0,64},{32,96},{1,65},{33,97},{2,66},{34,98},{3,67},{35,99},{4,68}... | collective-permute-start | bytes 786440 | tf_op jit(solution)/shard_map/ppermute | solution.py:435
  7.1 19.5 %collective-permute-start.1 = (f32[2,256,128]{2,1,0:T(8,128)S(1)}, f32[2,256,128]{2,1,0:T(8,128)S(1)}, u32[]{:S(2)}, u32[]{:S(2)}) collective-permute-start(f32[2,256,128]{2,1,0:T(8,128)S(1)} %bitcast.32), channel_id=1, source_target_pairs={{0,192},{32,224},{1,193},{33,225},{2,194},{34,226},{3,195},{35,227... | collective-permute-start | bytes 786440 | tf_op jit(solution)/shard_map/ppermute | solution.py:435
  9.5 17.1 %collective-permute-start.2 = (f32[2,256,128]{2,1,0:T(8,128)S(1)}, f32[2,256,128]{2,1,0:T(8,128)S(1)}, u32[]{:S(2)}, u32[]{:S(2)}) collective-permute-start(f32[2,256,128]{2,1,0:T(8,128)S(1)} %bitcast.31), channel_id=1, source_target_pairs={{0,128},{32,160},{1,129},{33,161},{2,130},{34,162},{3,131},{35,163... | collective-permute-start | bytes 786440 | tf_op jit(solution)/shard_map/ppermute | solution.py:435
  26.6 8.4 %collective-permute-start.3 = (f32[2,256,128]{2,1,0:T(8,128)S(1)}, f32[2,256,128]{2,1,0:T(8,128)}, u32[]{:S(2)}, u32[]{:S(2)}) collective-permute-start(f32[2,256,128]{2,1,0:T(8,128)S(1)} %fusion.1), channel_id=1, source_target_pairs={{0,256},{32,288},{64,320},{96,352},{128,384},{160,416},{192,448},{... | collective-permute-start | bytes 786440 | tf_op jit(solution)/shard_map/ppermute | solution.py:443
  28.6 30.8 %collective-permute-start.10 = (f32[8,256,128]{2,1,0:T(8,128)S(1)}, f32[8,256,128]{2,1,0:T(8,128)S(1)}, u32[]{:S(2)}, u32[]{:S(2)}) collective-permute-start(f32[8,256,128]{2,1,0:T(8,128)S(1)} %bitcast.18), channel_id=1, source_target_pairs={{0,1},{1,2},{2,3},{3,4},{4,5},{5,6},{6,7},{7,8},{8,9},{9,10},{10,1... | collective-permute-start | bytes 3145736 | tf_op jit(solution)/shard_map/ppermute | solution.py:400
  33.1 31.8 %collective-permute-start.11 = (f32[8,256,128]{2,1,0:T(8,128)S(1)}, f32[8,256,128]{2,1,0:T(8,128)}, u32[]{:S(2)}, u32[]{:S(2)}) collective-permute-start(f32[8,256,128]{2,1,0:T(8,128)S(1)} %bitcast.19), channel_id=1, source_target_pairs={{1,0},{2,1},{3,2},{4,3},{5,4},{6,5},{7,6},{8,7},{9,8},{10,9},{11,1... | collective-permute-start | bytes 3145736 | tf_op jit(solution)/shard_map/ppermute | solution.py:401
  35.1 7.4 %collective-permute-start.5 = (f32[2,256,128]{2,1,0:T(8,128)S(1)}, f32[2,256,128]{2,1,0:T(8,128)S(1)}, u32[]{:S(2)}, u32[]{:S(2)}) collective-permute-start(f32[2,256,128]{2,1,0:T(8,128)S(1)} %broadcast_select_fusion.refs_0_), channel_id=1, source_target_pairs={{0,224},{32,0},{64,32},{96,64},{128,96},{160,128},{192,160},{224,1... | collective-permute-start | bytes 786440 | tf_op jit(solution)/shard_map/ppermute | solution.py:395
  37.0 10.5 %collective-permute-start.4 = (f32[2,256,128]{2,1,0:T(8,128)S(1)}, f32[2,256,128]{2,1,0:T(8,128)S(1)}, u32[]{:S(2)}, u32[]{:S(2)}) collective-permute-start(f32[2,256,128]{2,1,0:T(8,128)S(1)} %broadcast_select_fusion.refs_0_), channel_id=1, source_target_pairs={{0,32},{32,64},{64,96},{96,128},{128,160},{160,192},{192,224},{224... | collective-permute-start | bytes 786440 | tf_op jit(solution)/shard_map/ppermute | solution.py:395
  42.5 9.0 %collective-permute-start.7 = (f32[2,256,128]{2,1,0:T(8,128)S(1)}, f32[2,256,128]{2,1,0:T(8,128)S(1)}, u32[]{:S(2)}, u32[]{:S(2)}) collective-permute-start(f32[2,256,128]{2,1,0:T(8,128)S(1)} %collective-permute-done.5.refs_2_), channel_id=1, source_target_pairs={{0,224},{32,0},{64,32},{96,64},{128,96},{160,128},{192,160},{224,1... | collective-permute-start | bytes 786440 | tf_op jit(solution)/shard_map/ppermute | solution.py:395
  47.6 9.0 %collective-permute-start.6 = (f32[2,256,128]{2,1,0:T(8,128)S(1)}, f32[2,256,128]{2,1,0:T(8,128)S(1)}, u32[]{:S(2)}, u32[]{:S(2)}) collective-permute-start(f32[2,256,128]{2,1,0:T(8,128)S(1)} %collective-permute-done.4.refs_1_), channel_id=1, source_target_pairs={{0,32},{32,64},{64,96},{96,128},{128,160},{160,192},{192,224},{224... | collective-permute-start | bytes 786440 | tf_op jit(solution)/shard_map/ppermute | solution.py:395
  51.5 13.5 %collective-permute-start.9 = (f32[2,256,128]{2,1,0:T(8,128)S(1)}, f32[2,256,128]{2,1,0:T(8,128)S(1)}, u32[]{:S(2)}, u32[]{:S(2)}) collective-permute-start(f32[2,256,128]{2,1,0:T(8,128)S(1)} %collective-permute-done.7.refs_4_), channel_id=1, source_target_pairs={{0,224},{32,0},{64,32},{96,64},{128,96},{160,128},{192,160},{224,1... | collective-permute-start | bytes 786440 | tf_op jit(solution)/shard_map/ppermute | solution.py:395
  56.6 10.3 %collective-permute-start.8 = (f32[2,256,128]{2,1,0:T(8,128)S(1)}, f32[2,256,128]{2,1,0:T(8,128)S(1)}, u32[]{:S(2)}, u32[]{:S(2)}) collective-permute-start(f32[2,256,128]{2,1,0:T(8,128)S(1)} %collective-permute-done.6.refs_3_), channel_id=1, source_target_pairs={{0,32},{32,64},{64,96},{96,128},{128,160},{160,192},{192,224},{224... | collective-permute-start | bytes 786440 | tf_op jit(solution)/shard_map/ppermute | solution.py:395
  65.0 10.5 %collective-permute-start.13 = (f32[1,256,128]{2,1,0:T(8,128)S(1)}, f32[1,256,128]{2,1,0:T(8,128)S(1)}, u32[]{:S(2)}, u32[]{:S(2)}) collective-permute-start(f32[1,256,128]{2,1,0:T(8,128)S(1)} %slice.36), channel_id=1, source_target_pairs={{0,224},{32,0},{64,32},{96,64},{128,96},{160,128},{192,160},{224,1... | collective-permute-start | bytes 393224 | tf_op jit(solution)/shard_map/ppermute | solution.py:395
  66.9 10.3 %collective-permute-start.12 = (f32[1,256,128]{2,1,0:T(8,128)S(1)}, f32[1,256,128]{2,1,0:T(8,128)S(1)}, u32[]{:S(2)}, u32[]{:S(2)}) collective-permute-start(f32[1,256,128]{2,1,0:T(8,128)S(1)} %slice.37), channel_id=1, source_target_pairs={{0,32},{32,64},{64,96},{96,128},{128,160},{160,192},{192,224},{224... | collective-permute-start | bytes 393224 | tf_op jit(solution)/shard_map/ppermute | solution.py:395
  103.3 28.1 %collective-permute-start.18 = (f32[8,256,128]{2,1,0:T(8,128)}, f32[8,256,128]{2,1,0:T(8,128)S(1)}, u32[]{:S(2)}, u32[]{:S(2)}) collective-permute-start(f32[8,256,128]{2,1,0:T(8,128)} %get-tuple-element.37.f_ref), channel_id=1, source_target_pairs={{0,31},{1,2},{2,1},{3,4},{4,3},{5,6},{6,5},{7,8},{8,7},{9,10},{10,... | collective-permute-start | bytes 3145736 | tf_op jit(solution)/shard_map/ppermute | solution.py:409
  105.4 26.0 %collective-permute-start.19 = (f32[8,256,128]{2,1,0:T(8,128)}, f32[8,256,128]{2,1,0:T(8,128)S(1)}, u32[]{:S(2)}, u32[]{:S(2)}) collective-permute-start(f32[8,256,128]{2,1,0:T(8,128)} %get-tuple-element.37.f_ref), channel_id=1, source_target_pairs={{0,1},{1,0},{2,3},{3,2},{4,5},{5,4},{6,7},{7,6},{8,9},{9,8},{10,11... | collective-permute-start | bytes 3145736 | tf_op jit(solution)/shard_map/ppermute | solution.py:409
  109.1 4.6 %collective-permute-start.14 = (f32[8,128]{1,0:T(8,128)S(1)}, f32[8,128]{1,0:T(8,128)S(1)}, u32[]{:S(2)}, u32[]{:S(2)}) collective-permute-start(f32[8,128]{1,0:T(8,128)S(1)} %shard_map.47.sums_ref.own_ref), channel_id=1, source_target_pairs={{0,32},{32,0},{1,33},{33,1},{2,34},{34,2},{3,35},{35,3},{4,36},{36... | collective-permute-start | bytes 12296 | tf_op jit(solution)/shard_map/ppermute | solution.py:492
  113.8 2.4 %collective-permute-start.15 = (f32[2,8,128]{2,1,0:T(8,128)S(1)}, f32[2,8,128]{2,1,0:T(8,128)S(1)}, u32[]{:S(2)}, u32[]{:S(2)}) collective-permute-start(f32[2,8,128]{2,1,0:T(8,128)S(1)} %maximum_select_fusion), channel_id=1, source_target_pairs={{0,128},{32,160},{1,129},{33,161},{2,130},{34,162},{3,131},{35,163... | collective-permute-start | bytes 24584 | tf_op jit(solution)/shard_map/ppermute | solution.py:495
  116.1 2.1 %collective-permute-start.16 = (f32[2,8,128]{2,1,0:T(8,128)S(1)}, f32[2,8,128]{2,1,0:T(8,128)S(1)}, u32[]{:S(2)}, u32[]{:S(2)}) collective-permute-start(f32[2,8,128]{2,1,0:T(8,128)S(1)} %fusion.2), channel_id=1, source_target_pairs={{0,64},{32,96},{128,192},{160,224},{1,65},{33,97},{129,193},{161,2... | collective-permute-start | bytes 24584 | tf_op jit(solution)/shard_map/ppermute | solution.py:496
  118.2 8.6 %collective-permute-start.17 = (f32[2,8,128]{2,1,0:T(8,128)S(1)}, f32[2,8,128]{2,1,0:T(8,128)S(1)}, u32[]{:S(2)}, u32[]{:S(2)}) collective-permute-start(f32[2,8,128]{2,1,0:T(8,128)S(1)} %fusion.3.near_ref), channel_id=1, source_target_pairs={{0,256},{32,288},{64,320},{96,352},{128,384},{160,416},{192,448},{... | collective-permute-start | bytes 24584 | tf_op jit(solution)/shard_map/ppermute | solution.py:497
  122.5 1.3 copy-start.1
  123.7 4.6 %copy-start.2 = (f32[8,256,128]{2,1,0:T(8,128)S(1)}, f32[8,256,128]{2,1,0:T(8,128)}, u32[]{:S(2)}) copy-start(f32[8,256,128]{2,1,0:T(8,128)} %get-tuple-element.37.f_ref) | copy-start | bytes 3145732

commit v16 on v15

--- a/solution.py
+++ b/solution.py
@@ -432,7 +432,8 @@
     own = orbitals.reshape(flat)
     quarters = [own[2 * k : 2 * k + 2] for k in range(4)]
     arrived = [
-        lax.ppermute(quarters[k], "band", [(0, 2 * k), (1, 2 * k + 1)]) for k in (1, 3, 2)
+        lax.ppermute(quarters[k], "band", [(0, place), (1, place + 1)])
+        for k, place in ((1, 2), (3, 6), (2, RING + 4))
     ]
     inner, sums = inner_part(orbitals, tile)
     arrived, inner, sums = lax.optimization_barrier((arrived, inner, sums))
@@ -440,8 +441,11 @@
     for part in arrived:
         piece = piece + part
     left, right = neighbours(own)
-    crossed = lax.ppermute(piece, "band", [(y, y + RING) for y in range(RING)])
-    piece = jnp.where(band < RING, piece, crossed)
+    far_first = (4, 5)
+    pairs = [(y + RING, y) if y in far_first else (y, y + RING) for y in range(RING)]
+    crossed = lax.ppermute(piece, "band", pairs)
+    from_far = ((band & 7) == far_first[0]) | ((band & 7) == far_first[1])
+    piece = jnp.where((band < RING) != from_far, piece, crossed)
 
     def stage(fresh, imaged, pieces, *sums, last=False):
         sources = (*pieces, own, *((image,) if imaged else ()), *sums)

time: 134 us -> 146 us (1.090)
  the two profiles are of different devices: /device:TPU:1 before, /device:TPU:24 now
where the time goes in v16:
time: 146 us; the launch traced here: 145 us
  starting transfers between devices  65.9 us (45%)
  waiting for transfers between devices  27.5 us (19%)
  blocking collectives  24.4 us (17%)
  Pallas kernels  23.5 us (16%)
  other arithmetic  1.49 us (1%)
    ppermute x8, starting transfers between devices, ring_shift(): return lax.ppermute(block, 'band', pairs)  33 us
    all_to_all x1, blocking collectives, domain_parts(): return lax.all_to_all(copies, 'domain', 0, 0)  24.4 us
    ppermute x1, starting transfers between devices, neighbours(): lax.ppermute(block, 'domain', [((i + 1) % count, i) for i in range(count)])  17 us
    ppermute x3, waiting for transfers between devices, local(): lax.ppermute(quarters[k], 'band', [(0, place), (1, place + 1)])  10.4 us
    pallas_call x4, Pallas kernels, stage(): call(lambda *refs: stage_kernel(len(pieces), fresh, imaged, last, *refs),...  6.13 us
    pallas_call x2, Pallas kernels, inner_part(): call(inner_kernel, (field, *sums), specs=[VMEM] * 2, flops=60 * big, byte...  6.04 us
    ppermute x1, waiting for transfers between devices, local(): lax.ppermute(shared, 'band', [(0, 2), (1, 3), (4, 6), (5, 7)])  6.01 us
    ppermute x1, waiting for transfers between devices, local(): far = lax.ppermute(shared, 'band', [(y, y + RING) for y in range(RING)])  5.27 us
  transfers between devices with their start and end apart: 20, of which 7 were waited for; matrix products, arithmetic and copies ran while one was open for 0% of the time, Pallas kernels for 11%

profile of v16, /device:TPU:24, one launch (start us, length us, event | category | flops | bytes accessed | tf_op | source)
XLA Modules:
  0.0 145.0 jit_solution(5489537784234874316)
XLA Ops:
  4.7 3.3 %shard_map.41 = (f32[8,4,64,128]{3,2,1,0:T(8,128)S(1)}, f32[8,128]{1,0:T(8,128)S(1)}) custom-call(f32[8,4,64,128]{3,2,1,0:T(8,128)S(1)} %copy-done, f32[4,64,128]{2,1,0:T(8,128)S(1)} %copy-done.3), custom_call_target="tpu_custom_call" | custom-call | flops 15728640 | bytes 2097152 | tf_op jit(solution)/shard_map/pallas_call | solution.py:424
  8.0 10.4 %collective-permute-done = f32[2,256,128]{2,1,0:T(8,128)S(1)} collective-permute-done((f32[2,256,128]{2,1,0:T(8,128)S(1)}, f32[2,256,128]{2,1,0:T(8,128)S(1)}, u32[]{:S(2)}, u32[]{:S(2)}) %collective-permute-start) | collective-permute-done | bytes 262176 | tf_op jit(solution)/shard_map/ppermute | solution.py:435
  18.4 2.0 %collective-permute-start.3 = (f32[2,256,128]{2,1,0:T(8,128)S(1)}, f32[2,256,128]{2,1,0:T(8,128)}, u32[]{:S(2)}, u32[]{:S(2)}) collective-permute-start(f32[2,256,128]{2,1,0:T(8,128)S(1)} %fusion.1), channel_id=1, source_target_pairs={{0,256},{32,288},{64,320},{96,352},{384,128},{416,160},{192,448},{... | collective-permute-start | bytes 786440 | tf_op jit(solution)/shard_map/ppermute | solution.py:446
  20.4 1.9 %collective-permute-start.10 = (f32[8,256,128]{2,1,0:T(8,128)S(1)}, f32[8,256,128]{2,1,0:T(8,128)S(1)}, u32[]{:S(2)}, u32[]{:S(2)}) collective-permute-start(f32[8,256,128]{2,1,0:T(8,128)S(1)} %bitcast.18), channel_id=1, source_target_pairs={{0,1},{1,2},{2,3},{3,4},{4,5},{5,6},{6,7},{7,8},{8,9},{9,10},{10,1... | collective-permute-start | bytes 3145736 | tf_op jit(solution)/shard_map/ppermute | solution.py:400
  22.4 17.0 %collective-permute-start.11 = (f32[8,256,128]{2,1,0:T(8,128)S(1)}, f32[8,256,128]{2,1,0:T(8,128)}, u32[]{:S(2)}, u32[]{:S(2)}) collective-permute-start(f32[8,256,128]{2,1,0:T(8,128)S(1)} %bitcast.19), channel_id=1, source_target_pairs={{1,0},{2,1},{3,2},{4,3},{5,4},{6,5},{7,6},{8,7},{9,8},{10,9},{11,1... | collective-permute-start | bytes 3145736 | tf_op jit(solution)/shard_map/ppermute | solution.py:401
  39.4 1.9 %collective-permute-start.5 = (f32[2,256,128]{2,1,0:T(8,128)S(1)}, f32[2,256,128]{2,1,0:T(8,128)S(1)}, u32[]{:S(2)}, u32[]{:S(2)}) collective-permute-start(f32[2,256,128]{2,1,0:T(8,128)S(1)} %broadcast_select_fusion.refs_0_), channel_id=1, source_target_pairs={{0,224},{32,0},{64,32},{96,64},{128,96},{160,128},{192,160},{224,1... | collective-permute-start | bytes 786440 | tf_op jit(solution)/shard_map/ppermute | solution.py:395
  41.4 9.9 %collective-permute-start.4 = (f32[2,256,128]{2,1,0:T(8,128)S(1)}, f32[2,256,128]{2,1,0:T(8,128)S(1)}, u32[]{:S(2)}, u32[]{:S(2)}) collective-permute-start(f32[2,256,128]{2,1,0:T(8,128)S(1)} %broadcast_select_fusion.refs_0_), channel_id=1, source_target_pairs={{0,32},{32,64},{64,96},{96,128},{128,160},{160,192},{192,224},{224... | collective-permute-start | bytes 786440 | tf_op jit(solution)/shard_map/ppermute | solution.py:395
  51.3 2.4 %collective-permute-done.5.refs_2_ = f32[2,256,128]{2,1,0:T(8,128)S(1)} collective-permute-done((f32[2,256,128]{2,1,0:T(8,128)S(1)}, f32[2,256,128]{2,1,0:T(8,128)S(1)}, u32[]{:S(2)}, u32[]{:S(2)}) %collective-permute-start.5) | collective-permute-done | bytes 262176 | tf_op jit(solution)/shard_map/ppermute | solution.py:395
  53.7 1.9 %collective-permute-start.7 = (f32[2,256,128]{2,1,0:T(8,128)S(1)}, f32[2,256,128]{2,1,0:T(8,128)S(1)}, u32[]{:S(2)}, u32[]{:S(2)}) collective-permute-start(f32[2,256,128]{2,1,0:T(8,128)S(1)} %collective-permute-done.5.refs_2_), channel_id=1, source_target_pairs={{0,224},{32,0},{64,32},{96,64},{128,96},{160,128},{192,160},{224,1... | collective-permute-start | bytes 786440 | tf_op jit(solution)/shard_map/ppermute | solution.py:395
  55.6 5.1 %collective-permute-start.6 = (f32[2,256,128]{2,1,0:T(8,128)S(1)}, f32[2,256,128]{2,1,0:T(8,128)S(1)}, u32[]{:S(2)}, u32[]{:S(2)}) collective-permute-start(f32[2,256,128]{2,1,0:T(8,128)S(1)} %collective-permute-done.4.refs_1_), channel_id=1, source_target_pairs={{0,32},{32,64},{64,96},{96,128},{128,160},{160,192},{192,224},{224... | collective-permute-start | bytes 786440 | tf_op jit(solution)/shard_map/ppermute | solution.py:395
  63.2 1.9 %collective-permute-start.9 = (f32[2,256,128]{2,1,0:T(8,128)S(1)}, f32[2,256,128]{2,1,0:T(8,128)S(1)}, u32[]{:S(2)}, u32[]{:S(2)}) collective-permute-start(f32[2,256,128]{2,1,0:T(8,128)S(1)} %collective-permute-done.7.refs_4_), channel_id=1, source_target_pairs={{0,224},{32,0},{64,32},{96,64},{128,96},{160,128},{192,160},{224,1... | collective-permute-start | bytes 786440 | tf_op jit(solution)/shard_map/ppermute | solution.py:395
  65.1 5.1 %collective-permute-start.8 = (f32[2,256,128]{2,1,0:T(8,128)S(1)}, f32[2,256,128]{2,1,0:T(8,128)S(1)}, u32[]{:S(2)}, u32[]{:S(2)}) collective-permute-start(f32[2,256,128]{2,1,0:T(8,128)S(1)} %collective-permute-done.6.refs_3_), channel_id=1, source_target_pairs={{0,32},{32,64},{64,96},{96,128},{128,160},{160,192},{192,224},{224... | collective-permute-start | bytes 786440 | tf_op jit(solution)/shard_map/ppermute | solution.py:395
  72.7 1.9 %collective-permute-start.13 = (f32[1,256,128]{2,1,0:T(8,128)S(1)}, f32[1,256,128]{2,1,0:T(8,128)S(1)}, u32[]{:S(2)}, u32[]{:S(2)}) collective-permute-start(f32[1,256,128]{2,1,0:T(8,128)S(1)} %slice.36), channel_id=1, source_target_pairs={{0,224},{32,0},{64,32},{96,64},{128,96},{160,128},{192,160},{224,1... | collective-permute-start | bytes 393224 | tf_op jit(solution)/shard_map/ppermute | solution.py:395
  74.6 5.2 %collective-permute-start.12 = (f32[1,256,128]{2,1,0:T(8,128)S(1)}, f32[1,256,128]{2,1,0:T(8,128)S(1)}, u32[]{:S(2)}, u32[]{:S(2)}) collective-permute-start(f32[1,256,128]{2,1,0:T(8,128)S(1)} %slice.37), channel_id=1, source_target_pairs={{0,32},{32,64},{64,96},{96,128},{128,160},{160,192},{192,224},{224... | collective-permute-start | bytes 393224 | tf_op jit(solution)/shard_map/ppermute | solution.py:395
  79.8 2.2 %shard_map.44 = (f32[8,256,128]{2,1,0:T(8,128)S(1)}, f32[8,128]{1,0:T(8,128)S(1)}) custom-call(f32[8,256,128]{2,1,0:T(8,128)S(1)} %bitcast.22, f32[8,256,128]{2,1,0:T(8,128)S(1)} %bitcast.29, f32[8,256,128]{2,1,0:T(8,128)S(1)} %collective-permute-done.10.left, f32[8,256,128]{2,1,0:T(8,128)} %collective-permute-done.11.right), custom_call_target="tpu_custom_call" | custom-call | flops 13107200 | bytes 5242880 | tf_op jit(solution)/shard_map/pallas_call | solution.py:472
  82.0 3.0 %shard_map.45.refs_11_ = f32[8,128]{1,0:T(8,128)S(1)} custom-call(f32[2,256,128]{2,1,0:T(8,128)S(1)} %broadcast_select_fusion.refs_0_, f32[2,256,128]{2,1,0:T(8,128)S(1)} %collective-permute-done.4.refs_1_, f32[2,256,128]{2,1,0:T(8,128)S(1)} %collective-permute-done.5.refs_2_, f32[2,256,128]{2,1,0:T(8,128)S(1)} %collective-permute-done.6.refs_3_, ...), custom_call_target="tpu_custom_call" | custom-call | flops 5242880 | bytes 2621440 | tf_op jit(solution)/shard_map/pallas_call | solution.py:452
  86.1 24.4 %all_to_all.5.refs_0_ = f32[32,8,128]{2,1,0:T(8,128)S(1)} all-to-all(f32[32,8,128]{2,1,0:T(8,128)S(1)} %shard_map.46), channel_id=1, replica_groups=mesh['band'=16,'domain'=32] {'domain'}, dimensions={0} | all-to-all | bytes 262144 | tf_op jit(solution)/shard_map/all_to_all | solution.py:390
  110.4 4.7 %shard_map.48 = (f32[8,256,128]{2,1,0:T(8,128)}, f32[8,128]{1,0:T(8,128)S(1)}, f32[8,128]{1,0:T(8,128)S(1)}) custom-call(f32[8,128]{1,0:T(8,128)S(1)} %shard_map.47.sums_ref.own_ref, f32[2,256,128]{2,1,0:T(8,128)S(1)} %broadcast_select_fusion.refs_0_, f32[2,256,128]{2,1,0:T(8,128)S(1)} %collective-permute-done.4.refs_1_, ...), custom_call_target="tpu_custom_call" | custom-call | flops 12582912 | bytes 4194304 | tf_op jit(solution)/shard_map/pallas_call | solution.py:485
  115.2 3.5 %collective-permute-start.18 = (f32[8,256,128]{2,1,0:T(8,128)}, f32[8,256,128]{2,1,0:T(8,128)S(1)}, u32[]{:S(2)}, u32[]{:S(2)}) collective-permute-start(f32[8,256,128]{2,1,0:T(8,128)} %get-tuple-element.37.f_ref), channel_id=1, source_target_pairs={{0,31},{1,2},{2,1},{3,4},{4,3},{5,6},{6,5},{7,8},{8,7},{9,10},{10,... | collective-permute-start | bytes 3145736 | tf_op jit(solution)/shard_map/ppermute | solution.py:409
  118.6 1.9 %collective-permute-start.19 = (f32[8,256,128]{2,1,0:T(8,128)}, f32[8,256,128]{2,1,0:T(8,128)S(1)}, u32[]{:S(2)}, u32[]{:S(2)}) collective-permute-start(f32[8,256,128]{2,1,0:T(8,128)} %get-tuple-element.37.f_ref), channel_id=1, source_target_pairs={{0,1},{1,0},{2,3},{3,2},{4,5},{5,4},{6,7},{7,6},{8,9},{9,8},{10,11... | collective-permute-start | bytes 3145736 | tf_op jit(solution)/shard_map/ppermute | solution.py:409
  123.3 6.0 %collective-permute-done.16 = f32[2,8,128]{2,1,0:T(8,128)S(1)} collective-permute-done((f32[2,8,128]{2,1,0:T(8,128)S(1)}, f32[2,8,128]{2,1,0:T(8,128)S(1)}, u32[]{:S(2)}, u32[]{:S(2)}) %collective-permute-start.16) | collective-permute-done | bytes 8224 | tf_op jit(solution)/shard_map/ppermute | solution.py:500
  132.6 2.7 %shard_map.49 = f32[8,4,64,128]{3,2,1,0:T(8,128)S(1)} custom-call(f32[8,4,64,128]{3,2,1,0:T(8,128)S(1)} %bitcast.27, f32[4,64,128]{2,1,0:T(8,128)S(1)} %copy-done.3), custom_call_target="tpu_custom_call" | custom-call | flops 15728640 | bytes 2097152 | tf_op jit(solution)/shard_map/pallas_call | solution.py:424
  135.4 5.3 %collective-permute-done.17.far_ref = f32[2,8,128]{2,1,0:T(8,128)S(1)} collective-permute-done((f32[2,8,128]{2,1,0:T(8,128)S(1)}, f32[2,8,128]{2,1,0:T(8,128)S(1)}, u32[]{:S(2)}, u32[]{:S(2)}) %collective-permute-start.17) | collective-permute-done | bytes 8224 | tf_op jit(solution)/shard_map/ppermute | solution.py:501
  140.6 1.6 %shard_map.51.splat = f32[8,8,128]{2,1,0:T(8,128)S(1)} custom-call(f32[8,128]{1,0:T(8,128)S(1)} %get-tuple-element.39.weights_ref, f32[8,128]{1,0:T(8,128)S(1)} %get-tuple-element.40.half_ref, f32[8,128]{1,0:T(8,128)S(1)} %get-tuple-element.41.gram_ref, f32[2,8,128]{2,1,0:T(8,128)S(1)} %fusion.3.near_ref, f32[2,8,128]{2,1,0:T(8,128)S(1)} %collective-permute-done.17.far_ref), custom_call_target="tpu_custom_call" | custom-call | tf_op jit(solution)/shard_map/pallas_call | solution.py:503
  (47 shorter events, 18.8 us)
Async XLA Ops:
  0.6 4.1 %copy-start = (f32[8,4,64,128]{3,2,1,0:T(8,128)S(1)}, f32[8,4,64,128]{3,2,1,0:T(8,128)}, u32[]{:S(2)}) copy-start(f32[8,4,64,128]{3,2,1,0:T(8,128)} %f_ref.1) | copy-start | bytes 3145732
  0.6 4.1 %copy-start.3 = (f32[4,64,128]{2,1,0:T(8,128)S(1)}, f32[4,64,128]{2,1,0:T(8,128)}, u32[]{:S(2)}) copy-start(f32[4,64,128]{2,1,0:T(8,128)} %v_ref.3) | copy-start | bytes 393220
  2.0 16.3 %collective-permute-start = (f32[2,256,128]{2,1,0:T(8,128)S(1)}, f32[2,256,128]{2,1,0:T(8,128)S(1)}, u32[]{:S(2)}, u32[]{:S(2)}) collective-permute-start(f32[2,256,128]{2,1,0:T(8,128)S(1)} %bitcast.33), channel_id=1, source_target_pairs={{0,64},{32,96},{1,65},{33,97},{2,66},{34,98},{3,67},{35,99},{4,68}... | collective-permute-start | bytes 786440 | tf_op jit(solution)/shard_map/ppermute | solution.py:435
  3.3 15.0 %collective-permute-start.1 = (f32[2,256,128]{2,1,0:T(8,128)S(1)}, f32[2,256,128]{2,1,0:T(8,128)S(1)}, u32[]{:S(2)}, u32[]{:S(2)}) collective-permute-start(f32[2,256,128]{2,1,0:T(8,128)S(1)} %bitcast.32), channel_id=1, source_target_pairs={{0,192},{32,224},{1,193},{33,225},{2,194},{34,226},{3,195},{35,227... | collective-permute-start | bytes 786440 | tf_op jit(solution)/shard_map/ppermute | solution.py:435
  4.0 14.4 %collective-permute-start.2 = (f32[2,256,128]{2,1,0:T(8,128)S(1)}, f32[2,256,128]{2,1,0:T(8,128)S(1)}, u32[]{:S(2)}, u32[]{:S(2)}) collective-permute-start(f32[2,256,128]{2,1,0:T(8,128)S(1)} %bitcast.31), channel_id=1, source_target_pairs={{0,384},{32,416},{1,385},{33,417},{2,386},{34,418},{3,387},{35,419... | collective-permute-start | bytes 786440 | tf_op jit(solution)/shard_map/ppermute | solution.py:435
  18.4 21.0 %collective-permute-start.3 = (f32[2,256,128]{2,1,0:T(8,128)S(1)}, f32[2,256,128]{2,1,0:T(8,128)}, u32[]{:S(2)}, u32[]{:S(2)}) collective-permute-start(f32[2,256,128]{2,1,0:T(8,128)S(1)} %fusion.1), channel_id=1, source_target_pairs={{0,256},{32,288},{64,320},{96,352},{384,128},{416,160},{192,448},{... | collective-permute-start | bytes 786440 | tf_op jit(solution)/shard_map/ppermute | solution.py:446
  20.4 50.8 %collective-permute-start.10 = (f32[8,256,128]{2,1,0:T(8,128)S(1)}, f32[8,256,128]{2,1,0:T(8,128)S(1)}, u32[]{:S(2)}, u32[]{:S(2)}) collective-permute-start(f32[8,256,128]{2,1,0:T(8,128)S(1)} %bitcast.18), channel_id=1, source_target_pairs={{0,1},{1,2},{2,3},{3,4},{4,5},{5,6},{6,7},{7,8},{8,9},{9,10},{10,1... | collective-permute-start | bytes 3145736 | tf_op jit(solution)/shard_map/ppermute | solution.py:400
  22.4 48.9 %collective-permute-start.11 = (f32[8,256,128]{2,1,0:T(8,128)S(1)}, f32[8,256,128]{2,1,0:T(8,128)}, u32[]{:S(2)}, u32[]{:S(2)}) collective-permute-start(f32[8,256,128]{2,1,0:T(8,128)S(1)} %bitcast.19), channel_id=1, source_target_pairs={{1,0},{2,1},{3,2},{4,3},{5,4},{6,5},{7,6},{8,7},{9,8},{10,9},{11,1... | collective-permute-start | bytes 3145736 | tf_op jit(solution)/shard_map/ppermute | solution.py:401
  39.4 14.3 %collective-permute-start.5 = (f32[2,256,128]{2,1,0:T(8,128)S(1)}, f32[2,256,128]{2,1,0:T(8,128)S(1)}, u32[]{:S(2)}, u32[]{:S(2)}) collective-permute-start(f32[2,256,128]{2,1,0:T(8,128)S(1)} %broadcast_select_fusion.refs_0_), channel_id=1, source_target_pairs={{0,224},{32,0},{64,32},{96,64},{128,96},{160,128},{192,160},{224,1... | collective-permute-start | bytes 786440 | tf_op jit(solution)/shard_map/ppermute | solution.py:395
  41.4 14.3 %collective-permute-start.4 = (f32[2,256,128]{2,1,0:T(8,128)S(1)}, f32[2,256,128]{2,1,0:T(8,128)S(1)}, u32[]{:S(2)}, u32[]{:S(2)}) collective-permute-start(f32[2,256,128]{2,1,0:T(8,128)S(1)} %broadcast_select_fusion.refs_0_), channel_id=1, source_target_pairs={{0,32},{32,64},{64,96},{96,128},{128,160},{160,192},{192,224},{224... | collective-permute-start | bytes 786440 | tf_op jit(solution)/shard_map/ppermute | solution.py:395
  53.7 9.5 %collective-permute-start.7 = (f32[2,256,128]{2,1,0:T(8,128)S(1)}, f32[2,256,128]{2,1,0:T(8,128)S(1)}, u32[]{:S(2)}, u32[]{:S(2)}) collective-permute-start(f32[2,256,128]{2,1,0:T(8,128)S(1)} %collective-permute-done.5.refs_2_), channel_id=1, source_target_pairs={{0,224},{32,0},{64,32},{96,64},{128,96},{160,128},{192,160},{224,1... | collective-permute-start | bytes 786440 | tf_op jit(solution)/shard_map/ppermute | solution.py:395
  55.6 9.5 %collective-permute-start.6 = (f32[2,256,128]{2,1,0:T(8,128)S(1)}, f32[2,256,128]{2,1,0:T(8,128)S(1)}, u32[]{:S(2)}, u32[]{:S(2)}) collective-permute-start(f32[2,256,128]{2,1,0:T(8,128)S(1)} %collective-permute-done.4.refs_1_), channel_id=1, source_target_pairs={{0,32},{32,64},{64,96},{96,128},{128,160},{160,192},{192,224},{224... | collective-permute-start | bytes 786440 | tf_op jit(solution)/shard_map/ppermute | solution.py:395
  63.2 9.5 %collective-permute-start.9 = (f32[2,256,128]{2,1,0:T(8,128)S(1)}, f32[2,256,128]{2,1,0:T(8,128)S(1)}, u32[]{:S(2)}, u32[]{:S(2)}) collective-permute-start(f32[2,256,128]{2,1,0:T(8,128)S(1)} %collective-permute-done.7.refs_4_), channel_id=1, source_target_pairs={{0,224},{32,0},{64,32},{96,64},{128,96},{160,128},{192,160},{224,1... | collective-permute-start | bytes 786440 | tf_op jit(solution)/shard_map/ppermute | solution.py:395
  65.1 9.5 %collective-permute-start.8 = (f32[2,256,128]{2,1,0:T(8,128)S(1)}, f32[2,256,128]{2,1,0:T(8,128)S(1)}, u32[]{:S(2)}, u32[]{:S(2)}) collective-permute-start(f32[2,256,128]{2,1,0:T(8,128)S(1)} %collective-permute-done.6.refs_3_), channel_id=1, source_target_pairs={{0,32},{32,64},{64,96},{96,128},{128,160},{160,192},{192,224},{224... | collective-permute-start | bytes 786440 | tf_op jit(solution)/shard_map/ppermute | solution.py:395
  72.7 12.3 %collective-permute-start.13 = (f32[1,256,128]{2,1,0:T(8,128)S(1)}, f32[1,256,128]{2,1,0:T(8,128)S(1)}, u32[]{:S(2)}, u32[]{:S(2)}) collective-permute-start(f32[1,256,128]{2,1,0:T(8,128)S(1)} %slice.36), channel_id=1, source_target_pairs={{0,224},{32,0},{64,32},{96,64},{128,96},{160,128},{192,160},{224,1... | collective-permute-start | bytes 393224 | tf_op jit(solution)/shard_map/ppermute | solution.py:395
  74.6 10.4 %collective-permute-start.12 = (f32[1,256,128]{2,1,0:T(8,128)S(1)}, f32[1,256,128]{2,1,0:T(8,128)S(1)}, u32[]{:S(2)}, u32[]{:S(2)}) collective-permute-start(f32[1,256,128]{2,1,0:T(8,128)S(1)} %slice.37), channel_id=1, source_target_pairs={{0,32},{32,64},{64,96},{96,128},{128,160},{160,192},{192,224},{224... | collective-permute-start | bytes 393224 | tf_op jit(solution)/shard_map/ppermute | solution.py:395
  115.2 28.5 %collective-permute-start.18 = (f32[8,256,128]{2,1,0:T(8,128)}, f32[8,256,128]{2,1,0:T(8,128)S(1)}, u32[]{:S(2)}, u32[]{:S(2)}) collective-permute-start(f32[8,256,128]{2,1,0:T(8,128)} %get-tuple-element.37.f_ref), channel_id=1, source_target_pairs={{0,31},{1,2},{2,1},{3,4},{4,3},{5,6},{6,5},{7,8},{8,7},{9,10},{10,... | collective-permute-start | bytes 3145736 | tf_op jit(solution)/shard_map/ppermute | solution.py:409
  118.6 25.0 %collective-permute-start.19 = (f32[8,256,128]{2,1,0:T(8,128)}, f32[8,256,128]{2,1,0:T(8,128)S(1)}, u32[]{:S(2)}, u32[]{:S(2)}) collective-permute-start(f32[8,256,128]{2,1,0:T(8,128)} %get-tuple-element.37.f_ref), channel_id=1, source_target_pairs={{0,1},{1,0},{2,3},{3,2},{4,5},{5,4},{6,7},{7,6},{8,9},{9,8},{10,11... | collective-permute-start | bytes 3145736 | tf_op jit(solution)/shard_map/ppermute | solution.py:409
  120.6 0.7 collective-permute-start.14
  121.3 0.7 collective-permute-start.15
  122.0 7.3 %collective-permute-start.16 = (f32[2,8,128]{2,1,0:T(8,128)S(1)}, f32[2,8,128]{2,1,0:T(8,128)S(1)}, u32[]{:S(2)}, u32[]{:S(2)}) collective-permute-start(f32[2,8,128]{2,1,0:T(8,128)S(1)} %fusion.2), channel_id=1, source_target_pairs={{0,64},{32,96},{128,192},{160,224},{1,65},{33,97},{129,193},{161,2... | collective-permute-start | bytes 24584 | tf_op jit(solution)/shard_map/ppermute | solution.py:500
  129.3 11.3 %collective-permute-start.17 = (f32[2,8,128]{2,1,0:T(8,128)S(1)}, f32[2,8,128]{2,1,0:T(8,128)S(1)}, u32[]{:S(2)}, u32[]{:S(2)}) collective-permute-start(f32[2,8,128]{2,1,0:T(8,128)S(1)} %fusion.3.near_ref), channel_id=1, source_target_pairs={{0,256},{32,288},{64,320},{96,352},{128,384},{160,416},{192,448},{... | collective-permute-start | bytes 24584 | tf_op jit(solution)/shard_map/ppermute | solution.py:501
  131.3 1.3 copy-start.1
  132.6 9.7 %copy-start.2 = (f32[8,256,128]{2,1,0:T(8,128)S(1)}, f32[8,256,128]{2,1,0:T(8,128)}, u32[]{:S(2)}) copy-start(f32[8,256,128]{2,1,0:T(8,128)} %get-tuple-element.37.f_ref) | copy-start | bytes 3145732

commit v17 on v15

--- a/solution.py
+++ b/solution.py
@@ -108,6 +108,7 @@
 
 OWN = list(range(16, 24))
 IMAGE = list(range(24, 32))
+BLOCK0_ROWS = (2, 3, 4, 5, 10, 11, 12, 13)
 
 
 def split(pairs, size=36):
@@ -169,27 +170,35 @@
     w0 = w0 + jnp.where(lane == 24 + sub, 1.0, 0.0)
     w1 = w1 + jnp.where(lane == 32 + sub, 1.0, 0.0)
     w2 = jnp.where(lane_in, w2, 0.0) + jnp.where(lane == 40 + sub, 1.0, 0.0)
-    tiles = [w0, w1, w2]
-    for k in range(16):
-        v, s = divmod(k, 8)
-        row = tiles[v][s : s + 1, :]
-        row = row / jnp.broadcast_to(row[:, k : k + 1], (1, 128))
-        row = jnp.broadcast_to(row, (8, 128))
-        for u in range(v, 3):
-            column = spread_lane(tiles[u], k)
-            if u == v:
-                column = jnp.where(sub > s, column, 0.0)
-            tiles[u] = tiles[u] - column * row
-    plain = tiles[2]
-    scaled = plain
-    for k in range(8):
-        row = scaled[k : k + 1, :]
-        row = row / jnp.broadcast_to(row[:, 16 + k : 17 + k], (1, 128))
-        column = jnp.where(sub > k, spread_lane(scaled, 16 + k), 0.0)
-        scaled = scaled - column * jnp.broadcast_to(row, (8, 128))
-    pivots = jnp.sum(jnp.where(lane == 16 + sub, scaled, 0.0), axis=1, keepdims=True)
-    scaled = scaled / jnp.sqrt(jnp.broadcast_to(pivots, (8, 128)))
-    weights = jnp.where(later, plain, scaled)
+    def subtracted(steps):
+        tiles = [w0, w1, w2]
+        for k in steps:
+            v, s = divmod(k, 8)
+            row = tiles[v][s : s + 1, :]
+            row = row / jnp.broadcast_to(row[:, k : k + 1], (1, 128))
+            row = jnp.broadcast_to(row, (8, 128))
+            for u in range(v, 3):
+                column = spread_lane(tiles[u], k)
+                if u == v:
+                    column = jnp.where(sub > s, column, 0.0)
+                tiles[u] = tiles[u] - column * row
+        return tiles[2]
+
+    def normalised(scaled):
+        for k in range(8):
+            row = scaled[k : k + 1, :]
+            row = row / jnp.broadcast_to(row[:, 16 + k : 17 + k], (1, 128))
+            column = jnp.where(sub > k, spread_lane(scaled, 16 + k), 0.0)
+            scaled = scaled - column * jnp.broadcast_to(row, (8, 128))
+        pivots = jnp.sum(jnp.where(lane == 16 + sub, scaled, 0.0), axis=1, keepdims=True)
+        return scaled / jnp.sqrt(jnp.broadcast_to(pivots, (8, 128)))
+
+    plain = lax.cond(
+        later,
+        lambda: subtracted(range(16)),
+        lambda: lax.cond(second, lambda: normalised(subtracted(BLOCK0_ROWS)), lambda: normalised(w2)),
+    )
+    weights = plain
     weights_ref[...] = weights
     gram_ref[...] = jnp.where(later, move(plain, 16, 0), jnp.where(lane == sub, 1.0, 0.0))
     for c in range(24):
@@ -217,7 +226,7 @@
         lax.fori_loop(0, own.shape[1] // 32, body, 0)
 
     pl.when(later)(lambda: combine(range(16), True))
-    pl.when(second)(lambda: combine((2, 3, 4, 5, 10, 11, 12, 13, *OWN), False))
+    pl.when(second)(lambda: combine((*BLOCK0_ROWS, *OWN), False))
     pl.when(band == 0)(lambda: combine(OWN, False))
 
 

time: 134 us -> 132 us (0.985)
  transfers between devices with their start and end apart: 20 -> 20, of which waited for: 12 -> 11; matrix products, arithmetic and copies ran while one was open for 0% -> 0% of each run, Pallas kernels for 12% -> 12%
where the time goes in v17:
time: 132 us
  starting transfers between devices  55.6 us (42%)
  waiting for transfers between devices  29.8 us (23%)
  Pallas kernels  21.3 us (16%)
  blocking collectives  21.2 us (16%)
  other arithmetic  1.49 us (1%)
    ppermute x8, starting transfers between devices, ring_shift(): return lax.ppermute(block, 'band', pairs)  23 us
    all_to_all x1, blocking collectives, domain_parts(): return lax.all_to_all(copies, 'domain', 0, 0)  21.2 us
    ppermute x3, waiting for transfers between devices, local(): lax.ppermute(quarters[k], 'band', [(0, 2 * k), (1, 2 * k + 1)])  11.6 us
    ppermute x3, starting transfers between devices, local(): lax.ppermute(quarters[k], 'band', [(0, 2 * k), (1, 2 * k + 1)])  9.65 us
    ppermute x8, waiting for transfers between devices, ring_shift(): return lax.ppermute(block, 'band', pairs)  6.34 us
    pallas_call x4, Pallas kernels, stage(): call(lambda *refs: stage_kernel(len(pieces), fresh, imaged, last, *refs),...  6.12 us
    pallas_call x2, Pallas kernels, inner_part(): call(inner_kernel, (field, *sums), specs=[VMEM] * 2, flops=60 * big, byte...  6.04 us
    ppermute x1, waiting for transfers between devices, neighbours(): lax.ppermute(block, 'domain', [((i + 1) % count, i) for i in range(count)])  5.5 us
  transfers between devices with their start and end apart: 20, of which 11 were waited for; matrix products, arithmetic and copies ran while one was open for 0% of the time, Pallas kernels for 12%

profile of v17, /device:TPU:1, one launch (start us, length us, event | category | flops | bytes accessed | tf_op | source)
XLA Modules:
  0.0 131.6 jit_solution(2427161765012275098)
XLA Ops:
  2.0 5.1 %collective-permute-start = (f32[2,256,128]{2,1,0:T(8,128)S(1)}, f32[2,256,128]{2,1,0:T(8,128)S(1)}, u32[]{:S(2)}, u32[]{:S(2)}) collective-permute-start(f32[2,256,128]{2,1,0:T(8,128)S(1)} %bitcast.33), channel_id=1, source_target_pairs={{0,64},{32,96},{1,65},{33,97},{2,66},{34,98},{3,67},{35,99},{4,68}... | collective-permute-start | bytes 786440 | tf_op jit(solution)/shard_map/ppermute | solution.py:444
  7.1 2.3 %collective-permute-start.1 = (f32[2,256,128]{2,1,0:T(8,128)S(1)}, f32[2,256,128]{2,1,0:T(8,128)S(1)}, u32[]{:S(2)}, u32[]{:S(2)}) collective-permute-start(f32[2,256,128]{2,1,0:T(8,128)S(1)} %bitcast.32), channel_id=1, source_target_pairs={{0,192},{32,224},{1,193},{33,225},{2,194},{34,226},{3,195},{35,227... | collective-permute-start | bytes 786440 | tf_op jit(solution)/shard_map/ppermute | solution.py:444
  9.5 2.2 %collective-permute-start.2 = (f32[2,256,128]{2,1,0:T(8,128)S(1)}, f32[2,256,128]{2,1,0:T(8,128)S(1)}, u32[]{:S(2)}, u32[]{:S(2)}) collective-permute-start(f32[2,256,128]{2,1,0:T(8,128)S(1)} %bitcast.31), channel_id=1, source_target_pairs={{0,128},{32,160},{1,129},{33,161},{2,130},{34,162},{3,131},{35,163... | collective-permute-start | bytes 786440 | tf_op jit(solution)/shard_map/ppermute | solution.py:444
  11.7 3.3 %shard_map.41 = (f32[8,4,64,128]{3,2,1,0:T(8,128)S(1)}, f32[8,128]{1,0:T(8,128)S(1)}) custom-call(f32[8,4,64,128]{3,2,1,0:T(8,128)S(1)} %copy-done, f32[4,64,128]{2,1,0:T(8,128)S(1)} %copy-done.3), custom_call_target="tpu_custom_call" | custom-call | flops 15728640 | bytes 2097152 | tf_op jit(solution)/shard_map/pallas_call | solution.py:433
  15.0 11.5 %collective-permute-done.1 = f32[2,256,128]{2,1,0:T(8,128)S(1)} collective-permute-done((f32[2,256,128]{2,1,0:T(8,128)S(1)}, f32[2,256,128]{2,1,0:T(8,128)S(1)}, u32[]{:S(2)}, u32[]{:S(2)}) %collective-permute-start.1) | collective-permute-done | bytes 262176 | tf_op jit(solution)/shard_map/ppermute | solution.py:444
  26.6 2.0 %collective-permute-start.3 = (f32[2,256,128]{2,1,0:T(8,128)S(1)}, f32[2,256,128]{2,1,0:T(8,128)}, u32[]{:S(2)}, u32[]{:S(2)}) collective-permute-start(f32[2,256,128]{2,1,0:T(8,128)S(1)} %fusion.1), channel_id=1, source_target_pairs={{0,256},{32,288},{64,320},{96,352},{128,384},{160,416},{192,448},{... | collective-permute-start | bytes 786440 | tf_op jit(solution)/shard_map/ppermute | solution.py:452
  28.6 4.5 %collective-permute-start.10 = (f32[8,256,128]{2,1,0:T(8,128)S(1)}, f32[8,256,128]{2,1,0:T(8,128)S(1)}, u32[]{:S(2)}, u32[]{:S(2)}) collective-permute-start(f32[8,256,128]{2,1,0:T(8,128)S(1)} %bitcast.18), channel_id=1, source_target_pairs={{0,1},{1,2},{2,3},{3,4},{4,5},{5,6},{6,7},{7,8},{8,9},{9,10},{10,1... | collective-permute-start | bytes 3145736 | tf_op jit(solution)/shard_map/ppermute | solution.py:409
  37.0 3.4 %collective-permute-start.4 = (f32[2,256,128]{2,1,0:T(8,128)S(1)}, f32[2,256,128]{2,1,0:T(8,128)S(1)}, u32[]{:S(2)}, u32[]{:S(2)}) collective-permute-start(f32[2,256,128]{2,1,0:T(8,128)S(1)} %broadcast_select_fusion.refs_0_), channel_id=1, source_target_pairs={{0,32},{32,64},{64,96},{96,128},{128,160},{160,192},{192,224},{224... | collective-permute-start | bytes 786440 | tf_op jit(solution)/shard_map/ppermute | solution.py:404
  40.4 2.1 %collective-permute-done.5.refs_2_ = f32[2,256,128]{2,1,0:T(8,128)S(1)} collective-permute-done((f32[2,256,128]{2,1,0:T(8,128)S(1)}, f32[2,256,128]{2,1,0:T(8,128)S(1)}, u32[]{:S(2)}, u32[]{:S(2)}) %collective-permute-start.5) | collective-permute-done | bytes 262176 | tf_op jit(solution)/shard_map/ppermute | solution.py:404
  42.5 4.3 %collective-permute-start.7 = (f32[2,256,128]{2,1,0:T(8,128)S(1)}, f32[2,256,128]{2,1,0:T(8,128)S(1)}, u32[]{:S(2)}, u32[]{:S(2)}) collective-permute-start(f32[2,256,128]{2,1,0:T(8,128)S(1)} %collective-permute-done.5.refs_2_), channel_id=1, source_target_pairs={{0,224},{32,0},{64,32},{96,64},{128,96},{160,128},{192,160},{224,1... | collective-permute-start | bytes 786440 | tf_op jit(solution)/shard_map/ppermute | solution.py:404
  51.5 4.3 %collective-permute-start.9 = (f32[2,256,128]{2,1,0:T(8,128)S(1)}, f32[2,256,128]{2,1,0:T(8,128)S(1)}, u32[]{:S(2)}, u32[]{:S(2)}) collective-permute-start(f32[2,256,128]{2,1,0:T(8,128)S(1)} %collective-permute-done.7.refs_4_), channel_id=1, source_target_pairs={{0,224},{32,0},{64,32},{96,64},{128,96},{160,128},{192,160},{224,1... | collective-permute-start | bytes 786440 | tf_op jit(solution)/shard_map/ppermute | solution.py:404
  59.4 5.5 %collective-permute-done.11.right = f32[8,256,128]{2,1,0:T(8,128)} collective-permute-done((f32[8,256,128]{2,1,0:T(8,128)S(1)}, f32[8,256,128]{2,1,0:T(8,128)}, u32[]{:S(2)}, u32[]{:S(2)}) %collective-permute-start.11) | collective-permute-done | bytes 1048608 | tf_op jit(solution)/shard_map/ppermute | solution.py:410
  66.9 3.4 %collective-permute-start.12 = (f32[1,256,128]{2,1,0:T(8,128)S(1)}, f32[1,256,128]{2,1,0:T(8,128)S(1)}, u32[]{:S(2)}, u32[]{:S(2)}) collective-permute-start(f32[1,256,128]{2,1,0:T(8,128)S(1)} %slice.37), channel_id=1, source_target_pairs={{0,32},{32,64},{64,96},{96,128},{128,160},{160,192},{192,224},{224... | collective-permute-start | bytes 393224 | tf_op jit(solution)/shard_map/ppermute | solution.py:404
  70.3 2.2 %shard_map.44 = (f32[8,256,128]{2,1,0:T(8,128)S(1)}, f32[8,128]{1,0:T(8,128)S(1)}) custom-call(f32[8,256,128]{2,1,0:T(8,128)S(1)} %bitcast.22, f32[8,256,128]{2,1,0:T(8,128)S(1)} %bitcast.29, f32[8,256,128]{2,1,0:T(8,128)S(1)} %collective-permute-done.10.left, f32[8,256,128]{2,1,0:T(8,128)} %collective-permute-done.11.right), custom_call_target="tpu_custom_call" | custom-call | flops 13107200 | bytes 5242880 | tf_op jit(solution)/shard_map/pallas_call | solution.py:477
  72.5 3.0 %shard_map.45.refs_11_ = f32[8,128]{1,0:T(8,128)S(1)} custom-call(f32[2,256,128]{2,1,0:T(8,128)S(1)} %broadcast_select_fusion.refs_0_, f32[2,256,128]{2,1,0:T(8,128)S(1)} %collective-permute-done.4.refs_1_, f32[2,256,128]{2,1,0:T(8,128)S(1)} %collective-permute-done.5.refs_2_, f32[2,256,128]{2,1,0:T(8,128)S(1)} %collective-permute-done.6.refs_3_, ...), custom_call_target="tpu_custom_call" | custom-call | flops 5242880 | bytes 2621440 | tf_op jit(solution)/shard_map/pallas_call | solution.py:457
  78.3 21.2 %all_to_all.5.refs_0_ = f32[32,8,128]{2,1,0:T(8,128)S(1)} all-to-all(f32[32,8,128]{2,1,0:T(8,128)S(1)} %shard_map.46), channel_id=1, replica_groups=mesh['band'=16,'domain'=32] {'domain'}, dimensions={0} | all-to-all | bytes 262144 | tf_op jit(solution)/shard_map/all_to_all | solution.py:399
  99.6 2.5 %shard_map.48 = (f32[8,256,128]{2,1,0:T(8,128)}, f32[8,128]{1,0:T(8,128)S(1)}, f32[8,128]{1,0:T(8,128)S(1)}) custom-call(f32[8,128]{1,0:T(8,128)S(1)} %shard_map.47.sums_ref.own_ref, f32[2,256,128]{2,1,0:T(8,128)S(1)} %broadcast_select_fusion.refs_0_, f32[2,256,128]{2,1,0:T(8,128)S(1)} %collective-permute-done.4.refs_1_, ...), custom_call_target="tpu_custom_call" | custom-call | flops 12582912 | bytes 4194304 | tf_op jit(solution)/shard_map/pallas_call | solution.py:490
  102.1 2.1 %collective-permute-start.18 = (f32[8,256,128]{2,1,0:T(8,128)}, f32[8,256,128]{2,1,0:T(8,128)S(1)}, u32[]{:S(2)}, u32[]{:S(2)}) collective-permute-start(f32[8,256,128]{2,1,0:T(8,128)} %get-tuple-element.37.f_ref), channel_id=1, source_target_pairs={{0,31},{1,2},{2,1},{3,4},{4,3},{5,6},{6,5},{7,8},{8,7},{9,10},{10,... | collective-permute-start | bytes 3145736 | tf_op jit(solution)/shard_map/ppermute | solution.py:418
  104.2 3.7 %collective-permute-start.19 = (f32[8,256,128]{2,1,0:T(8,128)}, f32[8,256,128]{2,1,0:T(8,128)S(1)}, u32[]{:S(2)}, u32[]{:S(2)}) collective-permute-start(f32[8,256,128]{2,1,0:T(8,128)} %get-tuple-element.37.f_ref), channel_id=1, source_target_pairs={{0,1},{1,0},{2,3},{3,2},{4,5},{5,4},{6,7},{7,6},{8,9},{9,8},{10,11... | collective-permute-start | bytes 3145736 | tf_op jit(solution)/shard_map/ppermute | solution.py:418
  109.8 2.7 %collective-permute-done.14 = f32[8,128]{1,0:T(8,128)S(1)} collective-permute-done((f32[8,128]{1,0:T(8,128)S(1)}, f32[8,128]{1,0:T(8,128)S(1)}, u32[]{:S(2)}, u32[]{:S(2)}) %collective-permute-start.14) | collective-permute-done | bytes 4128 | tf_op jit(solution)/shard_map/ppermute | solution.py:501
  112.5 2.2 %collective-permute-start.15 = (f32[2,8,128]{2,1,0:T(8,128)S(1)}, f32[2,8,128]{2,1,0:T(8,128)S(1)}, u32[]{:S(2)}, u32[]{:S(2)}) collective-permute-start(f32[2,8,128]{2,1,0:T(8,128)S(1)} %maximum_select_fusion), channel_id=1, source_target_pairs={{0,128},{32,160},{1,129},{33,161},{2,130},{34,162},{3,131},{35,163... | collective-permute-start | bytes 24584 | tf_op jit(solution)/shard_map/ppermute | solution.py:504
  117.5 3.5 %collective-permute-start.17 = (f32[2,8,128]{2,1,0:T(8,128)S(1)}, f32[2,8,128]{2,1,0:T(8,128)S(1)}, u32[]{:S(2)}, u32[]{:S(2)}) collective-permute-start(f32[2,8,128]{2,1,0:T(8,128)S(1)} %fusion.3.near_ref), channel_id=1, source_target_pairs={{0,256},{32,288},{64,320},{96,352},{128,384},{160,416},{192,448},{... | collective-permute-start | bytes 24584 | tf_op jit(solution)/shard_map/ppermute | solution.py:506
  123.1 2.7 %shard_map.49 = f32[8,4,64,128]{3,2,1,0:T(8,128)S(1)} custom-call(f32[8,4,64,128]{3,2,1,0:T(8,128)S(1)} %bitcast.27, f32[4,64,128]{2,1,0:T(8,128)S(1)} %copy-done.3), custom_call_target="tpu_custom_call" | custom-call | flops 15728640 | bytes 2097152 | tf_op jit(solution)/shard_map/pallas_call | solution.py:433
  128.1 2.1 %collective-permute-done.18.across = f32[8,256,128]{2,1,0:T(8,128)S(1)} collective-permute-done((f32[8,256,128]{2,1,0:T(8,128)}, f32[8,256,128]{2,1,0:T(8,128)S(1)}, u32[]{:S(2)}, u32[]{:S(2)}) %collective-permute-start.18) | collective-permute-done | bytes 1048608 | tf_op jit(solution)/shard_map/ppermute | solution.py:418
  (47 shorter events, 28.9 us)
Async XLA Ops:
  0.6 11.1 %copy-start = (f32[8,4,64,128]{3,2,1,0:T(8,128)S(1)}, f32[8,4,64,128]{3,2,1,0:T(8,128)}, u32[]{:S(2)}) copy-start(f32[8,4,64,128]{3,2,1,0:T(8,128)} %f_ref.1) | copy-start | bytes 3145732
  0.6 11.1 %copy-start.3 = (f32[4,64,128]{2,1,0:T(8,128)S(1)}, f32[4,64,128]{2,1,0:T(8,128)}, u32[]{:S(2)}) copy-start(f32[4,64,128]{2,1,0:T(8,128)} %v_ref.3) | copy-start | bytes 393220
  2.0 13.0 %collective-permute-start = (f32[2,256,128]{2,1,0:T(8,128)S(1)}, f32[2,256,128]{2,1,0:T(8,128)S(1)}, u32[]{:S(2)}, u32[]{:S(2)}) collective-permute-start(f32[2,256,128]{2,1,0:T(8,128)S(1)} %bitcast.33), channel_id=1, source_target_pairs={{0,64},{32,96},{1,65},{33,97},{2,66},{34,98},{3,67},{35,99},{4,68}... | collective-permute-start | bytes 786440 | tf_op jit(solution)/shard_map/ppermute | solution.py:444
  7.1 19.5 %collective-permute-start.1 = (f32[2,256,128]{2,1,0:T(8,128)S(1)}, f32[2,256,128]{2,1,0:T(8,128)S(1)}, u32[]{:S(2)}, u32[]{:S(2)}) collective-permute-start(f32[2,256,128]{2,1,0:T(8,128)S(1)} %bitcast.32), channel_id=1, source_target_pairs={{0,192},{32,224},{1,193},{33,225},{2,194},{34,226},{3,195},{35,227... | collective-permute-start | bytes 786440 | tf_op jit(solution)/shard_map/ppermute | solution.py:444
  9.5 17.1 %collective-permute-start.2 = (f32[2,256,128]{2,1,0:T(8,128)S(1)}, f32[2,256,128]{2,1,0:T(8,128)S(1)}, u32[]{:S(2)}, u32[]{:S(2)}) collective-permute-start(f32[2,256,128]{2,1,0:T(8,128)S(1)} %bitcast.31), channel_id=1, source_target_pairs={{0,128},{32,160},{1,129},{33,161},{2,130},{34,162},{3,131},{35,163... | collective-permute-start | bytes 786440 | tf_op jit(solution)/shard_map/ppermute | solution.py:444
  26.6 8.4 %collective-permute-start.3 = (f32[2,256,128]{2,1,0:T(8,128)S(1)}, f32[2,256,128]{2,1,0:T(8,128)}, u32[]{:S(2)}, u32[]{:S(2)}) collective-permute-start(f32[2,256,128]{2,1,0:T(8,128)S(1)} %fusion.1), channel_id=1, source_target_pairs={{0,256},{32,288},{64,320},{96,352},{128,384},{160,416},{192,448},{... | collective-permute-start | bytes 786440 | tf_op jit(solution)/shard_map/ppermute | solution.py:452
  28.6 30.8 %collective-permute-start.10 = (f32[8,256,128]{2,1,0:T(8,128)S(1)}, f32[8,256,128]{2,1,0:T(8,128)S(1)}, u32[]{:S(2)}, u32[]{:S(2)}) collective-permute-start(f32[8,256,128]{2,1,0:T(8,128)S(1)} %bitcast.18), channel_id=1, source_target_pairs={{0,1},{1,2},{2,3},{3,4},{4,5},{5,6},{6,7},{7,8},{8,9},{9,10},{10,1... | collective-permute-start | bytes 3145736 | tf_op jit(solution)/shard_map/ppermute | solution.py:409
  33.1 31.8 %collective-permute-start.11 = (f32[8,256,128]{2,1,0:T(8,128)S(1)}, f32[8,256,128]{2,1,0:T(8,128)}, u32[]{:S(2)}, u32[]{:S(2)}) collective-permute-start(f32[8,256,128]{2,1,0:T(8,128)S(1)} %bitcast.19), channel_id=1, source_target_pairs={{1,0},{2,1},{3,2},{4,3},{5,4},{6,5},{7,6},{8,7},{9,8},{10,9},{11,1... | collective-permute-start | bytes 3145736 | tf_op jit(solution)/shard_map/ppermute | solution.py:410
  35.1 7.4 %collective-permute-start.5 = (f32[2,256,128]{2,1,0:T(8,128)S(1)}, f32[2,256,128]{2,1,0:T(8,128)S(1)}, u32[]{:S(2)}, u32[]{:S(2)}) collective-permute-start(f32[2,256,128]{2,1,0:T(8,128)S(1)} %broadcast_select_fusion.refs_0_), channel_id=1, source_target_pairs={{0,224},{32,0},{64,32},{96,64},{128,96},{160,128},{192,160},{224,1... | collective-permute-start | bytes 786440 | tf_op jit(solution)/shard_map/ppermute | solution.py:404
  37.0 10.5 %collective-permute-start.4 = (f32[2,256,128]{2,1,0:T(8,128)S(1)}, f32[2,256,128]{2,1,0:T(8,128)S(1)}, u32[]{:S(2)}, u32[]{:S(2)}) collective-permute-start(f32[2,256,128]{2,1,0:T(8,128)S(1)} %broadcast_select_fusion.refs_0_), channel_id=1, source_target_pairs={{0,32},{32,64},{64,96},{96,128},{128,160},{160,192},{192,224},{224... | collective-permute-start | bytes 786440 | tf_op jit(solution)/shard_map/ppermute | solution.py:404
  42.5 9.0 %collective-permute-start.7 = (f32[2,256,128]{2,1,0:T(8,128)S(1)}, f32[2,256,128]{2,1,0:T(8,128)S(1)}, u32[]{:S(2)}, u32[]{:S(2)}) collective-permute-start(f32[2,256,128]{2,1,0:T(8,128)S(1)} %collective-permute-done.5.refs_2_), channel_id=1, source_target_pairs={{0,224},{32,0},{64,32},{96,64},{128,96},{160,128},{192,160},{224,1... | collective-permute-start | bytes 786440 | tf_op jit(solution)/shard_map/ppermute | solution.py:404
  47.6 9.0 %collective-permute-start.6 = (f32[2,256,128]{2,1,0:T(8,128)S(1)}, f32[2,256,128]{2,1,0:T(8,128)S(1)}, u32[]{:S(2)}, u32[]{:S(2)}) collective-permute-start(f32[2,256,128]{2,1,0:T(8,128)S(1)} %collective-permute-done.4.refs_1_), channel_id=1, source_target_pairs={{0,32},{32,64},{64,96},{96,128},{128,160},{160,192},{192,224},{224... | collective-permute-start | bytes 786440 | tf_op jit(solution)/shard_map/ppermute | solution.py:404
  51.5 13.5 %collective-permute-start.9 = (f32[2,256,128]{2,1,0:T(8,128)S(1)}, f32[2,256,128]{2,1,0:T(8,128)S(1)}, u32[]{:S(2)}, u32[]{:S(2)}) collective-permute-start(f32[2,256,128]{2,1,0:T(8,128)S(1)} %collective-permute-done.7.refs_4_), channel_id=1, source_target_pairs={{0,224},{32,0},{64,32},{96,64},{128,96},{160,128},{192,160},{224,1... | collective-permute-start | bytes 786440 | tf_op jit(solution)/shard_map/ppermute | solution.py:404
  56.6 10.3 %collective-permute-start.8 = (f32[2,256,128]{2,1,0:T(8,128)S(1)}, f32[2,256,128]{2,1,0:T(8,128)S(1)}, u32[]{:S(2)}, u32[]{:S(2)}) collective-permute-start(f32[2,256,128]{2,1,0:T(8,128)S(1)} %collective-permute-done.6.refs_3_), channel_id=1, source_target_pairs={{0,32},{32,64},{64,96},{96,128},{128,160},{160,192},{192,224},{224... | collective-permute-start | bytes 786440 | tf_op jit(solution)/shard_map/ppermute | solution.py:404
  65.0 10.5 %collective-permute-start.13 = (f32[1,256,128]{2,1,0:T(8,128)S(1)}, f32[1,256,128]{2,1,0:T(8,128)S(1)}, u32[]{:S(2)}, u32[]{:S(2)}) collective-permute-start(f32[1,256,128]{2,1,0:T(8,128)S(1)} %slice.36), channel_id=1, source_target_pairs={{0,224},{32,0},{64,32},{96,64},{128,96},{160,128},{192,160},{224,1... | collective-permute-start | bytes 393224 | tf_op jit(solution)/shard_map/ppermute | solution.py:404
  66.9 10.3 %collective-permute-start.12 = (f32[1,256,128]{2,1,0:T(8,128)S(1)}, f32[1,256,128]{2,1,0:T(8,128)S(1)}, u32[]{:S(2)}, u32[]{:S(2)}) collective-permute-start(f32[1,256,128]{2,1,0:T(8,128)S(1)} %slice.37), channel_id=1, source_target_pairs={{0,32},{32,64},{64,96},{96,128},{128,160},{160,192},{192,224},{224... | collective-permute-start | bytes 393224 | tf_op jit(solution)/shard_map/ppermute | solution.py:404
  102.1 28.1 %collective-permute-start.18 = (f32[8,256,128]{2,1,0:T(8,128)}, f32[8,256,128]{2,1,0:T(8,128)S(1)}, u32[]{:S(2)}, u32[]{:S(2)}) collective-permute-start(f32[8,256,128]{2,1,0:T(8,128)} %get-tuple-element.37.f_ref), channel_id=1, source_target_pairs={{0,31},{1,2},{2,1},{3,4},{4,3},{5,6},{6,5},{7,8},{8,7},{9,10},{10,... | collective-permute-start | bytes 3145736 | tf_op jit(solution)/shard_map/ppermute | solution.py:418
  104.2 26.0 %collective-permute-start.19 = (f32[8,256,128]{2,1,0:T(8,128)}, f32[8,256,128]{2,1,0:T(8,128)S(1)}, u32[]{:S(2)}, u32[]{:S(2)}) collective-permute-start(f32[8,256,128]{2,1,0:T(8,128)} %get-tuple-element.37.f_ref), channel_id=1, source_target_pairs={{0,1},{1,0},{2,3},{3,2},{4,5},{5,4},{6,7},{7,6},{8,9},{9,8},{10,11... | collective-permute-start | bytes 3145736 | tf_op jit(solution)/shard_map/ppermute | solution.py:418
  107.8 4.6 %collective-permute-start.14 = (f32[8,128]{1,0:T(8,128)S(1)}, f32[8,128]{1,0:T(8,128)S(1)}, u32[]{:S(2)}, u32[]{:S(2)}) collective-permute-start(f32[8,128]{1,0:T(8,128)S(1)} %shard_map.47.sums_ref.own_ref), channel_id=1, source_target_pairs={{0,32},{32,0},{1,33},{33,1},{2,34},{34,2},{3,35},{35,3},{4,36},{36... | collective-permute-start | bytes 12296 | tf_op jit(solution)/shard_map/ppermute | solution.py:501
  112.5 2.9 %collective-permute-start.15 = (f32[2,8,128]{2,1,0:T(8,128)S(1)}, f32[2,8,128]{2,1,0:T(8,128)S(1)}, u32[]{:S(2)}, u32[]{:S(2)}) collective-permute-start(f32[2,8,128]{2,1,0:T(8,128)S(1)} %maximum_select_fusion), channel_id=1, source_target_pairs={{0,128},{32,160},{1,129},{33,161},{2,130},{34,162},{3,131},{35,163... | collective-permute-start | bytes 24584 | tf_op jit(solution)/shard_map/ppermute | solution.py:504
  115.5 2.1 %collective-permute-start.16 = (f32[2,8,128]{2,1,0:T(8,128)S(1)}, f32[2,8,128]{2,1,0:T(8,128)S(1)}, u32[]{:S(2)}, u32[]{:S(2)}) collective-permute-start(f32[2,8,128]{2,1,0:T(8,128)S(1)} %fusion.2), channel_id=1, source_target_pairs={{0,64},{32,96},{128,192},{160,224},{1,65},{33,97},{129,193},{161,2... | collective-permute-start | bytes 24584 | tf_op jit(solution)/shard_map/ppermute | solution.py:505
  117.5 8.3 %collective-permute-start.17 = (f32[2,8,128]{2,1,0:T(8,128)S(1)}, f32[2,8,128]{2,1,0:T(8,128)S(1)}, u32[]{:S(2)}, u32[]{:S(2)}) collective-permute-start(f32[2,8,128]{2,1,0:T(8,128)S(1)} %fusion.3.near_ref), channel_id=1, source_target_pairs={{0,256},{32,288},{64,320},{96,352},{128,384},{160,416},{192,448},{... | collective-permute-start | bytes 24584 | tf_op jit(solution)/shard_map/ppermute | solution.py:506
  121.8 1.3 copy-start.1
  123.0 4.4 %copy-start.2 = (f32[8,256,128]{2,1,0:T(8,128)S(1)}, f32[8,256,128]{2,1,0:T(8,128)}, u32[]{:S(2)}) copy-start(f32[8,256,128]{2,1,0:T(8,128)} %get-tuple-element.37.f_ref) | copy-start | bytes 3145732

commit v18 on v17

--- a/solution.py
+++ b/solution.py
@@ -10,14 +10,15 @@
 RING = 8
 F32 = jnp.float32
 VMEM = pl.BlockSpec(memory_space=pltpu.VMEM)
-
-
-def call(kernel, outs, scratch=(), specs=None, flops=0, bytes_moved=0):
+ANY = pl.BlockSpec(memory_space=pl.ANY)
+
+
+def call(kernel, outs, scratch=(), specs=None, flops=0, bytes_moved=0, out_specs=None):
     return pl.pallas_call(
         kernel,
         out_shape=outs,
         in_specs=specs,
-        out_specs=jax.tree.map(lambda _: VMEM, outs),
+        out_specs=out_specs or jax.tree.map(lambda _: VMEM, outs),
         scratch_shapes=scratch,
         compiler_params=pltpu.CompilerParams(vmem_limit_bytes=32 * 1024 * 1024),
         cost_estimate=pl.CostEstimate(flops=flops, bytes_accessed=bytes_moved, transcendentals=0),
@@ -146,7 +147,7 @@
 
 
 def combine_kernel(sums_ref, *refs):
-    *pieces, own, out, weights_ref, gram_ref, splat = refs
+    *pieces, own, result, weights_ref, gram_ref, splat, out, sems = refs
     band = lax.axis_index("band")
     lane, sub = lanes(), subs()
     tiles = unpacked(sums_ref[...])
@@ -205,6 +206,10 @@
         splat[c] = spread_lane(weights, 24 + c)
     rows = rows_of(pieces) + [(own, i) for i in range(BLK)]
 
+    def copy(c):
+        part = pl.ds(pl.multiple_of(c * 32, 32), 32)
+        return pltpu.make_async_copy(out.at[:, part, :], result.at[:, part, :], sems.at[c])
+
     def combine(places, plus_own):
         def body(c, carry):
             part = pl.ds(pl.multiple_of(c * 32, 32), 32)
@@ -221,6 +226,7 @@
                     ]
                 for k in range(4):
                     out[low + k, part, :] = totals[k]
+            copy(c).start()
             return carry
 
         lax.fori_loop(0, own.shape[1] // 32, body, 0)
@@ -228,6 +234,8 @@
     pl.when(later)(lambda: combine(range(16), True))
     pl.when(second)(lambda: combine((*BLOCK0_ROWS, *OWN), False))
     pl.when(band == 0)(lambda: combine(OWN, False))
+    for c in range(8):
+        copy(c).wait()
 
 
 def inner_kernel(f_ref, v_ref, out, *sums):
@@ -375,7 +383,10 @@
     lax.fori_loop(0, f_ref.shape[1] // 32, body, 0)
 
 
-def edge_kernel(partial, across, beside, out):
+def edge_kernel(partial, across, beside, result, out, sems):
+    def copy(i):
+        return pltpu.make_async_copy(out.at[i], result.at[i], sems.at[i])
+
     def run(left, right):
         def body(i, carry):
             for x in range(4):
@@ -386,6 +397,7 @@
                     lambda n: left[i, pl.ds(64 * n, 64), :],
                     lambda n: right[i, pl.ds(64 * n, 64), :],
                 )
+            copy(i).start()
             return carry
 
         lax.fori_loop(0, BLK, body, 0)
@@ -393,6 +405,8 @@
     odd = lax.axis_index("domain") & 1
     pl.when(odd == 0)(lambda: run(across, beside))
     pl.when(odd == 1)(lambda: run(beside, across))
+    for i in range(BLK):
+        copy(i).wait()
 
 
 def domain_parts(copies):
@@ -490,7 +504,12 @@
     basis, weights, gram = call(
         combine_kernel,
         (slab, tile, tile),
-        scratch=[pltpu.VMEM((24, 8, 128), F32)],
+        scratch=[
+            pltpu.VMEM((24, 8, 128), F32),
+            pltpu.VMEM(flat, F32),
+            pltpu.SemaphoreType.DMA((8,)),
+        ],
+        out_specs=(ANY, VMEM, VMEM),
         specs=[VMEM] * 11,
         flops=48 * big,
         bytes_moved=16 * big,
@@ -512,7 +531,13 @@
         partial_kernel, slab, specs=[VMEM] * 3, flops=16 * big, bytes_moved=12 * big
     )(basis, inner, splat)
     residual = call(
-        edge_kernel, slab, specs=[VMEM] * 3, flops=20 * big, bytes_moved=16 * big
+        edge_kernel,
+        slab,
+        scratch=[pltpu.VMEM(flat, F32), pltpu.SemaphoreType.DMA((BLK,))],
+        specs=[VMEM] * 3,
+        out_specs=ANY,
+        flops=20 * big,
+        bytes_moved=16 * big,
     )(partial, across, beside)
     return (basis.reshape(orbitals.shape), residual.reshape(orbitals.shape))
 

time: 132 us -> 132 us (level)
  no operation moved by 1% of the time
where the time goes in v18:
time: 132 us; the launch traced here: 131 us
  starting transfers between devices  55.6 us (42%)
  waiting for transfers between devices  29.8 us (23%)
  blocking collectives  21.2 us (16%)
  Pallas kernels  20.8 us (16%)
  other arithmetic  1.49 us (1%)
    ppermute x8, starting transfers between devices, ring_shift(): return lax.ppermute(block, 'band', pairs)  23 us
    all_to_all x1, blocking collectives, domain_parts(): return lax.all_to_all(copies, 'domain', 0, 0)  21.2 us
    ppermute x3, waiting for transfers between devices, local(): lax.ppermute(quarters[k], 'band', [(0, 2 * k), (1, 2 * k + 1)])  11.6 us
    ppermute x3, starting transfers between devices, local(): lax.ppermute(quarters[k], 'band', [(0, 2 * k), (1, 2 * k + 1)])  9.65 us
    ppermute x8, waiting for transfers between devices, ring_shift(): return lax.ppermute(block, 'band', pairs)  6.34 us
    pallas_call x4, Pallas kernels, stage(): call(lambda *refs: stage_kernel(len(pieces), fresh, imaged, last, *refs),...  6.12 us
    pallas_call x2, Pallas kernels, inner_part(): call(inner_kernel, (field, *sums), specs=[VMEM] * 2, flops=60 * big, byte...  6.04 us
    ppermute x1, waiting for transfers between devices, neighbours(): lax.ppermute(block, 'domain', [((i + 1) % count, i) for i in range(count)])  5.5 us
  transfers between devices with their start and end apart: 20, of which 11 were waited for; matrix products, arithmetic and copies ran while one was open for 0% of the time, Pallas kernels for 12%

profile of v18, /device:TPU:1, one launch (start us, length us, event | category | flops | bytes accessed | tf_op | source)
XLA Modules:
  0.0 131.1 jit_solution(6208058814040114767)
XLA Ops:
  2.0 5.1 %collective-permute-start = (f32[2,256,128]{2,1,0:T(8,128)S(1)}, f32[2,256,128]{2,1,0:T(8,128)S(1)}, u32[]{:S(2)}, u32[]{:S(2)}) collective-permute-start(f32[2,256,128]{2,1,0:T(8,128)S(1)} %bitcast.33), channel_id=1, source_target_pairs={{0,64},{32,96},{1,65},{33,97},{2,66},{34,98},{3,67},{35,99},{4,68}... | collective-permute-start | bytes 786440 | tf_op jit(solution)/shard_map/ppermute | solution.py:458
  7.1 2.3 %collective-permute-start.1 = (f32[2,256,128]{2,1,0:T(8,128)S(1)}, f32[2,256,128]{2,1,0:T(8,128)S(1)}, u32[]{:S(2)}, u32[]{:S(2)}) collective-permute-start(f32[2,256,128]{2,1,0:T(8,128)S(1)} %bitcast.32), channel_id=1, source_target_pairs={{0,192},{32,224},{1,193},{33,225},{2,194},{34,226},{3,195},{35,227... | collective-permute-start | bytes 786440 | tf_op jit(solution)/shard_map/ppermute | solution.py:458
  9.5 2.2 %collective-permute-start.2 = (f32[2,256,128]{2,1,0:T(8,128)S(1)}, f32[2,256,128]{2,1,0:T(8,128)S(1)}, u32[]{:S(2)}, u32[]{:S(2)}) collective-permute-start(f32[2,256,128]{2,1,0:T(8,128)S(1)} %bitcast.31), channel_id=1, source_target_pairs={{0,128},{32,160},{1,129},{33,161},{2,130},{34,162},{3,131},{35,163... | collective-permute-start | bytes 786440 | tf_op jit(solution)/shard_map/ppermute | solution.py:458
  11.7 3.3 %shard_map.41 = (f32[8,4,64,128]{3,2,1,0:T(8,128)S(1)}, f32[8,128]{1,0:T(8,128)S(1)}) custom-call(f32[8,4,64,128]{3,2,1,0:T(8,128)S(1)} %copy-done, f32[4,64,128]{2,1,0:T(8,128)S(1)} %copy-done.3), custom_call_target="tpu_custom_call" | custom-call | flops 15728640 | bytes 2097152 | tf_op jit(solution)/shard_map/pallas_call | solution.py:447
  15.0 11.5 %collective-permute-done.1 = f32[2,256,128]{2,1,0:T(8,128)S(1)} collective-permute-done((f32[2,256,128]{2,1,0:T(8,128)S(1)}, f32[2,256,128]{2,1,0:T(8,128)S(1)}, u32[]{:S(2)}, u32[]{:S(2)}) %collective-permute-start.1) | collective-permute-done | bytes 262176 | tf_op jit(solution)/shard_map/ppermute | solution.py:458
  26.6 2.0 %collective-permute-start.3 = (f32[2,256,128]{2,1,0:T(8,128)S(1)}, f32[2,256,128]{2,1,0:T(8,128)}, u32[]{:S(2)}, u32[]{:S(2)}) collective-permute-start(f32[2,256,128]{2,1,0:T(8,128)S(1)} %fusion.1), channel_id=1, source_target_pairs={{0,256},{32,288},{64,320},{96,352},{128,384},{160,416},{192,448},{... | collective-permute-start | bytes 786440 | tf_op jit(solution)/shard_map/ppermute | solution.py:466
  28.6 4.5 %collective-permute-start.10 = (f32[8,256,128]{2,1,0:T(8,128)S(1)}, f32[8,256,128]{2,1,0:T(8,128)S(1)}, u32[]{:S(2)}, u32[]{:S(2)}) collective-permute-start(f32[8,256,128]{2,1,0:T(8,128)S(1)} %bitcast.18), channel_id=1, source_target_pairs={{0,1},{1,2},{2,3},{3,4},{4,5},{5,6},{6,7},{7,8},{8,9},{9,10},{10,1... | collective-permute-start | bytes 3145736 | tf_op jit(solution)/shard_map/ppermute | solution.py:423
  37.0 3.4 %collective-permute-start.4 = (f32[2,256,128]{2,1,0:T(8,128)S(1)}, f32[2,256,128]{2,1,0:T(8,128)S(1)}, u32[]{:S(2)}, u32[]{:S(2)}) collective-permute-start(f32[2,256,128]{2,1,0:T(8,128)S(1)} %broadcast_select_fusion.refs_0_), channel_id=1, source_target_pairs={{0,32},{32,64},{64,96},{96,128},{128,160},{160,192},{192,224},{224... | collective-permute-start | bytes 786440 | tf_op jit(solution)/shard_map/ppermute | solution.py:418
  40.4 2.1 %collective-permute-done.5.refs_2_ = f32[2,256,128]{2,1,0:T(8,128)S(1)} collective-permute-done((f32[2,256,128]{2,1,0:T(8,128)S(1)}, f32[2,256,128]{2,1,0:T(8,128)S(1)}, u32[]{:S(2)}, u32[]{:S(2)}) %collective-permute-start.5) | collective-permute-done | bytes 262176 | tf_op jit(solution)/shard_map/ppermute | solution.py:418
  42.5 4.3 %collective-permute-start.7 = (f32[2,256,128]{2,1,0:T(8,128)S(1)}, f32[2,256,128]{2,1,0:T(8,128)S(1)}, u32[]{:S(2)}, u32[]{:S(2)}) collective-permute-start(f32[2,256,128]{2,1,0:T(8,128)S(1)} %collective-permute-done.5.refs_2_), channel_id=1, source_target_pairs={{0,224},{32,0},{64,32},{96,64},{128,96},{160,128},{192,160},{224,1... | collective-permute-start | bytes 786440 | tf_op jit(solution)/shard_map/ppermute | solution.py:418
  51.5 4.3 %collective-permute-start.9 = (f32[2,256,128]{2,1,0:T(8,128)S(1)}, f32[2,256,128]{2,1,0:T(8,128)S(1)}, u32[]{:S(2)}, u32[]{:S(2)}) collective-permute-start(f32[2,256,128]{2,1,0:T(8,128)S(1)} %collective-permute-done.7.refs_4_), channel_id=1, source_target_pairs={{0,224},{32,0},{64,32},{96,64},{128,96},{160,128},{192,160},{224,1... | collective-permute-start | bytes 786440 | tf_op jit(solution)/shard_map/ppermute | solution.py:418
  59.4 5.5 %collective-permute-done.11.right = f32[8,256,128]{2,1,0:T(8,128)} collective-permute-done((f32[8,256,128]{2,1,0:T(8,128)S(1)}, f32[8,256,128]{2,1,0:T(8,128)}, u32[]{:S(2)}, u32[]{:S(2)}) %collective-permute-start.11) | collective-permute-done | bytes 1048608 | tf_op jit(solution)/shard_map/ppermute | solution.py:424
  66.9 3.4 %collective-permute-start.12 = (f32[1,256,128]{2,1,0:T(8,128)S(1)}, f32[1,256,128]{2,1,0:T(8,128)S(1)}, u32[]{:S(2)}, u32[]{:S(2)}) collective-permute-start(f32[1,256,128]{2,1,0:T(8,128)S(1)} %slice.37), channel_id=1, source_target_pairs={{0,32},{32,64},{64,96},{96,128},{128,160},{160,192},{192,224},{224... | collective-permute-start | bytes 393224 | tf_op jit(solution)/shard_map/ppermute | solution.py:418
  70.3 2.2 %shard_map.44 = (f32[8,256,128]{2,1,0:T(8,128)S(1)}, f32[8,128]{1,0:T(8,128)S(1)}) custom-call(f32[8,256,128]{2,1,0:T(8,128)S(1)} %bitcast.22, f32[8,256,128]{2,1,0:T(8,128)S(1)} %bitcast.29, f32[8,256,128]{2,1,0:T(8,128)S(1)} %collective-permute-done.10.left, f32[8,256,128]{2,1,0:T(8,128)} %collective-permute-done.11.right), custom_call_target="tpu_custom_call" | custom-call | flops 13107200 | bytes 5242880 | tf_op jit(solution)/shard_map/pallas_call | solution.py:491
  72.5 3.0 %shard_map.45.refs_11_ = f32[8,128]{1,0:T(8,128)S(1)} custom-call(f32[2,256,128]{2,1,0:T(8,128)S(1)} %broadcast_select_fusion.refs_0_, f32[2,256,128]{2,1,0:T(8,128)S(1)} %collective-permute-done.4.refs_1_, f32[2,256,128]{2,1,0:T(8,128)S(1)} %collective-permute-done.5.refs_2_, f32[2,256,128]{2,1,0:T(8,128)S(1)} %collective-permute-done.6.refs_3_, ...), custom_call_target="tpu_custom_call" | custom-call | flops 5242880 | bytes 2621440 | tf_op jit(solution)/shard_map/pallas_call | solution.py:471
  78.3 21.2 %all_to_all.5.refs_0_ = f32[32,8,128]{2,1,0:T(8,128)S(1)} all-to-all(f32[32,8,128]{2,1,0:T(8,128)S(1)} %shard_map.46), channel_id=1, replica_groups=mesh['band'=16,'domain'=32] {'domain'}, dimensions={0} | all-to-all | bytes 262144 | tf_op jit(solution)/shard_map/all_to_all | solution.py:413
  99.6 2.3 %shard_map.48 = (f32[8,256,128]{2,1,0:T(8,128)}, f32[8,128]{1,0:T(8,128)S(1)}, f32[8,128]{1,0:T(8,128)S(1)}) custom-call(f32[8,128]{1,0:T(8,128)S(1)} %shard_map.47.sums_ref.own_ref, f32[2,256,128]{2,1,0:T(8,128)S(1)} %broadcast_select_fusion.refs_0_, f32[2,256,128]{2,1,0:T(8,128)S(1)} %collective-permute-done.4.refs_1_, ...), custom_call_target="tpu_custom_call" | custom-call | flops 12582912 | bytes 4194304 | tf_op jit(solution)/shard_map/pallas_call | solution.py:504
  101.8 2.1 %collective-permute-start.18 = (f32[8,256,128]{2,1,0:T(8,128)}, f32[8,256,128]{2,1,0:T(8,128)S(1)}, u32[]{:S(2)}, u32[]{:S(2)}) collective-permute-start(f32[8,256,128]{2,1,0:T(8,128)} %get-tuple-element.37.f_ref), channel_id=1, source_target_pairs={{0,31},{1,2},{2,1},{3,4},{4,3},{5,6},{6,5},{7,8},{8,7},{9,10},{10,... | collective-permute-start | bytes 3145736 | tf_op jit(solution)/shard_map/ppermute | solution.py:432
  103.9 3.7 %collective-permute-start.19 = (f32[8,256,128]{2,1,0:T(8,128)}, f32[8,256,128]{2,1,0:T(8,128)S(1)}, u32[]{:S(2)}, u32[]{:S(2)}) collective-permute-start(f32[8,256,128]{2,1,0:T(8,128)} %get-tuple-element.37.f_ref), channel_id=1, source_target_pairs={{0,1},{1,0},{2,3},{3,2},{4,5},{5,4},{6,7},{7,6},{8,9},{9,8},{10,11... | collective-permute-start | bytes 3145736 | tf_op jit(solution)/shard_map/ppermute | solution.py:432
  109.6 2.7 %collective-permute-done.14 = f32[8,128]{1,0:T(8,128)S(1)} collective-permute-done((f32[8,128]{1,0:T(8,128)S(1)}, f32[8,128]{1,0:T(8,128)S(1)}, u32[]{:S(2)}, u32[]{:S(2)}) %collective-permute-start.14) | collective-permute-done | bytes 4128 | tf_op jit(solution)/shard_map/ppermute | solution.py:520
  112.3 2.2 %collective-permute-start.15 = (f32[2,8,128]{2,1,0:T(8,128)S(1)}, f32[2,8,128]{2,1,0:T(8,128)S(1)}, u32[]{:S(2)}, u32[]{:S(2)}) collective-permute-start(f32[2,8,128]{2,1,0:T(8,128)S(1)} %maximum_select_fusion), channel_id=1, source_target_pairs={{0,128},{32,160},{1,129},{33,161},{2,130},{34,162},{3,131},{35,163... | collective-permute-start | bytes 24584 | tf_op jit(solution)/shard_map/ppermute | solution.py:523
  117.3 3.5 %collective-permute-start.17 = (f32[2,8,128]{2,1,0:T(8,128)S(1)}, f32[2,8,128]{2,1,0:T(8,128)S(1)}, u32[]{:S(2)}, u32[]{:S(2)}) collective-permute-start(f32[2,8,128]{2,1,0:T(8,128)S(1)} %fusion.3.near_ref), channel_id=1, source_target_pairs={{0,256},{32,288},{64,320},{96,352},{128,384},{160,416},{192,448},{... | collective-permute-start | bytes 24584 | tf_op jit(solution)/shard_map/ppermute | solution.py:525
  122.8 2.7 %shard_map.49 = f32[8,4,64,128]{3,2,1,0:T(8,128)S(1)} custom-call(f32[8,4,64,128]{3,2,1,0:T(8,128)S(1)} %bitcast.27, f32[4,64,128]{2,1,0:T(8,128)S(1)} %copy-done.3), custom_call_target="tpu_custom_call" | custom-call | flops 15728640 | bytes 2097152 | tf_op jit(solution)/shard_map/pallas_call | solution.py:447
  127.9 2.1 %collective-permute-done.18.across = f32[8,256,128]{2,1,0:T(8,128)S(1)} collective-permute-done((f32[8,256,128]{2,1,0:T(8,128)}, f32[8,256,128]{2,1,0:T(8,128)S(1)}, u32[]{:S(2)}, u32[]{:S(2)}) %collective-permute-start.18) | collective-permute-done | bytes 1048608 | tf_op jit(solution)/shard_map/ppermute | solution.py:432
  (47 shorter events, 28.7 us)
Async XLA Ops:
  0.6 11.1 %copy-start = (f32[8,4,64,128]{3,2,1,0:T(8,128)S(1)}, f32[8,4,64,128]{3,2,1,0:T(8,128)}, u32[]{:S(2)}) copy-start(f32[8,4,64,128]{3,2,1,0:T(8,128)} %f_ref.1) | copy-start | bytes 3145732
  0.6 11.1 %copy-start.3 = (f32[4,64,128]{2,1,0:T(8,128)S(1)}, f32[4,64,128]{2,1,0:T(8,128)}, u32[]{:S(2)}) copy-start(f32[4,64,128]{2,1,0:T(8,128)} %v_ref.3) | copy-start | bytes 393220
  2.0 13.0 %collective-permute-start = (f32[2,256,128]{2,1,0:T(8,128)S(1)}, f32[2,256,128]{2,1,0:T(8,128)S(1)}, u32[]{:S(2)}, u32[]{:S(2)}) collective-permute-start(f32[2,256,128]{2,1,0:T(8,128)S(1)} %bitcast.33), channel_id=1, source_target_pairs={{0,64},{32,96},{1,65},{33,97},{2,66},{34,98},{3,67},{35,99},{4,68}... | collective-permute-start | bytes 786440 | tf_op jit(solution)/shard_map/ppermute | solution.py:458
  7.1 19.5 %collective-permute-start.1 = (f32[2,256,128]{2,1,0:T(8,128)S(1)}, f32[2,256,128]{2,1,0:T(8,128)S(1)}, u32[]{:S(2)}, u32[]{:S(2)}) collective-permute-start(f32[2,256,128]{2,1,0:T(8,128)S(1)} %bitcast.32), channel_id=1, source_target_pairs={{0,192},{32,224},{1,193},{33,225},{2,194},{34,226},{3,195},{35,227... | collective-permute-start | bytes 786440 | tf_op jit(solution)/shard_map/ppermute | solution.py:458
  9.5 17.1 %collective-permute-start.2 = (f32[2,256,128]{2,1,0:T(8,128)S(1)}, f32[2,256,128]{2,1,0:T(8,128)S(1)}, u32[]{:S(2)}, u32[]{:S(2)}) collective-permute-start(f32[2,256,128]{2,1,0:T(8,128)S(1)} %bitcast.31), channel_id=1, source_target_pairs={{0,128},{32,160},{1,129},{33,161},{2,130},{34,162},{3,131},{35,163... | collective-permute-start | bytes 786440 | tf_op jit(solution)/shard_map/ppermute | solution.py:458
  26.6 8.4 %collective-permute-start.3 = (f32[2,256,128]{2,1,0:T(8,128)S(1)}, f32[2,256,128]{2,1,0:T(8,128)}, u32[]{:S(2)}, u32[]{:S(2)}) collective-permute-start(f32[2,256,128]{2,1,0:T(8,128)S(1)} %fusion.1), channel_id=1, source_target_pairs={{0,256},{32,288},{64,320},{96,352},{128,384},{160,416},{192,448},{... | collective-permute-start | bytes 786440 | tf_op jit(solution)/shard_map/ppermute | solution.py:466
  28.6 30.8 %collective-permute-start.10 = (f32[8,256,128]{2,1,0:T(8,128)S(1)}, f32[8,256,128]{2,1,0:T(8,128)S(1)}, u32[]{:S(2)}, u32[]{:S(2)}) collective-permute-start(f32[8,256,128]{2,1,0:T(8,128)S(1)} %bitcast.18), channel_id=1, source_target_pairs={{0,1},{1,2},{2,3},{3,4},{4,5},{5,6},{6,7},{7,8},{8,9},{9,10},{10,1... | collective-permute-start | bytes 3145736 | tf_op jit(solution)/shard_map/ppermute | solution.py:423
  33.1 31.8 %collective-permute-start.11 = (f32[8,256,128]{2,1,0:T(8,128)S(1)}, f32[8,256,128]{2,1,0:T(8,128)}, u32[]{:S(2)}, u32[]{:S(2)}) collective-permute-start(f32[8,256,128]{2,1,0:T(8,128)S(1)} %bitcast.19), channel_id=1, source_target_pairs={{1,0},{2,1},{3,2},{4,3},{5,4},{6,5},{7,6},{8,7},{9,8},{10,9},{11,1... | collective-permute-start | bytes 3145736 | tf_op jit(solution)/shard_map/ppermute | solution.py:424
  35.1 7.4 %collective-permute-start.5 = (f32[2,256,128]{2,1,0:T(8,128)S(1)}, f32[2,256,128]{2,1,0:T(8,128)S(1)}, u32[]{:S(2)}, u32[]{:S(2)}) collective-permute-start(f32[2,256,128]{2,1,0:T(8,128)S(1)} %broadcast_select_fusion.refs_0_), channel_id=1, source_target_pairs={{0,224},{32,0},{64,32},{96,64},{128,96},{160,128},{192,160},{224,1... | collective-permute-start | bytes 786440 | tf_op jit(solution)/shard_map/ppermute | solution.py:418
  37.0 10.5 %collective-permute-start.4 = (f32[2,256,128]{2,1,0:T(8,128)S(1)}, f32[2,256,128]{2,1,0:T(8,128)S(1)}, u32[]{:S(2)}, u32[]{:S(2)}) collective-permute-start(f32[2,256,128]{2,1,0:T(8,128)S(1)} %broadcast_select_fusion.refs_0_), channel_id=1, source_target_pairs={{0,32},{32,64},{64,96},{96,128},{128,160},{160,192},{192,224},{224... | collective-permute-start | bytes 786440 | tf_op jit(solution)/shard_map/ppermute | solution.py:418
  42.5 9.0 %collective-permute-start.7 = (f32[2,256,128]{2,1,0:T(8,128)S(1)}, f32[2,256,128]{2,1,0:T(8,128)S(1)}, u32[]{:S(2)}, u32[]{:S(2)}) collective-permute-start(f32[2,256,128]{2,1,0:T(8,128)S(1)} %collective-permute-done.5.refs_2_), channel_id=1, source_target_pairs={{0,224},{32,0},{64,32},{96,64},{128,96},{160,128},{192,160},{224,1... | collective-permute-start | bytes 786440 | tf_op jit(solution)/shard_map/ppermute | solution.py:418
  47.6 9.0 %collective-permute-start.6 = (f32[2,256,128]{2,1,0:T(8,128)S(1)}, f32[2,256,128]{2,1,0:T(8,128)S(1)}, u32[]{:S(2)}, u32[]{:S(2)}) collective-permute-start(f32[2,256,128]{2,1,0:T(8,128)S(1)} %collective-permute-done.4.refs_1_), channel_id=1, source_target_pairs={{0,32},{32,64},{64,96},{96,128},{128,160},{160,192},{192,224},{224... | collective-permute-start | bytes 786440 | tf_op jit(solution)/shard_map/ppermute | solution.py:418
  51.5 13.5 %collective-permute-start.9 = (f32[2,256,128]{2,1,0:T(8,128)S(1)}, f32[2,256,128]{2,1,0:T(8,128)S(1)}, u32[]{:S(2)}, u32[]{:S(2)}) collective-permute-start(f32[2,256,128]{2,1,0:T(8,128)S(1)} %collective-permute-done.7.refs_4_), channel_id=1, source_target_pairs={{0,224},{32,0},{64,32},{96,64},{128,96},{160,128},{192,160},{224,1... | collective-permute-start | bytes 786440 | tf_op jit(solution)/shard_map/ppermute | solution.py:418
  56.6 10.3 %collective-permute-start.8 = (f32[2,256,128]{2,1,0:T(8,128)S(1)}, f32[2,256,128]{2,1,0:T(8,128)S(1)}, u32[]{:S(2)}, u32[]{:S(2)}) collective-permute-start(f32[2,256,128]{2,1,0:T(8,128)S(1)} %collective-permute-done.6.refs_3_), channel_id=1, source_target_pairs={{0,32},{32,64},{64,96},{96,128},{128,160},{160,192},{192,224},{224... | collective-permute-start | bytes 786440 | tf_op jit(solution)/shard_map/ppermute | solution.py:418
  65.0 10.5 %collective-permute-start.13 = (f32[1,256,128]{2,1,0:T(8,128)S(1)}, f32[1,256,128]{2,1,0:T(8,128)S(1)}, u32[]{:S(2)}, u32[]{:S(2)}) collective-permute-start(f32[1,256,128]{2,1,0:T(8,128)S(1)} %slice.36), channel_id=1, source_target_pairs={{0,224},{32,0},{64,32},{96,64},{128,96},{160,128},{192,160},{224,1... | collective-permute-start | bytes 393224 | tf_op jit(solution)/shard_map/ppermute | solution.py:418
  66.9 10.3 %collective-permute-start.12 = (f32[1,256,128]{2,1,0:T(8,128)S(1)}, f32[1,256,128]{2,1,0:T(8,128)S(1)}, u32[]{:S(2)}, u32[]{:S(2)}) collective-permute-start(f32[1,256,128]{2,1,0:T(8,128)S(1)} %slice.37), channel_id=1, source_target_pairs={{0,32},{32,64},{64,96},{96,128},{128,160},{160,192},{192,224},{224... | collective-permute-start | bytes 393224 | tf_op jit(solution)/shard_map/ppermute | solution.py:418
  101.8 28.1 %collective-permute-start.18 = (f32[8,256,128]{2,1,0:T(8,128)}, f32[8,256,128]{2,1,0:T(8,128)S(1)}, u32[]{:S(2)}, u32[]{:S(2)}) collective-permute-start(f32[8,256,128]{2,1,0:T(8,128)} %get-tuple-element.37.f_ref), channel_id=1, source_target_pairs={{0,31},{1,2},{2,1},{3,4},{4,3},{5,6},{6,5},{7,8},{8,7},{9,10},{10,... | collective-permute-start | bytes 3145736 | tf_op jit(solution)/shard_map/ppermute | solution.py:432
  103.9 26.0 %collective-permute-start.19 = (f32[8,256,128]{2,1,0:T(8,128)}, f32[8,256,128]{2,1,0:T(8,128)S(1)}, u32[]{:S(2)}, u32[]{:S(2)}) collective-permute-start(f32[8,256,128]{2,1,0:T(8,128)} %get-tuple-element.37.f_ref), channel_id=1, source_target_pairs={{0,1},{1,0},{2,3},{3,2},{4,5},{5,4},{6,7},{7,6},{8,9},{9,8},{10,11... | collective-permute-start | bytes 3145736 | tf_op jit(solution)/shard_map/ppermute | solution.py:432
  107.6 4.6 %collective-permute-start.14 = (f32[8,128]{1,0:T(8,128)S(1)}, f32[8,128]{1,0:T(8,128)S(1)}, u32[]{:S(2)}, u32[]{:S(2)}) collective-permute-start(f32[8,128]{1,0:T(8,128)S(1)} %shard_map.47.sums_ref.own_ref), channel_id=1, source_target_pairs={{0,32},{32,0},{1,33},{33,1},{2,34},{34,2},{3,35},{35,3},{4,36},{36... | collective-permute-start | bytes 12296 | tf_op jit(solution)/shard_map/ppermute | solution.py:520
  112.3 2.9 %collective-permute-start.15 = (f32[2,8,128]{2,1,0:T(8,128)S(1)}, f32[2,8,128]{2,1,0:T(8,128)S(1)}, u32[]{:S(2)}, u32[]{:S(2)}) collective-permute-start(f32[2,8,128]{2,1,0:T(8,128)S(1)} %maximum_select_fusion), channel_id=1, source_target_pairs={{0,128},{32,160},{1,129},{33,161},{2,130},{34,162},{3,131},{35,163... | collective-permute-start | bytes 24584 | tf_op jit(solution)/shard_map/ppermute | solution.py:523
  115.2 2.1 %collective-permute-start.16 = (f32[2,8,128]{2,1,0:T(8,128)S(1)}, f32[2,8,128]{2,1,0:T(8,128)S(1)}, u32[]{:S(2)}, u32[]{:S(2)}) collective-permute-start(f32[2,8,128]{2,1,0:T(8,128)S(1)} %fusion.2), channel_id=1, source_target_pairs={{0,64},{32,96},{128,192},{160,224},{1,65},{33,97},{129,193},{161,2... | collective-permute-start | bytes 24584 | tf_op jit(solution)/shard_map/ppermute | solution.py:524
  117.3 8.3 %collective-permute-start.17 = (f32[2,8,128]{2,1,0:T(8,128)S(1)}, f32[2,8,128]{2,1,0:T(8,128)S(1)}, u32[]{:S(2)}, u32[]{:S(2)}) collective-permute-start(f32[2,8,128]{2,1,0:T(8,128)S(1)} %fusion.3.near_ref), channel_id=1, source_target_pairs={{0,256},{32,288},{64,320},{96,352},{128,384},{160,416},{192,448},{... | collective-permute-start | bytes 24584 | tf_op jit(solution)/shard_map/ppermute | solution.py:525
  121.6 1.3 copy-start.1
  122.8 4.4 %copy-start.2 = (f32[8,256,128]{2,1,0:T(8,128)S(1)}, f32[8,256,128]{2,1,0:T(8,128)}, u32[]{:S(2)}) copy-start(f32[8,256,128]{2,1,0:T(8,128)} %get-tuple-element.37.f_ref) | copy-start | bytes 3145732
